TPU v7x, 32 devices: a whole 2x2x4 slice. The times are simulated.
32 devices in a mesh: groups: 2 (over y), dp: 4 (over z), section: 2 (over x), tensor: 2 (over core).
Axes of the slice: x: 2, y: 2, z: 4, core: 2. Of those that a mesh axis runs over, the one named last changes fastest.
Arguments:
- cotangent: bfloat16 [2, 1024, 2048], P('section', ('groups', 'dp')), parts along dimension 1, may hold values from -6 to 6
- routes: int32 [2, 8, 2], P('section', ('groups', 'dp')), parts along dimension 1, may hold values from 0 to 3, all different within a row
- gate_values: float32 [2, 1024, 2], P('section', ('groups', 'dp')), parts along dimension 1, may hold values from 0.1 to 0.9
- up_weight: bfloat16 [2, 4, 2048, 7168], P('section', 'dp', None, 'tensor'), may hold values from -0.125 to 0.125
- down_weight: bfloat16 [2, 4, 7168, 2048], P('section', 'dp', 'tensor'), may hold values from -0.0625 to 0.0625
- pre_activation: bfloat16 [2, 8, 4, 128, 7168], P('section', ('groups', 'dp'), None, None, 'tensor'), parts along dimension 1, may hold values from -6 to 6
- input_sketch: float32 [2, 1024, 64], P('section', ('groups', 'dp')), parts along dimension 1, may hold values from -6 to 6
- model_sketch: bfloat16 [2, 2048, 64], P('section'), may hold values from -0.125 to 0.125
- hidden_sketch: bfloat16 [2, 4, 7168, 64], P('section', 'dp', 'tensor'), may hold values from -0.0625 to 0.0625
- lengths: int32 [2, 8, 4], P('section', ('groups', 'dp')), parts along dimension 1, may hold values from 1 to 64, 128 in all within a row
Outputs:
- handed: bfloat16 [2, 1024, 2048], P('section', ('groups', 'dp')), parts along dimension 1
- features: float32 [2, 32, 64, 128], P('section', ('groups', 'dp')), parts along dimension 1
There are 2 independent parts, one for each index of `groups`. A program takes and returns all parts, laid end to end along the dimension named above; an argument that names none is the same for every part. Nothing has to cross between parts.
Inputs may be any that keep to these rules, and one draw needn't show every extreme that they name: `routes`: the two experts of a block differ. `lengths`: each row of counts sums to 128, and its largest is 64.
All inputs are finite; a program needn't handle non-finite values.
Results may differ from a plain program's by a relative error of at most 0.0037.
Values may be sent and summed in bfloat16 or wider, within the bound.
No kernel may reach another device: no remote copies, remote signals or barrier semaphores. Data moves between devices by JAX's collectives and lax.ppermute only.
A program may use at most 128 MiB of HBM per device.

v0:
```python
import functools

import jax
import jax.numpy as jnp
from jax import lax
from jax.experimental import pallas as pl
from jax.experimental.pallas import tpu as pltpu
from jax.sharding import PartitionSpec as P

EXPERTS = 4
CHUNKS = 2
NT = (((1,), (1,)), ((), ()))


def xored(block, axis, bits):
    n = lax.axis_size(axis)
    return lax.ppermute(block, axis, [(i, i ^ bits) for i in range(n)])


ANYWHERE = pl.BlockSpec(memory_space=pl.ANY)
RESIDENT = pl.BlockSpec(memory_space=pltpu.VMEM)


def held_kernel(block_ref, *refs):
    refs[-1][...] = block_ref[...]


def held(block, *events):
    return pl.pallas_call(
        held_kernel,
        in_specs=[RESIDENT] + [ANYWHERE] * len(events),
        out_specs=RESIDENT,
        out_shape=jax.ShapeDtypeStruct(block.shape, block.dtype),
        compiler_params=pltpu.CompilerParams(vmem_limit_bytes=1 << 20),
        name="held",
    )(block, *events)


def merge_kernel(keep_ref, came_ref, own_ref, *sent_refs):
    rows = own_ref.shape[0]
    own_ref[...] = keep_ref[:rows] + came_ref[:rows].astype(jnp.float32)
    for at, sent_ref in enumerate(sent_refs):
        part = slice((at + 1) * rows, (at + 2) * rows)
        total = keep_ref[part] + came_ref[part].astype(jnp.float32)
        sent_ref[...] = total.astype(jnp.bfloat16)


def merged(keep, came, rows):
    count, wide = keep.shape
    others = count // rows - 1
    return pl.pallas_call(
        merge_kernel,
        in_specs=[RESIDENT] * 2,
        out_specs=[RESIDENT] * (1 + others),
        out_shape=[jax.ShapeDtypeStruct((rows, wide), jnp.float32)]
        + [jax.ShapeDtypeStruct((rows, wide), jnp.bfloat16)] * others,
        compiler_params=pltpu.CompilerParams(vmem_limit_bytes=4 << 20),
        cost_estimate=pl.CostEstimate(
            flops=count * wide, bytes_accessed=8 * count * wide, transcendentals=0
        ),
        name="merge",
    )(keep, came)


def finish_kernel(slots, own_ref, cot_ref, weight_ref, *refs):
    grad_ref, vec_ref = refs[-2:]
    width = grad_ref.shape[1]
    total = weight_ref[:, :1] * own_ref[...]
    for slot in range(1, slots):
        total += weight_ref[:, slot : slot + 1] * refs[slot - 1][...].astype(jnp.float32)
    grad_ref[...] = (cot_ref[...].astype(jnp.float32) + total[:, :width]).astype(jnp.bfloat16)
    vec_ref[...] = total[:, width:]


def finished(own, cot, weight, backs, *events):
    rows, wide = own.shape
    width = cot.shape[1]
    return pl.pallas_call(
        functools.partial(finish_kernel, 1 + len(backs)),
        in_specs=[RESIDENT] * (3 + len(backs)) + [ANYWHERE] * len(events),
        out_specs=[RESIDENT] * 2,
        out_shape=[
            jax.ShapeDtypeStruct((rows, width), jnp.bfloat16),
            jax.ShapeDtypeStruct((rows, wide - width), jnp.float32),
        ],
        compiler_params=pltpu.CompilerParams(vmem_limit_bytes=4 << 20),
        cost_estimate=pl.CostEstimate(
            flops=8 * rows * wide, bytes_accessed=12 * rows * wide, transcendentals=0
        ),
        name="finish",
    )(own, cot, weight, *backs, *events)


def tile_of(size, most):
    best = 128
    for tile in range(128, most + 1, 128):
        if size % tile == 0:
            best = tile
    return best


def slope_kernel(groups, index_ref, *refs):
    del index_ref
    pre_refs, sketch_ref = refs[:groups], refs[groups]
    slope_ref, down_ref = refs[-2:]
    pre = jnp.concatenate([r[0, 0, 0] for r in pre_refs], axis=0).astype(jnp.float32)
    sig = 0.5 + 0.5 * jnp.tanh(0.5 * pre)
    hidden = pre * sig
    slope = sig + hidden * (1.0 - sig)
    slope_ref[0] = slope.T.astype(slope_ref.dtype)
    term = lax.dot_general(
        hidden.astype(jnp.bfloat16), sketch_ref[...], NT, preferred_element_type=jnp.float32
    )

    @pl.when(pl.program_id(1) == 0)
    def _():
        down_ref[...] = jnp.zeros_like(down_ref)

    down_ref[0] += term


def slopes(pre, sketch_t, place, core):
    n, _, chunks, rows, cols = pre.shape
    rank = sketch_t.shape[0]
    groups = 2 * n
    tile = tile_of(cols, 896)
    index = jnp.stack([place, core]).astype(jnp.int32)

    def spec_of(h, slot):
        return pl.BlockSpec(
            (1, 1, 1, rows, tile), lambda a, j, ix: (ix[0] ^ slot, ix[1] ^ h, a, 0, j)
        )

    return pl.pallas_call(
        functools.partial(slope_kernel, groups),
        grid_spec=pltpu.PrefetchScalarGridSpec(
            num_scalar_prefetch=1,
            grid=(chunks, cols // tile),
            in_specs=[spec_of(h, slot) for h in range(2) for slot in range(n)]
            + [pl.BlockSpec((rank, tile), lambda a, j, ix: (0, j))],
            out_specs=[
                pl.BlockSpec((1, tile, groups * rows), lambda a, j, ix: (a, j, 0)),
                pl.BlockSpec((1, groups * rows, rank), lambda a, j, ix: (a, 0, 0)),
            ],
        ),
        out_shape=[
            jax.ShapeDtypeStruct((chunks, cols, groups * rows), jnp.bfloat16),
            jax.ShapeDtypeStruct((chunks, groups * rows, rank), jnp.float32),
        ],
        cost_estimate=pl.CostEstimate(
            flops=2 * chunks * groups * rows * cols * rank,
            bytes_accessed=4 * chunks * groups * rows * cols,
            transcendentals=chunks * groups * rows * cols,
        ),
        compiler_params=pltpu.CompilerParams(vmem_limit_bytes=7 << 20),
        name="slopes",
    )(index, *([pre] * groups), sketch_t)


def expert_kernel(
    tile_f, tile_d, rows_ref, slope_ref, down_part_ref, sketch_ref, down_ref, up_hbm, *refs
):
    keep_ref, give_ref, rows_buf, grad_buf, up_buf, up_sem = refs[-6:]
    hidden_cols, width = down_ref.shape
    steps_f, steps_d = hidden_cols // tile_f, width // tile_d
    half = keep_ref.shape[0]

    def tile(j, size):
        return pl.ds(pl.multiple_of(j * size, size), size)

    def up_copy(j):
        part = tile(j, tile_d)
        return pltpu.make_async_copy(up_hbm.at[part], up_buf.at[part], up_sem.at[j])

    for j in range(steps_d):
        if j == 0 or j > steps_f:
            up_copy(j).start()
    rows_buf[...] = rows_ref[...].T

    def first(j, carry):
        @pl.when(j + 1 < steps_d)
        def _():
            up_copy(j + 1).start()

        part = tile(j, tile_f)
        grad_hidden = jnp.dot(
            down_ref[part, :], rows_buf[...], preferred_element_type=jnp.float32
        )
        slope = slope_ref[0, part, :].astype(jnp.float32)
        grad_buf[part, :] = (grad_hidden * slope).astype(jnp.bfloat16)
        return carry

    lax.fori_loop(0, steps_f, first, 0)

    up_part = jnp.dot(sketch_ref[...], grad_buf[...], preferred_element_type=jnp.float32).T
    vectors = jnp.concatenate([down_part_ref[0], up_part], axis=1)
    keep_ref[:, width:] = vectors[:half]
    give_ref[:, width:] = vectors[half:].astype(jnp.bfloat16)

    def second(j, carry):
        up_copy(j).wait()
        part = tile(j, tile_d)
        term = jnp.dot(up_buf[part, :], grad_buf[...], preferred_element_type=jnp.float32).T
        keep_ref[:, part] = term[:half]
        give_ref[:, part] = term[half:].astype(jnp.bfloat16)
        return carry

    lax.fori_loop(0, steps_d, second, 0)


def expert(chunk, rows, slope, down_part, sketch_t, down_local, up_local, *events):
    count, width = rows.shape
    hidden_cols = down_local.shape[0]
    rank = sketch_t.shape[0]
    wide = width + 2 * rank
    tile_f, tile_d = tile_of(hidden_cols, 1792), tile_of(width, 1024)
    return pl.pallas_call(
        functools.partial(expert_kernel, tile_f, tile_d),
        grid=(1,),
        in_specs=[
            RESIDENT,
            pl.BlockSpec((1, hidden_cols, count), lambda i: (chunk, 0, 0)),
            pl.BlockSpec((1, count, rank), lambda i: (chunk, 0, 0)),
        ]
        + [RESIDENT] * 2
        + [pl.BlockSpec(memory_space=pltpu.HBM)]
        + [ANYWHERE] * len(events),
        out_specs=[RESIDENT] * 2,
        out_shape=[
            jax.ShapeDtypeStruct((count // 2, wide), jnp.float32),
            jax.ShapeDtypeStruct((count // 2, wide), jnp.bfloat16),
        ],
        scratch_shapes=[
            pltpu.VMEM((width, count), jnp.bfloat16),
            pltpu.VMEM((hidden_cols, count), jnp.bfloat16),
            pltpu.VMEM((width, hidden_cols), jnp.bfloat16),
            pltpu.SemaphoreType.DMA((width // tile_d,)),
        ],
        compiler_params=pltpu.CompilerParams(vmem_limit_bytes=26 << 20),
        cost_estimate=pl.CostEstimate(
            flops=4 * count * hidden_cols * width,
            bytes_accessed=4 * hidden_cols * width,
            transcendentals=0,
        ),
        name="expert",
    )(rows, slope, down_part, sketch_t, down_local, up_local, *events)


def per_device(
    cotangent,
    routes,
    gate_values,
    up_weight,
    down_weight,
    pre_activation,
    input_sketch,
    model_sketch,
    hidden_sketch,
    lengths,
):
    pieces = lax.axis_size("dp")
    sections = lax.axis_size("section")
    per_expert = pieces // EXPERTS
    place = lax.axis_index("dp")
    core = lax.axis_index("tensor")
    cot = cotangent[0]
    tok_dev, width = cot.shape
    half = tok_dev // 2
    rows = half // CHUNKS
    rank = model_sketch.shape[2]
    blocks = routes.shape[1]
    block_len = tok_dev // blocks
    sketch_local = hidden_sketch[0, 0]
    pre_all = pre_activation[0, 0]
    hidden_cols = pre_all.shape[2]
    pre_all = pre_all.reshape(pieces, 2, CHUNKS, rows, hidden_cols)

    def below(block):
        return lax.ppermute(block, "section", [(s, (s - 1) % sections) for s in range(sections)])

    token_routes = jnp.broadcast_to(routes[0][:, None, :], (blocks, block_len, 2)).reshape(
        tok_dev, 2
    )
    half_routes = lax.dynamic_slice_in_dim(token_routes, core * half, half, 0)
    half_gates = lax.dynamic_slice_in_dim(gate_values[0], core * half, half, 0)
    slot_expert = (place ^ jnp.arange(pieces, dtype=jnp.int32)) // per_expert
    hits = half_routes[:, None, :] == slot_expert[None, :, None]
    weight = jnp.sum(jnp.where(hits, half_gates[:, None, :], 0.0), axis=2)

    sketch_t = sketch_local.T
    cot_mine = lax.dynamic_slice_in_dim(cot, core * half, half, 0)
    cot_theirs = lax.dynamic_slice_in_dim(cot, (1 - core) * half, half, 0)
    order = sorted(range(1, pieces), reverse=True)
    slope, down_part = slopes(pre_all, sketch_t, place, core)
    mark, keep, sent, grad, passed = (), (), (), (), ()
    below_mine, vectors = [], []
    for a in range(CHUNKS):
        part = slice(a * rows, (a + 1) * rows)
        mine, theirs = {0: cot_mine[part]}, {0: cot_theirs[part]}
        if mark:
            mine[0] = held(mine[0], *mark)
        for slot in order:
            mine[slot] = xored(mine[0], "dp", slot)
        mark = (mine[1],)
        if keep:
            for slot in order:
                mine[slot] = held(mine[slot], *keep)
        traded = xored(jnp.concatenate([mine[slot] for slot in order], axis=0), "tensor", 1)
        for at, slot in enumerate(order):
            theirs[slot] = traded[at * rows : (at + 1) * rows]
        rows_in = jnp.concatenate(
            [mine[k] for k in range(pieces)] + [theirs[k] for k in range(pieces)], axis=0
        )

        kept, give = expert(
            a, rows_in, slope, down_part, sketch_t, down_weight[0, 0], up_weight[0, 0], *sent
        )
        keep = (kept,)
        if grad:
            give = held(give, *backs)
        own, *sent = merged(kept, xored(give, "tensor", 1), rows)
        backs = [xored(out, "dp", slot + 1) for slot, out in enumerate(sent)]
        if grad:
            passed = (below(held(*grad, backs[0])),)
            below_mine.append(*passed)
        new, vec = finished(own, cot_mine[part], weight[part], backs, *passed)
        grad = (new,)
        vectors.append(vec)
    below_mine.append(below(*grad))

    mine = jnp.concatenate(below_mine, axis=0)
    theirs = jnp.concatenate([xored(f, "tensor", 1) for f in below_mine], axis=0)
    handed = jnp.concatenate(
        [jnp.where(core == 0, mine, theirs), jnp.where(core == 0, theirs, mine)], axis=0
    )

    vec_mine = jnp.concatenate(vectors, axis=0)
    vec_theirs = xored(vec_mine, "tensor", 1)
    sketch_sum = jnp.concatenate(
        [jnp.where(core == 0, vec_mine, vec_theirs), jnp.where(core == 0, vec_theirs, vec_mine)],
        axis=0,
    )
    out_vec = jnp.dot(cot, model_sketch[0], preferred_element_type=jnp.float32)
    counts = lengths[0, 0]
    upto = jnp.arange(counts.shape[0])
    ends = jnp.sum(jnp.where(upto[None, :] <= upto[:, None], counts[None, :], 0), axis=1)
    starts = ends - counts
    position = jnp.arange(tok_dev, dtype=jnp.int32)
    member = ((position[None, :] >= starts[:, None]) & (position[None, :] < ends[:, None])).astype(
        jnp.float32
    )
    down_feat = jnp.einsum(
        "et,ta,tb->eab", member, out_vec, sketch_sum[:, :rank], precision=lax.Precision.HIGHEST
    )
    up_feat = jnp.einsum(
        "et,ta,tb->eab",
        member,
        sketch_sum[:, rank:],
        input_sketch[0],
        precision=lax.Precision.HIGHEST,
    )
    features = jnp.concatenate([down_feat, up_feat], axis=2)
    return (handed[None], features[None])


def solution(mesh):
    in_specs = (
        P("section", ("groups", "dp"), None),
        P("section", ("groups", "dp"), None),
        P("section", ("groups", "dp"), None),
        P("section", "dp", None, "tensor"),
        P("section", "dp", "tensor", None),
        P("section", ("groups", "dp"), None, None, "tensor"),
        P("section", ("groups", "dp"), None),
        P("section", None, None),
        P("section", "dp", "tensor", None),
        P("section", ("groups", "dp"), None),
    )
    out_specs = (P("section", ("groups", "dp"), None), P("section", ("groups", "dp"), None, None))
    return jax.shard_map(
        per_device, mesh=mesh, in_specs=in_specs, out_specs=out_specs, check_vma=False
    )
```

profile of v0, /device:TPU:0, one launch (start us, length us, event | category | flops | bytes accessed | tf_op | source)
XLA Modules:
  0.0 81.5 jit_solution(8134889909234934395)
XLA Ops:
  0.7 1.0 %constant_dynamic-update-slice_fusion.3 = (bf16[256,2048]{1,0:T(8,128)(2,1)S(1)}, bf16[32,2048]{1,0:T(8,128)(2,1)S(1)}) fusion(bf16[1,128,2048]{2,1,0:T(8,128)(2,1)} %param.10, s32[]{:T(128)S(6)} %select_n.45), kind=kLoop, calls=%fused_computation.38 | loop fusion | bytes 393220
  1.6 5.1 %collective-permute-start.2 = (bf16[32,2048]{1,0:T(8,128)(2,1)S(1)}, bf16[32,2048]{1,0:T(8,128)(2,1)S(1)}, u32[]{:S(2)}, u32[]{:S(2)}) collective-permute-start(bf16[32,2048]{1,0:T(8,128)(2,1)S(1)} %get-tuple-element.39.cot_ref), channel_id=1, source_target_pairs={{0,12},{4,8},{8,4},{12,0},{1,13},{5,9},{9,5},{13,1},{2,14},{6,10},... | collective-permute-start | bytes 393224 | tf_op jit(solution)/shard_map/ppermute | solution.py:17
  8.1 0.9 %dynamic-slice_bitcast_fusion.1.block_ref.cot_ref = bf16[32,2048]{1,0:T(8,128)(2,1)S(1)} fusion(bf16[1,128,2048]{2,1,0:T(8,128)(2,1)} %param.10, s32[]{:T(128)S(6)} %add.13), kind=kLoop, calls=%fused_computation.15 | loop fusion | bytes 262148 | tf_op jit(solution)/shard_map/slice | solution.py:299
  9.1 2.0 %copy-done.1 = bf16[1,1,4,128,3584]{4,3,2,1,0:T(8,128)(2,1)S(1)} copy-done((bf16[1,1,4,128,3584]{4,3,2,1,0:T(8,128)(2,1)S(1)}, bf16[1,1,4,128,3584]{4,3,2,1,0:T(8,128)(2,1)}, u32[]{:S(2)}) %copy-start.1) | copy-done | bytes 3670040
  11.2 1.0 %copy-done.4 = bf16[1,1,3584,64]{2,3,1,0:T(8,128)(2,1)S(1)} copy-done((bf16[1,1,3584,64]{2,3,1,0:T(8,128)(2,1)S(1)}, bf16[1,1,3584,64]{2,3,1,0:T(8,128)(2,1)}, u32[]{:S(2)}) %copy-start.4) | copy-done | bytes 458776
  12.2 5.6 %slopes.1 = (bf16[2,3584,256]{2,1,0:T(8,128)(2,1)S(1)}, f32[2,256,64]{2,1,0:T(8,128)S(1)}) custom-call(s32[2]{0:T(128)S(1)} %pad_add_fusion.index_ref, bf16[4,2,2,32,3584]{4,3,2,1,0:T(8,128)(2,1)S(1)} %bitcast.49, bf16[4,2,2,32,3584]{4,3,2,1,0:T(8,128)(2,1)S(1)} %bitcast.50, bf16[4,2,2,32,3584]{4,3,2,1,0:T(8,128)(2,1)S(1)} %bitcast.51, ...), custom_call_target="tpu_custom_call" | custom-call | flops 234881024 | bytes 7340032 | tf_op jit(solution)/shard_map/slopes/pallas_call | solution.py:134
  17.9 3.8 %collective-permute-start.10 = (bf16[32,2048]{1,0:T(8,128)(2,1)S(1)}, bf16[32,2048]{1,0:T(8,128)(2,1)S(1)}, u32[]{:S(2)}, u32[]{:S(2)}) collective-permute-start(bf16[32,2048]{1,0:T(8,128)(2,1)S(1)} %held.6), channel_id=1, source_target_pairs={{0,12},{4,8},{8,4},{12,0},{1,13},{5,9},{9,5},{13,1},{2,14},{6,10},... | collective-permute-start | bytes 393224 | tf_op jit(solution)/shard_map/ppermute | solution.py:17
  22.6 1.6 %collective-permute-done.3 = bf16[96,2048]{1,0:T(8,128)(2,1)S(1)} collective-permute-done((bf16[96,2048]{1,0:T(8,128)(2,1)S(1)}, bf16[96,2048]{1,0:T(8,128)(2,1)S(1)}, u32[]{:S(2)}, u32[]{:S(2)}) %collective-permute-start.3) | collective-permute-done | bytes 393248 | tf_op jit(solution)/shard_map/ppermute | solution.py:17
  24.3 9.4 %expert.2 = (f32[128,2176]{1,0:T(8,128)S(1)}, bf16[128,2176]{1,0:T(8,128)(2,1)S(1)}) custom-call(bf16[256,2048]{1,0:T(8,128)(2,1)S(1)} %slice_dynamic-update-slice_fusion.3.rows_ref, bf16[2,3584,256]{2,1,0:T(8,128)(2,1)S(1)} %get-tuple-element.20.slope_ref, f32[2,256,64]{2,1,0:T(8,128)S(1)} %get-tuple-element.21.down_part_ref, ...), custom_call_target="tpu_custom_call" | custom-call | flops 7516192768 | bytes 29360128 | tf_op jit(solution)/shard_map/expert/pallas_call | solution.py:217
  34.5 1.2 %collective-permute-done.11 = bf16[96,2048]{1,0:T(8,128)(2,1)S(1)} collective-permute-done((bf16[96,2048]{1,0:T(8,128)(2,1)S(1)}, bf16[96,2048]{1,0:T(8,128)(2,1)S(1)}, u32[]{:S(2)}, u32[]{:S(2)}) %collective-permute-start.11) | collective-permute-done | bytes 393248 | tf_op jit(solution)/shard_map/ppermute | solution.py:17
  36.6 1.5 %collective-permute-start.5 = (bf16[32,2176]{1,0:T(8,128)(2,1)S(1)}, bf16[32,2176]{1,0:T(8,128)(2,1)S(1)}, u32[]{:S(2)}, u32[]{:S(2)}) collective-permute-start(bf16[32,2176]{1,0:T(8,128)(2,1)S(1)} %get-tuple-element.25.refs_0_), channel_id=1, source_target_pairs={{0,4},{4,0},{8,12},{12,8},{1,5},{5,1},{9,13},{13,9},{2,6},{6,2},{1... | collective-permute-start | bytes 417800 | tf_op jit(solution)/shard_map/ppermute | solution.py:17
  38.0 2.9 %collective-permute-start.6 = (bf16[32,2176]{1,0:T(8,128)(2,1)S(1)}, bf16[32,2176]{1,0:T(8,128)(2,1)S(1)}, u32[]{:S(2)}, u32[]{:S(2)}) collective-permute-start(bf16[32,2176]{1,0:T(8,128)(2,1)S(1)} %get-tuple-element.26.refs_1_), channel_id=1, source_target_pairs={{0,8},{4,12},{8,0},{12,4},{1,9},{5,13},{9,1},{13,5},{2,10},{6,14},... | collective-permute-start | bytes 417800 | tf_op jit(solution)/shard_map/ppermute | solution.py:17
  41.0 5.2 %copy-done.3 = bf16[1,1,3584,2048]{3,2,1,0:T(8,128)(2,1)S(1)} copy-done((bf16[1,1,3584,2048]{3,2,1,0:T(8,128)(2,1)S(1)}, bf16[1,1,3584,2048]{3,2,1,0:T(8,128)(2,1)}, u32[]{:S(2)}) %copy-start.3) | copy-done | bytes 14680088
  46.2 9.4 %expert.3 = (f32[128,2176]{1,0:T(8,128)S(1)}, bf16[128,2176]{1,0:T(8,128)(2,1)S(1)}) custom-call(bf16[256,2048]{1,0:T(8,128)(2,1)S(1)} %slice_dynamic-update-slice_fusion.rows_ref, bf16[2,3584,256]{2,1,0:T(8,128)(2,1)S(1)} %get-tuple-element.20.slope_ref, f32[2,256,64]{2,1,0:T(8,128)S(1)} %get-tuple-element.21.down_part_ref, bf16[64,3584]{1,0:T(8,128)(2,1)S(1)} %bitcast.61, ...), custom_call_target="tpu_custom_call" | custom-call | flops 7516192768 | bytes 29360128 | tf_op jit(solution)/shard_map/expert/pallas_call | solution.py:217
  56.1 1.3 %fusion = f32[128,64]{0,1:T(8,128)S(1)} fusion(bf16[1,128,2048]{2,1,0:T(8,128)(2,1)} %param.10, bf16[1,2048,64]{1,2,0:T(8,128)(2,1)S(1)} %copy-done), kind=kOutput, calls=%fused_computation.3 | convolution fusion | flops 33554432 | bytes 819200 | tf_op jit(solution)/shard_map/dot_general | solution.py:343
  58.6 3.9 %collective-permute-start.15 = (bf16[32,2176]{1,0:T(8,128)(2,1)S(1)}, bf16[32,2176]{1,0:T(8,128)(2,1)S(1)}, u32[]{:S(2)}, u32[]{:S(2)}) collective-permute-start(bf16[32,2176]{1,0:T(8,128)(2,1)S(1)} %get-tuple-element.33), channel_id=1, source_target_pairs={{0,8},{4,12},{8,0},{12,4},{1,9},{5,13},{9,1},{13,5},{2,10},{6,14},... | collective-permute-start | bytes 417800 | tf_op jit(solution)/shard_map/ppermute | solution.py:17
  62.6 3.4 %collective-permute-done.13.refs_0_ = bf16[32,2176]{1,0:T(8,128)(2,1)S(1)} collective-permute-done((bf16[32,2176]{1,0:T(8,128)(2,1)S(1)}, bf16[32,2176]{1,0:T(8,128)(2,1)S(1)}, u32[]{:S(2)}, u32[]{:S(2)}) %collective-permute-start.13) | collective-permute-done | bytes 139296 | tf_op jit(solution)/shard_map/ppermute | solution.py:17
  66.0 1.8 %collective-permute-start.14 = (bf16[32,2048]{1,0:T(8,128)(2,1)S(1)}, bf16[32,2048]{1,0:T(8,128)(2,1)S(1)}, u32[]{:S(2)}, u32[]{:S(2)}) collective-permute-start(bf16[32,2048]{1,0:T(8,128)(2,1)S(1)} %held.11), channel_id=1, source_target_pairs={{0,2},{2,0},{1,3},{3,1},{4,6},{6,4},{5,7},{7,5},{8,10},{10,8},{9,1... | collective-permute-start | bytes 393224 | tf_op jit(solution)/shard_map/ppermute | solution.py:279
  67.9 5.1 %collective-permute-done.15.refs_1_ = bf16[32,2176]{1,0:T(8,128)(2,1)S(1)} collective-permute-done((bf16[32,2176]{1,0:T(8,128)(2,1)S(1)}, bf16[32,2176]{1,0:T(8,128)(2,1)S(1)}, u32[]{:S(2)}, u32[]{:S(2)}) %collective-permute-start.15) | collective-permute-done | bytes 139296 | tf_op jit(solution)/shard_map/ppermute | solution.py:17
  73.3 1.6 %collective-permute-start.17 = (bf16[32,2048]{1,0:T(8,128)(2,1)S(1)}, bf16[32,2048]{1,0:T(8,128)(2,1)S(1)}, u32[]{:S(2)}, u32[]{:S(2)}) collective-permute-start(bf16[32,2048]{1,0:T(8,128)(2,1)S(1)} %get-tuple-element.35), channel_id=1, source_target_pairs={{0,2},{2,0},{1,3},{3,1},{4,6},{6,4},{5,7},{7,5},{8,10},{10,8},{9,1... | collective-permute-start | bytes 393224 | tf_op jit(solution)/shard_map/ppermute | solution.py:279
  75.8 0.8 maximum_bitcast_fusion.1
  76.5 2.7 %collective-permute-done.17 = bf16[32,2048]{1,0:T(8,128)(2,1)S(1)} collective-permute-done((bf16[32,2048]{1,0:T(8,128)(2,1)S(1)}, bf16[32,2048]{1,0:T(8,128)(2,1)S(1)}, u32[]{:S(2)}, u32[]{:S(2)}) %collective-permute-start.17) | collective-permute-done | bytes 131104 | tf_op jit(solution)/shard_map/ppermute | solution.py:279
  79.2 1.3 %collective-permute-done.19 = bf16[32,2048]{1,0:T(8,128)(2,1)S(1)} collective-permute-done((bf16[32,2048]{1,0:T(8,128)(2,1)S(1)}, bf16[32,2048]{1,0:T(8,128)(2,1)S(1)}, u32[]{:S(2)}, u32[]{:S(2)}) %collective-permute-start.19) | collective-permute-done | bytes 131104 | tf_op jit(solution)/shard_map/ppermute | solution.py:17
  80.6 0.8 %maximum_bitcast_fusion = bf16[1,128,2048]{2,1,0:T(8,128)(2,1)} fusion(bf16[64,2048]{1,0:T(8,128)(2,1)S(1)} %get-tuple-element.41, bf16[64,2048]{1,0:T(8,128)(2,1)S(1)} %get-tuple-element.40), kind=kLoop, calls=%fused_computation.2 | loop fusion | flops 1048576 | bytes 1048576 | tf_op jit(solution)/shard_map/broadcast_in_dim | solution.py:363
  (95 shorter events, 7.1 us)
Async XLA Ops:
  0.6 55.4 %copy-start = (bf16[1,2048,64]{1,2,0:T(8,128)(2,1)S(1)}, bf16[1,2048,64]{1,2,0:T(8,128)(2,1)}, u32[]{:S(2)}) copy-start(bf16[1,2048,64]{1,2,0:T(8,128)(2,1)} %param.17) | copy-start | bytes 786436
  1.6 20.8 %collective-permute-start.2 = (bf16[32,2048]{1,0:T(8,128)(2,1)S(1)}, bf16[32,2048]{1,0:T(8,128)(2,1)S(1)}, u32[]{:S(2)}, u32[]{:S(2)}) collective-permute-start(bf16[32,2048]{1,0:T(8,128)(2,1)S(1)} %get-tuple-element.39.cot_ref), channel_id=1, source_target_pairs={{0,12},{4,8},{8,4},{12,0},{1,13},{5,9},{9,5},{13,1},{2,14},{6,10},... | collective-permute-start | bytes 393224 | tf_op jit(solution)/shard_map/ppermute | solution.py:17
  6.7 15.7 %collective-permute-start.1 = (bf16[32,2048]{1,0:T(8,128)(2,1)S(1)}, bf16[32,2048]{1,0:T(8,128)(2,1)S(1)}, u32[]{:S(2)}, u32[]{:S(2)}) collective-permute-start(bf16[32,2048]{1,0:T(8,128)(2,1)S(1)} %get-tuple-element.39.cot_ref), channel_id=1, source_target_pairs={{0,8},{4,12},{8,0},{12,4},{1,9},{5,13},{9,1},{13,5},{2,10},{6,14},... | collective-permute-start | bytes 393224 | tf_op jit(solution)/shard_map/ppermute | solution.py:17
  6.7 11.2 %collective-permute-start = (bf16[32,2048]{1,0:T(8,128)(2,1)S(1)}, bf16[32,2048]{1,0:T(8,128)(2,1)S(1)}, u32[]{:S(2)}, u32[]{:S(2)}) collective-permute-start(bf16[32,2048]{1,0:T(8,128)(2,1)S(1)} %get-tuple-element.39.cot_ref), channel_id=1, source_target_pairs={{0,4},{4,0},{8,12},{12,8},{1,5},{5,1},{9,13},{13,9},{2,6},{6,2},{1... | collective-permute-start | bytes 393224 | tf_op jit(solution)/shard_map/ppermute | solution.py:17
  12.2 12.1 %copy-start.5 = (bf16[1,1,3584,64]{2,3,1,0:T(8,128)(2,1)S(1)}, bf16[1,1,3584,64]{2,3,1,0:T(8,128)(2,1)}, u32[]{:S(2)}) copy-start(bf16[1,1,3584,64]{2,3,1,0:T(8,128)(2,1)} %param.18) | copy-start | bytes 1376260
  17.9 15.9 %collective-permute-start.10 = (bf16[32,2048]{1,0:T(8,128)(2,1)S(1)}, bf16[32,2048]{1,0:T(8,128)(2,1)S(1)}, u32[]{:S(2)}, u32[]{:S(2)}) collective-permute-start(bf16[32,2048]{1,0:T(8,128)(2,1)S(1)} %held.6), channel_id=1, source_target_pairs={{0,12},{4,8},{8,4},{12,0},{1,13},{5,9},{9,5},{13,1},{2,14},{6,10},... | collective-permute-start | bytes 393224 | tf_op jit(solution)/shard_map/ppermute | solution.py:17
  21.7 12.0 %collective-permute-start.9 = (bf16[32,2048]{1,0:T(8,128)(2,1)S(1)}, bf16[32,2048]{1,0:T(8,128)(2,1)S(1)}, u32[]{:S(2)}, u32[]{:S(2)}) collective-permute-start(bf16[32,2048]{1,0:T(8,128)(2,1)S(1)} %held.6), channel_id=1, source_target_pairs={{0,8},{4,12},{8,0},{12,4},{1,9},{5,13},{9,1},{13,5},{2,10},{6,14},... | collective-permute-start | bytes 393224 | tf_op jit(solution)/shard_map/ppermute | solution.py:17
  21.7 12.0 %collective-permute-start.8 = (bf16[32,2048]{1,0:T(8,128)(2,1)S(1)}, bf16[32,2048]{1,0:T(8,128)(2,1)S(1)}, u32[]{:S(2)}, u32[]{:S(2)}) collective-permute-start(bf16[32,2048]{1,0:T(8,128)(2,1)S(1)} %held.6), channel_id=1, source_target_pairs={{0,4},{4,0},{8,12},{12,8},{1,5},{5,1},{9,13},{13,9},{2,6},{6,2},{1... | collective-permute-start | bytes 393224 | tf_op jit(solution)/shard_map/ppermute | solution.py:17
  22.4 1.8 %collective-permute-start.3 = (bf16[96,2048]{1,0:T(8,128)(2,1)S(1)}, bf16[96,2048]{1,0:T(8,128)(2,1)S(1)}, u32[]{:S(2)}, u32[]{:S(2)}) collective-permute-start(bf16[96,2048]{1,0:T(8,128)(2,1)S(1)} %pad_maximum_fusion), channel_id=1, source_target_pairs={{0,1},{1,0},{2,3},{3,2},{4,5},{5,4},{6,7},{7,6},{8,9},{9,8},{10,11... | collective-permute-start | bytes 1179656 | tf_op jit(solution)/shard_map/ppermute | solution.py:17
  33.9 1.8 %collective-permute-start.11 = (bf16[96,2048]{1,0:T(8,128)(2,1)S(1)}, bf16[96,2048]{1,0:T(8,128)(2,1)S(1)}, u32[]{:S(2)}, u32[]{:S(2)}) collective-permute-start(bf16[96,2048]{1,0:T(8,128)(2,1)S(1)} %pad_maximum_fusion.1), channel_id=1, source_target_pairs={{0,1},{1,0},{2,3},{3,2},{4,5},{5,4},{6,7},{7,6},{8,9},{9,8},{10,11... | collective-permute-start | bytes 1179656 | tf_op jit(solution)/shard_map/ppermute | solution.py:17
  34.1 2.4 %collective-permute-start.4 = (bf16[128,2176]{1,0:T(8,128)(2,1)S(1)}, bf16[128,2176]{1,0:T(8,128)(2,1)S(1)}, u32[]{:S(2)}, u32[]{:S(2)}) collective-permute-start(bf16[128,2176]{1,0:T(8,128)(2,1)S(1)} %get-tuple-element.23), channel_id=1, source_target_pairs={{0,1},{1,0},{2,3},{3,2},{4,5},{5,4},{6,7},{7,6},{8,9},{9,8},{10,11... | collective-permute-start | bytes 1671176 | tf_op jit(solution)/shard_map/ppermute | solution.py:17
  36.6 19.1 %collective-permute-start.5 = (bf16[32,2176]{1,0:T(8,128)(2,1)S(1)}, bf16[32,2176]{1,0:T(8,128)(2,1)S(1)}, u32[]{:S(2)}, u32[]{:S(2)}) collective-permute-start(bf16[32,2176]{1,0:T(8,128)(2,1)S(1)} %get-tuple-element.25.refs_0_), channel_id=1, source_target_pairs={{0,4},{4,0},{8,12},{12,8},{1,5},{5,1},{9,13},{13,9},{2,6},{6,2},{1... | collective-permute-start | bytes 417800 | tf_op jit(solution)/shard_map/ppermute | solution.py:17
  38.0 17.6 %collective-permute-start.6 = (bf16[32,2176]{1,0:T(8,128)(2,1)S(1)}, bf16[32,2176]{1,0:T(8,128)(2,1)S(1)}, u32[]{:S(2)}, u32[]{:S(2)}) collective-permute-start(bf16[32,2176]{1,0:T(8,128)(2,1)S(1)} %get-tuple-element.26.refs_1_), channel_id=1, source_target_pairs={{0,8},{4,12},{8,0},{12,4},{1,9},{5,13},{9,1},{13,5},{2,10},{6,14},... | collective-permute-start | bytes 417800 | tf_op jit(solution)/shard_map/ppermute | solution.py:17
  40.9 14.7 %collective-permute-start.7 = (bf16[32,2176]{1,0:T(8,128)(2,1)S(1)}, bf16[32,2176]{1,0:T(8,128)(2,1)S(1)}, u32[]{:S(2)}, u32[]{:S(2)}) collective-permute-start(bf16[32,2176]{1,0:T(8,128)(2,1)S(1)} %get-tuple-element.27.refs_2_), channel_id=1, source_target_pairs={{0,12},{4,8},{8,4},{12,0},{1,13},{5,9},{9,5},{13,1},{2,14},{6,10},... | collective-permute-start | bytes 417800 | tf_op jit(solution)/shard_map/ppermute | solution.py:17
  55.6 19.6 %copy-start.7 = (f32[1,128,64]{1,2,0:T(8,128)S(1)}, f32[1,128,64]{1,2,0:T(8,128)}, u32[]{:S(2)}) copy-start(f32[1,128,64]{1,2,0:T(8,128)} %param.16) | copy-start | bytes 98308
  55.7 2.0 %collective-permute-start.12 = (bf16[128,2176]{1,0:T(8,128)(2,1)S(1)}, bf16[128,2176]{1,0:T(8,128)(2,1)S(1)}, u32[]{:S(2)}, u32[]{:S(2)}) collective-permute-start(bf16[128,2176]{1,0:T(8,128)(2,1)S(1)} %held.10), channel_id=1, source_target_pairs={{0,1},{1,0},{2,3},{3,2},{4,5},{5,4},{6,7},{7,6},{8,9},{9,8},{10,11... | collective-permute-start | bytes 1671176 | tf_op jit(solution)/shard_map/ppermute | solution.py:17
  57.9 8.1 %collective-permute-start.13 = (bf16[32,2176]{1,0:T(8,128)(2,1)S(1)}, bf16[32,2176]{1,0:T(8,128)(2,1)S(1)}, u32[]{:S(2)}, u32[]{:S(2)}) collective-permute-start(bf16[32,2176]{1,0:T(8,128)(2,1)S(1)} %get-tuple-element.31), channel_id=1, source_target_pairs={{0,4},{4,0},{8,12},{12,8},{1,5},{5,1},{9,13},{13,9},{2,6},{6,2},{1... | collective-permute-start | bytes 417800 | tf_op jit(solution)/shard_map/ppermute | solution.py:17
  58.6 14.4 %collective-permute-start.15 = (bf16[32,2176]{1,0:T(8,128)(2,1)S(1)}, bf16[32,2176]{1,0:T(8,128)(2,1)S(1)}, u32[]{:S(2)}, u32[]{:S(2)}) collective-permute-start(bf16[32,2176]{1,0:T(8,128)(2,1)S(1)} %get-tuple-element.33), channel_id=1, source_target_pairs={{0,8},{4,12},{8,0},{12,4},{1,9},{5,13},{9,1},{13,5},{2,10},{6,14},... | collective-permute-start | bytes 417800 | tf_op jit(solution)/shard_map/ppermute | solution.py:17
  62.5 10.5 %collective-permute-start.16 = (bf16[32,2176]{1,0:T(8,128)(2,1)S(1)}, bf16[32,2176]{1,0:T(8,128)(2,1)S(1)}, u32[]{:S(2)}, u32[]{:S(2)}) collective-permute-start(bf16[32,2176]{1,0:T(8,128)(2,1)S(1)} %get-tuple-element.34), channel_id=1, source_target_pairs={{0,12},{4,8},{8,4},{12,0},{1,13},{5,9},{9,5},{13,1},{2,14},{6,10},... | collective-permute-start | bytes 417800 | tf_op jit(solution)/shard_map/ppermute | solution.py:17
  66.0 7.0 %collective-permute-start.14 = (bf16[32,2048]{1,0:T(8,128)(2,1)S(1)}, bf16[32,2048]{1,0:T(8,128)(2,1)S(1)}, u32[]{:S(2)}, u32[]{:S(2)}) collective-permute-start(bf16[32,2048]{1,0:T(8,128)(2,1)S(1)} %held.11), channel_id=1, source_target_pairs={{0,2},{2,0},{1,3},{3,1},{4,6},{6,4},{5,7},{7,5},{8,10},{10,8},{9,1... | collective-permute-start | bytes 393224 | tf_op jit(solution)/shard_map/ppermute | solution.py:279
  73.2 1.8 %collective-permute-start.20 = (f32[64,128]{1,0:T(8,128)S(1)}, f32[64,128]{1,0:T(8,128)S(1)}, u32[]{:S(2)}, u32[]{:S(2)}) collective-permute-start(f32[64,128]{1,0:T(8,128)S(1)} %constant_dynamic-update-slice_fusion.12), channel_id=1, source_target_pairs={{0,1},{1,0},{2,3},{3,2},{4,5},{5,4},{6,7},{7,6},{8,9},{9,8},{10,11... | collective-permute-start | bytes 98312 | tf_op jit(solution)/shard_map/ppermute | solution.py:17
  73.3 5.9 %collective-permute-start.17 = (bf16[32,2048]{1,0:T(8,128)(2,1)S(1)}, bf16[32,2048]{1,0:T(8,128)(2,1)S(1)}, u32[]{:S(2)}, u32[]{:S(2)}) collective-permute-start(bf16[32,2048]{1,0:T(8,128)(2,1)S(1)} %get-tuple-element.35), channel_id=1, source_target_pairs={{0,2},{2,0},{1,3},{3,1},{4,6},{6,4},{5,7},{7,5},{8,10},{10,8},{9,1... | collective-permute-start | bytes 393224 | tf_op jit(solution)/shard_map/ppermute | solution.py:279
  74.8 1.7 %collective-permute-start.18 = (bf16[32,2048]{1,0:T(8,128)(2,1)S(1)}, bf16[32,2048]{1,0:T(8,128)(2,1)S(1)}, u32[]{:S(2)}, u32[]{:S(2)}) collective-permute-start(bf16[32,2048]{1,0:T(8,128)(2,1)S(1)} %collective-permute-done.14.refs_3_), channel_id=1, source_target_pairs={{0,1},{1,0},{2,3},{3,2},{4,5},{5,4},{6,7},{7,6},{8,9},{9,8},{10,11... | collective-permute-start | bytes 393224 | tf_op jit(solution)/shard_map/ppermute | solution.py:17
  79.2 1.3 %collective-permute-start.19 = (bf16[32,2048]{1,0:T(8,128)(2,1)S(1)}, bf16[32,2048]{1,0:T(8,128)(2,1)S(1)}, u32[]{:S(2)}, u32[]{:S(2)}) collective-permute-start(bf16[32,2048]{1,0:T(8,128)(2,1)S(1)} %collective-permute-done.17), channel_id=1, source_target_pairs={{0,1},{1,0},{2,3},{3,2},{4,5},{5,4},{6,7},{7,6},{8,9},{9,8},{10,11... | collective-permute-start | bytes 393224 | tf_op jit(solution)/shard_map/ppermute | solution.py:17
  (7 other events, 46.1 us)
where the time goes:
time: 81.9 us; the launch traced here: 81.5 us
  Pallas kernels  25.1 us (31%)
  starting transfers between devices  23.5 us (29%)
  waiting for transfers between devices  16.4 us (20%)
  local copies, waits for them, and re-layouts  11.4 us (14%)
  other arithmetic  2.14 us (3%)
  matrix products  1.86 us (2%)
  between operations  1.09 us (1%)
    ppermute x19, starting transfers between devices, xored(): return lax.ppermute(block, axis, [(i, i ^ bits) for i in range(n)])  20.1 us
    pallas_call x2, Pallas kernels, expert(): pl.pallas_call(functools.partial(expert_kernel, tile_f, tile_d), grid=(1,...  18.8 us
    ppermute x19, waiting for transfers between devices, xored(): return lax.ppermute(block, axis, [(i, i ^ bits) for i in range(n)])  13.7 us
    unnamed x39, local copies, waits for them, and re-layouts  9.59 us
    pallas_call x1, Pallas kernels, slopes(): pl.pallas_call(functools.partial(slope_kernel, groups), grid_spec=pltpu.P...  5.6 us
    ppermute x2, starting transfers between devices, below(): lax.ppermute(block, 'section', [(s, (s - 1) % sections) for s in range(se...  3.32 us
    ppermute x2, waiting for transfers between devices, below(): lax.ppermute(block, 'section', [(s, (s - 1) % sections) for s in range(se...  2.65 us
  transfers between devices with their start and end apart: 21, of which 8 were waited for; matrix products, arithmetic and copies ran while one was open for 6% of the time, Pallas kernels for 30%

commit v1 on v0

--- a/solution.py
+++ b/solution.py
@@ -25,13 +25,16 @@
     refs[-1][...] = block_ref[...]
 
 
-def held(block, *events):
+def held(block, *events, beside=0):
     return pl.pallas_call(
         held_kernel,
         in_specs=[RESIDENT] + [ANYWHERE] * len(events),
         out_specs=RESIDENT,
         out_shape=jax.ShapeDtypeStruct(block.shape, block.dtype),
         compiler_params=pltpu.CompilerParams(vmem_limit_bytes=1 << 20),
+        cost_estimate=pl.CostEstimate(
+            flops=0, bytes_accessed=4 * block.size + beside, transcendentals=0
+        ),
         name="held",
     )(block, *events)
 
@@ -125,6 +128,8 @@
     groups = 2 * n
     tile = tile_of(cols, 896)
     index = jnp.stack([place, core]).astype(jnp.int32)
+    pre = pltpu.with_memory_space_constraint(pre, pltpu.HBM)
+    sketch_t = pltpu.with_memory_space_constraint(sketch_t, pltpu.HBM)
 
     def spec_of(h, slot):
         return pl.BlockSpec(
@@ -304,7 +309,7 @@
         mark = (mine[1],)
         if keep:
             for slot in order:
-                mine[slot] = held(mine[slot], *keep)
+                mine[slot] = held(mine[slot], *keep, beside=2 * down_weight.size)
         traded = xored(jnp.concatenate([mine[slot] for slot in order], axis=0), "tensor", 1)
         for at, slot in enumerate(order):
             theirs[slot] = traded[at * rows : (at + 1) * rows]

time: 81.9 us -> 82.6 us (level)
  Pallas kernels: 25.1 us -> 28.8 us
  local copies, waits for them, and re-layouts: 11.4 us -> 8.4 us
    pallas_call x1, Pallas kernels: 5.6 us -> 9.33 us  [slopes(): pl.pallas_call(functools.partial(slope_kernel, groups), grid_spec=pltpu.P...]
    unnamed x39 -> x41, local copies, waits for them, and re-layouts: 9.59 us -> 6.56 us
  transfers between devices with their start and end apart: 21 -> 21, of which waited for: 8 -> 8; matrix products, arithmetic and copies ran while one was open for 6% -> 6% of each run, Pallas kernels for 30% -> 35%
where the time goes in v1:
time: 82.6 us; the launch traced here: 82.2 us
  Pallas kernels  28.8 us (35%)
  starting transfers between devices  23.5 us (28%)
  waiting for transfers between devices  16.4 us (20%)
  local copies, waits for them, and re-layouts  8.4 us (10%)
  other arithmetic  2.14 us (3%)
  matrix products  1.86 us (2%)
  between operations  1.14 us (1%)
    ppermute x19, starting transfers between devices, xored(): return lax.ppermute(block, axis, [(i, i ^ bits) for i in range(n)])  20.1 us
    pallas_call x2, Pallas kernels, expert(): pl.pallas_call(functools.partial(expert_kernel, tile_f, tile_d), grid=(1,...  18.8 us
    ppermute x19, waiting for transfers between devices, xored(): return lax.ppermute(block, axis, [(i, i ^ bits) for i in range(n)])  13.7 us
    pallas_call x1, Pallas kernels, slopes(): pl.pallas_call(functools.partial(slope_kernel, groups), grid_spec=pltpu.P...  9.33 us
    unnamed x41, local copies, waits for them, and re-layouts  6.56 us
    ppermute x2, starting transfers between devices, below(): lax.ppermute(block, 'section', [(s, (s - 1) % sections) for s in range(se...  3.32 us
    ppermute x2, waiting for transfers between devices, below(): lax.ppermute(block, 'section', [(s, (s - 1) % sections) for s in range(se...  2.65 us
  transfers between devices with their start and end apart: 21, of which 8 were waited for; matrix products, arithmetic and copies ran while one was open for 6% of the time, Pallas kernels for 35%

profile of v1, /device:TPU:0, one launch (start us, length us, event | category | flops | bytes accessed | tf_op | source)
XLA Modules:
  0.0 82.2 jit_solution(10834422908959662446)
XLA Ops:
  0.7 1.0 %constant_dynamic-update-slice_fusion.3 = (bf16[256,2048]{1,0:T(8,128)(2,1)S(1)}, bf16[32,2048]{1,0:T(8,128)(2,1)S(1)}) fusion(bf16[1,128,2048]{2,1,0:T(8,128)(2,1)} %param.10, s32[]{:T(128)S(6)} %select_n.45), kind=kLoop, calls=%fused_computation.38 | loop fusion | bytes 393220
  1.6 5.1 %collective-permute-start.2 = (bf16[32,2048]{1,0:T(8,128)(2,1)S(1)}, bf16[32,2048]{1,0:T(8,128)(2,1)S(1)}, u32[]{:S(2)}, u32[]{:S(2)}) collective-permute-start(bf16[32,2048]{1,0:T(8,128)(2,1)S(1)} %get-tuple-element.39.cot_ref), channel_id=1, source_target_pairs={{0,12},{4,8},{8,4},{12,0},{1,13},{5,9},{9,5},{13,1},{2,14},{6,10},... | collective-permute-start | bytes 393224 | tf_op jit(solution)/shard_map/ppermute | solution.py:17
  7.4 0.7 fusion.17
  8.1 0.9 %dynamic-slice_bitcast_fusion.1.block_ref.cot_ref = bf16[32,2048]{1,0:T(8,128)(2,1)S(1)} fusion(bf16[1,128,2048]{2,1,0:T(8,128)(2,1)} %param.10, s32[]{:T(128)S(6)} %add.13), kind=kLoop, calls=%fused_computation.15 | loop fusion | bytes 262148 | tf_op jit(solution)/shard_map/slice | solution.py:304
  9.2 9.3 %slopes.1 = (bf16[2,3584,256]{2,1,0:T(8,128)(2,1)S(1)}, f32[2,256,64]{2,1,0:T(8,128)S(1)}) custom-call(s32[2]{0:T(128)S(1)} %pad_add_fusion.index_ref, bf16[4,2,2,32,3584]{4,3,2,1,0:T(8,128)(2,1)} %bitcast.56, bf16[4,2,2,32,3584]{4,3,2,1,0:T(8,128)(2,1)} %bitcast.57, bf16[4,2,2,32,3584]{4,3,2,1,0:T(8,128)(2,1)} %bitcast.58, ...), custom_call_target="tpu_custom_call" | custom-call | flops 234881024 | bytes 7340032 | tf_op jit(solution)/shard_map/slopes/pallas_call | solution.py:139
  18.6 3.8 %collective-permute-start.10 = (bf16[32,2048]{1,0:T(8,128)(2,1)S(1)}, bf16[32,2048]{1,0:T(8,128)(2,1)S(1)}, u32[]{:S(2)}, u32[]{:S(2)}) collective-permute-start(bf16[32,2048]{1,0:T(8,128)(2,1)S(1)} %held.6), channel_id=1, source_target_pairs={{0,12},{4,8},{8,4},{12,0},{1,13},{5,9},{9,5},{13,1},{2,14},{6,10},... | collective-permute-start | bytes 393224 | tf_op jit(solution)/shard_map/ppermute | solution.py:17
  23.3 1.6 %collective-permute-done.3 = bf16[96,2048]{1,0:T(8,128)(2,1)S(1)} collective-permute-done((bf16[96,2048]{1,0:T(8,128)(2,1)S(1)}, bf16[96,2048]{1,0:T(8,128)(2,1)S(1)}, u32[]{:S(2)}, u32[]{:S(2)}) %collective-permute-start.3) | collective-permute-done | bytes 393248 | tf_op jit(solution)/shard_map/ppermute | solution.py:17
  25.0 9.4 %expert.2 = (f32[128,2176]{1,0:T(8,128)S(1)}, bf16[128,2176]{1,0:T(8,128)(2,1)S(1)}) custom-call(bf16[256,2048]{1,0:T(8,128)(2,1)S(1)} %slice_dynamic-update-slice_fusion.3.rows_ref, bf16[2,3584,256]{2,1,0:T(8,128)(2,1)S(1)} %get-tuple-element.20.slope_ref, f32[2,256,64]{2,1,0:T(8,128)S(1)} %get-tuple-element.21.down_part_ref, ...), custom_call_target="tpu_custom_call" | custom-call | flops 7516192768 | bytes 29360128 | tf_op jit(solution)/shard_map/expert/pallas_call | solution.py:222
  35.2 1.2 %collective-permute-done.11 = bf16[96,2048]{1,0:T(8,128)(2,1)S(1)} collective-permute-done((bf16[96,2048]{1,0:T(8,128)(2,1)S(1)}, bf16[96,2048]{1,0:T(8,128)(2,1)S(1)}, u32[]{:S(2)}, u32[]{:S(2)}) %collective-permute-start.11) | collective-permute-done | bytes 393248 | tf_op jit(solution)/shard_map/ppermute | solution.py:17
  36.5 0.7 collective-permute-done.4.came_ref
  37.3 1.5 %collective-permute-start.5 = (bf16[32,2176]{1,0:T(8,128)(2,1)S(1)}, bf16[32,2176]{1,0:T(8,128)(2,1)S(1)}, u32[]{:S(2)}, u32[]{:S(2)}) collective-permute-start(bf16[32,2176]{1,0:T(8,128)(2,1)S(1)} %get-tuple-element.25.refs_0_), channel_id=1, source_target_pairs={{0,4},{4,0},{8,12},{12,8},{1,5},{5,1},{9,13},{13,9},{2,6},{6,2},{1... | collective-permute-start | bytes 417800 | tf_op jit(solution)/shard_map/ppermute | solution.py:17
  38.8 2.9 %collective-permute-start.6 = (bf16[32,2176]{1,0:T(8,128)(2,1)S(1)}, bf16[32,2176]{1,0:T(8,128)(2,1)S(1)}, u32[]{:S(2)}, u32[]{:S(2)}) collective-permute-start(bf16[32,2176]{1,0:T(8,128)(2,1)S(1)} %get-tuple-element.26.refs_1_), channel_id=1, source_target_pairs={{0,8},{4,12},{8,0},{12,4},{1,9},{5,13},{9,1},{13,5},{2,10},{6,14},... | collective-permute-start | bytes 417800 | tf_op jit(solution)/shard_map/ppermute | solution.py:17
  41.8 5.2 %copy-done.1 = bf16[1,1,3584,2048]{3,2,1,0:T(8,128)(2,1)S(1)} copy-done((bf16[1,1,3584,2048]{3,2,1,0:T(8,128)(2,1)S(1)}, bf16[1,1,3584,2048]{3,2,1,0:T(8,128)(2,1)}, u32[]{:S(2)}) %copy-start.1) | copy-done | bytes 14680088
  46.9 9.4 %expert.3 = (f32[128,2176]{1,0:T(8,128)S(1)}, bf16[128,2176]{1,0:T(8,128)(2,1)S(1)}) custom-call(bf16[256,2048]{1,0:T(8,128)(2,1)S(1)} %slice_dynamic-update-slice_fusion.rows_ref, bf16[2,3584,256]{2,1,0:T(8,128)(2,1)S(1)} %get-tuple-element.20.slope_ref, f32[2,256,64]{2,1,0:T(8,128)S(1)} %get-tuple-element.21.down_part_ref, bf16[64,3584]{1,0:T(8,128)(2,1)S(1)} %bitcast.55, ...), custom_call_target="tpu_custom_call" | custom-call | flops 7516192768 | bytes 29360128 | tf_op jit(solution)/shard_map/expert/pallas_call | solution.py:222
  56.8 1.3 %fusion = f32[128,64]{0,1:T(8,128)S(1)} fusion(bf16[1,128,2048]{2,1,0:T(8,128)(2,1)} %param.10, bf16[1,2048,64]{1,2,0:T(8,128)(2,1)S(1)} %copy-done), kind=kOutput, calls=%fused_computation.3 | convolution fusion | flops 33554432 | bytes 819200 | tf_op jit(solution)/shard_map/dot_general | solution.py:348
  59.4 3.9 %collective-permute-start.15 = (bf16[32,2176]{1,0:T(8,128)(2,1)S(1)}, bf16[32,2176]{1,0:T(8,128)(2,1)S(1)}, u32[]{:S(2)}, u32[]{:S(2)}) collective-permute-start(bf16[32,2176]{1,0:T(8,128)(2,1)S(1)} %get-tuple-element.33), channel_id=1, source_target_pairs={{0,8},{4,12},{8,0},{12,4},{1,9},{5,13},{9,1},{13,5},{2,10},{6,14},... | collective-permute-start | bytes 417800 | tf_op jit(solution)/shard_map/ppermute | solution.py:17
  63.3 3.4 %collective-permute-done.13.refs_0_ = bf16[32,2176]{1,0:T(8,128)(2,1)S(1)} collective-permute-done((bf16[32,2176]{1,0:T(8,128)(2,1)S(1)}, bf16[32,2176]{1,0:T(8,128)(2,1)S(1)}, u32[]{:S(2)}, u32[]{:S(2)}) %collective-permute-start.13) | collective-permute-done | bytes 139296 | tf_op jit(solution)/shard_map/ppermute | solution.py:17
  66.7 1.8 %collective-permute-start.14 = (bf16[32,2048]{1,0:T(8,128)(2,1)S(1)}, bf16[32,2048]{1,0:T(8,128)(2,1)S(1)}, u32[]{:S(2)}, u32[]{:S(2)}) collective-permute-start(bf16[32,2048]{1,0:T(8,128)(2,1)S(1)} %held.11), channel_id=1, source_target_pairs={{0,2},{2,0},{1,3},{3,1},{4,6},{6,4},{5,7},{7,5},{8,10},{10,8},{9,1... | collective-permute-start | bytes 393224 | tf_op jit(solution)/shard_map/ppermute | solution.py:284
  68.7 5.1 %collective-permute-done.15.refs_1_ = bf16[32,2176]{1,0:T(8,128)(2,1)S(1)} collective-permute-done((bf16[32,2176]{1,0:T(8,128)(2,1)S(1)}, bf16[32,2176]{1,0:T(8,128)(2,1)S(1)}, u32[]{:S(2)}, u32[]{:S(2)}) %collective-permute-start.15) | collective-permute-done | bytes 139296 | tf_op jit(solution)/shard_map/ppermute | solution.py:17
  74.0 1.6 %collective-permute-start.17 = (bf16[32,2048]{1,0:T(8,128)(2,1)S(1)}, bf16[32,2048]{1,0:T(8,128)(2,1)S(1)}, u32[]{:S(2)}, u32[]{:S(2)}) collective-permute-start(bf16[32,2048]{1,0:T(8,128)(2,1)S(1)} %get-tuple-element.35), channel_id=1, source_target_pairs={{0,2},{2,0},{1,3},{3,1},{4,6},{6,4},{5,7},{7,5},{8,10},{10,8},{9,1... | collective-permute-start | bytes 393224 | tf_op jit(solution)/shard_map/ppermute | solution.py:284
  76.5 0.8 maximum_bitcast_fusion.1
  77.3 2.7 %collective-permute-done.17 = bf16[32,2048]{1,0:T(8,128)(2,1)S(1)} collective-permute-done((bf16[32,2048]{1,0:T(8,128)(2,1)S(1)}, bf16[32,2048]{1,0:T(8,128)(2,1)S(1)}, u32[]{:S(2)}, u32[]{:S(2)}) %collective-permute-start.17) | collective-permute-done | bytes 131104 | tf_op jit(solution)/shard_map/ppermute | solution.py:284
  80.0 1.3 %collective-permute-done.19 = bf16[32,2048]{1,0:T(8,128)(2,1)S(1)} collective-permute-done((bf16[32,2048]{1,0:T(8,128)(2,1)S(1)}, bf16[32,2048]{1,0:T(8,128)(2,1)S(1)}, u32[]{:S(2)}, u32[]{:S(2)}) %collective-permute-start.19) | collective-permute-done | bytes 131104 | tf_op jit(solution)/shard_map/ppermute | solution.py:17
  81.4 0.8 %maximum_bitcast_fusion = bf16[1,128,2048]{2,1,0:T(8,128)(2,1)} fusion(bf16[64,2048]{1,0:T(8,128)(2,1)S(1)} %get-tuple-element.41, bf16[64,2048]{1,0:T(8,128)(2,1)S(1)} %get-tuple-element.40), kind=kLoop, calls=%fused_computation.2 | loop fusion | flops 1048576 | bytes 1048576 | tf_op jit(solution)/shard_map/broadcast_in_dim | solution.py:368
  (98 shorter events, 5.7 us)
Async XLA Ops:
  0.6 56.2 %copy-start = (bf16[1,2048,64]{1,2,0:T(8,128)(2,1)S(1)}, bf16[1,2048,64]{1,2,0:T(8,128)(2,1)}, u32[]{:S(2)}) copy-start(bf16[1,2048,64]{1,2,0:T(8,128)(2,1)} %param.17) | copy-start | bytes 786436
  1.6 21.5 %collective-permute-start.2 = (bf16[32,2048]{1,0:T(8,128)(2,1)S(1)}, bf16[32,2048]{1,0:T(8,128)(2,1)S(1)}, u32[]{:S(2)}, u32[]{:S(2)}) collective-permute-start(bf16[32,2048]{1,0:T(8,128)(2,1)S(1)} %get-tuple-element.39.cot_ref), channel_id=1, source_target_pairs={{0,12},{4,8},{8,4},{12,0},{1,13},{5,9},{9,5},{13,1},{2,14},{6,10},... | collective-permute-start | bytes 393224 | tf_op jit(solution)/shard_map/ppermute | solution.py:17
  6.7 16.4 %collective-permute-start.1 = (bf16[32,2048]{1,0:T(8,128)(2,1)S(1)}, bf16[32,2048]{1,0:T(8,128)(2,1)S(1)}, u32[]{:S(2)}, u32[]{:S(2)}) collective-permute-start(bf16[32,2048]{1,0:T(8,128)(2,1)S(1)} %get-tuple-element.39.cot_ref), channel_id=1, source_target_pairs={{0,8},{4,12},{8,0},{12,4},{1,9},{5,13},{9,1},{13,5},{2,10},{6,14},... | collective-permute-start | bytes 393224 | tf_op jit(solution)/shard_map/ppermute | solution.py:17
  6.7 11.9 %collective-permute-start = (bf16[32,2048]{1,0:T(8,128)(2,1)S(1)}, bf16[32,2048]{1,0:T(8,128)(2,1)S(1)}, u32[]{:S(2)}, u32[]{:S(2)}) collective-permute-start(bf16[32,2048]{1,0:T(8,128)(2,1)S(1)} %get-tuple-element.39.cot_ref), channel_id=1, source_target_pairs={{0,4},{4,0},{8,12},{12,8},{1,5},{5,1},{9,13},{13,9},{2,6},{6,2},{1... | collective-permute-start | bytes 393224 | tf_op jit(solution)/shard_map/ppermute | solution.py:17
  9.1 15.9 %slice-start.2 = ((s8[14680064]{0:T(1024)(128)(4,1)}), s8[4194304]{0:T(1024)(128)(4,1)S(1)}, s32[]{:S(2)}) async-start(s8[14680064]{0:T(1024)(128)(4,1)} %bitcast.49), calls=%async_computation.2 | async-start | bytes 8388608
  18.6 15.9 %collective-permute-start.10 = (bf16[32,2048]{1,0:T(8,128)(2,1)S(1)}, bf16[32,2048]{1,0:T(8,128)(2,1)S(1)}, u32[]{:S(2)}, u32[]{:S(2)}) collective-permute-start(bf16[32,2048]{1,0:T(8,128)(2,1)S(1)} %held.6), channel_id=1, source_target_pairs={{0,12},{4,8},{8,4},{12,0},{1,13},{5,9},{9,5},{13,1},{2,14},{6,10},... | collective-permute-start | bytes 393224 | tf_op jit(solution)/shard_map/ppermute | solution.py:17
  22.4 12.1 %collective-permute-start.9 = (bf16[32,2048]{1,0:T(8,128)(2,1)S(1)}, bf16[32,2048]{1,0:T(8,128)(2,1)S(1)}, u32[]{:S(2)}, u32[]{:S(2)}) collective-permute-start(bf16[32,2048]{1,0:T(8,128)(2,1)S(1)} %held.6), channel_id=1, source_target_pairs={{0,8},{4,12},{8,0},{12,4},{1,9},{5,13},{9,1},{13,5},{2,10},{6,14},... | collective-permute-start | bytes 393224 | tf_op jit(solution)/shard_map/ppermute | solution.py:17
  22.4 12.0 %collective-permute-start.8 = (bf16[32,2048]{1,0:T(8,128)(2,1)S(1)}, bf16[32,2048]{1,0:T(8,128)(2,1)S(1)}, u32[]{:S(2)}, u32[]{:S(2)}) collective-permute-start(bf16[32,2048]{1,0:T(8,128)(2,1)S(1)} %held.6), channel_id=1, source_target_pairs={{0,4},{4,0},{8,12},{12,8},{1,5},{5,1},{9,13},{13,9},{2,6},{6,2},{1... | collective-permute-start | bytes 393224 | tf_op jit(solution)/shard_map/ppermute | solution.py:17
  23.1 1.8 %collective-permute-start.3 = (bf16[96,2048]{1,0:T(8,128)(2,1)S(1)}, bf16[96,2048]{1,0:T(8,128)(2,1)S(1)}, u32[]{:S(2)}, u32[]{:S(2)}) collective-permute-start(bf16[96,2048]{1,0:T(8,128)(2,1)S(1)} %pad_maximum_fusion), channel_id=1, source_target_pairs={{0,1},{1,0},{2,3},{3,2},{4,5},{5,4},{6,7},{7,6},{8,9},{9,8},{10,11... | collective-permute-start | bytes 1179656 | tf_op jit(solution)/shard_map/ppermute | solution.py:17
  34.6 1.8 %collective-permute-start.11 = (bf16[96,2048]{1,0:T(8,128)(2,1)S(1)}, bf16[96,2048]{1,0:T(8,128)(2,1)S(1)}, u32[]{:S(2)}, u32[]{:S(2)}) collective-permute-start(bf16[96,2048]{1,0:T(8,128)(2,1)S(1)} %pad_maximum_fusion.1), channel_id=1, source_target_pairs={{0,1},{1,0},{2,3},{3,2},{4,5},{5,4},{6,7},{7,6},{8,9},{9,8},{10,11... | collective-permute-start | bytes 1179656 | tf_op jit(solution)/shard_map/ppermute | solution.py:17
  34.8 2.4 %collective-permute-start.4 = (bf16[128,2176]{1,0:T(8,128)(2,1)S(1)}, bf16[128,2176]{1,0:T(8,128)(2,1)S(1)}, u32[]{:S(2)}, u32[]{:S(2)}) collective-permute-start(bf16[128,2176]{1,0:T(8,128)(2,1)S(1)} %get-tuple-element.23), channel_id=1, source_target_pairs={{0,1},{1,0},{2,3},{3,2},{4,5},{5,4},{6,7},{7,6},{8,9},{9,8},{10,11... | collective-permute-start | bytes 1671176 | tf_op jit(solution)/shard_map/ppermute | solution.py:17
  37.3 19.1 %collective-permute-start.5 = (bf16[32,2176]{1,0:T(8,128)(2,1)S(1)}, bf16[32,2176]{1,0:T(8,128)(2,1)S(1)}, u32[]{:S(2)}, u32[]{:S(2)}) collective-permute-start(bf16[32,2176]{1,0:T(8,128)(2,1)S(1)} %get-tuple-element.25.refs_0_), channel_id=1, source_target_pairs={{0,4},{4,0},{8,12},{12,8},{1,5},{5,1},{9,13},{13,9},{2,6},{6,2},{1... | collective-permute-start | bytes 417800 | tf_op jit(solution)/shard_map/ppermute | solution.py:17
  38.8 17.6 %collective-permute-start.6 = (bf16[32,2176]{1,0:T(8,128)(2,1)S(1)}, bf16[32,2176]{1,0:T(8,128)(2,1)S(1)}, u32[]{:S(2)}, u32[]{:S(2)}) collective-permute-start(bf16[32,2176]{1,0:T(8,128)(2,1)S(1)} %get-tuple-element.26.refs_1_), channel_id=1, source_target_pairs={{0,8},{4,12},{8,0},{12,4},{1,9},{5,13},{9,1},{13,5},{2,10},{6,14},... | collective-permute-start | bytes 417800 | tf_op jit(solution)/shard_map/ppermute | solution.py:17
  41.7 14.7 %collective-permute-start.7 = (bf16[32,2176]{1,0:T(8,128)(2,1)S(1)}, bf16[32,2176]{1,0:T(8,128)(2,1)S(1)}, u32[]{:S(2)}, u32[]{:S(2)}) collective-permute-start(bf16[32,2176]{1,0:T(8,128)(2,1)S(1)} %get-tuple-element.27.refs_2_), channel_id=1, source_target_pairs={{0,12},{4,8},{8,4},{12,0},{1,13},{5,9},{9,5},{13,1},{2,14},{6,10},... | collective-permute-start | bytes 417800 | tf_op jit(solution)/shard_map/ppermute | solution.py:17
  56.4 19.6 %copy-start.4 = (f32[1,128,64]{1,2,0:T(8,128)S(1)}, f32[1,128,64]{1,2,0:T(8,128)}, u32[]{:S(2)}) copy-start(f32[1,128,64]{1,2,0:T(8,128)} %param.16) | copy-start | bytes 98308
  56.4 2.0 %collective-permute-start.12 = (bf16[128,2176]{1,0:T(8,128)(2,1)S(1)}, bf16[128,2176]{1,0:T(8,128)(2,1)S(1)}, u32[]{:S(2)}, u32[]{:S(2)}) collective-permute-start(bf16[128,2176]{1,0:T(8,128)(2,1)S(1)} %held.10), channel_id=1, source_target_pairs={{0,1},{1,0},{2,3},{3,2},{4,5},{5,4},{6,7},{7,6},{8,9},{9,8},{10,11... | collective-permute-start | bytes 1671176 | tf_op jit(solution)/shard_map/ppermute | solution.py:17
  58.6 8.1 %collective-permute-start.13 = (bf16[32,2176]{1,0:T(8,128)(2,1)S(1)}, bf16[32,2176]{1,0:T(8,128)(2,1)S(1)}, u32[]{:S(2)}, u32[]{:S(2)}) collective-permute-start(bf16[32,2176]{1,0:T(8,128)(2,1)S(1)} %get-tuple-element.31), channel_id=1, source_target_pairs={{0,4},{4,0},{8,12},{12,8},{1,5},{5,1},{9,13},{13,9},{2,6},{6,2},{1... | collective-permute-start | bytes 417800 | tf_op jit(solution)/shard_map/ppermute | solution.py:17
  59.4 14.4 %collective-permute-start.15 = (bf16[32,2176]{1,0:T(8,128)(2,1)S(1)}, bf16[32,2176]{1,0:T(8,128)(2,1)S(1)}, u32[]{:S(2)}, u32[]{:S(2)}) collective-permute-start(bf16[32,2176]{1,0:T(8,128)(2,1)S(1)} %get-tuple-element.33), channel_id=1, source_target_pairs={{0,8},{4,12},{8,0},{12,4},{1,9},{5,13},{9,1},{13,5},{2,10},{6,14},... | collective-permute-start | bytes 417800 | tf_op jit(solution)/shard_map/ppermute | solution.py:17
  63.2 10.5 %collective-permute-start.16 = (bf16[32,2176]{1,0:T(8,128)(2,1)S(1)}, bf16[32,2176]{1,0:T(8,128)(2,1)S(1)}, u32[]{:S(2)}, u32[]{:S(2)}) collective-permute-start(bf16[32,2176]{1,0:T(8,128)(2,1)S(1)} %get-tuple-element.34), channel_id=1, source_target_pairs={{0,12},{4,8},{8,4},{12,0},{1,13},{5,9},{9,5},{13,1},{2,14},{6,10},... | collective-permute-start | bytes 417800 | tf_op jit(solution)/shard_map/ppermute | solution.py:17
  66.7 7.0 %collective-permute-start.14 = (bf16[32,2048]{1,0:T(8,128)(2,1)S(1)}, bf16[32,2048]{1,0:T(8,128)(2,1)S(1)}, u32[]{:S(2)}, u32[]{:S(2)}) collective-permute-start(bf16[32,2048]{1,0:T(8,128)(2,1)S(1)} %held.11), channel_id=1, source_target_pairs={{0,2},{2,0},{1,3},{3,1},{4,6},{6,4},{5,7},{7,5},{8,10},{10,8},{9,1... | collective-permute-start | bytes 393224 | tf_op jit(solution)/shard_map/ppermute | solution.py:284
  74.0 1.8 %collective-permute-start.20 = (f32[64,128]{1,0:T(8,128)S(1)}, f32[64,128]{1,0:T(8,128)S(1)}, u32[]{:S(2)}, u32[]{:S(2)}) collective-permute-start(f32[64,128]{1,0:T(8,128)S(1)} %constant_dynamic-update-slice_fusion.12), channel_id=1, source_target_pairs={{0,1},{1,0},{2,3},{3,2},{4,5},{5,4},{6,7},{7,6},{8,9},{9,8},{10,11... | collective-permute-start | bytes 98312 | tf_op jit(solution)/shard_map/ppermute | solution.py:17
  74.0 5.9 %collective-permute-start.17 = (bf16[32,2048]{1,0:T(8,128)(2,1)S(1)}, bf16[32,2048]{1,0:T(8,128)(2,1)S(1)}, u32[]{:S(2)}, u32[]{:S(2)}) collective-permute-start(bf16[32,2048]{1,0:T(8,128)(2,1)S(1)} %get-tuple-element.35), channel_id=1, source_target_pairs={{0,2},{2,0},{1,3},{3,1},{4,6},{6,4},{5,7},{7,5},{8,10},{10,8},{9,1... | collective-permute-start | bytes 393224 | tf_op jit(solution)/shard_map/ppermute | solution.py:284
  75.6 1.7 %collective-permute-start.18 = (bf16[32,2048]{1,0:T(8,128)(2,1)S(1)}, bf16[32,2048]{1,0:T(8,128)(2,1)S(1)}, u32[]{:S(2)}, u32[]{:S(2)}) collective-permute-start(bf16[32,2048]{1,0:T(8,128)(2,1)S(1)} %collective-permute-done.14.refs_3_), channel_id=1, source_target_pairs={{0,1},{1,0},{2,3},{3,2},{4,5},{5,4},{6,7},{7,6},{8,9},{9,8},{10,11... | collective-permute-start | bytes 393224 | tf_op jit(solution)/shard_map/ppermute | solution.py:17
  79.9 1.3 %collective-permute-start.19 = (bf16[32,2048]{1,0:T(8,128)(2,1)S(1)}, bf16[32,2048]{1,0:T(8,128)(2,1)S(1)}, u32[]{:S(2)}, u32[]{:S(2)}) collective-permute-start(bf16[32,2048]{1,0:T(8,128)(2,1)S(1)} %collective-permute-done.17), channel_id=1, source_target_pairs={{0,1},{1,0},{2,3},{3,2},{4,5},{5,4},{6,7},{7,6},{8,9},{9,8},{10,11... | collective-permute-start | bytes 393224 | tf_op jit(solution)/shard_map/ppermute | solution.py:17
  (8 other events, 101.9 us)

commit v2 on v0

--- a/solution.py
+++ b/solution.py
@@ -25,15 +25,17 @@
     refs[-1][...] = block_ref[...]
 
 
-def held(block, *events):
+def held(block, *events, beside=()):
     return pl.pallas_call(
         held_kernel,
-        in_specs=[RESIDENT] + [ANYWHERE] * len(events),
+        in_specs=[RESIDENT]
+        + [ANYWHERE] * len(events)
+        + [pl.BlockSpec(memory_space=pltpu.HBM)] * len(beside),
         out_specs=RESIDENT,
         out_shape=jax.ShapeDtypeStruct(block.shape, block.dtype),
         compiler_params=pltpu.CompilerParams(vmem_limit_bytes=1 << 20),
         name="held",
-    )(block, *events)
+    )(block, *events, *beside)
 
 
 def merge_kernel(keep_ref, came_ref, own_ref, *sent_refs):
@@ -304,7 +306,9 @@
         mark = (mine[1],)
         if keep:
             for slot in order:
-                mine[slot] = held(mine[slot], *keep)
+                mine[slot] = held(
+                    mine[slot], *keep, beside=(up_weight[0, 0], down_weight[0, 0])
+                )
         traded = xored(jnp.concatenate([mine[slot] for slot in order], axis=0), "tensor", 1)
         for at, slot in enumerate(order):
             theirs[slot] = traded[at * rows : (at + 1) * rows]

time: 81.9 us -> 89.5 us (1.093)
  local copies, waits for them, and re-layouts: 11.4 us -> 19.2 us
    unnamed x39 -> x51, local copies, waits for them, and re-layouts: 9.59 us -> 17.3 us
  transfers between devices with their start and end apart: 21 -> 21, of which waited for: 8 -> 8; matrix products, arithmetic and copies ran while one was open for 6% -> 6% of each run, Pallas kernels for 30% -> 28%
where the time goes in v2:
time: 89.5 us; the launch traced here: 89.1 us
  Pallas kernels  24.9 us (28%)
  starting transfers between devices  23.4 us (26%)
  local copies, waits for them, and re-layouts  19.2 us (21%)
  waiting for transfers between devices  16.4 us (18%)
  other arithmetic  2.14 us (2%)
  matrix products  1.87 us (2%)
  between operations  1.12 us (1%)
    ppermute x19, starting transfers between devices, xored(): return lax.ppermute(block, axis, [(i, i ^ bits) for i in range(n)])  20.1 us
    pallas_call x2, Pallas kernels, expert(): pl.pallas_call(functools.partial(expert_kernel, tile_f, tile_d), grid=(1,...  18.7 us
    unnamed x51, local copies, waits for them, and re-layouts  17.3 us
    ppermute x19, waiting for transfers between devices, xored(): return lax.ppermute(block, axis, [(i, i ^ bits) for i in range(n)])  13.7 us
    pallas_call x1, Pallas kernels, slopes(): pl.pallas_call(functools.partial(slope_kernel, groups), grid_spec=pltpu.P...  5.6 us
    ppermute x2, starting transfers between devices, below(): lax.ppermute(block, 'section', [(s, (s - 1) % sections) for s in range(se...  3.31 us
    ppermute x2, waiting for transfers between devices, below(): lax.ppermute(block, 'section', [(s, (s - 1) % sections) for s in range(se...  2.65 us
  transfers between devices with their start and end apart: 21, of which 8 were waited for; matrix products, arithmetic and copies ran while one was open for 6% of the time, Pallas kernels for 28%

profile of v2, /device:TPU:0, one launch (start us, length us, event | category | flops | bytes accessed | tf_op | source)
XLA Modules:
  0.0 89.1 jit_solution(7371162677254872296)
XLA Ops:
  0.7 1.0 %constant_dynamic-update-slice_fusion.3 = (bf16[256,2048]{1,0:T(8,128)(2,1)S(1)}, bf16[32,2048]{1,0:T(8,128)(2,1)S(1)}) fusion(bf16[1,128,2048]{2,1,0:T(8,128)(2,1)} %param.10, s32[]{:T(128)S(6)} %select_n.45), kind=kLoop, calls=%fused_computation.38 | loop fusion | bytes 393220
  1.6 5.1 %collective-permute-start.2 = (bf16[32,2048]{1,0:T(8,128)(2,1)S(1)}, bf16[32,2048]{1,0:T(8,128)(2,1)S(1)}, u32[]{:S(2)}, u32[]{:S(2)}) collective-permute-start(bf16[32,2048]{1,0:T(8,128)(2,1)S(1)} %get-tuple-element.39.cot_ref), channel_id=1, source_target_pairs={{0,12},{4,8},{8,4},{12,0},{1,13},{5,9},{9,5},{13,1},{2,14},{6,10},... | collective-permute-start | bytes 393224 | tf_op jit(solution)/shard_map/ppermute | solution.py:17
  9.1 2.2 %copy-done.3 = bf16[1,1,4,128,3584]{4,3,2,1,0:T(8,128)(2,1)S(1)} copy-done((bf16[1,1,4,128,3584]{4,3,2,1,0:T(8,128)(2,1)S(1)}, bf16[1,1,4,128,3584]{4,3,2,1,0:T(8,128)(2,1)}, u32[]{:S(2)}) %copy-start.3) | copy-done | bytes 3670040
  11.3 1.2 %copy-done.4 = bf16[1,1,3584,64]{2,3,1,0:T(8,128)(2,1)S(1)} copy-done((bf16[1,1,3584,64]{2,3,1,0:T(8,128)(2,1)S(1)}, bf16[1,1,3584,64]{2,3,1,0:T(8,128)(2,1)}, u32[]{:S(2)}) %copy-start.4) | copy-done | bytes 458776
  12.5 5.6 %slopes.1 = (bf16[2,3584,256]{2,1,0:T(8,128)(2,1)S(1)}, f32[2,256,64]{2,1,0:T(8,128)S(1)}) custom-call(s32[2]{0:T(128)S(1)} %pad_add_fusion.index_ref, bf16[4,2,2,32,3584]{4,3,2,1,0:T(8,128)(2,1)S(1)} %bitcast.61, bf16[4,2,2,32,3584]{4,3,2,1,0:T(8,128)(2,1)S(1)} %bitcast.62, bf16[4,2,2,32,3584]{4,3,2,1,0:T(8,128)(2,1)S(1)} %bitcast.63, ...), custom_call_target="tpu_custom_call" | custom-call | flops 234881024 | bytes 7340032 | tf_op jit(solution)/shard_map/slopes/pallas_call | solution.py:136
  18.3 3.8 %collective-permute-start.10 = (bf16[32,2048]{1,0:T(8,128)(2,1)S(1)}, bf16[32,2048]{1,0:T(8,128)(2,1)S(1)}, u32[]{:S(2)}, u32[]{:S(2)}) collective-permute-start(bf16[32,2048]{1,0:T(8,128)(2,1)S(1)} %held.6), channel_id=1, source_target_pairs={{0,12},{4,8},{8,4},{12,0},{1,13},{5,9},{9,5},{13,1},{2,14},{6,10},... | collective-permute-start | bytes 393224 | tf_op jit(solution)/shard_map/ppermute | solution.py:17
  23.0 1.6 %collective-permute-done.3 = bf16[96,2048]{1,0:T(8,128)(2,1)S(1)} collective-permute-done((bf16[96,2048]{1,0:T(8,128)(2,1)S(1)}, bf16[96,2048]{1,0:T(8,128)(2,1)S(1)}, u32[]{:S(2)}, u32[]{:S(2)}) %collective-permute-start.3) | collective-permute-done | bytes 393248 | tf_op jit(solution)/shard_map/ppermute | solution.py:17
  24.7 9.4 %expert.2 = (f32[128,2176]{1,0:T(8,128)S(1)}, bf16[128,2176]{1,0:T(8,128)(2,1)S(1)}) custom-call(bf16[256,2048]{1,0:T(8,128)(2,1)S(1)} %slice_dynamic-update-slice_fusion.3.rows_ref, bf16[2,3584,256]{2,1,0:T(8,128)(2,1)S(1)} %get-tuple-element.20.slope_ref, f32[2,256,64]{2,1,0:T(8,128)S(1)} %get-tuple-element.21.down_part_ref, ...), custom_call_target="tpu_custom_call" | custom-call | flops 7516192768 | bytes 29360128 | tf_op jit(solution)/shard_map/expert/pallas_call | solution.py:219
  34.1 5.2 %copy-done.2 = bf16[1,1,2048,3584]{3,2,1,0:T(8,128)(2,1)S(1)} copy-done((bf16[1,1,2048,3584]{3,2,1,0:T(8,128)(2,1)S(1)}, bf16[1,1,2048,3584]{3,2,1,0:T(8,128)(2,1)}, u32[]{:S(2)}) %copy-start.2) | copy-done | bytes 14680088
  40.0 1.2 %collective-permute-done.11 = bf16[96,2048]{1,0:T(8,128)(2,1)S(1)} collective-permute-done((bf16[96,2048]{1,0:T(8,128)(2,1)S(1)}, bf16[96,2048]{1,0:T(8,128)(2,1)S(1)}, u32[]{:S(2)}, u32[]{:S(2)}) %collective-permute-start.11) | collective-permute-done | bytes 393248 | tf_op jit(solution)/shard_map/ppermute | solution.py:17
  42.1 1.4 %collective-permute-start.5 = (bf16[32,2176]{1,0:T(8,128)(2,1)S(1)}, bf16[32,2176]{1,0:T(8,128)(2,1)S(1)}, u32[]{:S(2)}, u32[]{:S(2)}) collective-permute-start(bf16[32,2176]{1,0:T(8,128)(2,1)S(1)} %get-tuple-element.25.refs_0_), channel_id=1, source_target_pairs={{0,4},{4,0},{8,12},{12,8},{1,5},{5,1},{9,13},{13,9},{2,6},{6,2},{1... | collective-permute-start | bytes 417800 | tf_op jit(solution)/shard_map/ppermute | solution.py:17
  43.5 2.9 %collective-permute-start.6 = (bf16[32,2176]{1,0:T(8,128)(2,1)S(1)}, bf16[32,2176]{1,0:T(8,128)(2,1)S(1)}, u32[]{:S(2)}, u32[]{:S(2)}) collective-permute-start(bf16[32,2176]{1,0:T(8,128)(2,1)S(1)} %get-tuple-element.26.refs_1_), channel_id=1, source_target_pairs={{0,8},{4,12},{8,0},{12,4},{1,9},{5,13},{9,1},{13,5},{2,10},{6,14},... | collective-permute-start | bytes 417800 | tf_op jit(solution)/shard_map/ppermute | solution.py:17
  46.5 5.2 %copy-done.1 = bf16[1,1,3584,2048]{3,2,1,0:T(8,128)(2,1)S(1)} copy-done((bf16[1,1,3584,2048]{3,2,1,0:T(8,128)(2,1)S(1)}, bf16[1,1,3584,2048]{3,2,1,0:T(8,128)(2,1)}, u32[]{:S(2)}) %copy-start.1) | copy-done | bytes 14680088
  51.7 9.3 %expert.3 = (f32[128,2176]{1,0:T(8,128)S(1)}, bf16[128,2176]{1,0:T(8,128)(2,1)S(1)}) custom-call(bf16[256,2048]{1,0:T(8,128)(2,1)S(1)} %slice_dynamic-update-slice_fusion.rows_ref, bf16[2,3584,256]{2,1,0:T(8,128)(2,1)S(1)} %get-tuple-element.20.slope_ref, f32[2,256,64]{2,1,0:T(8,128)S(1)} %get-tuple-element.21.down_part_ref, bf16[64,3584]{1,0:T(8,128)(2,1)S(1)} %bitcast.71, ...), custom_call_target="tpu_custom_call" | custom-call | flops 7516192768 | bytes 29360128 | tf_op jit(solution)/shard_map/expert/pallas_call | solution.py:219
  61.0 1.0 %copy-done.6 = f32[128,2176]{1,0:T(8,128)} copy-done((f32[128,2176]{1,0:T(8,128)}, f32[128,2176]{1,0:T(8,128)S(1)}, u32[]{:S(2)}) %copy-start.6) | copy-done | bytes 1114136
  62.5 1.3 %fusion = f32[128,64]{0,1:T(8,128)S(1)} fusion(bf16[1,128,2048]{2,1,0:T(8,128)(2,1)} %param.10, bf16[1,2048,64]{1,2,0:T(8,128)(2,1)S(1)} %copy-done), kind=kOutput, calls=%fused_computation.3 | convolution fusion | flops 33554432 | bytes 819200 | tf_op jit(solution)/shard_map/dot_general | solution.py:347
  64.1 1.2 %copy-done.7 = f32[128,2176]{1,0:T(8,128)S(1)} copy-done((f32[128,2176]{1,0:T(8,128)S(1)}, f32[128,2176]{1,0:T(8,128)}, u32[]{:S(2)}) %copy-start.7) | copy-done | bytes 1114136
  66.2 3.9 %collective-permute-start.15 = (bf16[32,2176]{1,0:T(8,128)(2,1)S(1)}, bf16[32,2176]{1,0:T(8,128)(2,1)S(1)}, u32[]{:S(2)}, u32[]{:S(2)}) collective-permute-start(bf16[32,2176]{1,0:T(8,128)(2,1)S(1)} %get-tuple-element.33), channel_id=1, source_target_pairs={{0,8},{4,12},{8,0},{12,4},{1,9},{5,13},{9,1},{13,5},{2,10},{6,14},... | collective-permute-start | bytes 417800 | tf_op jit(solution)/shard_map/ppermute | solution.py:17
  70.2 3.4 %collective-permute-done.13.refs_0_ = bf16[32,2176]{1,0:T(8,128)(2,1)S(1)} collective-permute-done((bf16[32,2176]{1,0:T(8,128)(2,1)S(1)}, bf16[32,2176]{1,0:T(8,128)(2,1)S(1)}, u32[]{:S(2)}, u32[]{:S(2)}) %collective-permute-start.13) | collective-permute-done | bytes 139296 | tf_op jit(solution)/shard_map/ppermute | solution.py:17
  73.6 1.8 %collective-permute-start.14 = (bf16[32,2048]{1,0:T(8,128)(2,1)S(1)}, bf16[32,2048]{1,0:T(8,128)(2,1)S(1)}, u32[]{:S(2)}, u32[]{:S(2)}) collective-permute-start(bf16[32,2048]{1,0:T(8,128)(2,1)S(1)} %held.11), channel_id=1, source_target_pairs={{0,2},{2,0},{1,3},{3,1},{4,6},{6,4},{5,7},{7,5},{8,10},{10,8},{9,1... | collective-permute-start | bytes 393224 | tf_op jit(solution)/shard_map/ppermute | solution.py:281
  75.5 5.1 %collective-permute-done.15.refs_1_ = bf16[32,2176]{1,0:T(8,128)(2,1)S(1)} collective-permute-done((bf16[32,2176]{1,0:T(8,128)(2,1)S(1)}, bf16[32,2176]{1,0:T(8,128)(2,1)S(1)}, u32[]{:S(2)}, u32[]{:S(2)}) %collective-permute-start.15) | collective-permute-done | bytes 139296 | tf_op jit(solution)/shard_map/ppermute | solution.py:17
  80.9 1.6 %collective-permute-start.17 = (bf16[32,2048]{1,0:T(8,128)(2,1)S(1)}, bf16[32,2048]{1,0:T(8,128)(2,1)S(1)}, u32[]{:S(2)}, u32[]{:S(2)}) collective-permute-start(bf16[32,2048]{1,0:T(8,128)(2,1)S(1)} %get-tuple-element.35), channel_id=1, source_target_pairs={{0,2},{2,0},{1,3},{3,1},{4,6},{6,4},{5,7},{7,5},{8,10},{10,8},{9,1... | collective-permute-start | bytes 393224 | tf_op jit(solution)/shard_map/ppermute | solution.py:281
  84.2 2.7 %collective-permute-done.17 = bf16[32,2048]{1,0:T(8,128)(2,1)S(1)} collective-permute-done((bf16[32,2048]{1,0:T(8,128)(2,1)S(1)}, bf16[32,2048]{1,0:T(8,128)(2,1)S(1)}, u32[]{:S(2)}, u32[]{:S(2)}) %collective-permute-start.17) | collective-permute-done | bytes 131104 | tf_op jit(solution)/shard_map/ppermute | solution.py:281
  86.8 1.3 %collective-permute-done.19 = bf16[32,2048]{1,0:T(8,128)(2,1)S(1)} collective-permute-done((bf16[32,2048]{1,0:T(8,128)(2,1)S(1)}, bf16[32,2048]{1,0:T(8,128)(2,1)S(1)}, u32[]{:S(2)}, u32[]{:S(2)}) %collective-permute-start.19) | collective-permute-done | bytes 131104 | tf_op jit(solution)/shard_map/ppermute | solution.py:17
  (108 shorter events, 9.6 us)
Async XLA Ops:
  0.6 61.9 %copy-start = (bf16[1,2048,64]{1,2,0:T(8,128)(2,1)S(1)}, bf16[1,2048,64]{1,2,0:T(8,128)(2,1)}, u32[]{:S(2)}) copy-start(bf16[1,2048,64]{1,2,0:T(8,128)(2,1)} %param.17) | copy-start | bytes 786436
  1.6 21.1 %collective-permute-start.2 = (bf16[32,2048]{1,0:T(8,128)(2,1)S(1)}, bf16[32,2048]{1,0:T(8,128)(2,1)S(1)}, u32[]{:S(2)}, u32[]{:S(2)}) collective-permute-start(bf16[32,2048]{1,0:T(8,128)(2,1)S(1)} %get-tuple-element.39.cot_ref), channel_id=1, source_target_pairs={{0,12},{4,8},{8,4},{12,0},{1,13},{5,9},{9,5},{13,1},{2,14},{6,10},... | collective-permute-start | bytes 393224 | tf_op jit(solution)/shard_map/ppermute | solution.py:17
  6.7 16.0 %collective-permute-start.1 = (bf16[32,2048]{1,0:T(8,128)(2,1)S(1)}, bf16[32,2048]{1,0:T(8,128)(2,1)S(1)}, u32[]{:S(2)}, u32[]{:S(2)}) collective-permute-start(bf16[32,2048]{1,0:T(8,128)(2,1)S(1)} %get-tuple-element.39.cot_ref), channel_id=1, source_target_pairs={{0,8},{4,12},{8,0},{12,4},{1,9},{5,13},{9,1},{13,5},{2,10},{6,14},... | collective-permute-start | bytes 393224 | tf_op jit(solution)/shard_map/ppermute | solution.py:17
  6.7 11.5 %collective-permute-start = (bf16[32,2048]{1,0:T(8,128)(2,1)S(1)}, bf16[32,2048]{1,0:T(8,128)(2,1)S(1)}, u32[]{:S(2)}, u32[]{:S(2)}) collective-permute-start(bf16[32,2048]{1,0:T(8,128)(2,1)S(1)} %get-tuple-element.39.cot_ref), channel_id=1, source_target_pairs={{0,4},{4,0},{8,12},{12,8},{1,5},{5,1},{9,13},{13,9},{2,6},{6,2},{1... | collective-permute-start | bytes 393224 | tf_op jit(solution)/shard_map/ppermute | solution.py:17
  9.1 15.5 %slice-start = ((s8[14680064]{0:T(1024)(128)(4,1)}), s8[4194304]{0:T(1024)(128)(4,1)S(1)}, s32[]{:S(2)}) async-start(s8[14680064]{0:T(1024)(128)(4,1)} %bitcast.49), calls=%async_computation | async-start | bytes 8388608
  18.3 21.1 %collective-permute-start.10 = (bf16[32,2048]{1,0:T(8,128)(2,1)S(1)}, bf16[32,2048]{1,0:T(8,128)(2,1)S(1)}, u32[]{:S(2)}, u32[]{:S(2)}) collective-permute-start(bf16[32,2048]{1,0:T(8,128)(2,1)S(1)} %held.6), channel_id=1, source_target_pairs={{0,12},{4,8},{8,4},{12,0},{1,13},{5,9},{9,5},{13,1},{2,14},{6,10},... | collective-permute-start | bytes 393224 | tf_op jit(solution)/shard_map/ppermute | solution.py:17
  22.1 17.2 %collective-permute-start.9 = (bf16[32,2048]{1,0:T(8,128)(2,1)S(1)}, bf16[32,2048]{1,0:T(8,128)(2,1)S(1)}, u32[]{:S(2)}, u32[]{:S(2)}) collective-permute-start(bf16[32,2048]{1,0:T(8,128)(2,1)S(1)} %held.6), channel_id=1, source_target_pairs={{0,8},{4,12},{8,0},{12,4},{1,9},{5,13},{9,1},{13,5},{2,10},{6,14},... | collective-permute-start | bytes 393224 | tf_op jit(solution)/shard_map/ppermute | solution.py:17
  22.1 12.0 %collective-permute-start.8 = (bf16[32,2048]{1,0:T(8,128)(2,1)S(1)}, bf16[32,2048]{1,0:T(8,128)(2,1)S(1)}, u32[]{:S(2)}, u32[]{:S(2)}) collective-permute-start(bf16[32,2048]{1,0:T(8,128)(2,1)S(1)} %held.6), channel_id=1, source_target_pairs={{0,4},{4,0},{8,12},{12,8},{1,5},{5,1},{9,13},{13,9},{2,6},{6,2},{1... | collective-permute-start | bytes 393224 | tf_op jit(solution)/shard_map/ppermute | solution.py:17
  22.8 1.8 %collective-permute-start.3 = (bf16[96,2048]{1,0:T(8,128)(2,1)S(1)}, bf16[96,2048]{1,0:T(8,128)(2,1)S(1)}, u32[]{:S(2)}, u32[]{:S(2)}) collective-permute-start(bf16[96,2048]{1,0:T(8,128)(2,1)S(1)} %pad_maximum_fusion), channel_id=1, source_target_pairs={{0,1},{1,0},{2,3},{3,2},{4,5},{5,4},{6,7},{7,6},{8,9},{9,8},{10,11... | collective-permute-start | bytes 1179656 | tf_op jit(solution)/shard_map/ppermute | solution.py:17
  39.4 1.8 %collective-permute-start.11 = (bf16[96,2048]{1,0:T(8,128)(2,1)S(1)}, bf16[96,2048]{1,0:T(8,128)(2,1)S(1)}, u32[]{:S(2)}, u32[]{:S(2)}) collective-permute-start(bf16[96,2048]{1,0:T(8,128)(2,1)S(1)} %pad_maximum_fusion.1), channel_id=1, source_target_pairs={{0,1},{1,0},{2,3},{3,2},{4,5},{5,4},{6,7},{7,6},{8,9},{9,8},{10,11... | collective-permute-start | bytes 1179656 | tf_op jit(solution)/shard_map/ppermute | solution.py:17
  39.6 2.4 %collective-permute-start.4 = (bf16[128,2176]{1,0:T(8,128)(2,1)S(1)}, bf16[128,2176]{1,0:T(8,128)(2,1)S(1)}, u32[]{:S(2)}, u32[]{:S(2)}) collective-permute-start(bf16[128,2176]{1,0:T(8,128)(2,1)S(1)} %get-tuple-element.23), channel_id=1, source_target_pairs={{0,1},{1,0},{2,3},{3,2},{4,5},{5,4},{6,7},{7,6},{8,9},{9,8},{10,11... | collective-permute-start | bytes 1671176 | tf_op jit(solution)/shard_map/ppermute | solution.py:17
  42.1 20.0 %collective-permute-start.5 = (bf16[32,2176]{1,0:T(8,128)(2,1)S(1)}, bf16[32,2176]{1,0:T(8,128)(2,1)S(1)}, u32[]{:S(2)}, u32[]{:S(2)}) collective-permute-start(bf16[32,2176]{1,0:T(8,128)(2,1)S(1)} %get-tuple-element.25.refs_0_), channel_id=1, source_target_pairs={{0,4},{4,0},{8,12},{12,8},{1,5},{5,1},{9,13},{13,9},{2,6},{6,2},{1... | collective-permute-start | bytes 417800 | tf_op jit(solution)/shard_map/ppermute | solution.py:17
  43.5 18.6 %collective-permute-start.6 = (bf16[32,2176]{1,0:T(8,128)(2,1)S(1)}, bf16[32,2176]{1,0:T(8,128)(2,1)S(1)}, u32[]{:S(2)}, u32[]{:S(2)}) collective-permute-start(bf16[32,2176]{1,0:T(8,128)(2,1)S(1)} %get-tuple-element.26.refs_1_), channel_id=1, source_target_pairs={{0,8},{4,12},{8,0},{12,4},{1,9},{5,13},{9,1},{13,5},{2,10},{6,14},... | collective-permute-start | bytes 417800 | tf_op jit(solution)/shard_map/ppermute | solution.py:17
  46.4 15.6 %collective-permute-start.7 = (bf16[32,2176]{1,0:T(8,128)(2,1)S(1)}, bf16[32,2176]{1,0:T(8,128)(2,1)S(1)}, u32[]{:S(2)}, u32[]{:S(2)}) collective-permute-start(bf16[32,2176]{1,0:T(8,128)(2,1)S(1)} %get-tuple-element.27.refs_2_), channel_id=1, source_target_pairs={{0,12},{4,8},{8,4},{12,0},{1,13},{5,9},{9,5},{13,1},{2,14},{6,10},... | collective-permute-start | bytes 417800 | tf_op jit(solution)/shard_map/ppermute | solution.py:17
  62.1 20.8 %copy-start.9 = (f32[1,128,64]{1,2,0:T(8,128)S(1)}, f32[1,128,64]{1,2,0:T(8,128)}, u32[]{:S(2)}) copy-start(f32[1,128,64]{1,2,0:T(8,128)} %param.16) | copy-start | bytes 98308
  62.1 2.0 %collective-permute-start.12 = (bf16[128,2176]{1,0:T(8,128)(2,1)S(1)}, bf16[128,2176]{1,0:T(8,128)(2,1)S(1)}, u32[]{:S(2)}, u32[]{:S(2)}) collective-permute-start(bf16[128,2176]{1,0:T(8,128)(2,1)S(1)} %held.10), channel_id=1, source_target_pairs={{0,1},{1,0},{2,3},{3,2},{4,5},{5,4},{6,7},{7,6},{8,9},{9,8},{10,11... | collective-permute-start | bytes 1671176 | tf_op jit(solution)/shard_map/ppermute | solution.py:17
  65.5 8.1 %collective-permute-start.13 = (bf16[32,2176]{1,0:T(8,128)(2,1)S(1)}, bf16[32,2176]{1,0:T(8,128)(2,1)S(1)}, u32[]{:S(2)}, u32[]{:S(2)}) collective-permute-start(bf16[32,2176]{1,0:T(8,128)(2,1)S(1)} %get-tuple-element.31), channel_id=1, source_target_pairs={{0,4},{4,0},{8,12},{12,8},{1,5},{5,1},{9,13},{13,9},{2,6},{6,2},{1... | collective-permute-start | bytes 417800 | tf_op jit(solution)/shard_map/ppermute | solution.py:17
  66.2 14.4 %collective-permute-start.15 = (bf16[32,2176]{1,0:T(8,128)(2,1)S(1)}, bf16[32,2176]{1,0:T(8,128)(2,1)S(1)}, u32[]{:S(2)}, u32[]{:S(2)}) collective-permute-start(bf16[32,2176]{1,0:T(8,128)(2,1)S(1)} %get-tuple-element.33), channel_id=1, source_target_pairs={{0,8},{4,12},{8,0},{12,4},{1,9},{5,13},{9,1},{13,5},{2,10},{6,14},... | collective-permute-start | bytes 417800 | tf_op jit(solution)/shard_map/ppermute | solution.py:17
  70.1 10.5 %collective-permute-start.16 = (bf16[32,2176]{1,0:T(8,128)(2,1)S(1)}, bf16[32,2176]{1,0:T(8,128)(2,1)S(1)}, u32[]{:S(2)}, u32[]{:S(2)}) collective-permute-start(bf16[32,2176]{1,0:T(8,128)(2,1)S(1)} %get-tuple-element.34), channel_id=1, source_target_pairs={{0,12},{4,8},{8,4},{12,0},{1,13},{5,9},{9,5},{13,1},{2,14},{6,10},... | collective-permute-start | bytes 417800 | tf_op jit(solution)/shard_map/ppermute | solution.py:17
  73.6 7.0 %collective-permute-start.14 = (bf16[32,2048]{1,0:T(8,128)(2,1)S(1)}, bf16[32,2048]{1,0:T(8,128)(2,1)S(1)}, u32[]{:S(2)}, u32[]{:S(2)}) collective-permute-start(bf16[32,2048]{1,0:T(8,128)(2,1)S(1)} %held.11), channel_id=1, source_target_pairs={{0,2},{2,0},{1,3},{3,1},{4,6},{6,4},{5,7},{7,5},{8,10},{10,8},{9,1... | collective-permute-start | bytes 393224 | tf_op jit(solution)/shard_map/ppermute | solution.py:281
  80.8 1.8 %collective-permute-start.20 = (f32[64,128]{1,0:T(8,128)S(1)}, f32[64,128]{1,0:T(8,128)S(1)}, u32[]{:S(2)}, u32[]{:S(2)}) collective-permute-start(f32[64,128]{1,0:T(8,128)S(1)} %constant_dynamic-update-slice_fusion.12), channel_id=1, source_target_pairs={{0,1},{1,0},{2,3},{3,2},{4,5},{5,4},{6,7},{7,6},{8,9},{9,8},{10,11... | collective-permute-start | bytes 98312 | tf_op jit(solution)/shard_map/ppermute | solution.py:17
  80.9 5.9 %collective-permute-start.17 = (bf16[32,2048]{1,0:T(8,128)(2,1)S(1)}, bf16[32,2048]{1,0:T(8,128)(2,1)S(1)}, u32[]{:S(2)}, u32[]{:S(2)}) collective-permute-start(bf16[32,2048]{1,0:T(8,128)(2,1)S(1)} %get-tuple-element.35), channel_id=1, source_target_pairs={{0,2},{2,0},{1,3},{3,1},{4,6},{6,4},{5,7},{7,5},{8,10},{10,8},{9,1... | collective-permute-start | bytes 393224 | tf_op jit(solution)/shard_map/ppermute | solution.py:281
  82.5 1.7 %collective-permute-start.18 = (bf16[32,2048]{1,0:T(8,128)(2,1)S(1)}, bf16[32,2048]{1,0:T(8,128)(2,1)S(1)}, u32[]{:S(2)}, u32[]{:S(2)}) collective-permute-start(bf16[32,2048]{1,0:T(8,128)(2,1)S(1)} %collective-permute-done.14.refs_3_), channel_id=1, source_target_pairs={{0,1},{1,0},{2,3},{3,2},{4,5},{5,4},{6,7},{7,6},{8,9},{9,8},{10,11... | collective-permute-start | bytes 393224 | tf_op jit(solution)/shard_map/ppermute | solution.py:17
  86.8 1.3 %collective-permute-start.19 = (bf16[32,2048]{1,0:T(8,128)(2,1)S(1)}, bf16[32,2048]{1,0:T(8,128)(2,1)S(1)}, u32[]{:S(2)}, u32[]{:S(2)}) collective-permute-start(bf16[32,2048]{1,0:T(8,128)(2,1)S(1)} %collective-permute-done.17), channel_id=1, source_target_pairs={{0,1},{1,0},{2,3},{3,2},{4,5},{5,4},{6,7},{7,6},{8,9},{9,8},{10,11... | collective-permute-start | bytes 393224 | tf_op jit(solution)/shard_map/ppermute | solution.py:17
  (13 other events, 91.2 us)

commit v3 on v0

--- a/solution.py
+++ b/solution.py
@@ -101,8 +101,14 @@
 
 def slope_kernel(groups, index_ref, *refs):
     del index_ref
-    pre_refs, sketch_ref = refs[:groups], refs[groups]
-    slope_ref, down_ref = refs[-2:]
+    pre_refs, sketch_ref, weight_hbm = refs[:groups], refs[groups], refs[groups + 1]
+    slope_ref, down_ref, weight_ref, weight_sem = refs[-4:]
+    load = pltpu.make_async_copy(weight_hbm, weight_ref, weight_sem)
+
+    @pl.when((pl.program_id(0) == 0) & (pl.program_id(1) == 0))
+    def _():
+        load.start()
+
     pre = jnp.concatenate([r[0, 0, 0] for r in pre_refs], axis=0).astype(jnp.float32)
     sig = 0.5 + 0.5 * jnp.tanh(0.5 * pre)
     hidden = pre * sig
@@ -118,13 +124,20 @@
 
     down_ref[0] += term
 
-
-def slopes(pre, sketch_t, place, core):
+    @pl.when(
+        (pl.program_id(0) == pl.num_programs(0) - 1) & (pl.program_id(1) == pl.num_programs(1) - 1)
+    )
+    def _():
+        load.wait()
+
+
+def slopes(pre, sketch_t, weight, place, core):
     n, _, chunks, rows, cols = pre.shape
     rank = sketch_t.shape[0]
     groups = 2 * n
     tile = tile_of(cols, 896)
     index = jnp.stack([place, core]).astype(jnp.int32)
+    weight = pltpu.with_memory_space_constraint(weight, pltpu.HBM)
 
     def spec_of(h, slot):
         return pl.BlockSpec(
@@ -137,15 +150,19 @@
             num_scalar_prefetch=1,
             grid=(chunks, cols // tile),
             in_specs=[spec_of(h, slot) for h in range(2) for slot in range(n)]
-            + [pl.BlockSpec((rank, tile), lambda a, j, ix: (0, j))],
+            + [pl.BlockSpec((rank, tile), lambda a, j, ix: (0, j))]
+            + [pl.BlockSpec(memory_space=pltpu.HBM)],
             out_specs=[
                 pl.BlockSpec((1, tile, groups * rows), lambda a, j, ix: (a, j, 0)),
                 pl.BlockSpec((1, groups * rows, rank), lambda a, j, ix: (a, 0, 0)),
+                RESIDENT,
             ],
+            scratch_shapes=[pltpu.SemaphoreType.DMA],
         ),
         out_shape=[
             jax.ShapeDtypeStruct((chunks, cols, groups * rows), jnp.bfloat16),
             jax.ShapeDtypeStruct((chunks, groups * rows, rank), jnp.float32),
+            jax.ShapeDtypeStruct(weight.shape, weight.dtype),
         ],
         cost_estimate=pl.CostEstimate(
             flops=2 * chunks * groups * rows * cols * rank,
@@ -154,7 +171,7 @@
         ),
         compiler_params=pltpu.CompilerParams(vmem_limit_bytes=7 << 20),
         name="slopes",
-    )(index, *([pre] * groups), sketch_t)
+    )(index, *([pre] * groups), sketch_t, weight)
 
 
 def expert_kernel(
@@ -214,6 +231,7 @@
     rank = sketch_t.shape[0]
     wide = width + 2 * rank
     tile_f, tile_d = tile_of(hidden_cols, 1792), tile_of(width, 1024)
+    up_local = pltpu.with_memory_space_constraint(up_local, pltpu.HBM)
     return pl.pallas_call(
         functools.partial(expert_kernel, tile_f, tile_d),
         grid=(1,),
@@ -291,7 +309,7 @@
     cot_mine = lax.dynamic_slice_in_dim(cot, core * half, half, 0)
     cot_theirs = lax.dynamic_slice_in_dim(cot, (1 - core) * half, half, 0)
     order = sorted(range(1, pieces), reverse=True)
-    slope, down_part = slopes(pre_all, sketch_t, place, core)
+    slope, down_part, down_here = slopes(pre_all, sketch_t, down_weight[0, 0], place, core)
     mark, keep, sent, grad, passed = (), (), (), (), ()
     below_mine, vectors = [], []
     for a in range(CHUNKS):
@@ -313,7 +331,7 @@
         )
 
         kept, give = expert(
-            a, rows_in, slope, down_part, sketch_t, down_weight[0, 0], up_weight[0, 0], *sent
+            a, rows_in, slope, down_part, sketch_t, down_here, up_weight[0, 0], *sent
         )
         keep = (kept,)
         if grad:

time: 81.9 us -> 79.6 us (0.972)
  local copies, waits for them, and re-layouts: 11.4 us -> 6.27 us
  waiting for transfers between devices: 16.4 us -> 18 us
    unnamed x39 -> x35, local copies, waits for them, and re-layouts: 9.59 us -> 4.42 us
    ppermute x19, waiting for transfers between devices: 13.7 us -> 15.4 us  [xored(): return lax.ppermute(block, axis, [(i, i ^ bits) for i in range(n)])]
    ppermute x19, starting transfers between devices: 20.1 us -> 21 us  [xored(): return lax.ppermute(block, axis, [(i, i ^ bits) for i in range(n)])]
  transfers between devices with their start and end apart: 21 -> 21, of which waited for: 8 -> 9; matrix products, arithmetic and copies ran while one was open for 6% -> 7% of each run, Pallas kernels for 30% -> 32%
where the time goes in v3:
time: 79.6 us; the launch traced here: 79.2 us
  Pallas kernels  25.8 us (32%)
  starting transfers between devices  24.1 us (30%)
  waiting for transfers between devices  18 us (23%)
  local copies, waits for them, and re-layouts  6.27 us (8%)
  other arithmetic  2.14 us (3%)
  matrix products  1.86 us (2%)
  between operations  1.06 us (1%)
    ppermute x19, starting transfers between devices, xored(): return lax.ppermute(block, axis, [(i, i ^ bits) for i in range(n)])  21 us
    pallas_call x2, Pallas kernels, expert(): pl.pallas_call(functools.partial(expert_kernel, tile_f, tile_d), grid=(1,...  18.8 us
    ppermute x19, waiting for transfers between devices, xored(): return lax.ppermute(block, axis, [(i, i ^ bits) for i in range(n)])  15.4 us
    pallas_call x1, Pallas kernels, slopes(): pl.pallas_call(functools.partial(slope_kernel, groups), grid_spec=pltpu.P...  6.27 us
    unnamed x35, local copies, waits for them, and re-layouts  4.42 us
    ppermute x2, starting transfers between devices, below(): lax.ppermute(block, 'section', [(s, (s - 1) % sections) for s in range(se...  3.12 us
    ppermute x2, waiting for transfers between devices, below(): lax.ppermute(block, 'section', [(s, (s - 1) % sections) for s in range(se...  2.66 us
    broadcast_in_dim x2, other arithmetic, per_device(): return (handed[None], features[None])  1.6 us
  transfers between devices with their start and end apart: 21, of which 9 were waited for; matrix products, arithmetic and copies ran while one was open for 7% of the time, Pallas kernels for 32%

profile of v3, /device:TPU:0, one launch (start us, length us, event | category | flops | bytes accessed | tf_op | source)
XLA Modules:
  0.0 79.2 jit_solution(14814391766661564890)
XLA Ops:
  0.7 1.0 %constant_dynamic-update-slice_fusion.3 = (bf16[256,2048]{1,0:T(8,128)(2,1)S(1)}, bf16[32,2048]{1,0:T(8,128)(2,1)S(1)}) fusion(bf16[1,128,2048]{2,1,0:T(8,128)(2,1)} %param.10, s32[]{:T(128)S(6)} %select_n.45), kind=kLoop, calls=%fused_computation.38 | loop fusion | bytes 393220
  1.6 5.1 %collective-permute-start.2 = (bf16[32,2048]{1,0:T(8,128)(2,1)S(1)}, bf16[32,2048]{1,0:T(8,128)(2,1)S(1)}, u32[]{:S(2)}, u32[]{:S(2)}) collective-permute-start(bf16[32,2048]{1,0:T(8,128)(2,1)S(1)} %get-tuple-element.41.cot_ref), channel_id=1, source_target_pairs={{0,12},{4,8},{8,4},{12,0},{1,13},{5,9},{9,5},{13,1},{2,14},{6,10},... | collective-permute-start | bytes 393224 | tf_op jit(solution)/shard_map/ppermute | solution.py:17
  8.1 0.9 %dynamic-slice_bitcast_fusion.1.block_ref.cot_ref = bf16[32,2048]{1,0:T(8,128)(2,1)S(1)} fusion(bf16[1,128,2048]{2,1,0:T(8,128)(2,1)} %param.10, s32[]{:T(128)S(6)} %add.13), kind=kLoop, calls=%fused_computation.15 | loop fusion | bytes 262148 | tf_op jit(solution)/shard_map/slice | solution.py:317
  9.1 2.0 %copy-done.1 = bf16[1,1,4,128,3584]{4,3,2,1,0:T(8,128)(2,1)S(1)} copy-done((bf16[1,1,4,128,3584]{4,3,2,1,0:T(8,128)(2,1)S(1)}, bf16[1,1,4,128,3584]{4,3,2,1,0:T(8,128)(2,1)}, u32[]{:S(2)}) %copy-start.1) | copy-done | bytes 3670040
  11.2 1.0 %copy-done.2 = bf16[1,1,3584,64]{2,3,1,0:T(8,128)(2,1)S(1)} copy-done((bf16[1,1,3584,64]{2,3,1,0:T(8,128)(2,1)S(1)}, bf16[1,1,3584,64]{2,3,1,0:T(8,128)(2,1)}, u32[]{:S(2)}) %copy-start.2) | copy-done | bytes 458776
  12.2 6.3 %slopes.1 = (bf16[2,3584,256]{2,1,0:T(8,128)(2,1)S(1)}, f32[2,256,64]{2,1,0:T(8,128)S(1)}, bf16[3584,2048]{1,0:T(8,128)(2,1)S(1)}) custom-call(s32[2]{0:T(128)S(1)} %pad_add_fusion.index_ref, bf16[4,2,2,32,3584]{4,3,2,1,0:T(8,128)(2,1)S(1)} %bitcast.49, bf16[4,2,2,32,3584]{4,3,2,1,0:T(8,128)(2,1)S(1)} %bitcast.50, bf16[4,2,2,32,3584]{4,3,2,1,0:T(8,128)(2,1)S(1)} %bitcast.51, ...), custom_call_target="tpu_custom_call" | custom-call | flops 234881024 | bytes 7340032 | tf_op jit(solution)/shard_map/slopes/pallas_call | solution.py:147
  18.6 3.8 %collective-permute-start.10 = (bf16[32,2048]{1,0:T(8,128)(2,1)S(1)}, bf16[32,2048]{1,0:T(8,128)(2,1)S(1)}, u32[]{:S(2)}, u32[]{:S(2)}) collective-permute-start(bf16[32,2048]{1,0:T(8,128)(2,1)S(1)} %held.6), channel_id=1, source_target_pairs={{0,12},{4,8},{8,4},{12,0},{1,13},{5,9},{9,5},{13,1},{2,14},{6,10},... | collective-permute-start | bytes 393224 | tf_op jit(solution)/shard_map/ppermute | solution.py:17
  23.3 1.6 %collective-permute-done.3 = bf16[96,2048]{1,0:T(8,128)(2,1)S(1)} collective-permute-done((bf16[96,2048]{1,0:T(8,128)(2,1)S(1)}, bf16[96,2048]{1,0:T(8,128)(2,1)S(1)}, u32[]{:S(2)}, u32[]{:S(2)}) %collective-permute-start.3) | collective-permute-done | bytes 393248 | tf_op jit(solution)/shard_map/ppermute | solution.py:17
  24.9 9.4 %expert.2 = (f32[128,2176]{1,0:T(8,128)S(1)}, bf16[128,2176]{1,0:T(8,128)(2,1)S(1)}) custom-call(bf16[256,2048]{1,0:T(8,128)(2,1)S(1)} %slice_dynamic-update-slice_fusion.3.rows_ref, bf16[2,3584,256]{2,1,0:T(8,128)(2,1)S(1)} %get-tuple-element.21.slope_ref, f32[2,256,64]{2,1,0:T(8,128)S(1)} %get-tuple-element.22.down_part_ref, ...), custom_call_target="tpu_custom_call" | custom-call | flops 7516192768 | bytes 29360128 | tf_op jit(solution)/shard_map/expert/pallas_call | solution.py:235
  35.1 1.2 %collective-permute-done.11 = bf16[96,2048]{1,0:T(8,128)(2,1)S(1)} collective-permute-done((bf16[96,2048]{1,0:T(8,128)(2,1)S(1)}, bf16[96,2048]{1,0:T(8,128)(2,1)S(1)}, u32[]{:S(2)}, u32[]{:S(2)}) %collective-permute-start.11) | collective-permute-done | bytes 393248 | tf_op jit(solution)/shard_map/ppermute | solution.py:17
  37.2 1.4 %collective-permute-start.5 = (bf16[32,2176]{1,0:T(8,128)(2,1)S(1)}, bf16[32,2176]{1,0:T(8,128)(2,1)S(1)}, u32[]{:S(2)}, u32[]{:S(2)}) collective-permute-start(bf16[32,2176]{1,0:T(8,128)(2,1)S(1)} %get-tuple-element.27.refs_0_), channel_id=1, source_target_pairs={{0,4},{4,0},{8,12},{12,8},{1,5},{5,1},{9,13},{13,9},{2,6},{6,2},{1... | collective-permute-start | bytes 417800 | tf_op jit(solution)/shard_map/ppermute | solution.py:17
  38.7 2.9 %collective-permute-start.6 = (bf16[32,2176]{1,0:T(8,128)(2,1)S(1)}, bf16[32,2176]{1,0:T(8,128)(2,1)S(1)}, u32[]{:S(2)}, u32[]{:S(2)}) collective-permute-start(bf16[32,2176]{1,0:T(8,128)(2,1)S(1)} %get-tuple-element.28.refs_1_), channel_id=1, source_target_pairs={{0,8},{4,12},{8,0},{12,4},{1,9},{5,13},{9,1},{13,5},{2,10},{6,14},... | collective-permute-start | bytes 417800 | tf_op jit(solution)/shard_map/ppermute | solution.py:17
  41.7 9.4 %expert.3 = (f32[128,2176]{1,0:T(8,128)S(1)}, bf16[128,2176]{1,0:T(8,128)(2,1)S(1)}) custom-call(bf16[256,2048]{1,0:T(8,128)(2,1)S(1)} %slice_dynamic-update-slice_fusion.rows_ref, bf16[2,3584,256]{2,1,0:T(8,128)(2,1)S(1)} %get-tuple-element.21.slope_ref, f32[2,256,64]{2,1,0:T(8,128)S(1)} %get-tuple-element.22.down_part_ref, bf16[64,3584]{1,0:T(8,128)(2,1)S(1)} %bitcast.59, ...), custom_call_target="tpu_custom_call" | custom-call | flops 7516192768 | bytes 29360128 | tf_op jit(solution)/shard_map/expert/pallas_call | solution.py:235
  51.1 1.0 %collective-permute-done.6.refs_1_ = bf16[32,2176]{1,0:T(8,128)(2,1)S(1)} collective-permute-done((bf16[32,2176]{1,0:T(8,128)(2,1)S(1)}, bf16[32,2176]{1,0:T(8,128)(2,1)S(1)}, u32[]{:S(2)}, u32[]{:S(2)}) %collective-permute-start.6) | collective-permute-done | bytes 139296 | tf_op jit(solution)/shard_map/ppermute | solution.py:17
  52.5 1.3 %fusion = f32[128,64]{0,1:T(8,128)S(1)} fusion(bf16[1,128,2048]{2,1,0:T(8,128)(2,1)} %param.10, bf16[1,2048,64]{1,2,0:T(8,128)(2,1)S(1)} %copy-done), kind=kOutput, calls=%fused_computation.3 | convolution fusion | flops 33554432 | bytes 819200 | tf_op jit(solution)/shard_map/dot_general | solution.py:361
  54.3 2.8 %collective-permute-start.13 = (bf16[32,2176]{1,0:T(8,128)(2,1)S(1)}, bf16[32,2176]{1,0:T(8,128)(2,1)S(1)}, u32[]{:S(2)}, u32[]{:S(2)}) collective-permute-start(bf16[32,2176]{1,0:T(8,128)(2,1)S(1)} %get-tuple-element.33), channel_id=1, source_target_pairs={{0,4},{4,0},{8,12},{12,8},{1,5},{5,1},{9,13},{13,9},{2,6},{6,2},{1... | collective-permute-start | bytes 417800 | tf_op jit(solution)/shard_map/ppermute | solution.py:17
  57.3 1.1 %collective-permute-start.15 = (bf16[32,2176]{1,0:T(8,128)(2,1)S(1)}, bf16[32,2176]{1,0:T(8,128)(2,1)S(1)}, u32[]{:S(2)}, u32[]{:S(2)}) collective-permute-start(bf16[32,2176]{1,0:T(8,128)(2,1)S(1)} %get-tuple-element.35), channel_id=1, source_target_pairs={{0,8},{4,12},{8,0},{12,4},{1,9},{5,13},{9,1},{13,5},{2,10},{6,14},... | collective-permute-start | bytes 417800 | tf_op jit(solution)/shard_map/ppermute | solution.py:17
  58.4 1.5 %collective-permute-start.16 = (bf16[32,2176]{1,0:T(8,128)(2,1)S(1)}, bf16[32,2176]{1,0:T(8,128)(2,1)S(1)}, u32[]{:S(2)}, u32[]{:S(2)}) collective-permute-start(bf16[32,2176]{1,0:T(8,128)(2,1)S(1)} %get-tuple-element.36), channel_id=1, source_target_pairs={{0,12},{4,8},{8,4},{12,0},{1,13},{5,9},{9,5},{13,1},{2,14},{6,10},... | collective-permute-start | bytes 417800 | tf_op jit(solution)/shard_map/ppermute | solution.py:17
  59.9 3.3 %collective-permute-done.13.refs_0_ = bf16[32,2176]{1,0:T(8,128)(2,1)S(1)} collective-permute-done((bf16[32,2176]{1,0:T(8,128)(2,1)S(1)}, bf16[32,2176]{1,0:T(8,128)(2,1)S(1)}, u32[]{:S(2)}, u32[]{:S(2)}) %collective-permute-start.13) | collective-permute-done | bytes 139296 | tf_op jit(solution)/shard_map/ppermute | solution.py:17
  63.2 1.6 %collective-permute-start.14 = (bf16[32,2048]{1,0:T(8,128)(2,1)S(1)}, bf16[32,2048]{1,0:T(8,128)(2,1)S(1)}, u32[]{:S(2)}, u32[]{:S(2)}) collective-permute-start(bf16[32,2048]{1,0:T(8,128)(2,1)S(1)} %held.11), channel_id=1, source_target_pairs={{0,2},{2,0},{1,3},{3,1},{4,6},{6,4},{5,7},{7,5},{8,10},{10,8},{9,1... | collective-permute-start | bytes 393224 | tf_op jit(solution)/shard_map/ppermute | solution.py:297
  64.9 5.9 %collective-permute-done.15.refs_1_ = bf16[32,2176]{1,0:T(8,128)(2,1)S(1)} collective-permute-done((bf16[32,2176]{1,0:T(8,128)(2,1)S(1)}, bf16[32,2176]{1,0:T(8,128)(2,1)S(1)}, u32[]{:S(2)}, u32[]{:S(2)}) %collective-permute-start.15) | collective-permute-done | bytes 139296 | tf_op jit(solution)/shard_map/ppermute | solution.py:17
  71.1 1.6 %collective-permute-start.17 = (bf16[32,2048]{1,0:T(8,128)(2,1)S(1)}, bf16[32,2048]{1,0:T(8,128)(2,1)S(1)}, u32[]{:S(2)}, u32[]{:S(2)}) collective-permute-start(bf16[32,2048]{1,0:T(8,128)(2,1)S(1)} %get-tuple-element.37), channel_id=1, source_target_pairs={{0,2},{2,0},{1,3},{3,1},{4,6},{6,4},{5,7},{7,5},{8,10},{10,8},{9,1... | collective-permute-start | bytes 393224 | tf_op jit(solution)/shard_map/ppermute | solution.py:297
  74.3 2.7 %collective-permute-done.17 = bf16[32,2048]{1,0:T(8,128)(2,1)S(1)} collective-permute-done((bf16[32,2048]{1,0:T(8,128)(2,1)S(1)}, bf16[32,2048]{1,0:T(8,128)(2,1)S(1)}, u32[]{:S(2)}, u32[]{:S(2)}) %collective-permute-start.17) | collective-permute-done | bytes 131104 | tf_op jit(solution)/shard_map/ppermute | solution.py:297
  77.0 1.3 %collective-permute-done.19 = bf16[32,2048]{1,0:T(8,128)(2,1)S(1)} collective-permute-done((bf16[32,2048]{1,0:T(8,128)(2,1)S(1)}, bf16[32,2048]{1,0:T(8,128)(2,1)S(1)}, u32[]{:S(2)}, u32[]{:S(2)}) %collective-permute-start.19) | collective-permute-done | bytes 131104 | tf_op jit(solution)/shard_map/ppermute | solution.py:17
  (91 shorter events, 8.1 us)
Async XLA Ops:
  0.6 51.9 %copy-start = (bf16[1,2048,64]{1,2,0:T(8,128)(2,1)S(1)}, bf16[1,2048,64]{1,2,0:T(8,128)(2,1)}, u32[]{:S(2)}) copy-start(bf16[1,2048,64]{1,2,0:T(8,128)(2,1)} %param.17) | copy-start | bytes 786436
  1.6 21.4 %collective-permute-start.2 = (bf16[32,2048]{1,0:T(8,128)(2,1)S(1)}, bf16[32,2048]{1,0:T(8,128)(2,1)S(1)}, u32[]{:S(2)}, u32[]{:S(2)}) collective-permute-start(bf16[32,2048]{1,0:T(8,128)(2,1)S(1)} %get-tuple-element.41.cot_ref), channel_id=1, source_target_pairs={{0,12},{4,8},{8,4},{12,0},{1,13},{5,9},{9,5},{13,1},{2,14},{6,10},... | collective-permute-start | bytes 393224 | tf_op jit(solution)/shard_map/ppermute | solution.py:17
  6.7 16.3 %collective-permute-start.1 = (bf16[32,2048]{1,0:T(8,128)(2,1)S(1)}, bf16[32,2048]{1,0:T(8,128)(2,1)S(1)}, u32[]{:S(2)}, u32[]{:S(2)}) collective-permute-start(bf16[32,2048]{1,0:T(8,128)(2,1)S(1)} %get-tuple-element.41.cot_ref), channel_id=1, source_target_pairs={{0,8},{4,12},{8,0},{12,4},{1,9},{5,13},{9,1},{13,5},{2,10},{6,14},... | collective-permute-start | bytes 393224 | tf_op jit(solution)/shard_map/ppermute | solution.py:17
  6.7 11.8 %collective-permute-start = (bf16[32,2048]{1,0:T(8,128)(2,1)S(1)}, bf16[32,2048]{1,0:T(8,128)(2,1)S(1)}, u32[]{:S(2)}, u32[]{:S(2)}) collective-permute-start(bf16[32,2048]{1,0:T(8,128)(2,1)S(1)} %get-tuple-element.41.cot_ref), channel_id=1, source_target_pairs={{0,4},{4,0},{8,12},{12,8},{1,5},{5,1},{9,13},{13,9},{2,6},{6,2},{1... | collective-permute-start | bytes 393224 | tf_op jit(solution)/shard_map/ppermute | solution.py:17
  12.2 12.8 %copy-start.3 = (bf16[1,1,3584,64]{2,3,1,0:T(8,128)(2,1)S(1)}, bf16[1,1,3584,64]{2,3,1,0:T(8,128)(2,1)}, u32[]{:S(2)}) copy-start(bf16[1,1,3584,64]{2,3,1,0:T(8,128)(2,1)} %param.18) | copy-start | bytes 1376260
  18.6 15.9 %collective-permute-start.10 = (bf16[32,2048]{1,0:T(8,128)(2,1)S(1)}, bf16[32,2048]{1,0:T(8,128)(2,1)S(1)}, u32[]{:S(2)}, u32[]{:S(2)}) collective-permute-start(bf16[32,2048]{1,0:T(8,128)(2,1)S(1)} %held.6), channel_id=1, source_target_pairs={{0,12},{4,8},{8,4},{12,0},{1,13},{5,9},{9,5},{13,1},{2,14},{6,10},... | collective-permute-start | bytes 393224 | tf_op jit(solution)/shard_map/ppermute | solution.py:17
  22.4 12.0 %collective-permute-start.9 = (bf16[32,2048]{1,0:T(8,128)(2,1)S(1)}, bf16[32,2048]{1,0:T(8,128)(2,1)S(1)}, u32[]{:S(2)}, u32[]{:S(2)}) collective-permute-start(bf16[32,2048]{1,0:T(8,128)(2,1)S(1)} %held.6), channel_id=1, source_target_pairs={{0,8},{4,12},{8,0},{12,4},{1,9},{5,13},{9,1},{13,5},{2,10},{6,14},... | collective-permute-start | bytes 393224 | tf_op jit(solution)/shard_map/ppermute | solution.py:17
  22.4 12.0 %collective-permute-start.8 = (bf16[32,2048]{1,0:T(8,128)(2,1)S(1)}, bf16[32,2048]{1,0:T(8,128)(2,1)S(1)}, u32[]{:S(2)}, u32[]{:S(2)}) collective-permute-start(bf16[32,2048]{1,0:T(8,128)(2,1)S(1)} %held.6), channel_id=1, source_target_pairs={{0,4},{4,0},{8,12},{12,8},{1,5},{5,1},{9,13},{13,9},{2,6},{6,2},{1... | collective-permute-start | bytes 393224 | tf_op jit(solution)/shard_map/ppermute | solution.py:17
  23.1 1.8 %collective-permute-start.3 = (bf16[96,2048]{1,0:T(8,128)(2,1)S(1)}, bf16[96,2048]{1,0:T(8,128)(2,1)S(1)}, u32[]{:S(2)}, u32[]{:S(2)}) collective-permute-start(bf16[96,2048]{1,0:T(8,128)(2,1)S(1)} %pad_maximum_fusion), channel_id=1, source_target_pairs={{0,1},{1,0},{2,3},{3,2},{4,5},{5,4},{6,7},{7,6},{8,9},{9,8},{10,11... | collective-permute-start | bytes 1179656 | tf_op jit(solution)/shard_map/ppermute | solution.py:17
  34.5 1.8 %collective-permute-start.11 = (bf16[96,2048]{1,0:T(8,128)(2,1)S(1)}, bf16[96,2048]{1,0:T(8,128)(2,1)S(1)}, u32[]{:S(2)}, u32[]{:S(2)}) collective-permute-start(bf16[96,2048]{1,0:T(8,128)(2,1)S(1)} %pad_maximum_fusion.1), channel_id=1, source_target_pairs={{0,1},{1,0},{2,3},{3,2},{4,5},{5,4},{6,7},{7,6},{8,9},{9,8},{10,11... | collective-permute-start | bytes 1179656 | tf_op jit(solution)/shard_map/ppermute | solution.py:17
  34.7 2.4 %collective-permute-start.4 = (bf16[128,2176]{1,0:T(8,128)(2,1)S(1)}, bf16[128,2176]{1,0:T(8,128)(2,1)S(1)}, u32[]{:S(2)}, u32[]{:S(2)}) collective-permute-start(bf16[128,2176]{1,0:T(8,128)(2,1)S(1)} %get-tuple-element.25), channel_id=1, source_target_pairs={{0,1},{1,0},{2,3},{3,2},{4,5},{5,4},{6,7},{7,6},{8,9},{9,8},{10,11... | collective-permute-start | bytes 1671176 | tf_op jit(solution)/shard_map/ppermute | solution.py:17
  37.2 13.9 %collective-permute-start.5 = (bf16[32,2176]{1,0:T(8,128)(2,1)S(1)}, bf16[32,2176]{1,0:T(8,128)(2,1)S(1)}, u32[]{:S(2)}, u32[]{:S(2)}) collective-permute-start(bf16[32,2176]{1,0:T(8,128)(2,1)S(1)} %get-tuple-element.27.refs_0_), channel_id=1, source_target_pairs={{0,4},{4,0},{8,12},{12,8},{1,5},{5,1},{9,13},{13,9},{2,6},{6,2},{1... | collective-permute-start | bytes 417800 | tf_op jit(solution)/shard_map/ppermute | solution.py:17
  38.7 13.4 %collective-permute-start.6 = (bf16[32,2176]{1,0:T(8,128)(2,1)S(1)}, bf16[32,2176]{1,0:T(8,128)(2,1)S(1)}, u32[]{:S(2)}, u32[]{:S(2)}) collective-permute-start(bf16[32,2176]{1,0:T(8,128)(2,1)S(1)} %get-tuple-element.28.refs_1_), channel_id=1, source_target_pairs={{0,8},{4,12},{8,0},{12,4},{1,9},{5,13},{9,1},{13,5},{2,10},{6,14},... | collective-permute-start | bytes 417800 | tf_op jit(solution)/shard_map/ppermute | solution.py:17
  41.6 10.5 %collective-permute-start.7 = (bf16[32,2176]{1,0:T(8,128)(2,1)S(1)}, bf16[32,2176]{1,0:T(8,128)(2,1)S(1)}, u32[]{:S(2)}, u32[]{:S(2)}) collective-permute-start(bf16[32,2176]{1,0:T(8,128)(2,1)S(1)} %get-tuple-element.29.refs_2_), channel_id=1, source_target_pairs={{0,12},{4,8},{8,4},{12,0},{1,13},{5,9},{9,5},{13,1},{2,14},{6,10},... | collective-permute-start | bytes 417800 | tf_op jit(solution)/shard_map/ppermute | solution.py:17
  51.1 21.9 %copy-start.5 = (f32[1,128,64]{1,2,0:T(8,128)S(1)}, f32[1,128,64]{1,2,0:T(8,128)}, u32[]{:S(2)}) copy-start(f32[1,128,64]{1,2,0:T(8,128)} %param.16) | copy-start | bytes 98308
  52.1 2.0 %collective-permute-start.12 = (bf16[128,2176]{1,0:T(8,128)(2,1)S(1)}, bf16[128,2176]{1,0:T(8,128)(2,1)S(1)}, u32[]{:S(2)}, u32[]{:S(2)}) collective-permute-start(bf16[128,2176]{1,0:T(8,128)(2,1)S(1)} %held.10), channel_id=1, source_target_pairs={{0,1},{1,0},{2,3},{3,2},{4,5},{5,4},{6,7},{7,6},{8,9},{9,8},{10,11... | collective-permute-start | bytes 1671176 | tf_op jit(solution)/shard_map/ppermute | solution.py:17
  54.3 8.8 %collective-permute-start.13 = (bf16[32,2176]{1,0:T(8,128)(2,1)S(1)}, bf16[32,2176]{1,0:T(8,128)(2,1)S(1)}, u32[]{:S(2)}, u32[]{:S(2)}) collective-permute-start(bf16[32,2176]{1,0:T(8,128)(2,1)S(1)} %get-tuple-element.33), channel_id=1, source_target_pairs={{0,4},{4,0},{8,12},{12,8},{1,5},{5,1},{9,13},{13,9},{2,6},{6,2},{1... | collective-permute-start | bytes 417800 | tf_op jit(solution)/shard_map/ppermute | solution.py:17
  57.3 13.5 %collective-permute-start.15 = (bf16[32,2176]{1,0:T(8,128)(2,1)S(1)}, bf16[32,2176]{1,0:T(8,128)(2,1)S(1)}, u32[]{:S(2)}, u32[]{:S(2)}) collective-permute-start(bf16[32,2176]{1,0:T(8,128)(2,1)S(1)} %get-tuple-element.35), channel_id=1, source_target_pairs={{0,8},{4,12},{8,0},{12,4},{1,9},{5,13},{9,1},{13,5},{2,10},{6,14},... | collective-permute-start | bytes 417800 | tf_op jit(solution)/shard_map/ppermute | solution.py:17
  58.4 12.4 %collective-permute-start.16 = (bf16[32,2176]{1,0:T(8,128)(2,1)S(1)}, bf16[32,2176]{1,0:T(8,128)(2,1)S(1)}, u32[]{:S(2)}, u32[]{:S(2)}) collective-permute-start(bf16[32,2176]{1,0:T(8,128)(2,1)S(1)} %get-tuple-element.36), channel_id=1, source_target_pairs={{0,12},{4,8},{8,4},{12,0},{1,13},{5,9},{9,5},{13,1},{2,14},{6,10},... | collective-permute-start | bytes 417800 | tf_op jit(solution)/shard_map/ppermute | solution.py:17
  63.2 7.6 %collective-permute-start.14 = (bf16[32,2048]{1,0:T(8,128)(2,1)S(1)}, bf16[32,2048]{1,0:T(8,128)(2,1)S(1)}, u32[]{:S(2)}, u32[]{:S(2)}) collective-permute-start(bf16[32,2048]{1,0:T(8,128)(2,1)S(1)} %held.11), channel_id=1, source_target_pairs={{0,2},{2,0},{1,3},{3,1},{4,6},{6,4},{5,7},{7,5},{8,10},{10,8},{9,1... | collective-permute-start | bytes 393224 | tf_op jit(solution)/shard_map/ppermute | solution.py:297
  71.0 1.8 %collective-permute-start.20 = (f32[64,128]{1,0:T(8,128)S(1)}, f32[64,128]{1,0:T(8,128)S(1)}, u32[]{:S(2)}, u32[]{:S(2)}) collective-permute-start(f32[64,128]{1,0:T(8,128)S(1)} %constant_dynamic-update-slice_fusion.12), channel_id=1, source_target_pairs={{0,1},{1,0},{2,3},{3,2},{4,5},{5,4},{6,7},{7,6},{8,9},{9,8},{10,11... | collective-permute-start | bytes 98312 | tf_op jit(solution)/shard_map/ppermute | solution.py:17
  71.1 5.9 %collective-permute-start.17 = (bf16[32,2048]{1,0:T(8,128)(2,1)S(1)}, bf16[32,2048]{1,0:T(8,128)(2,1)S(1)}, u32[]{:S(2)}, u32[]{:S(2)}) collective-permute-start(bf16[32,2048]{1,0:T(8,128)(2,1)S(1)} %get-tuple-element.37), channel_id=1, source_target_pairs={{0,2},{2,0},{1,3},{3,1},{4,6},{6,4},{5,7},{7,5},{8,10},{10,8},{9,1... | collective-permute-start | bytes 393224 | tf_op jit(solution)/shard_map/ppermute | solution.py:297
  72.6 1.7 %collective-permute-start.18 = (bf16[32,2048]{1,0:T(8,128)(2,1)S(1)}, bf16[32,2048]{1,0:T(8,128)(2,1)S(1)}, u32[]{:S(2)}, u32[]{:S(2)}) collective-permute-start(bf16[32,2048]{1,0:T(8,128)(2,1)S(1)} %collective-permute-done.14.refs_3_), channel_id=1, source_target_pairs={{0,1},{1,0},{2,3},{3,2},{4,5},{5,4},{6,7},{7,6},{8,9},{9,8},{10,11... | collective-permute-start | bytes 393224 | tf_op jit(solution)/shard_map/ppermute | solution.py:17
  77.0 1.3 %collective-permute-start.19 = (bf16[32,2048]{1,0:T(8,128)(2,1)S(1)}, bf16[32,2048]{1,0:T(8,128)(2,1)S(1)}, u32[]{:S(2)}, u32[]{:S(2)}) collective-permute-start(bf16[32,2048]{1,0:T(8,128)(2,1)S(1)} %collective-permute-done.17), channel_id=1, source_target_pairs={{0,1},{1,0},{2,3},{3,2},{4,5},{5,4},{6,7},{7,6},{8,9},{9,8},{10,11... | collective-permute-start | bytes 393224 | tf_op jit(solution)/shard_map/ppermute | solution.py:17
  (5 other events, 31.2 us)

commit v4 on v3

--- a/solution.py
+++ b/solution.py
@@ -193,6 +193,7 @@
         if j == 0 or j > steps_f:
             up_copy(j).start()
     rows_buf[...] = rows_ref[...].T
+    up_buf[width:, :] = sketch_ref[...]
 
     def first(j, carry):
         @pl.when(j + 1 < steps_d)
@@ -209,20 +210,20 @@
 
     lax.fori_loop(0, steps_f, first, 0)
 
-    up_part = jnp.dot(sketch_ref[...], grad_buf[...], preferred_element_type=jnp.float32).T
-    vectors = jnp.concatenate([down_part_ref[0], up_part], axis=1)
-    keep_ref[:, width:] = vectors[:half]
-    give_ref[:, width:] = vectors[half:].astype(jnp.bfloat16)
-
-    def second(j, carry):
+    for j in range(steps_d):
         up_copy(j).wait()
-        part = tile(j, tile_d)
-        term = jnp.dot(up_buf[part, :], grad_buf[...], preferred_element_type=jnp.float32).T
-        keep_ref[:, part] = term[:half]
-        give_ref[:, part] = term[half:].astype(jnp.bfloat16)
-        return carry
-
-    lax.fori_loop(0, steps_d, second, 0)
+        last = j == steps_d - 1
+        end = up_buf.shape[0] if last else (j + 1) * tile_d
+        term = jnp.dot(
+            up_buf[j * tile_d : end, :], grad_buf[...], preferred_element_type=jnp.float32
+        ).T
+        if last:
+            term = jnp.concatenate(
+                [term[:, :tile_d], down_part_ref[0], term[:, tile_d:]], axis=1
+            )
+        start = j * tile_d
+        keep_ref[:, start : start + term.shape[1]] = term[:half]
+        give_ref[:, start : start + term.shape[1]] = term[half:].astype(jnp.bfloat16)
 
 
 def expert(chunk, rows, slope, down_part, sketch_t, down_local, up_local, *events):
@@ -251,7 +252,7 @@
         scratch_shapes=[
             pltpu.VMEM((width, count), jnp.bfloat16),
             pltpu.VMEM((hidden_cols, count), jnp.bfloat16),
-            pltpu.VMEM((width, hidden_cols), jnp.bfloat16),
+            pltpu.VMEM((width + rank, hidden_cols), jnp.bfloat16),
             pltpu.SemaphoreType.DMA((width // tile_d,)),
         ],
         compiler_params=pltpu.CompilerParams(vmem_limit_bytes=26 << 20),
@@ -308,24 +309,25 @@
     sketch_t = sketch_local.T
     cot_mine = lax.dynamic_slice_in_dim(cot, core * half, half, 0)
     cot_theirs = lax.dynamic_slice_in_dim(cot, (1 - core) * half, half, 0)
-    order = sorted(range(1, pieces), reverse=True)
+    order = sorted(range(2, pieces), reverse=True)
     slope, down_part, down_here = slopes(pre_all, sketch_t, down_weight[0, 0], place, core)
-    mark, keep, sent, grad, passed = (), (), (), (), ()
+    near_rows = xored(cot_mine, "dp", 1)
+    fetched = {slot: xored(cot_mine[:rows], "dp", slot) for slot in order}
+    own, sent, grad, passed, backs = (), (), (), (), ()
     below_mine, vectors = [], []
     for a in range(CHUNKS):
         part = slice(a * rows, (a + 1) * rows)
-        mine, theirs = {0: cot_mine[part]}, {0: cot_theirs[part]}
-        if mark:
-            mine[0] = held(mine[0], *mark)
-        for slot in order:
-            mine[slot] = xored(mine[0], "dp", slot)
-        mark = (mine[1],)
-        if keep:
-            for slot in order:
-                mine[slot] = held(mine[slot], *keep)
-        traded = xored(jnp.concatenate([mine[slot] for slot in order], axis=0), "tensor", 1)
-        for at, slot in enumerate(order):
-            theirs[slot] = traded[at * rows : (at + 1) * rows]
+        blocks = [fetched[slot] for slot in order] + [near_rows] * (a == 0)
+        blocks = jnp.concatenate(blocks, axis=0)
+        if a > 0:
+            blocks = held(blocks, own)
+        traded = xored(blocks, "tensor", 1)
+        mine = dict(fetched)
+        theirs = {slot: traded[at * rows : (at + 1) * rows] for at, slot in enumerate(order)}
+        if a == 0:
+            near_theirs = traded[len(order) * rows :]
+        mine[0], mine[1] = cot_mine[part], near_rows[part]
+        theirs[0], theirs[1] = cot_theirs[part], near_theirs[part]
         rows_in = jnp.concatenate(
             [mine[k] for k in range(pieces)] + [theirs[k] for k in range(pieces)], axis=0
         )
@@ -333,8 +335,11 @@
         kept, give = expert(
             a, rows_in, slope, down_part, sketch_t, down_here, up_weight[0, 0], *sent
         )
-        keep = (kept,)
-        if grad:
+        if a + 1 < CHUNKS:
+            coming = held(cot_mine[(a + 1) * rows : (a + 2) * rows], near_rows)
+            fetched = {slot: held(xored(coming, "dp", slot), kept) for slot in order}
+            give = held(give, *fetched.values(), *backs)
+        else:
             give = held(give, *backs)
         own, *sent = merged(kept, xored(give, "tensor", 1), rows)
         backs = [xored(out, "dp", slot + 1) for slot, out in enumerate(sent)]

time: 79.6 us -> 81.1 us (1.019)
  Pallas kernels: 25.8 us -> 32.8 us
  waiting for transfers between devices: 18 us -> 13 us
  starting transfers between devices: 24.1 us -> 22.6 us
    pallas_call x2, Pallas kernels: 18.8 us -> 25.8 us  [expert(): pl.pallas_call(functools.partial(expert_kernel, tile_f, tile_d), grid=(1,...]
    ppermute x2, waiting for transfers between devices: 2.66 us -> 0.03 us  [below(): lax.ppermute(block, 'section', [(s, (s - 1) % sections) for s in range(se...]
    ppermute x19 -> x18, waiting for transfers between devices: 15.4 us -> 12.9 us  [xored(): return lax.ppermute(block, axis, [(i, i ^ bits) for i in range(n)])]
    ppermute x19 -> x18, starting transfers between devices: 21 us -> 19.5 us  [xored(): return lax.ppermute(block, axis, [(i, i ^ bits) for i in range(n)])]
    dynamic_slice x0 -> x1, local copies, waits for them, and re-layouts: none -> 0.97 us  [per_device(): cot_mine = lax.dynamic_slice_in_dim(cot, core * half, half, 0)]
    slice x1 -> x0, local copies, waits for them, and re-layouts: 0.91 us -> none  [per_device(): mine, theirs = ({0: cot_mine[part]}, {0: cot_theirs[part]})]
    unnamed x35 -> x32, local copies, waits for them, and re-layouts: 4.42 us -> 4.41 us
  transfers between devices with their start and end apart: 21 -> 20, of which waited for: 9 -> 7; matrix products, arithmetic and copies ran while one was open for 7% -> 8% of each run, Pallas kernels for 32% -> 40%
where the time goes in v4:
time: 81.1 us; the launch traced here: 80.4 us
  Pallas kernels  32.8 us (40%)
  starting transfers between devices  22.6 us (28%)
  waiting for transfers between devices  13 us (16%)
  local copies, waits for them, and re-layouts  6.31 us (8%)
  matrix products  2.64 us (3%)
  other arithmetic  2.13 us (3%)
  between operations  1.04 us (1%)
    pallas_call x2, Pallas kernels, expert(): pl.pallas_call(functools.partial(expert_kernel, tile_f, tile_d), grid=(1,...  25.8 us
    ppermute x18, starting transfers between devices, xored(): return lax.ppermute(block, axis, [(i, i ^ bits) for i in range(n)])  19.5 us
    ppermute x18, waiting for transfers between devices, xored(): return lax.ppermute(block, axis, [(i, i ^ bits) for i in range(n)])  12.9 us
    pallas_call x1, Pallas kernels, slopes(): pl.pallas_call(functools.partial(slope_kernel, groups), grid_spec=pltpu.P...  6.27 us
    unnamed x32, local copies, waits for them, and re-layouts  4.41 us
    ppermute x2, starting transfers between devices, below(): lax.ppermute(block, 'section', [(s, (s - 1) % sections) for s in range(se...  3.11 us
  transfers between devices with their start and end apart: 20, of which 7 were waited for; matrix products, arithmetic and copies ran while one was open for 8% of the time, Pallas kernels for 40%

profile of v4, /device:TPU:0, one launch (start us, length us, event | category | flops | bytes accessed | tf_op | source)
XLA Modules:
  0.0 80.4 jit_solution(5673049928940626455)
XLA Ops:
  0.7 1.0 %constant_dynamic-update-slice_fusion.2 = (bf16[256,2048]{1,0:T(8,128)(2,1)S(1)}, bf16[32,2048]{1,0:T(8,128)(2,1)S(1)}) fusion(bf16[1,128,2048]{2,1,0:T(8,128)(2,1)} %param.10, s32[]{:T(128)S(6)} %select_n.45), kind=kLoop, calls=%fused_computation.40 | loop fusion | bytes 393220
  1.6 4.1 %collective-permute-start.1 = (bf16[32,2048]{1,0:T(8,128)(2,1)S(1)}, bf16[32,2048]{1,0:T(8,128)(2,1)S(1)}, u32[]{:S(2)}, u32[]{:S(2)}) collective-permute-start(bf16[32,2048]{1,0:T(8,128)(2,1)S(1)} %get-tuple-element.43.cot_ref), channel_id=1, source_target_pairs={{0,8},{4,12},{8,0},{12,4},{1,9},{5,13},{9,1},{13,5},{2,10},{6,14},... | collective-permute-start | bytes 393224 | tf_op jit(solution)/shard_map/ppermute | solution.py:17
  5.7 1.3 %collective-permute-start.2 = (bf16[32,2048]{1,0:T(8,128)(2,1)S(1)}, bf16[32,2048]{1,0:T(8,128)(2,1)S(1)}, u32[]{:S(2)}, u32[]{:S(2)}) collective-permute-start(bf16[32,2048]{1,0:T(8,128)(2,1)S(1)} %get-tuple-element.43.cot_ref), channel_id=1, source_target_pairs={{0,12},{4,8},{8,4},{12,0},{1,13},{5,9},{9,5},{13,1},{2,14},{6,10},... | collective-permute-start | bytes 393224 | tf_op jit(solution)/shard_map/ppermute | solution.py:17
  7.1 1.0 %dynamic-slice_bitcast_fusion = bf16[64,2048]{1,0:T(8,128)(2,1)S(1)} fusion(bf16[1,128,2048]{2,1,0:T(8,128)(2,1)} %param.10, s32[]{:T(128)S(6)} %select_n.45), kind=kLoop, calls=%fused_computation.8 | loop fusion | bytes 524292 | tf_op jit(solution)/shard_map/dynamic_slice | solution.py:310
  9.2 2.0 %copy-done.1 = bf16[1,1,4,128,3584]{4,3,2,1,0:T(8,128)(2,1)S(1)} copy-done((bf16[1,1,4,128,3584]{4,3,2,1,0:T(8,128)(2,1)S(1)}, bf16[1,1,4,128,3584]{4,3,2,1,0:T(8,128)(2,1)}, u32[]{:S(2)}) %copy-start.1) | copy-done | bytes 3670040
  11.2 1.0 %copy-done.2 = bf16[1,1,3584,64]{2,3,1,0:T(8,128)(2,1)S(1)} copy-done((bf16[1,1,3584,64]{2,3,1,0:T(8,128)(2,1)S(1)}, bf16[1,1,3584,64]{2,3,1,0:T(8,128)(2,1)}, u32[]{:S(2)}) %copy-start.2) | copy-done | bytes 458776
  12.2 6.3 %slopes.1 = (bf16[2,3584,256]{2,1,0:T(8,128)(2,1)S(1)}, f32[2,256,64]{2,1,0:T(8,128)S(1)}, bf16[3584,2048]{1,0:T(8,128)(2,1)S(1)}) custom-call(s32[2]{0:T(128)S(1)} %pad_add_fusion.index_ref, bf16[4,2,2,32,3584]{4,3,2,1,0:T(8,128)(2,1)S(1)} %bitcast.52, bf16[4,2,2,32,3584]{4,3,2,1,0:T(8,128)(2,1)S(1)} %bitcast.53, bf16[4,2,2,32,3584]{4,3,2,1,0:T(8,128)(2,1)S(1)} %bitcast.54, ...), custom_call_target="tpu_custom_call" | custom-call | flops 234881024 | bytes 7340032 | tf_op jit(solution)/shard_map/slopes/pallas_call | solution.py:147
  18.6 1.3 %collective-permute-done.refs_0_ = bf16[64,2048]{1,0:T(8,128)(2,1)S(1)} collective-permute-done((bf16[64,2048]{1,0:T(8,128)(2,1)S(1)}, bf16[64,2048]{1,0:T(8,128)(2,1)S(1)}, u32[]{:S(2)}, u32[]{:S(2)}) %collective-permute-start) | collective-permute-done | bytes 262176 | tf_op jit(solution)/shard_map/ppermute | solution.py:17
  20.2 3.3 %collective-permute-start.4 = (bf16[32,2048]{1,0:T(8,128)(2,1)S(1)}, bf16[32,2048]{1,0:T(8,128)(2,1)S(1)}, u32[]{:S(2)}, u32[]{:S(2)}) collective-permute-start(bf16[32,2048]{1,0:T(8,128)(2,1)S(1)} %held.7), channel_id=1, source_target_pairs={{0,12},{4,8},{8,4},{12,0},{1,13},{5,9},{9,5},{13,1},{2,14},{6,10},... | collective-permute-start | bytes 393224 | tf_op jit(solution)/shard_map/ppermute | solution.py:17
  23.6 12.8 %expert.2 = (f32[128,2176]{1,0:T(8,128)S(1)}, bf16[128,2176]{1,0:T(8,128)(2,1)S(1)}) custom-call(bf16[256,2048]{1,0:T(8,128)(2,1)S(1)} %slice_dynamic-update-slice_fusion.4.rows_ref, bf16[2,3584,256]{2,1,0:T(8,128)(2,1)S(1)} %get-tuple-element.21.slope_ref, f32[2,256,64]{2,1,0:T(8,128)S(1)} %get-tuple-element.22.down_part_ref, ...), custom_call_target="tpu_custom_call" | custom-call | flops 7516192768 | bytes 29360128 | tf_op jit(solution)/shard_map/expert/pallas_call | solution.py:236
  36.9 1.7 %collective-permute-done.6.came_ref = bf16[128,2176]{1,0:T(8,128)(2,1)S(1)} collective-permute-done((bf16[128,2176]{1,0:T(8,128)(2,1)S(1)}, bf16[128,2176]{1,0:T(8,128)(2,1)S(1)}, u32[]{:S(2)}, u32[]{:S(2)}) %collective-permute-start.6) | collective-permute-done | bytes 557088 | tf_op jit(solution)/shard_map/ppermute | solution.py:17
  39.0 1.1 %collective-permute-start.7 = (bf16[32,2176]{1,0:T(8,128)(2,1)S(1)}, bf16[32,2176]{1,0:T(8,128)(2,1)S(1)}, u32[]{:S(2)}, u32[]{:S(2)}) collective-permute-start(bf16[32,2176]{1,0:T(8,128)(2,1)S(1)} %get-tuple-element.27.refs_0_), channel_id=1, source_target_pairs={{0,4},{4,0},{8,12},{12,8},{1,5},{5,1},{9,13},{13,9},{2,6},{6,2},{1... | collective-permute-start | bytes 417800 | tf_op jit(solution)/shard_map/ppermute | solution.py:17
  40.1 1.9 %collective-permute-start.8 = (bf16[32,2176]{1,0:T(8,128)(2,1)S(1)}, bf16[32,2176]{1,0:T(8,128)(2,1)S(1)}, u32[]{:S(2)}, u32[]{:S(2)}) collective-permute-start(bf16[32,2176]{1,0:T(8,128)(2,1)S(1)} %get-tuple-element.28.refs_1_), channel_id=1, source_target_pairs={{0,8},{4,12},{8,0},{12,4},{1,9},{5,13},{9,1},{13,5},{2,10},{6,14},... | collective-permute-start | bytes 417800 | tf_op jit(solution)/shard_map/ppermute | solution.py:17
  42.0 1.4 %collective-permute-start.9 = (bf16[32,2176]{1,0:T(8,128)(2,1)S(1)}, bf16[32,2176]{1,0:T(8,128)(2,1)S(1)}, u32[]{:S(2)}, u32[]{:S(2)}) collective-permute-start(bf16[32,2176]{1,0:T(8,128)(2,1)S(1)} %get-tuple-element.29.refs_2_), channel_id=1, source_target_pairs={{0,12},{4,8},{8,4},{12,0},{1,13},{5,9},{9,5},{13,1},{2,14},{6,10},... | collective-permute-start | bytes 417800 | tf_op jit(solution)/shard_map/ppermute | solution.py:17
  43.5 13.0 %expert.3 = (f32[128,2176]{1,0:T(8,128)S(1)}, bf16[128,2176]{1,0:T(8,128)(2,1)S(1)}) custom-call(bf16[256,2048]{1,0:T(8,128)(2,1)S(1)} %slice_dynamic-update-slice_fusion.rows_ref, bf16[2,3584,256]{2,1,0:T(8,128)(2,1)S(1)} %get-tuple-element.21.slope_ref, f32[2,256,64]{2,1,0:T(8,128)S(1)} %get-tuple-element.22.down_part_ref, bf16[64,3584]{1,0:T(8,128)(2,1)S(1)} %bitcast.62, ...), custom_call_target="tpu_custom_call" | custom-call | flops 7516192768 | bytes 29360128 | tf_op jit(solution)/shard_map/expert/pallas_call | solution.py:236
  56.9 1.3 %fusion = f32[128,64]{0,1:T(8,128)S(1)} fusion(bf16[1,128,2048]{2,1,0:T(8,128)(2,1)} %param.10, bf16[1,2048,64]{1,2,0:T(8,128)(2,1)S(1)} %copy-done), kind=kOutput, calls=%fused_computation.4 | convolution fusion | flops 33554432 | bytes 819200 | tf_op jit(solution)/shard_map/dot_general | solution.py:366
  59.4 2.5 %collective-permute-start.14 = (bf16[32,2176]{1,0:T(8,128)(2,1)S(1)}, bf16[32,2176]{1,0:T(8,128)(2,1)S(1)}, u32[]{:S(2)}, u32[]{:S(2)}) collective-permute-start(bf16[32,2176]{1,0:T(8,128)(2,1)S(1)} %get-tuple-element.35), channel_id=1, source_target_pairs={{0,8},{4,12},{8,0},{12,4},{1,9},{5,13},{9,1},{13,5},{2,10},{6,14},... | collective-permute-start | bytes 417800 | tf_op jit(solution)/shard_map/ppermute | solution.py:17
  61.9 1.4 %collective-permute-start.15 = (bf16[32,2176]{1,0:T(8,128)(2,1)S(1)}, bf16[32,2176]{1,0:T(8,128)(2,1)S(1)}, u32[]{:S(2)}, u32[]{:S(2)}) collective-permute-start(bf16[32,2176]{1,0:T(8,128)(2,1)S(1)} %get-tuple-element.36), channel_id=1, source_target_pairs={{0,12},{4,8},{8,4},{12,0},{1,13},{5,9},{9,5},{13,1},{2,14},{6,10},... | collective-permute-start | bytes 417800 | tf_op jit(solution)/shard_map/ppermute | solution.py:17
  63.4 3.6 %collective-permute-done.12.refs_0_ = bf16[32,2176]{1,0:T(8,128)(2,1)S(1)} collective-permute-done((bf16[32,2176]{1,0:T(8,128)(2,1)S(1)}, bf16[32,2176]{1,0:T(8,128)(2,1)S(1)}, u32[]{:S(2)}, u32[]{:S(2)}) %collective-permute-start.12) | collective-permute-done | bytes 139296 | tf_op jit(solution)/shard_map/ppermute | solution.py:17
  67.1 1.6 %collective-permute-start.13 = (bf16[32,2048]{1,0:T(8,128)(2,1)S(1)}, bf16[32,2048]{1,0:T(8,128)(2,1)S(1)}, u32[]{:S(2)}, u32[]{:S(2)}) collective-permute-start(bf16[32,2048]{1,0:T(8,128)(2,1)S(1)} %held.13), channel_id=1, source_target_pairs={{0,2},{2,0},{1,3},{3,1},{4,6},{6,4},{5,7},{7,5},{8,10},{10,8},{9,1... | collective-permute-start | bytes 393224 | tf_op jit(solution)/shard_map/ppermute | solution.py:298
  68.8 4.2 %collective-permute-done.14.refs_1_ = bf16[32,2176]{1,0:T(8,128)(2,1)S(1)} collective-permute-done((bf16[32,2176]{1,0:T(8,128)(2,1)S(1)}, bf16[32,2176]{1,0:T(8,128)(2,1)S(1)}, u32[]{:S(2)}, u32[]{:S(2)}) %collective-permute-start.14) | collective-permute-done | bytes 139296 | tf_op jit(solution)/shard_map/ppermute | solution.py:17
  73.1 1.6 %collective-permute-start.16 = (bf16[32,2048]{1,0:T(8,128)(2,1)S(1)}, bf16[32,2048]{1,0:T(8,128)(2,1)S(1)}, u32[]{:S(2)}, u32[]{:S(2)}) collective-permute-start(bf16[32,2048]{1,0:T(8,128)(2,1)S(1)} %get-tuple-element.37), channel_id=1, source_target_pairs={{0,2},{2,0},{1,3},{3,1},{4,6},{6,4},{5,7},{7,5},{8,10},{10,8},{9,1... | collective-permute-start | bytes 393224 | tf_op jit(solution)/shard_map/ppermute | solution.py:298
  76.0 1.0 %convolution_bitcast_fusion = f32[4,64,64]{2,1,0:T(8,128)S(1)} fusion(f32[128,64]{0,1:T(8,128)S(1)} %copy.18, f32[128,4]{0,1:T(4,128)S(1)} %convert_bitcast_fusion, f32[1,128,64]{1,2,0:T(8,128)} %param.16), kind=kOutput, calls=%fused_computation | convolution fusion | flops 25198592 | bytes 133120 | tf_op jit(solution)/shard_map/et,ta,tb->eab/dot_general | solution.py:378
  78.3 1.2 %collective-permute-done.18 = bf16[32,2048]{1,0:T(8,128)(2,1)S(1)} collective-permute-done((bf16[32,2048]{1,0:T(8,128)(2,1)S(1)}, bf16[32,2048]{1,0:T(8,128)(2,1)S(1)}, u32[]{:S(2)}, u32[]{:S(2)}) %collective-permute-start.18) | collective-permute-done | bytes 131104 | tf_op jit(solution)/shard_map/ppermute | solution.py:17
  (87 shorter events, 7.7 us)
Async XLA Ops:
  0.6 56.3 %copy-start = (bf16[1,2048,64]{1,2,0:T(8,128)(2,1)S(1)}, bf16[1,2048,64]{1,2,0:T(8,128)(2,1)}, u32[]{:S(2)}) copy-start(bf16[1,2048,64]{1,2,0:T(8,128)(2,1)} %param.17) | copy-start | bytes 786436
  1.6 17.0 %collective-permute-start.1 = (bf16[32,2048]{1,0:T(8,128)(2,1)S(1)}, bf16[32,2048]{1,0:T(8,128)(2,1)S(1)}, u32[]{:S(2)}, u32[]{:S(2)}) collective-permute-start(bf16[32,2048]{1,0:T(8,128)(2,1)S(1)} %get-tuple-element.43.cot_ref), channel_id=1, source_target_pairs={{0,8},{4,12},{8,0},{12,4},{1,9},{5,13},{9,1},{13,5},{2,10},{6,14},... | collective-permute-start | bytes 393224 | tf_op jit(solution)/shard_map/ppermute | solution.py:17
  5.7 12.9 %collective-permute-start.2 = (bf16[32,2048]{1,0:T(8,128)(2,1)S(1)}, bf16[32,2048]{1,0:T(8,128)(2,1)S(1)}, u32[]{:S(2)}, u32[]{:S(2)}) collective-permute-start(bf16[32,2048]{1,0:T(8,128)(2,1)S(1)} %get-tuple-element.43.cot_ref), channel_id=1, source_target_pairs={{0,12},{4,8},{8,4},{12,0},{1,13},{5,9},{9,5},{13,1},{2,14},{6,10},... | collective-permute-start | bytes 393224 | tf_op jit(solution)/shard_map/ppermute | solution.py:17
  8.0 11.9 %collective-permute-start = (bf16[64,2048]{1,0:T(8,128)(2,1)S(1)}, bf16[64,2048]{1,0:T(8,128)(2,1)S(1)}, u32[]{:S(2)}, u32[]{:S(2)}) collective-permute-start(bf16[64,2048]{1,0:T(8,128)(2,1)S(1)} %dynamic-slice_bitcast_fusion), channel_id=1, source_target_pairs={{0,4},{4,0},{8,12},{12,8},{1,5},{5,1},{9,13},{13,9},{2,6},{6,2},{1... | collective-permute-start | bytes 786440 | tf_op jit(solution)/shard_map/ppermute | solution.py:17
  12.2 6.3 %copy-start.5 = (s32[1,1,2]{2,1,0:T(1,128)S(1)}, s32[1,1,2]{2,1,0:T(1,128)}, u32[]{:S(2)}) copy-start(s32[1,1,2]{2,1,0:T(1,128)} %param.11) | copy-start | bytes 28
  12.2 7.9 %copy-start.4 = (bf16[1,128,2048]{2,1,0:T(8,128)(2,1)S(1)}, bf16[1,128,2048]{2,1,0:T(8,128)(2,1)}, u32[]{:S(2)}) copy-start(bf16[1,128,2048]{2,1,0:T(8,128)(2,1)} %param.10) | copy-start | bytes 1572868
  20.0 3.6 %collective-permute-start.3 = (bf16[128,2048]{1,0:T(8,128)(2,1)S(1)}, bf16[128,2048]{1,0:T(8,128)(2,1)S(1)}, u32[]{:S(2)}, u32[]{:S(2)}) collective-permute-start(bf16[128,2048]{1,0:T(8,128)(2,1)S(1)} %pad_maximum_fusion), channel_id=1, source_target_pairs={{0,1},{1,0},{2,3},{3,2},{4,5},{5,4},{6,7},{7,6},{8,9},{9,8},{10,11... | collective-permute-start | bytes 1572872 | tf_op jit(solution)/shard_map/ppermute | solution.py:17
  20.2 16.2 %collective-permute-start.4 = (bf16[32,2048]{1,0:T(8,128)(2,1)S(1)}, bf16[32,2048]{1,0:T(8,128)(2,1)S(1)}, u32[]{:S(2)}, u32[]{:S(2)}) collective-permute-start(bf16[32,2048]{1,0:T(8,128)(2,1)S(1)} %held.7), channel_id=1, source_target_pairs={{0,12},{4,8},{8,4},{12,0},{1,13},{5,9},{9,5},{13,1},{2,14},{6,10},... | collective-permute-start | bytes 393224 | tf_op jit(solution)/shard_map/ppermute | solution.py:17
  23.5 12.9 %collective-permute-start.5 = (bf16[32,2048]{1,0:T(8,128)(2,1)S(1)}, bf16[32,2048]{1,0:T(8,128)(2,1)S(1)}, u32[]{:S(2)}, u32[]{:S(2)}) collective-permute-start(bf16[32,2048]{1,0:T(8,128)(2,1)S(1)} %held.7), channel_id=1, source_target_pairs={{0,8},{4,12},{8,0},{12,4},{1,9},{5,13},{9,1},{13,5},{2,10},{6,14},... | collective-permute-start | bytes 393224 | tf_op jit(solution)/shard_map/ppermute | solution.py:17
  36.5 2.0 %collective-permute-start.6 = (bf16[128,2176]{1,0:T(8,128)(2,1)S(1)}, bf16[128,2176]{1,0:T(8,128)(2,1)S(1)}, u32[]{:S(2)}, u32[]{:S(2)}) collective-permute-start(bf16[128,2176]{1,0:T(8,128)(2,1)S(1)} %held.10), channel_id=1, source_target_pairs={{0,1},{1,0},{2,3},{3,2},{4,5},{5,4},{6,7},{7,6},{8,9},{9,8},{10,11... | collective-permute-start | bytes 1671176 | tf_op jit(solution)/shard_map/ppermute | solution.py:17
  38.7 4.7 %collective-permute-start.10 = (bf16[64,2048]{1,0:T(8,128)(2,1)S(1)}, bf16[64,2048]{1,0:T(8,128)(2,1)S(1)}, u32[]{:S(2)}, u32[]{:S(2)}) collective-permute-start(bf16[64,2048]{1,0:T(8,128)(2,1)S(1)} %held.11), channel_id=1, source_target_pairs={{0,1},{1,0},{2,3},{3,2},{4,5},{5,4},{6,7},{7,6},{8,9},{9,8},{10,11... | collective-permute-start | bytes 786440 | tf_op jit(solution)/shard_map/ppermute | solution.py:17
  39.0 17.5 %collective-permute-start.7 = (bf16[32,2176]{1,0:T(8,128)(2,1)S(1)}, bf16[32,2176]{1,0:T(8,128)(2,1)S(1)}, u32[]{:S(2)}, u32[]{:S(2)}) collective-permute-start(bf16[32,2176]{1,0:T(8,128)(2,1)S(1)} %get-tuple-element.27.refs_0_), channel_id=1, source_target_pairs={{0,4},{4,0},{8,12},{12,8},{1,5},{5,1},{9,13},{13,9},{2,6},{6,2},{1... | collective-permute-start | bytes 417800 | tf_op jit(solution)/shard_map/ppermute | solution.py:17
  40.1 16.4 %collective-permute-start.8 = (bf16[32,2176]{1,0:T(8,128)(2,1)S(1)}, bf16[32,2176]{1,0:T(8,128)(2,1)S(1)}, u32[]{:S(2)}, u32[]{:S(2)}) collective-permute-start(bf16[32,2176]{1,0:T(8,128)(2,1)S(1)} %get-tuple-element.28.refs_1_), channel_id=1, source_target_pairs={{0,8},{4,12},{8,0},{12,4},{1,9},{5,13},{9,1},{13,5},{2,10},{6,14},... | collective-permute-start | bytes 417800 | tf_op jit(solution)/shard_map/ppermute | solution.py:17
  42.0 14.5 %collective-permute-start.9 = (bf16[32,2176]{1,0:T(8,128)(2,1)S(1)}, bf16[32,2176]{1,0:T(8,128)(2,1)S(1)}, u32[]{:S(2)}, u32[]{:S(2)}) collective-permute-start(bf16[32,2176]{1,0:T(8,128)(2,1)S(1)} %get-tuple-element.29.refs_2_), channel_id=1, source_target_pairs={{0,12},{4,8},{8,4},{12,0},{1,13},{5,9},{9,5},{13,1},{2,14},{6,10},... | collective-permute-start | bytes 417800 | tf_op jit(solution)/shard_map/ppermute | solution.py:17
  43.5 13.3 %copy-start.6 = (s32[1,1,4]{2,1,0:T(1,128)S(1)}, s32[1,1,4]{2,1,0:T(1,128)}, u32[]{:S(2)}) copy-start(s32[1,1,4]{2,1,0:T(1,128)} %param.19) | copy-start | bytes 52
  56.6 2.0 %collective-permute-start.11 = (bf16[128,2176]{1,0:T(8,128)(2,1)S(1)}, bf16[128,2176]{1,0:T(8,128)(2,1)S(1)}, u32[]{:S(2)}, u32[]{:S(2)}) collective-permute-start(bf16[128,2176]{1,0:T(8,128)(2,1)S(1)} %held.12), channel_id=1, source_target_pairs={{0,1},{1,0},{2,3},{3,2},{4,5},{5,4},{6,7},{7,6},{8,9},{9,8},{10,11... | collective-permute-start | bytes 1671176 | tf_op jit(solution)/shard_map/ppermute | solution.py:17
  58.7 8.4 %collective-permute-start.12 = (bf16[32,2176]{1,0:T(8,128)(2,1)S(1)}, bf16[32,2176]{1,0:T(8,128)(2,1)S(1)}, u32[]{:S(2)}, u32[]{:S(2)}) collective-permute-start(bf16[32,2176]{1,0:T(8,128)(2,1)S(1)} %get-tuple-element.33), channel_id=1, source_target_pairs={{0,4},{4,0},{8,12},{12,8},{1,5},{5,1},{9,13},{13,9},{2,6},{6,2},{1... | collective-permute-start | bytes 417800 | tf_op jit(solution)/shard_map/ppermute | solution.py:17
  59.4 13.5 %collective-permute-start.14 = (bf16[32,2176]{1,0:T(8,128)(2,1)S(1)}, bf16[32,2176]{1,0:T(8,128)(2,1)S(1)}, u32[]{:S(2)}, u32[]{:S(2)}) collective-permute-start(bf16[32,2176]{1,0:T(8,128)(2,1)S(1)} %get-tuple-element.35), channel_id=1, source_target_pairs={{0,8},{4,12},{8,0},{12,4},{1,9},{5,13},{9,1},{13,5},{2,10},{6,14},... | collective-permute-start | bytes 417800 | tf_op jit(solution)/shard_map/ppermute | solution.py:17
  61.9 11.0 %collective-permute-start.15 = (bf16[32,2176]{1,0:T(8,128)(2,1)S(1)}, bf16[32,2176]{1,0:T(8,128)(2,1)S(1)}, u32[]{:S(2)}, u32[]{:S(2)}) collective-permute-start(bf16[32,2176]{1,0:T(8,128)(2,1)S(1)} %get-tuple-element.36), channel_id=1, source_target_pairs={{0,12},{4,8},{8,4},{12,0},{1,13},{5,9},{9,5},{13,1},{2,14},{6,10},... | collective-permute-start | bytes 417800 | tf_op jit(solution)/shard_map/ppermute | solution.py:17
  67.1 5.9 %collective-permute-start.13 = (bf16[32,2048]{1,0:T(8,128)(2,1)S(1)}, bf16[32,2048]{1,0:T(8,128)(2,1)S(1)}, u32[]{:S(2)}, u32[]{:S(2)}) collective-permute-start(bf16[32,2048]{1,0:T(8,128)(2,1)S(1)} %held.13), channel_id=1, source_target_pairs={{0,2},{2,0},{1,3},{3,1},{4,6},{6,4},{5,7},{7,5},{8,10},{10,8},{9,1... | collective-permute-start | bytes 393224 | tf_op jit(solution)/shard_map/ppermute | solution.py:298
  73.1 5.0 %collective-permute-start.16 = (bf16[32,2048]{1,0:T(8,128)(2,1)S(1)}, bf16[32,2048]{1,0:T(8,128)(2,1)S(1)}, u32[]{:S(2)}, u32[]{:S(2)}) collective-permute-start(bf16[32,2048]{1,0:T(8,128)(2,1)S(1)} %get-tuple-element.37), channel_id=1, source_target_pairs={{0,2},{2,0},{1,3},{3,1},{4,6},{6,4},{5,7},{7,5},{8,10},{10,8},{9,1... | collective-permute-start | bytes 393224 | tf_op jit(solution)/shard_map/ppermute | solution.py:298
  74.7 1.2 %collective-permute-start.19 = (f32[64,128]{1,0:T(8,128)S(1)}, f32[64,128]{1,0:T(8,128)S(1)}, u32[]{:S(2)}, u32[]{:S(2)}) collective-permute-start(f32[64,128]{1,0:T(8,128)S(1)} %constant_dynamic-update-slice_fusion.10), channel_id=1, source_target_pairs={{0,1},{1,0},{2,3},{3,2},{4,5},{5,4},{6,7},{7,6},{8,9},{9,8},{10,11... | collective-permute-start | bytes 98312 | tf_op jit(solution)/shard_map/ppermute | solution.py:17
  74.7 3.6 %collective-permute-start.17 = (bf16[32,2048]{1,0:T(8,128)(2,1)S(1)}, bf16[32,2048]{1,0:T(8,128)(2,1)S(1)}, u32[]{:S(2)}, u32[]{:S(2)}) collective-permute-start(bf16[32,2048]{1,0:T(8,128)(2,1)S(1)} %collective-permute-done.13.refs_3_), channel_id=1, source_target_pairs={{0,1},{1,0},{2,3},{3,2},{4,5},{5,4},{6,7},{7,6},{8,9},{9,8},{10,11... | collective-permute-start | bytes 393224 | tf_op jit(solution)/shard_map/ppermute | solution.py:17
  78.2 1.3 %collective-permute-start.18 = (bf16[32,2048]{1,0:T(8,128)(2,1)S(1)}, bf16[32,2048]{1,0:T(8,128)(2,1)S(1)}, u32[]{:S(2)}, u32[]{:S(2)}) collective-permute-start(bf16[32,2048]{1,0:T(8,128)(2,1)S(1)} %collective-permute-done.16), channel_id=1, source_target_pairs={{0,1},{1,0},{2,3},{3,2},{4,5},{5,4},{6,7},{7,6},{8,9},{9,8},{10,11... | collective-permute-start | bytes 393224 | tf_op jit(solution)/shard_map/ppermute | solution.py:17
  (3 other events, 8.2 us)

commit v5 on v4

--- a/solution.py
+++ b/solution.py
@@ -193,7 +193,6 @@
         if j == 0 or j > steps_f:
             up_copy(j).start()
     rows_buf[...] = rows_ref[...].T
-    up_buf[width:, :] = sketch_ref[...]
 
     def first(j, carry):
         @pl.when(j + 1 < steps_d)
@@ -210,20 +209,20 @@
 
     lax.fori_loop(0, steps_f, first, 0)
 
-    for j in range(steps_d):
+    up_part = jnp.dot(sketch_ref[...], grad_buf[...], preferred_element_type=jnp.float32).T
+    vectors = jnp.concatenate([down_part_ref[0], up_part], axis=1)
+    keep_ref[:, width:] = vectors[:half]
+    give_ref[:, width:] = vectors[half:].astype(jnp.bfloat16)
+
+    def second(j, carry):
         up_copy(j).wait()
-        last = j == steps_d - 1
-        end = up_buf.shape[0] if last else (j + 1) * tile_d
-        term = jnp.dot(
-            up_buf[j * tile_d : end, :], grad_buf[...], preferred_element_type=jnp.float32
-        ).T
-        if last:
-            term = jnp.concatenate(
-                [term[:, :tile_d], down_part_ref[0], term[:, tile_d:]], axis=1
-            )
-        start = j * tile_d
-        keep_ref[:, start : start + term.shape[1]] = term[:half]
-        give_ref[:, start : start + term.shape[1]] = term[half:].astype(jnp.bfloat16)
+        part = tile(j, tile_d)
+        term = jnp.dot(up_buf[part, :], grad_buf[...], preferred_element_type=jnp.float32).T
+        keep_ref[:, part] = term[:half]
+        give_ref[:, part] = term[half:].astype(jnp.bfloat16)
+        return carry
+
+    lax.fori_loop(0, steps_d, second, 0)
 
 
 def expert(chunk, rows, slope, down_part, sketch_t, down_local, up_local, *events):
@@ -252,7 +251,7 @@
         scratch_shapes=[
             pltpu.VMEM((width, count), jnp.bfloat16),
             pltpu.VMEM((hidden_cols, count), jnp.bfloat16),
-            pltpu.VMEM((width + rank, hidden_cols), jnp.bfloat16),
+            pltpu.VMEM((width, hidden_cols), jnp.bfloat16),
             pltpu.SemaphoreType.DMA((width // tile_d,)),
         ],
         compiler_params=pltpu.CompilerParams(vmem_limit_bytes=26 << 20),

time: 81.1 us -> 77.3 us (0.953)
  Pallas kernels: 32.8 us -> 25.8 us
  waiting for transfers between devices: 13 us -> 15.8 us
    pallas_call x2, Pallas kernels: 25.8 us -> 18.8 us  [expert(): pl.pallas_call(functools.partial(expert_kernel, tile_f, tile_d), grid=(1,...]
    ppermute x18, waiting for transfers between devices: 12.9 us -> 15.8 us  [xored(): return lax.ppermute(block, axis, [(i, i ^ bits) for i in range(n)])]
  transfers between devices with their start and end apart: 20 -> 20, of which waited for: 7 -> 8; matrix products, arithmetic and copies ran while one was open for 8% -> 8% of each run, Pallas kernels for 40% -> 33%
where the time goes in v5:
time: 77.3 us; the launch traced here: 76.9 us
  Pallas kernels  25.8 us (33%)
  starting transfers between devices  23.2 us (30%)
  waiting for transfers between devices  15.8 us (20%)
  local copies, waits for them, and re-layouts  6.31 us (8%)
  matrix products  2.65 us (3%)
  other arithmetic  2.13 us (3%)
  between operations  1.04 us (1%)
    ppermute x18, starting transfers between devices, xored(): return lax.ppermute(block, axis, [(i, i ^ bits) for i in range(n)])  20.1 us
    pallas_call x2, Pallas kernels, expert(): pl.pallas_call(functools.partial(expert_kernel, tile_f, tile_d), grid=(1,...  18.8 us
    ppermute x18, waiting for transfers between devices, xored(): return lax.ppermute(block, axis, [(i, i ^ bits) for i in range(n)])  15.8 us
    pallas_call x1, Pallas kernels, slopes(): pl.pallas_call(functools.partial(slope_kernel, groups), grid_spec=pltpu.P...  6.27 us
    unnamed x32, local copies, waits for them, and re-layouts  4.41 us
    ppermute x2, starting transfers between devices, below(): lax.ppermute(block, 'section', [(s, (s - 1) % sections) for s in range(se...  3.12 us
    broadcast_in_dim x2, other arithmetic, per_device(): return (handed[None], features[None])  1.6 us
  transfers between devices with their start and end apart: 20, of which 8 were waited for; matrix products, arithmetic and copies ran while one was open for 8% of the time, Pallas kernels for 33%

profile of v5, /device:TPU:0, one launch (start us, length us, event | category | flops | bytes accessed | tf_op | source)
XLA Modules:
  0.0 76.9 jit_solution(1458221895487208417)
XLA Ops:
  0.7 1.0 %constant_dynamic-update-slice_fusion.2 = (bf16[256,2048]{1,0:T(8,128)(2,1)S(1)}, bf16[32,2048]{1,0:T(8,128)(2,1)S(1)}) fusion(bf16[1,128,2048]{2,1,0:T(8,128)(2,1)} %param.10, s32[]{:T(128)S(6)} %select_n.45), kind=kLoop, calls=%fused_computation.40 | loop fusion | bytes 393220
  1.6 4.1 %collective-permute-start.1 = (bf16[32,2048]{1,0:T(8,128)(2,1)S(1)}, bf16[32,2048]{1,0:T(8,128)(2,1)S(1)}, u32[]{:S(2)}, u32[]{:S(2)}) collective-permute-start(bf16[32,2048]{1,0:T(8,128)(2,1)S(1)} %get-tuple-element.43.cot_ref), channel_id=1, source_target_pairs={{0,8},{4,12},{8,0},{12,4},{1,9},{5,13},{9,1},{13,5},{2,10},{6,14},... | collective-permute-start | bytes 393224 | tf_op jit(solution)/shard_map/ppermute | solution.py:17
  5.7 1.3 %collective-permute-start.2 = (bf16[32,2048]{1,0:T(8,128)(2,1)S(1)}, bf16[32,2048]{1,0:T(8,128)(2,1)S(1)}, u32[]{:S(2)}, u32[]{:S(2)}) collective-permute-start(bf16[32,2048]{1,0:T(8,128)(2,1)S(1)} %get-tuple-element.43.cot_ref), channel_id=1, source_target_pairs={{0,12},{4,8},{8,4},{12,0},{1,13},{5,9},{9,5},{13,1},{2,14},{6,10},... | collective-permute-start | bytes 393224 | tf_op jit(solution)/shard_map/ppermute | solution.py:17
  9.2 2.0 %copy-done.1 = bf16[1,1,4,128,3584]{4,3,2,1,0:T(8,128)(2,1)S(1)} copy-done((bf16[1,1,4,128,3584]{4,3,2,1,0:T(8,128)(2,1)S(1)}, bf16[1,1,4,128,3584]{4,3,2,1,0:T(8,128)(2,1)}, u32[]{:S(2)}) %copy-start.1) | copy-done | bytes 3670040
  11.2 1.0 %copy-done.2 = bf16[1,1,3584,64]{2,3,1,0:T(8,128)(2,1)S(1)} copy-done((bf16[1,1,3584,64]{2,3,1,0:T(8,128)(2,1)S(1)}, bf16[1,1,3584,64]{2,3,1,0:T(8,128)(2,1)}, u32[]{:S(2)}) %copy-start.2) | copy-done | bytes 458776
  12.2 6.3 %slopes.1 = (bf16[2,3584,256]{2,1,0:T(8,128)(2,1)S(1)}, f32[2,256,64]{2,1,0:T(8,128)S(1)}, bf16[3584,2048]{1,0:T(8,128)(2,1)S(1)}) custom-call(s32[2]{0:T(128)S(1)} %pad_add_fusion.index_ref, bf16[4,2,2,32,3584]{4,3,2,1,0:T(8,128)(2,1)S(1)} %bitcast.52, bf16[4,2,2,32,3584]{4,3,2,1,0:T(8,128)(2,1)S(1)} %bitcast.53, bf16[4,2,2,32,3584]{4,3,2,1,0:T(8,128)(2,1)S(1)} %bitcast.54, ...), custom_call_target="tpu_custom_call" | custom-call | flops 234881024 | bytes 7340032 | tf_op jit(solution)/shard_map/slopes/pallas_call | solution.py:147
  18.6 1.3 %collective-permute-done.refs_0_ = bf16[64,2048]{1,0:T(8,128)(2,1)S(1)} collective-permute-done((bf16[64,2048]{1,0:T(8,128)(2,1)S(1)}, bf16[64,2048]{1,0:T(8,128)(2,1)S(1)}, u32[]{:S(2)}, u32[]{:S(2)}) %collective-permute-start) | collective-permute-done | bytes 262176 | tf_op jit(solution)/shard_map/ppermute | solution.py:17
  20.2 3.3 %collective-permute-start.4 = (bf16[32,2048]{1,0:T(8,128)(2,1)S(1)}, bf16[32,2048]{1,0:T(8,128)(2,1)S(1)}, u32[]{:S(2)}, u32[]{:S(2)}) collective-permute-start(bf16[32,2048]{1,0:T(8,128)(2,1)S(1)} %held.7), channel_id=1, source_target_pairs={{0,12},{4,8},{8,4},{12,0},{1,13},{5,9},{9,5},{13,1},{2,14},{6,10},... | collective-permute-start | bytes 393224 | tf_op jit(solution)/shard_map/ppermute | solution.py:17
  23.6 9.4 %expert.2 = (f32[128,2176]{1,0:T(8,128)S(1)}, bf16[128,2176]{1,0:T(8,128)(2,1)S(1)}) custom-call(bf16[256,2048]{1,0:T(8,128)(2,1)S(1)} %slice_dynamic-update-slice_fusion.4.rows_ref, bf16[2,3584,256]{2,1,0:T(8,128)(2,1)S(1)} %get-tuple-element.21.slope_ref, f32[2,256,64]{2,1,0:T(8,128)S(1)} %get-tuple-element.22.down_part_ref, ...), custom_call_target="tpu_custom_call" | custom-call | flops 7516192768 | bytes 29360128 | tf_op jit(solution)/shard_map/expert/pallas_call | solution.py:235
  33.1 1.4 %collective-permute-done.5.block_ref = bf16[32,2048]{1,0:T(8,128)(2,1)S(1)} collective-permute-done((bf16[32,2048]{1,0:T(8,128)(2,1)S(1)}, bf16[32,2048]{1,0:T(8,128)(2,1)S(1)}, u32[]{:S(2)}, u32[]{:S(2)}) %collective-permute-start.5) | collective-permute-done | bytes 131104 | tf_op jit(solution)/shard_map/ppermute | solution.py:17
  34.7 1.9 %collective-permute-done.6.came_ref = bf16[128,2176]{1,0:T(8,128)(2,1)S(1)} collective-permute-done((bf16[128,2176]{1,0:T(8,128)(2,1)S(1)}, bf16[128,2176]{1,0:T(8,128)(2,1)S(1)}, u32[]{:S(2)}, u32[]{:S(2)}) %collective-permute-start.6) | collective-permute-done | bytes 557088 | tf_op jit(solution)/shard_map/ppermute | solution.py:17
  37.0 3.0 %collective-permute-start.8 = (bf16[32,2176]{1,0:T(8,128)(2,1)S(1)}, bf16[32,2176]{1,0:T(8,128)(2,1)S(1)}, u32[]{:S(2)}, u32[]{:S(2)}) collective-permute-start(bf16[32,2176]{1,0:T(8,128)(2,1)S(1)} %get-tuple-element.28.refs_1_), channel_id=1, source_target_pairs={{0,8},{4,12},{8,0},{12,4},{1,9},{5,13},{9,1},{13,5},{2,10},{6,14},... | collective-permute-start | bytes 417800 | tf_op jit(solution)/shard_map/ppermute | solution.py:17
  40.0 1.3 %collective-permute-start.9 = (bf16[32,2176]{1,0:T(8,128)(2,1)S(1)}, bf16[32,2176]{1,0:T(8,128)(2,1)S(1)}, u32[]{:S(2)}, u32[]{:S(2)}) collective-permute-start(bf16[32,2176]{1,0:T(8,128)(2,1)S(1)} %get-tuple-element.29.refs_2_), channel_id=1, source_target_pairs={{0,12},{4,8},{8,4},{12,0},{1,13},{5,9},{9,5},{13,1},{2,14},{6,10},... | collective-permute-start | bytes 417800 | tf_op jit(solution)/shard_map/ppermute | solution.py:17
  41.4 9.4 %expert.3 = (f32[128,2176]{1,0:T(8,128)S(1)}, bf16[128,2176]{1,0:T(8,128)(2,1)S(1)}) custom-call(bf16[256,2048]{1,0:T(8,128)(2,1)S(1)} %slice_dynamic-update-slice_fusion.rows_ref, bf16[2,3584,256]{2,1,0:T(8,128)(2,1)S(1)} %get-tuple-element.21.slope_ref, f32[2,256,64]{2,1,0:T(8,128)S(1)} %get-tuple-element.22.down_part_ref, bf16[64,3584]{1,0:T(8,128)(2,1)S(1)} %bitcast.62, ...), custom_call_target="tpu_custom_call" | custom-call | flops 7516192768 | bytes 29360128 | tf_op jit(solution)/shard_map/expert/pallas_call | solution.py:235
  51.3 1.3 %fusion = f32[128,64]{0,1:T(8,128)S(1)} fusion(bf16[1,128,2048]{2,1,0:T(8,128)(2,1)} %param.10, bf16[1,2048,64]{1,2,0:T(8,128)(2,1)S(1)} %copy-done), kind=kOutput, calls=%fused_computation.4 | convolution fusion | flops 33554432 | bytes 819200 | tf_op jit(solution)/shard_map/dot_general | solution.py:365
  53.1 2.7 %collective-permute-start.12 = (bf16[32,2176]{1,0:T(8,128)(2,1)S(1)}, bf16[32,2176]{1,0:T(8,128)(2,1)S(1)}, u32[]{:S(2)}, u32[]{:S(2)}) collective-permute-start(bf16[32,2176]{1,0:T(8,128)(2,1)S(1)} %get-tuple-element.33), channel_id=1, source_target_pairs={{0,4},{4,0},{8,12},{12,8},{1,5},{5,1},{9,13},{13,9},{2,6},{6,2},{1... | collective-permute-start | bytes 417800 | tf_op jit(solution)/shard_map/ppermute | solution.py:17
  55.9 1.2 %collective-permute-start.14 = (bf16[32,2176]{1,0:T(8,128)(2,1)S(1)}, bf16[32,2176]{1,0:T(8,128)(2,1)S(1)}, u32[]{:S(2)}, u32[]{:S(2)}) collective-permute-start(bf16[32,2176]{1,0:T(8,128)(2,1)S(1)} %get-tuple-element.35), channel_id=1, source_target_pairs={{0,8},{4,12},{8,0},{12,4},{1,9},{5,13},{9,1},{13,5},{2,10},{6,14},... | collective-permute-start | bytes 417800 | tf_op jit(solution)/shard_map/ppermute | solution.py:17
  57.1 1.5 %collective-permute-start.15 = (bf16[32,2176]{1,0:T(8,128)(2,1)S(1)}, bf16[32,2176]{1,0:T(8,128)(2,1)S(1)}, u32[]{:S(2)}, u32[]{:S(2)}) collective-permute-start(bf16[32,2176]{1,0:T(8,128)(2,1)S(1)} %get-tuple-element.36), channel_id=1, source_target_pairs={{0,12},{4,8},{8,4},{12,0},{1,13},{5,9},{9,5},{13,1},{2,14},{6,10},... | collective-permute-start | bytes 417800 | tf_op jit(solution)/shard_map/ppermute | solution.py:17
  58.7 3.2 %collective-permute-done.12.refs_0_ = bf16[32,2176]{1,0:T(8,128)(2,1)S(1)} collective-permute-done((bf16[32,2176]{1,0:T(8,128)(2,1)S(1)}, bf16[32,2176]{1,0:T(8,128)(2,1)S(1)}, u32[]{:S(2)}, u32[]{:S(2)}) %collective-permute-start.12) | collective-permute-done | bytes 139296 | tf_op jit(solution)/shard_map/ppermute | solution.py:17
  61.8 1.6 %collective-permute-start.13 = (bf16[32,2048]{1,0:T(8,128)(2,1)S(1)}, bf16[32,2048]{1,0:T(8,128)(2,1)S(1)}, u32[]{:S(2)}, u32[]{:S(2)}) collective-permute-start(bf16[32,2048]{1,0:T(8,128)(2,1)S(1)} %held.13), channel_id=1, source_target_pairs={{0,2},{2,0},{1,3},{3,1},{4,6},{6,4},{5,7},{7,5},{8,10},{10,8},{9,1... | collective-permute-start | bytes 393224 | tf_op jit(solution)/shard_map/ppermute | solution.py:297
  63.6 5.9 %collective-permute-done.14.refs_1_ = bf16[32,2176]{1,0:T(8,128)(2,1)S(1)} collective-permute-done((bf16[32,2176]{1,0:T(8,128)(2,1)S(1)}, bf16[32,2176]{1,0:T(8,128)(2,1)S(1)}, u32[]{:S(2)}, u32[]{:S(2)}) %collective-permute-start.14) | collective-permute-done | bytes 139296 | tf_op jit(solution)/shard_map/ppermute | solution.py:17
  69.6 1.6 %collective-permute-start.16 = (bf16[32,2048]{1,0:T(8,128)(2,1)S(1)}, bf16[32,2048]{1,0:T(8,128)(2,1)S(1)}, u32[]{:S(2)}, u32[]{:S(2)}) collective-permute-start(bf16[32,2048]{1,0:T(8,128)(2,1)S(1)} %get-tuple-element.37), channel_id=1, source_target_pairs={{0,2},{2,0},{1,3},{3,1},{4,6},{6,4},{5,7},{7,5},{8,10},{10,8},{9,1... | collective-permute-start | bytes 393224 | tf_op jit(solution)/shard_map/ppermute | solution.py:297
  72.5 1.0 %convolution_bitcast_fusion = f32[4,64,64]{2,1,0:T(8,128)S(1)} fusion(f32[128,64]{0,1:T(8,128)S(1)} %copy.18, f32[128,4]{0,1:T(4,128)S(1)} %convert_bitcast_fusion, f32[1,128,64]{1,2,0:T(8,128)} %param.16), kind=kOutput, calls=%fused_computation | convolution fusion | flops 25198592 | bytes 133120 | tf_op jit(solution)/shard_map/et,ta,tb->eab/dot_general | solution.py:377
  74.8 1.2 %collective-permute-done.18 = bf16[32,2048]{1,0:T(8,128)(2,1)S(1)} collective-permute-done((bf16[32,2048]{1,0:T(8,128)(2,1)S(1)}, bf16[32,2048]{1,0:T(8,128)(2,1)S(1)}, u32[]{:S(2)}, u32[]{:S(2)}) %collective-permute-start.18) | collective-permute-done | bytes 131104 | tf_op jit(solution)/shard_map/ppermute | solution.py:17
  (87 shorter events, 7.9 us)
Async XLA Ops:
  0.6 50.7 %copy-start = (bf16[1,2048,64]{1,2,0:T(8,128)(2,1)S(1)}, bf16[1,2048,64]{1,2,0:T(8,128)(2,1)}, u32[]{:S(2)}) copy-start(bf16[1,2048,64]{1,2,0:T(8,128)(2,1)} %param.17) | copy-start | bytes 786436
  1.6 17.0 %collective-permute-start.1 = (bf16[32,2048]{1,0:T(8,128)(2,1)S(1)}, bf16[32,2048]{1,0:T(8,128)(2,1)S(1)}, u32[]{:S(2)}, u32[]{:S(2)}) collective-permute-start(bf16[32,2048]{1,0:T(8,128)(2,1)S(1)} %get-tuple-element.43.cot_ref), channel_id=1, source_target_pairs={{0,8},{4,12},{8,0},{12,4},{1,9},{5,13},{9,1},{13,5},{2,10},{6,14},... | collective-permute-start | bytes 393224 | tf_op jit(solution)/shard_map/ppermute | solution.py:17
  5.7 12.9 %collective-permute-start.2 = (bf16[32,2048]{1,0:T(8,128)(2,1)S(1)}, bf16[32,2048]{1,0:T(8,128)(2,1)S(1)}, u32[]{:S(2)}, u32[]{:S(2)}) collective-permute-start(bf16[32,2048]{1,0:T(8,128)(2,1)S(1)} %get-tuple-element.43.cot_ref), channel_id=1, source_target_pairs={{0,12},{4,8},{8,4},{12,0},{1,13},{5,9},{9,5},{13,1},{2,14},{6,10},... | collective-permute-start | bytes 393224 | tf_op jit(solution)/shard_map/ppermute | solution.py:17
  8.0 11.9 %collective-permute-start = (bf16[64,2048]{1,0:T(8,128)(2,1)S(1)}, bf16[64,2048]{1,0:T(8,128)(2,1)S(1)}, u32[]{:S(2)}, u32[]{:S(2)}) collective-permute-start(bf16[64,2048]{1,0:T(8,128)(2,1)S(1)} %dynamic-slice_bitcast_fusion), channel_id=1, source_target_pairs={{0,4},{4,0},{8,12},{12,8},{1,5},{5,1},{9,13},{13,9},{2,6},{6,2},{1... | collective-permute-start | bytes 786440 | tf_op jit(solution)/shard_map/ppermute | solution.py:17
  12.2 6.3 %copy-start.5 = (s32[1,1,2]{2,1,0:T(1,128)S(1)}, s32[1,1,2]{2,1,0:T(1,128)}, u32[]{:S(2)}) copy-start(s32[1,1,2]{2,1,0:T(1,128)} %param.11) | copy-start | bytes 28
  12.2 7.9 %copy-start.4 = (bf16[1,128,2048]{2,1,0:T(8,128)(2,1)S(1)}, bf16[1,128,2048]{2,1,0:T(8,128)(2,1)}, u32[]{:S(2)}) copy-start(bf16[1,128,2048]{2,1,0:T(8,128)(2,1)} %param.10) | copy-start | bytes 1572868
  20.0 3.6 %collective-permute-start.3 = (bf16[128,2048]{1,0:T(8,128)(2,1)S(1)}, bf16[128,2048]{1,0:T(8,128)(2,1)S(1)}, u32[]{:S(2)}, u32[]{:S(2)}) collective-permute-start(bf16[128,2048]{1,0:T(8,128)(2,1)S(1)} %pad_maximum_fusion), channel_id=1, source_target_pairs={{0,1},{1,0},{2,3},{3,2},{4,5},{5,4},{6,7},{7,6},{8,9},{9,8},{10,11... | collective-permute-start | bytes 1572872 | tf_op jit(solution)/shard_map/ppermute | solution.py:17
  20.2 12.9 %collective-permute-start.4 = (bf16[32,2048]{1,0:T(8,128)(2,1)S(1)}, bf16[32,2048]{1,0:T(8,128)(2,1)S(1)}, u32[]{:S(2)}, u32[]{:S(2)}) collective-permute-start(bf16[32,2048]{1,0:T(8,128)(2,1)S(1)} %held.7), channel_id=1, source_target_pairs={{0,12},{4,8},{8,4},{12,0},{1,13},{5,9},{9,5},{13,1},{2,14},{6,10},... | collective-permute-start | bytes 393224 | tf_op jit(solution)/shard_map/ppermute | solution.py:17
  23.5 11.0 %collective-permute-start.5 = (bf16[32,2048]{1,0:T(8,128)(2,1)S(1)}, bf16[32,2048]{1,0:T(8,128)(2,1)S(1)}, u32[]{:S(2)}, u32[]{:S(2)}) collective-permute-start(bf16[32,2048]{1,0:T(8,128)(2,1)S(1)} %held.7), channel_id=1, source_target_pairs={{0,8},{4,12},{8,0},{12,4},{1,9},{5,13},{9,1},{13,5},{2,10},{6,14},... | collective-permute-start | bytes 393224 | tf_op jit(solution)/shard_map/ppermute | solution.py:17
  34.6 2.0 %collective-permute-start.6 = (bf16[128,2176]{1,0:T(8,128)(2,1)S(1)}, bf16[128,2176]{1,0:T(8,128)(2,1)S(1)}, u32[]{:S(2)}, u32[]{:S(2)}) collective-permute-start(bf16[128,2176]{1,0:T(8,128)(2,1)S(1)} %held.10), channel_id=1, source_target_pairs={{0,1},{1,0},{2,3},{3,2},{4,5},{5,4},{6,7},{7,6},{8,9},{9,8},{10,11... | collective-permute-start | bytes 1671176 | tf_op jit(solution)/shard_map/ppermute | solution.py:17
  36.7 4.7 %collective-permute-start.10 = (bf16[64,2048]{1,0:T(8,128)(2,1)S(1)}, bf16[64,2048]{1,0:T(8,128)(2,1)S(1)}, u32[]{:S(2)}, u32[]{:S(2)}) collective-permute-start(bf16[64,2048]{1,0:T(8,128)(2,1)S(1)} %held.11), channel_id=1, source_target_pairs={{0,1},{1,0},{2,3},{3,2},{4,5},{5,4},{6,7},{7,6},{8,9},{9,8},{10,11... | collective-permute-start | bytes 786440 | tf_op jit(solution)/shard_map/ppermute | solution.py:17
  36.9 13.9 %collective-permute-start.7 = (bf16[32,2176]{1,0:T(8,128)(2,1)S(1)}, bf16[32,2176]{1,0:T(8,128)(2,1)S(1)}, u32[]{:S(2)}, u32[]{:S(2)}) collective-permute-start(bf16[32,2176]{1,0:T(8,128)(2,1)S(1)} %get-tuple-element.27.refs_0_), channel_id=1, source_target_pairs={{0,4},{4,0},{8,12},{12,8},{1,5},{5,1},{9,13},{13,9},{2,6},{6,2},{1... | collective-permute-start | bytes 417800 | tf_op jit(solution)/shard_map/ppermute | solution.py:17
  37.0 13.9 %collective-permute-start.8 = (bf16[32,2176]{1,0:T(8,128)(2,1)S(1)}, bf16[32,2176]{1,0:T(8,128)(2,1)S(1)}, u32[]{:S(2)}, u32[]{:S(2)}) collective-permute-start(bf16[32,2176]{1,0:T(8,128)(2,1)S(1)} %get-tuple-element.28.refs_1_), channel_id=1, source_target_pairs={{0,8},{4,12},{8,0},{12,4},{1,9},{5,13},{9,1},{13,5},{2,10},{6,14},... | collective-permute-start | bytes 417800 | tf_op jit(solution)/shard_map/ppermute | solution.py:17
  40.0 10.8 %collective-permute-start.9 = (bf16[32,2176]{1,0:T(8,128)(2,1)S(1)}, bf16[32,2176]{1,0:T(8,128)(2,1)S(1)}, u32[]{:S(2)}, u32[]{:S(2)}) collective-permute-start(bf16[32,2176]{1,0:T(8,128)(2,1)S(1)} %get-tuple-element.29.refs_2_), channel_id=1, source_target_pairs={{0,12},{4,8},{8,4},{12,0},{1,13},{5,9},{9,5},{13,1},{2,14},{6,10},... | collective-permute-start | bytes 417800 | tf_op jit(solution)/shard_map/ppermute | solution.py:17
  41.4 9.8 %copy-start.6 = (s32[1,1,4]{2,1,0:T(1,128)S(1)}, s32[1,1,4]{2,1,0:T(1,128)}, u32[]{:S(2)}) copy-start(s32[1,1,4]{2,1,0:T(1,128)} %param.19) | copy-start | bytes 52
  50.9 2.0 %collective-permute-start.11 = (bf16[128,2176]{1,0:T(8,128)(2,1)S(1)}, bf16[128,2176]{1,0:T(8,128)(2,1)S(1)}, u32[]{:S(2)}, u32[]{:S(2)}) collective-permute-start(bf16[128,2176]{1,0:T(8,128)(2,1)S(1)} %held.12), channel_id=1, source_target_pairs={{0,1},{1,0},{2,3},{3,2},{4,5},{5,4},{6,7},{7,6},{8,9},{9,8},{10,11... | collective-permute-start | bytes 1671176 | tf_op jit(solution)/shard_map/ppermute | solution.py:17
  53.1 8.8 %collective-permute-start.12 = (bf16[32,2176]{1,0:T(8,128)(2,1)S(1)}, bf16[32,2176]{1,0:T(8,128)(2,1)S(1)}, u32[]{:S(2)}, u32[]{:S(2)}) collective-permute-start(bf16[32,2176]{1,0:T(8,128)(2,1)S(1)} %get-tuple-element.33), channel_id=1, source_target_pairs={{0,4},{4,0},{8,12},{12,8},{1,5},{5,1},{9,13},{13,9},{2,6},{6,2},{1... | collective-permute-start | bytes 417800 | tf_op jit(solution)/shard_map/ppermute | solution.py:17
  55.9 13.5 %collective-permute-start.14 = (bf16[32,2176]{1,0:T(8,128)(2,1)S(1)}, bf16[32,2176]{1,0:T(8,128)(2,1)S(1)}, u32[]{:S(2)}, u32[]{:S(2)}) collective-permute-start(bf16[32,2176]{1,0:T(8,128)(2,1)S(1)} %get-tuple-element.35), channel_id=1, source_target_pairs={{0,8},{4,12},{8,0},{12,4},{1,9},{5,13},{9,1},{13,5},{2,10},{6,14},... | collective-permute-start | bytes 417800 | tf_op jit(solution)/shard_map/ppermute | solution.py:17
  57.1 12.3 %collective-permute-start.15 = (bf16[32,2176]{1,0:T(8,128)(2,1)S(1)}, bf16[32,2176]{1,0:T(8,128)(2,1)S(1)}, u32[]{:S(2)}, u32[]{:S(2)}) collective-permute-start(bf16[32,2176]{1,0:T(8,128)(2,1)S(1)} %get-tuple-element.36), channel_id=1, source_target_pairs={{0,12},{4,8},{8,4},{12,0},{1,13},{5,9},{9,5},{13,1},{2,14},{6,10},... | collective-permute-start | bytes 417800 | tf_op jit(solution)/shard_map/ppermute | solution.py:17
  61.8 7.6 %collective-permute-start.13 = (bf16[32,2048]{1,0:T(8,128)(2,1)S(1)}, bf16[32,2048]{1,0:T(8,128)(2,1)S(1)}, u32[]{:S(2)}, u32[]{:S(2)}) collective-permute-start(bf16[32,2048]{1,0:T(8,128)(2,1)S(1)} %held.13), channel_id=1, source_target_pairs={{0,2},{2,0},{1,3},{3,1},{4,6},{6,4},{5,7},{7,5},{8,10},{10,8},{9,1... | collective-permute-start | bytes 393224 | tf_op jit(solution)/shard_map/ppermute | solution.py:297
  69.6 5.0 %collective-permute-start.16 = (bf16[32,2048]{1,0:T(8,128)(2,1)S(1)}, bf16[32,2048]{1,0:T(8,128)(2,1)S(1)}, u32[]{:S(2)}, u32[]{:S(2)}) collective-permute-start(bf16[32,2048]{1,0:T(8,128)(2,1)S(1)} %get-tuple-element.37), channel_id=1, source_target_pairs={{0,2},{2,0},{1,3},{3,1},{4,6},{6,4},{5,7},{7,5},{8,10},{10,8},{9,1... | collective-permute-start | bytes 393224 | tf_op jit(solution)/shard_map/ppermute | solution.py:297
  71.2 1.2 %collective-permute-start.19 = (f32[64,128]{1,0:T(8,128)S(1)}, f32[64,128]{1,0:T(8,128)S(1)}, u32[]{:S(2)}, u32[]{:S(2)}) collective-permute-start(f32[64,128]{1,0:T(8,128)S(1)} %constant_dynamic-update-slice_fusion.10), channel_id=1, source_target_pairs={{0,1},{1,0},{2,3},{3,2},{4,5},{5,4},{6,7},{7,6},{8,9},{9,8},{10,11... | collective-permute-start | bytes 98312 | tf_op jit(solution)/shard_map/ppermute | solution.py:17
  71.2 3.6 %collective-permute-start.17 = (bf16[32,2048]{1,0:T(8,128)(2,1)S(1)}, bf16[32,2048]{1,0:T(8,128)(2,1)S(1)}, u32[]{:S(2)}, u32[]{:S(2)}) collective-permute-start(bf16[32,2048]{1,0:T(8,128)(2,1)S(1)} %collective-permute-done.13.refs_3_), channel_id=1, source_target_pairs={{0,1},{1,0},{2,3},{3,2},{4,5},{5,4},{6,7},{7,6},{8,9},{9,8},{10,11... | collective-permute-start | bytes 393224 | tf_op jit(solution)/shard_map/ppermute | solution.py:17
  74.7 1.3 %collective-permute-start.18 = (bf16[32,2048]{1,0:T(8,128)(2,1)S(1)}, bf16[32,2048]{1,0:T(8,128)(2,1)S(1)}, u32[]{:S(2)}, u32[]{:S(2)}) collective-permute-start(bf16[32,2048]{1,0:T(8,128)(2,1)S(1)} %collective-permute-done.16), channel_id=1, source_target_pairs={{0,1},{1,0},{2,3},{3,2},{4,5},{5,4},{6,7},{7,6},{8,9},{9,8},{10,11... | collective-permute-start | bytes 393224 | tf_op jit(solution)/shard_map/ppermute | solution.py:17
  (3 other events, 8.2 us)

commit v6 on v5

--- a/solution.py
+++ b/solution.py
@@ -19,6 +19,33 @@
 
 ANYWHERE = pl.BlockSpec(memory_space=pl.ANY)
 RESIDENT = pl.BlockSpec(memory_space=pltpu.VMEM)
+
+
+def halves_kernel(core_ref, cot_ref, mine_ref, theirs_ref, first_ref):
+    half = mine_ref.shape[0]
+    for h, out_ref in enumerate((mine_ref, theirs_ref)):
+        start = pl.multiple_of((core_ref[0] ^ h) * half, half)
+        out_ref[...] = cot_ref[pl.ds(start, half), :]
+    start = pl.multiple_of(core_ref[0] * half, half)
+    first_ref[...] = cot_ref[pl.ds(start, first_ref.shape[0]), :]
+
+
+def halves(cot, core, rows):
+    tok_dev, width = cot.shape
+    cot = pltpu.with_memory_space_constraint(cot, pltpu.HBM)
+    counts = (tok_dev // 2, tok_dev // 2, rows)
+    return pl.pallas_call(
+        halves_kernel,
+        grid_spec=pltpu.PrefetchScalarGridSpec(
+            num_scalar_prefetch=1,
+            grid=(1,),
+            in_specs=[pl.BlockSpec((tok_dev, width), lambda i, core: (0, 0))],
+            out_specs=[RESIDENT] * 3,
+        ),
+        out_shape=[jax.ShapeDtypeStruct((count, width), cot.dtype) for count in counts],
+        compiler_params=pltpu.CompilerParams(vmem_limit_bytes=4 << 20),
+        name="halves",
+    )(core.astype(jnp.int32).reshape(1), cot)
 
 
 def held_kernel(block_ref, *refs):
@@ -67,7 +94,8 @@
     width = grad_ref.shape[1]
     total = weight_ref[:, :1] * own_ref[...]
     for slot in range(1, slots):
-        total += weight_ref[:, slot : slot + 1] * refs[slot - 1][...].astype(jnp.float32)
+        back = refs[slots - 1 - slot][...].astype(jnp.float32)
+        total += weight_ref[:, slot : slot + 1] * back
     grad_ref[...] = (cot_ref[...].astype(jnp.float32) + total[:, :width]).astype(jnp.bfloat16)
     vec_ref[...] = total[:, width:]
 
@@ -306,12 +334,11 @@
     weight = jnp.sum(jnp.where(hits, half_gates[:, None, :], 0.0), axis=2)
 
     sketch_t = sketch_local.T
-    cot_mine = lax.dynamic_slice_in_dim(cot, core * half, half, 0)
-    cot_theirs = lax.dynamic_slice_in_dim(cot, (1 - core) * half, half, 0)
+    cot_mine, cot_theirs, cot_first = halves(cot, core, rows)
     order = sorted(range(2, pieces), reverse=True)
     slope, down_part, down_here = slopes(pre_all, sketch_t, down_weight[0, 0], place, core)
     near_rows = xored(cot_mine, "dp", 1)
-    fetched = {slot: xored(cot_mine[:rows], "dp", slot) for slot in order}
+    fetched = {slot: xored(cot_first, "dp", slot) for slot in order}
     own, sent, grad, passed, backs = (), (), (), (), ()
     below_mine, vectors = [], []
     for a in range(CHUNKS):
@@ -335,15 +362,15 @@
             a, rows_in, slope, down_part, sketch_t, down_here, up_weight[0, 0], *sent
         )
         if a + 1 < CHUNKS:
-            coming = held(cot_mine[(a + 1) * rows : (a + 2) * rows], near_rows)
+            coming = held(cot_mine[(a + 1) * rows : (a + 2) * rows], *fetched.values())
             fetched = {slot: held(xored(coming, "dp", slot), kept) for slot in order}
             give = held(give, *fetched.values(), *backs)
         else:
             give = held(give, *backs)
         own, *sent = merged(kept, xored(give, "tensor", 1), rows)
-        backs = [xored(out, "dp", slot + 1) for slot, out in enumerate(sent)]
+        backs = [xored(out, "dp", slot + 1) for slot, out in enumerate(sent)][::-1]
         if grad:
-            passed = (below(held(*grad, backs[0])),)
+            passed = (below(held(*grad, own)),)
             below_mine.append(*passed)
         new, vec = finished(own, cot_mine[part], weight[part], backs, *passed)
         grad = (new,)
@@ -351,7 +378,8 @@
     below_mine.append(below(*grad))
 
     mine = jnp.concatenate(below_mine, axis=0)
-    theirs = jnp.concatenate([xored(f, "tensor", 1) for f in below_mine], axis=0)
+    theirs = [held(block, *grad) for block in below_mine[:-1]] + below_mine[-1:]
+    theirs = jnp.concatenate([xored(block, "tensor", 1) for block in theirs], axis=0)
     handed = jnp.concatenate(
         [jnp.where(core == 0, mine, theirs), jnp.where(core == 0, theirs, mine)], axis=0
     )

time: 77.3 us -> 80.1 us (1.036)
  waiting for transfers between devices: 15.8 us -> 18.7 us
  matrix products: 2.65 us -> 0.82 us
  other arithmetic: 2.13 us -> 3.74 us
  starting transfers between devices: 23.2 us -> 21.8 us
  Pallas kernels: 25.8 us -> 26.9 us
    ppermute x2, waiting for transfers between devices: 0.03 us -> 3.29 us  [below(): lax.ppermute(block, 'section', [(s, (s - 1) % sections) for s in range(se...]
    pallas_call x0 -> x1, Pallas kernels: none -> 1.13 us  [halves(): pl.pallas_call(halves_kernel, grid_spec=pltpu.PrefetchScalarGridSpec(num_...]
    dot_general x1, matrix products: 1.34 us -> 0.3 us  [per_device(): out_vec = jnp.dot(cot, model_sketch[0], preferred_element_type=jnp.float32)]
    dynamic_slice x1 -> x0, local copies, waits for them, and re-layouts: 0.97 us -> none  [per_device(): cot_mine = lax.dynamic_slice_in_dim(cot, core * half, half, 0)]
    ppermute x2, starting transfers between devices: 3.12 us -> 2.16 us  [below(): lax.ppermute(block, 'section', [(s, (s - 1) % sections) for s in range(se...]
    concatenate x2, other arithmetic: 0.05 us -> 1.01 us  [per_device(): blocks = jnp.concatenate(blocks, axis=0)]
    unnamed x32 -> x33, local copies, waits for them, and re-layouts: 4.41 us -> 5.12 us
  transfers between devices with their start and end apart: 20 -> 20, of which waited for: 8 -> 9; matrix products, arithmetic and copies ran while one was open for 8% -> 9% of each run, Pallas kernels for 33% -> 32%
where the time goes in v6:
time: 80.1 us; the launch traced here: 79.7 us
  Pallas kernels  26.9 us (34%)
  starting transfers between devices  21.8 us (27%)
  waiting for transfers between devices  18.7 us (23%)
  local copies, waits for them, and re-layouts  6.64 us (8%)
  other arithmetic  3.74 us (5%)
  between operations  1.06 us (1%)
  matrix products  0.82 us (1%)
    ppermute x18, starting transfers between devices, xored(): return lax.ppermute(block, axis, [(i, i ^ bits) for i in range(n)])  19.7 us
    pallas_call x2, Pallas kernels, expert(): pl.pallas_call(functools.partial(expert_kernel, tile_f, tile_d), grid=(1,...  18.7 us
    ppermute x18, waiting for transfers between devices, xored(): return lax.ppermute(block, axis, [(i, i ^ bits) for i in range(n)])  15.4 us
    pallas_call x1, Pallas kernels, slopes(): pl.pallas_call(functools.partial(slope_kernel, groups), grid_spec=pltpu.P...  6.27 us
    unnamed x33, local copies, waits for them, and re-layouts  5.12 us
    ppermute x2, waiting for transfers between devices, below(): lax.ppermute(block, 'section', [(s, (s - 1) % sections) for s in range(se...  3.29 us
    ppermute x2, starting transfers between devices, below(): lax.ppermute(block, 'section', [(s, (s - 1) % sections) for s in range(se...  2.16 us
    broadcast_in_dim x2, other arithmetic, per_device(): return (handed[None], features[None])  1.6 us
  transfers between devices with their start and end apart: 20, of which 9 were waited for; matrix products, arithmetic and copies ran while one was open for 9% of the time, Pallas kernels for 32%

profile of v6, /device:TPU:0, one launch (start us, length us, event | category | flops | bytes accessed | tf_op | source)
XLA Modules:
  0.0 79.7 jit_solution(16127437162221641939)
XLA Ops:
  0.6 1.1 %halves.1 = (bf16[64,2048]{1,0:T(8,128)(2,1)S(1)}, bf16[64,2048]{1,0:T(8,128)(2,1)S(1)}, bf16[32,2048]{1,0:T(8,128)(2,1)S(1)}) custom-call(s32[1]{0:T(128)} %bitcast.core_ref, bf16[128,2048]{1,0:T(8,128)(2,1)} %bitcast.50), custom_call_target="tpu_custom_call" | custom-call | tf_op jit(solution)/shard_map/halves/pallas_call | solution.py:37
  1.8 4.1 %collective-permute-start.1 = (bf16[32,2048]{1,0:T(8,128)(2,1)S(1)}, bf16[32,2048]{1,0:T(8,128)(2,1)S(1)}, u32[]{:S(2)}, u32[]{:S(2)}) collective-permute-start(bf16[32,2048]{1,0:T(8,128)(2,1)S(1)} %get-tuple-element.25), channel_id=1, source_target_pairs={{0,8},{4,12},{8,0},{12,4},{1,9},{5,13},{9,1},{13,5},{2,10},{6,14},... | collective-permute-start | bytes 393224 | tf_op jit(solution)/shard_map/ppermute | solution.py:17
  5.9 1.3 %collective-permute-start.2 = (bf16[32,2048]{1,0:T(8,128)(2,1)S(1)}, bf16[32,2048]{1,0:T(8,128)(2,1)S(1)}, u32[]{:S(2)}, u32[]{:S(2)}) collective-permute-start(bf16[32,2048]{1,0:T(8,128)(2,1)S(1)} %get-tuple-element.25), channel_id=1, source_target_pairs={{0,12},{4,8},{8,4},{12,0},{1,13},{5,9},{9,5},{13,1},{2,14},{6,10},... | collective-permute-start | bytes 393224 | tf_op jit(solution)/shard_map/ppermute | solution.py:17
  10.5 2.0 %copy-done.1 = bf16[1,1,4,128,3584]{4,3,2,1,0:T(8,128)(2,1)S(1)} copy-done((bf16[1,1,4,128,3584]{4,3,2,1,0:T(8,128)(2,1)S(1)}, bf16[1,1,4,128,3584]{4,3,2,1,0:T(8,128)(2,1)}, u32[]{:S(2)}) %copy-start.1) | copy-done | bytes 3670040
  12.6 1.0 %copy-done.2 = bf16[1,1,3584,64]{2,3,1,0:T(8,128)(2,1)S(1)} copy-done((bf16[1,1,3584,64]{2,3,1,0:T(8,128)(2,1)S(1)}, bf16[1,1,3584,64]{2,3,1,0:T(8,128)(2,1)}, u32[]{:S(2)}) %copy-start.2) | copy-done | bytes 458776
  13.6 6.3 %slopes.1 = (bf16[2,3584,256]{2,1,0:T(8,128)(2,1)S(1)}, f32[2,256,64]{2,1,0:T(8,128)S(1)}, bf16[3584,2048]{1,0:T(8,128)(2,1)S(1)}) custom-call(s32[2]{0:T(128)S(1)} %pad_add_fusion.index_ref, bf16[4,2,2,32,3584]{4,3,2,1,0:T(8,128)(2,1)S(1)} %bitcast.36, bf16[4,2,2,32,3584]{4,3,2,1,0:T(8,128)(2,1)S(1)} %bitcast.37, bf16[4,2,2,32,3584]{4,3,2,1,0:T(8,128)(2,1)S(1)} %bitcast.38, ...), custom_call_target="tpu_custom_call" | custom-call | flops 234881024 | bytes 7340032 | tf_op jit(solution)/shard_map/slopes/pallas_call | solution.py:175
  19.9 2.9 %collective-permute-start.5 = (bf16[32,2048]{1,0:T(8,128)(2,1)S(1)}, bf16[32,2048]{1,0:T(8,128)(2,1)S(1)}, u32[]{:S(2)}, u32[]{:S(2)}) collective-permute-start(bf16[32,2048]{1,0:T(8,128)(2,1)S(1)} %held.8), channel_id=1, source_target_pairs={{0,8},{4,12},{8,0},{12,4},{1,9},{5,13},{9,1},{13,5},{2,10},{6,14},... | collective-permute-start | bytes 393224 | tf_op jit(solution)/shard_map/ppermute | solution.py:17
  22.8 1.3 %collective-permute-start.4 = (bf16[32,2048]{1,0:T(8,128)(2,1)S(1)}, bf16[32,2048]{1,0:T(8,128)(2,1)S(1)}, u32[]{:S(2)}, u32[]{:S(2)}) collective-permute-start(bf16[32,2048]{1,0:T(8,128)(2,1)S(1)} %held.8), channel_id=1, source_target_pairs={{0,12},{4,8},{8,4},{12,0},{1,13},{5,9},{9,5},{13,1},{2,14},{6,10},... | collective-permute-start | bytes 393224 | tf_op jit(solution)/shard_map/ppermute | solution.py:17
  24.1 1.0 %pad_maximum_fusion = bf16[128,2048]{1,0:T(8,128)(2,1)S(1)} fusion(bf16[64,2048]{1,0:T(8,128)(2,1)} %collective-permute-done, bf16[32,2048]{1,0:T(8,128)(2,1)S(1)} %collective-permute-done.1.refs_1_, bf16[32,2048]{1,0:T(8,128)(2,1)S(1)} %collective-permute-done.2.refs_0_), kind=kLoop, calls=%fused_computation.2 | loop fusion | flops 1572864 | bytes 1048576 | tf_op jit(solution)/shard_map/concatenate | solution.py:347
  25.2 1.0 %slice_dynamic-update-slice_fusion.3 = (bf16[256,2048]{1,0:T(8,128)(2,1)S(1)}, bf16[256,2048]{1,0:T(8,128)(2,1)S(1)}) fusion(bf16[256,2048]{1,0:T(8,128)(2,1)S(1)} %get-tuple-element.50, bf16[64,2048]{1,0:T(8,128)(2,1)} %collective-permute-done, bf16[256,2048]{1,0:T(8,128)(2,1)S(1)} %get-tuple-element.51), kind=kLoop, calls=%fused_computation.12 | loop fusion | bytes 524288
  26.3 0.8 %collective-permute-done.3 = bf16[128,2048]{1,0:T(8,128)(2,1)S(1)} collective-permute-done((bf16[128,2048]{1,0:T(8,128)(2,1)S(1)}, bf16[128,2048]{1,0:T(8,128)(2,1)S(1)}, u32[]{:S(2)}, u32[]{:S(2)}) %collective-permute-start.3) | collective-permute-done | bytes 524320 | tf_op jit(solution)/shard_map/ppermute | solution.py:17
  27.2 9.4 %expert.2 = (f32[128,2176]{1,0:T(8,128)S(1)}, bf16[128,2176]{1,0:T(8,128)(2,1)S(1)}) custom-call(bf16[256,2048]{1,0:T(8,128)(2,1)S(1)} %slice_dynamic-update-slice_fusion.4.rows_ref, bf16[2,3584,256]{2,1,0:T(8,128)(2,1)S(1)} %get-tuple-element.27.slope_ref, f32[2,256,64]{2,1,0:T(8,128)S(1)} %get-tuple-element.28.down_part_ref, ...), custom_call_target="tpu_custom_call" | custom-call | flops 7516192768 | bytes 29360128 | tf_op jit(solution)/shard_map/expert/pallas_call | solution.py:263
  36.9 1.8 %collective-permute-done.6.came_ref = bf16[128,2176]{1,0:T(8,128)(2,1)S(1)} collective-permute-done((bf16[128,2176]{1,0:T(8,128)(2,1)S(1)}, bf16[128,2176]{1,0:T(8,128)(2,1)S(1)}, u32[]{:S(2)}, u32[]{:S(2)}) %collective-permute-start.6) | collective-permute-done | bytes 557088 | tf_op jit(solution)/shard_map/ppermute | solution.py:17
  39.1 2.6 %collective-permute-start.7 = (bf16[32,2176]{1,0:T(8,128)(2,1)S(1)}, bf16[32,2176]{1,0:T(8,128)(2,1)S(1)}, u32[]{:S(2)}, u32[]{:S(2)}) collective-permute-start(bf16[32,2176]{1,0:T(8,128)(2,1)S(1)} %get-tuple-element.33.refs_2_), channel_id=1, source_target_pairs={{0,12},{4,8},{8,4},{12,0},{1,13},{5,9},{9,5},{13,1},{2,14},{6,10},... | collective-permute-start | bytes 417800 | tf_op jit(solution)/shard_map/ppermute | solution.py:17
  41.6 1.9 %collective-permute-start.9 = (bf16[32,2176]{1,0:T(8,128)(2,1)S(1)}, bf16[32,2176]{1,0:T(8,128)(2,1)S(1)}, u32[]{:S(2)}, u32[]{:S(2)}) collective-permute-start(bf16[32,2176]{1,0:T(8,128)(2,1)S(1)} %get-tuple-element.35.refs_0_), channel_id=1, source_target_pairs={{0,4},{4,0},{8,12},{12,8},{1,5},{5,1},{9,13},{13,9},{2,6},{6,2},{1... | collective-permute-start | bytes 417800 | tf_op jit(solution)/shard_map/ppermute | solution.py:17
  43.6 9.4 %expert.3 = (f32[128,2176]{1,0:T(8,128)S(1)}, bf16[128,2176]{1,0:T(8,128)(2,1)S(1)}) custom-call(bf16[256,2048]{1,0:T(8,128)(2,1)S(1)} %slice_dynamic-update-slice_fusion.rows_ref, bf16[2,3584,256]{2,1,0:T(8,128)(2,1)S(1)} %get-tuple-element.27.slope_ref, f32[2,256,64]{2,1,0:T(8,128)S(1)} %get-tuple-element.28.down_part_ref, bf16[64,3584]{1,0:T(8,128)(2,1)S(1)} %bitcast.46, ...), custom_call_target="tpu_custom_call" | custom-call | flops 7516192768 | bytes 29360128 | tf_op jit(solution)/shard_map/expert/pallas_call | solution.py:263
  53.9 1.3 %collective-permute-done.11.came_ref = bf16[128,2176]{1,0:T(8,128)(2,1)S(1)} collective-permute-done((bf16[128,2176]{1,0:T(8,128)(2,1)S(1)}, bf16[128,2176]{1,0:T(8,128)(2,1)S(1)}, u32[]{:S(2)}, u32[]{:S(2)}) %collective-permute-start.11) | collective-permute-done | bytes 557088 | tf_op jit(solution)/shard_map/ppermute | solution.py:17
  55.3 1.6 %collective-permute-start.12 = (bf16[32,2048]{1,0:T(8,128)(2,1)S(1)}, bf16[32,2048]{1,0:T(8,128)(2,1)S(1)}, u32[]{:S(2)}, u32[]{:S(2)}) collective-permute-start(bf16[32,2048]{1,0:T(8,128)(2,1)S(1)} %held.14), channel_id=1, source_target_pairs={{0,2},{2,0},{1,3},{3,1},{4,6},{6,4},{5,7},{7,5},{8,10},{10,8},{9,1... | collective-permute-start | bytes 393224 | tf_op jit(solution)/shard_map/ppermute | solution.py:325
  56.9 2.6 %collective-permute-start.13 = (bf16[32,2176]{1,0:T(8,128)(2,1)S(1)}, bf16[32,2176]{1,0:T(8,128)(2,1)S(1)}, u32[]{:S(2)}, u32[]{:S(2)}) collective-permute-start(bf16[32,2176]{1,0:T(8,128)(2,1)S(1)} %get-tuple-element.40), channel_id=1, source_target_pairs={{0,12},{4,8},{8,4},{12,0},{1,13},{5,9},{9,5},{13,1},{2,14},{6,10},... | collective-permute-start | bytes 417800 | tf_op jit(solution)/shard_map/ppermute | solution.py:17
  59.5 1.7 %collective-permute-start.15 = (bf16[32,2176]{1,0:T(8,128)(2,1)S(1)}, bf16[32,2176]{1,0:T(8,128)(2,1)S(1)}, u32[]{:S(2)}, u32[]{:S(2)}) collective-permute-start(bf16[32,2176]{1,0:T(8,128)(2,1)S(1)} %get-tuple-element.42), channel_id=1, source_target_pairs={{0,4},{4,0},{8,12},{12,8},{1,5},{5,1},{9,13},{13,9},{2,6},{6,2},{1... | collective-permute-start | bytes 417800 | tf_op jit(solution)/shard_map/ppermute | solution.py:17
  61.4 3.9 %collective-permute-done.13.refs_0_ = bf16[32,2176]{1,0:T(8,128)(2,1)S(1)} collective-permute-done((bf16[32,2176]{1,0:T(8,128)(2,1)S(1)}, bf16[32,2176]{1,0:T(8,128)(2,1)S(1)}, u32[]{:S(2)}, u32[]{:S(2)}) %collective-permute-start.13) | collective-permute-done | bytes 139296 | tf_op jit(solution)/shard_map/ppermute | solution.py:17
  65.3 5.9 %collective-permute-done.14.refs_1_ = bf16[32,2176]{1,0:T(8,128)(2,1)S(1)} collective-permute-done((bf16[32,2176]{1,0:T(8,128)(2,1)S(1)}, bf16[32,2176]{1,0:T(8,128)(2,1)S(1)}, u32[]{:S(2)}, u32[]{:S(2)}) %collective-permute-start.14) | collective-permute-done | bytes 139296 | tf_op jit(solution)/shard_map/ppermute | solution.py:17
  74.2 3.3 %collective-permute-done.16 = bf16[32,2048]{1,0:T(8,128)(2,1)S(1)} collective-permute-done((bf16[32,2048]{1,0:T(8,128)(2,1)S(1)}, bf16[32,2048]{1,0:T(8,128)(2,1)S(1)}, u32[]{:S(2)}, u32[]{:S(2)}) %collective-permute-start.16) | collective-permute-done | bytes 131104 | tf_op jit(solution)/shard_map/ppermute | solution.py:325
  77.5 1.3 %collective-permute-done.18 = bf16[32,2048]{1,0:T(8,128)(2,1)S(1)} collective-permute-done((bf16[32,2048]{1,0:T(8,128)(2,1)S(1)}, bf16[32,2048]{1,0:T(8,128)(2,1)S(1)}, u32[]{:S(2)}, u32[]{:S(2)}) %collective-permute-start.18) | collective-permute-done | bytes 131104 | tf_op jit(solution)/shard_map/ppermute | solution.py:17
  (89 shorter events, 9.1 us)
Async XLA Ops:
  0.6 52.7 %copy-start = (bf16[1,2048,64]{1,2,0:T(8,128)(2,1)S(1)}, bf16[1,2048,64]{1,2,0:T(8,128)(2,1)}, u32[]{:S(2)}) copy-start(bf16[1,2048,64]{1,2,0:T(8,128)(2,1)} %param.17) | copy-start | bytes 786436
  1.8 18.1 %collective-permute-start.1 = (bf16[32,2048]{1,0:T(8,128)(2,1)S(1)}, bf16[32,2048]{1,0:T(8,128)(2,1)S(1)}, u32[]{:S(2)}, u32[]{:S(2)}) collective-permute-start(bf16[32,2048]{1,0:T(8,128)(2,1)S(1)} %get-tuple-element.25), channel_id=1, source_target_pairs={{0,8},{4,12},{8,0},{12,4},{1,9},{5,13},{9,1},{13,5},{2,10},{6,14},... | collective-permute-start | bytes 393224 | tf_op jit(solution)/shard_map/ppermute | solution.py:17
  5.9 14.0 %collective-permute-start.2 = (bf16[32,2048]{1,0:T(8,128)(2,1)S(1)}, bf16[32,2048]{1,0:T(8,128)(2,1)S(1)}, u32[]{:S(2)}, u32[]{:S(2)}) collective-permute-start(bf16[32,2048]{1,0:T(8,128)(2,1)S(1)} %get-tuple-element.25), channel_id=1, source_target_pairs={{0,12},{4,8},{8,4},{12,0},{1,13},{5,9},{9,5},{13,1},{2,14},{6,10},... | collective-permute-start | bytes 393224 | tf_op jit(solution)/shard_map/ppermute | solution.py:17
  7.2 16.9 %collective-permute-start = (bf16[64,2048]{1,0:T(8,128)(2,1)S(1)}, bf16[64,2048]{1,0:T(8,128)(2,1)}, u32[]{:S(2)}, u32[]{:S(2)}) collective-permute-start(bf16[64,2048]{1,0:T(8,128)(2,1)S(1)} %get-tuple-element.24), channel_id=1, source_target_pairs={{0,4},{4,0},{8,12},{12,8},{1,5},{5,1},{9,13},{13,9},{2,6},{6,2},{1... | collective-permute-start | bytes 786440 | tf_op jit(solution)/shard_map/ppermute | solution.py:17
  19.9 16.6 %collective-permute-start.5 = (bf16[32,2048]{1,0:T(8,128)(2,1)S(1)}, bf16[32,2048]{1,0:T(8,128)(2,1)S(1)}, u32[]{:S(2)}, u32[]{:S(2)}) collective-permute-start(bf16[32,2048]{1,0:T(8,128)(2,1)S(1)} %held.8), channel_id=1, source_target_pairs={{0,8},{4,12},{8,0},{12,4},{1,9},{5,13},{9,1},{13,5},{2,10},{6,14},... | collective-permute-start | bytes 393224 | tf_op jit(solution)/shard_map/ppermute | solution.py:17
  22.8 13.8 %collective-permute-start.4 = (bf16[32,2048]{1,0:T(8,128)(2,1)S(1)}, bf16[32,2048]{1,0:T(8,128)(2,1)S(1)}, u32[]{:S(2)}, u32[]{:S(2)}) collective-permute-start(bf16[32,2048]{1,0:T(8,128)(2,1)S(1)} %held.8), channel_id=1, source_target_pairs={{0,12},{4,8},{8,4},{12,0},{1,13},{5,9},{9,5},{13,1},{2,14},{6,10},... | collective-permute-start | bytes 393224 | tf_op jit(solution)/shard_map/ppermute | solution.py:17
  25.1 2.0 %collective-permute-start.3 = (bf16[128,2048]{1,0:T(8,128)(2,1)S(1)}, bf16[128,2048]{1,0:T(8,128)(2,1)S(1)}, u32[]{:S(2)}, u32[]{:S(2)}) collective-permute-start(bf16[128,2048]{1,0:T(8,128)(2,1)S(1)} %pad_maximum_fusion), channel_id=1, source_target_pairs={{0,1},{1,0},{2,3},{3,2},{4,5},{5,4},{6,7},{7,6},{8,9},{9,8},{10,11... | collective-permute-start | bytes 1572872 | tf_op jit(solution)/shard_map/ppermute | solution.py:17
  36.7 2.0 %collective-permute-start.6 = (bf16[128,2176]{1,0:T(8,128)(2,1)S(1)}, bf16[128,2176]{1,0:T(8,128)(2,1)S(1)}, u32[]{:S(2)}, u32[]{:S(2)}) collective-permute-start(bf16[128,2176]{1,0:T(8,128)(2,1)S(1)} %held.11), channel_id=1, source_target_pairs={{0,1},{1,0},{2,3},{3,2},{4,5},{5,4},{6,7},{7,6},{8,9},{9,8},{10,11... | collective-permute-start | bytes 1671176 | tf_op jit(solution)/shard_map/ppermute | solution.py:17
  38.8 4.7 %collective-permute-start.10 = (bf16[64,2048]{1,0:T(8,128)(2,1)S(1)}, bf16[64,2048]{1,0:T(8,128)(2,1)S(1)}, u32[]{:S(2)}, u32[]{:S(2)}) collective-permute-start(bf16[64,2048]{1,0:T(8,128)(2,1)S(1)} %held.12), channel_id=1, source_target_pairs={{0,1},{1,0},{2,3},{3,2},{4,5},{5,4},{6,7},{7,6},{8,9},{9,8},{10,11... | collective-permute-start | bytes 786440 | tf_op jit(solution)/shard_map/ppermute | solution.py:17
  39.1 13.9 %collective-permute-start.7 = (bf16[32,2176]{1,0:T(8,128)(2,1)S(1)}, bf16[32,2176]{1,0:T(8,128)(2,1)S(1)}, u32[]{:S(2)}, u32[]{:S(2)}) collective-permute-start(bf16[32,2176]{1,0:T(8,128)(2,1)S(1)} %get-tuple-element.33.refs_2_), channel_id=1, source_target_pairs={{0,12},{4,8},{8,4},{12,0},{1,13},{5,9},{9,5},{13,1},{2,14},{6,10},... | collective-permute-start | bytes 417800 | tf_op jit(solution)/shard_map/ppermute | solution.py:17
  41.6 11.5 %collective-permute-start.8 = (bf16[32,2176]{1,0:T(8,128)(2,1)S(1)}, bf16[32,2176]{1,0:T(8,128)(2,1)S(1)}, u32[]{:S(2)}, u32[]{:S(2)}) collective-permute-start(bf16[32,2176]{1,0:T(8,128)(2,1)S(1)} %get-tuple-element.34.refs_1_), channel_id=1, source_target_pairs={{0,8},{4,12},{8,0},{12,4},{1,9},{5,13},{9,1},{13,5},{2,10},{6,14},... | collective-permute-start | bytes 417800 | tf_op jit(solution)/shard_map/ppermute | solution.py:17
  41.6 11.5 %collective-permute-start.9 = (bf16[32,2176]{1,0:T(8,128)(2,1)S(1)}, bf16[32,2176]{1,0:T(8,128)(2,1)S(1)}, u32[]{:S(2)}, u32[]{:S(2)}) collective-permute-start(bf16[32,2176]{1,0:T(8,128)(2,1)S(1)} %get-tuple-element.35.refs_0_), channel_id=1, source_target_pairs={{0,4},{4,0},{8,12},{12,8},{1,5},{5,1},{9,13},{13,9},{2,6},{6,2},{1... | collective-permute-start | bytes 417800 | tf_op jit(solution)/shard_map/ppermute | solution.py:17
  43.6 9.7 %copy-start.7 = (s32[1,1,4]{2,1,0:T(1,128)S(1)}, s32[1,1,4]{2,1,0:T(1,128)}, u32[]{:S(2)}) copy-start(s32[1,1,4]{2,1,0:T(1,128)} %param.19) | copy-start | bytes 52
  43.6 9.8 %copy-start.4 = (bf16[1,128,2048]{2,1,0:T(8,128)(2,1)S(1)}, bf16[1,128,2048]{2,1,0:T(8,128)(2,1)}, u32[]{:S(2)}) copy-start(bf16[1,128,2048]{2,1,0:T(8,128)(2,1)} %param.10) | copy-start | bytes 1572868
  53.1 19.8 %copy-start.5 = (f32[1,128,64]{1,2,0:T(8,128)S(1)}, f32[1,128,64]{1,2,0:T(8,128)}, u32[]{:S(2)}) copy-start(f32[1,128,64]{1,2,0:T(8,128)} %param.16) | copy-start | bytes 98308
  53.1 2.0 %collective-permute-start.11 = (bf16[128,2176]{1,0:T(8,128)(2,1)S(1)}, bf16[128,2176]{1,0:T(8,128)(2,1)S(1)}, u32[]{:S(2)}, u32[]{:S(2)}) collective-permute-start(bf16[128,2176]{1,0:T(8,128)(2,1)S(1)} %held.13), channel_id=1, source_target_pairs={{0,1},{1,0},{2,3},{3,2},{4,5},{5,4},{6,7},{7,6},{8,9},{9,8},{10,11... | collective-permute-start | bytes 1671176 | tf_op jit(solution)/shard_map/ppermute | solution.py:17
  55.3 6.1 %collective-permute-start.12 = (bf16[32,2048]{1,0:T(8,128)(2,1)S(1)}, bf16[32,2048]{1,0:T(8,128)(2,1)S(1)}, u32[]{:S(2)}, u32[]{:S(2)}) collective-permute-start(bf16[32,2048]{1,0:T(8,128)(2,1)S(1)} %held.14), channel_id=1, source_target_pairs={{0,2},{2,0},{1,3},{3,1},{4,6},{6,4},{5,7},{7,5},{8,10},{10,8},{9,1... | collective-permute-start | bytes 393224 | tf_op jit(solution)/shard_map/ppermute | solution.py:325
  56.9 8.4 %collective-permute-start.13 = (bf16[32,2176]{1,0:T(8,128)(2,1)S(1)}, bf16[32,2176]{1,0:T(8,128)(2,1)S(1)}, u32[]{:S(2)}, u32[]{:S(2)}) collective-permute-start(bf16[32,2176]{1,0:T(8,128)(2,1)S(1)} %get-tuple-element.40), channel_id=1, source_target_pairs={{0,12},{4,8},{8,4},{12,0},{1,13},{5,9},{9,5},{13,1},{2,14},{6,10},... | collective-permute-start | bytes 417800 | tf_op jit(solution)/shard_map/ppermute | solution.py:17
  59.5 11.7 %collective-permute-start.14 = (bf16[32,2176]{1,0:T(8,128)(2,1)S(1)}, bf16[32,2176]{1,0:T(8,128)(2,1)S(1)}, u32[]{:S(2)}, u32[]{:S(2)}) collective-permute-start(bf16[32,2176]{1,0:T(8,128)(2,1)S(1)} %get-tuple-element.41), channel_id=1, source_target_pairs={{0,8},{4,12},{8,0},{12,4},{1,9},{5,13},{9,1},{13,5},{2,10},{6,14},... | collective-permute-start | bytes 417800 | tf_op jit(solution)/shard_map/ppermute | solution.py:17
  59.5 11.7 %collective-permute-start.15 = (bf16[32,2176]{1,0:T(8,128)(2,1)S(1)}, bf16[32,2176]{1,0:T(8,128)(2,1)S(1)}, u32[]{:S(2)}, u32[]{:S(2)}) collective-permute-start(bf16[32,2176]{1,0:T(8,128)(2,1)S(1)} %get-tuple-element.42), channel_id=1, source_target_pairs={{0,4},{4,0},{8,12},{12,8},{1,5},{5,1},{9,13},{13,9},{2,6},{6,2},{1... | collective-permute-start | bytes 417800 | tf_op jit(solution)/shard_map/ppermute | solution.py:17
  71.4 1.3 %collective-permute-start.19 = (f32[64,128]{1,0:T(8,128)S(1)}, f32[64,128]{1,0:T(8,128)S(1)}, u32[]{:S(2)}, u32[]{:S(2)}) collective-permute-start(f32[64,128]{1,0:T(8,128)S(1)} %constant_dynamic-update-slice_fusion.10), channel_id=1, source_target_pairs={{0,1},{1,0},{2,3},{3,2},{4,5},{5,4},{6,7},{7,6},{8,9},{9,8},{10,11... | collective-permute-start | bytes 98312 | tf_op jit(solution)/shard_map/ppermute | solution.py:17
  71.5 6.0 %collective-permute-start.16 = (bf16[32,2048]{1,0:T(8,128)(2,1)S(1)}, bf16[32,2048]{1,0:T(8,128)(2,1)S(1)}, u32[]{:S(2)}, u32[]{:S(2)}) collective-permute-start(bf16[32,2048]{1,0:T(8,128)(2,1)S(1)} %get-tuple-element.43.refs_0_), channel_id=1, source_target_pairs={{0,2},{2,0},{1,3},{3,1},{4,6},{6,4},{5,7},{7,5},{8,10},{10,8},{9,1... | collective-permute-start | bytes 393224 | tf_op jit(solution)/shard_map/ppermute | solution.py:325
  72.1 2.0 %collective-permute-start.17 = (bf16[32,2048]{1,0:T(8,128)(2,1)S(1)}, bf16[32,2048]{1,0:T(8,128)(2,1)S(1)}, u32[]{:S(2)}, u32[]{:S(2)}) collective-permute-start(bf16[32,2048]{1,0:T(8,128)(2,1)S(1)} %held.15), channel_id=1, source_target_pairs={{0,1},{1,0},{2,3},{3,2},{4,5},{5,4},{6,7},{7,6},{8,9},{9,8},{10,11... | collective-permute-start | bytes 393224 | tf_op jit(solution)/shard_map/ppermute | solution.py:17
  77.5 1.3 %collective-permute-start.18 = (bf16[32,2048]{1,0:T(8,128)(2,1)S(1)}, bf16[32,2048]{1,0:T(8,128)(2,1)S(1)}, u32[]{:S(2)}, u32[]{:S(2)}) collective-permute-start(bf16[32,2048]{1,0:T(8,128)(2,1)S(1)} %collective-permute-done.16), channel_id=1, source_target_pairs={{0,1},{1,0},{2,3},{3,2},{4,5},{5,4},{6,7},{7,6},{8,9},{9,8},{10,11... | collective-permute-start | bytes 393224 | tf_op jit(solution)/shard_map/ppermute | solution.py:17
  (4 other events, 18.7 us)

commit v7 on v5

--- a/solution.py
+++ b/solution.py
@@ -67,7 +67,8 @@
     width = grad_ref.shape[1]
     total = weight_ref[:, :1] * own_ref[...]
     for slot in range(1, slots):
-        total += weight_ref[:, slot : slot + 1] * refs[slot - 1][...].astype(jnp.float32)
+        back = refs[slots - 1 - slot][...].astype(jnp.float32)
+        total += weight_ref[:, slot : slot + 1] * back
     grad_ref[...] = (cot_ref[...].astype(jnp.float32) + total[:, :width]).astype(jnp.bfloat16)
     vec_ref[...] = total[:, width:]
 
@@ -341,7 +342,7 @@
         else:
             give = held(give, *backs)
         own, *sent = merged(kept, xored(give, "tensor", 1), rows)
-        backs = [xored(out, "dp", slot + 1) for slot, out in enumerate(sent)]
+        backs = [xored(out, "dp", slot + 1) for slot, out in enumerate(sent)][::-1]
         if grad:
             passed = (below(held(*grad, backs[0])),)
             below_mine.append(*passed)

time: 77.3 us -> 76.1 us (0.984)
  starting transfers between devices: 23.2 us -> 22.2 us
    ppermute x18, starting transfers between devices: 20.1 us -> 19.1 us  [xored(): return lax.ppermute(block, axis, [(i, i ^ bits) for i in range(n)])]
  transfers between devices with their start and end apart: 20 -> 20, of which waited for: 8 -> 10; matrix products, arithmetic and copies ran while one was open for 8% -> 8% of each run, Pallas kernels for 33% -> 33%
where the time goes in v7:
time: 76.1 us; the launch traced here: 75.6 us
  Pallas kernels  25.8 us (34%)
  starting transfers between devices  22.2 us (29%)
  waiting for transfers between devices  15.6 us (20%)
  local copies, waits for them, and re-layouts  6.31 us (8%)
  matrix products  2.64 us (3%)
  other arithmetic  2.13 us (3%)
  between operations  1.03 us (1%)
    ppermute x18, starting transfers between devices, xored(): return lax.ppermute(block, axis, [(i, i ^ bits) for i in range(n)])  19.1 us
    pallas_call x2, Pallas kernels, expert(): pl.pallas_call(functools.partial(expert_kernel, tile_f, tile_d), grid=(1,...  18.8 us
    ppermute x18, waiting for transfers between devices, xored(): return lax.ppermute(block, axis, [(i, i ^ bits) for i in range(n)])  15.3 us
    pallas_call x1, Pallas kernels, slopes(): pl.pallas_call(functools.partial(slope_kernel, groups), grid_spec=pltpu.P...  6.27 us
    unnamed x32, local copies, waits for them, and re-layouts  4.41 us
    ppermute x2, starting transfers between devices, below(): lax.ppermute(block, 'section', [(s, (s - 1) % sections) for s in range(se...  3.11 us
    broadcast_in_dim x2, other arithmetic, per_device(): return (handed[None], features[None])  1.6 us
  transfers between devices with their start and end apart: 20, of which 10 were waited for; matrix products, arithmetic and copies ran while one was open for 8% of the time, Pallas kernels for 33%

profile of v7, /device:TPU:0, one launch (start us, length us, event | category | flops | bytes accessed | tf_op | source)
XLA Modules:
  0.0 75.6 jit_solution(12869768187340948171)
XLA Ops:
  0.7 1.0 %constant_dynamic-update-slice_fusion.2 = (bf16[256,2048]{1,0:T(8,128)(2,1)S(1)}, bf16[32,2048]{1,0:T(8,128)(2,1)S(1)}) fusion(bf16[1,128,2048]{2,1,0:T(8,128)(2,1)} %param.10, s32[]{:T(128)S(6)} %select_n.45), kind=kLoop, calls=%fused_computation.40 | loop fusion | bytes 393220
  1.6 4.1 %collective-permute-start.1 = (bf16[32,2048]{1,0:T(8,128)(2,1)S(1)}, bf16[32,2048]{1,0:T(8,128)(2,1)S(1)}, u32[]{:S(2)}, u32[]{:S(2)}) collective-permute-start(bf16[32,2048]{1,0:T(8,128)(2,1)S(1)} %get-tuple-element.43.cot_ref), channel_id=1, source_target_pairs={{0,8},{4,12},{8,0},{12,4},{1,9},{5,13},{9,1},{13,5},{2,10},{6,14},... | collective-permute-start | bytes 393224 | tf_op jit(solution)/shard_map/ppermute | solution.py:17
  5.7 1.3 %collective-permute-start.2 = (bf16[32,2048]{1,0:T(8,128)(2,1)S(1)}, bf16[32,2048]{1,0:T(8,128)(2,1)S(1)}, u32[]{:S(2)}, u32[]{:S(2)}) collective-permute-start(bf16[32,2048]{1,0:T(8,128)(2,1)S(1)} %get-tuple-element.43.cot_ref), channel_id=1, source_target_pairs={{0,12},{4,8},{8,4},{12,0},{1,13},{5,9},{9,5},{13,1},{2,14},{6,10},... | collective-permute-start | bytes 393224 | tf_op jit(solution)/shard_map/ppermute | solution.py:17
  7.1 1.0 %dynamic-slice_bitcast_fusion = bf16[64,2048]{1,0:T(8,128)(2,1)S(1)} fusion(bf16[1,128,2048]{2,1,0:T(8,128)(2,1)} %param.10, s32[]{:T(128)S(6)} %select_n.45), kind=kLoop, calls=%fused_computation.8 | loop fusion | bytes 524292 | tf_op jit(solution)/shard_map/dynamic_slice | solution.py:310
  9.2 2.0 %copy-done.1 = bf16[1,1,4,128,3584]{4,3,2,1,0:T(8,128)(2,1)S(1)} copy-done((bf16[1,1,4,128,3584]{4,3,2,1,0:T(8,128)(2,1)S(1)}, bf16[1,1,4,128,3584]{4,3,2,1,0:T(8,128)(2,1)}, u32[]{:S(2)}) %copy-start.1) | copy-done | bytes 3670040
  11.2 1.0 %copy-done.2 = bf16[1,1,3584,64]{2,3,1,0:T(8,128)(2,1)S(1)} copy-done((bf16[1,1,3584,64]{2,3,1,0:T(8,128)(2,1)S(1)}, bf16[1,1,3584,64]{2,3,1,0:T(8,128)(2,1)}, u32[]{:S(2)}) %copy-start.2) | copy-done | bytes 458776
  12.2 6.3 %slopes.1 = (bf16[2,3584,256]{2,1,0:T(8,128)(2,1)S(1)}, f32[2,256,64]{2,1,0:T(8,128)S(1)}, bf16[3584,2048]{1,0:T(8,128)(2,1)S(1)}) custom-call(s32[2]{0:T(128)S(1)} %pad_add_fusion.index_ref, bf16[4,2,2,32,3584]{4,3,2,1,0:T(8,128)(2,1)S(1)} %bitcast.52, bf16[4,2,2,32,3584]{4,3,2,1,0:T(8,128)(2,1)S(1)} %bitcast.53, bf16[4,2,2,32,3584]{4,3,2,1,0:T(8,128)(2,1)S(1)} %bitcast.54, ...), custom_call_target="tpu_custom_call" | custom-call | flops 234881024 | bytes 7340032 | tf_op jit(solution)/shard_map/slopes/pallas_call | solution.py:148
  18.6 1.3 %collective-permute-done.refs_0_ = bf16[64,2048]{1,0:T(8,128)(2,1)S(1)} collective-permute-done((bf16[64,2048]{1,0:T(8,128)(2,1)S(1)}, bf16[64,2048]{1,0:T(8,128)(2,1)S(1)}, u32[]{:S(2)}, u32[]{:S(2)}) %collective-permute-start) | collective-permute-done | bytes 262176 | tf_op jit(solution)/shard_map/ppermute | solution.py:17
  20.2 3.3 %collective-permute-start.4 = (bf16[32,2048]{1,0:T(8,128)(2,1)S(1)}, bf16[32,2048]{1,0:T(8,128)(2,1)S(1)}, u32[]{:S(2)}, u32[]{:S(2)}) collective-permute-start(bf16[32,2048]{1,0:T(8,128)(2,1)S(1)} %held.7), channel_id=1, source_target_pairs={{0,12},{4,8},{8,4},{12,0},{1,13},{5,9},{9,5},{13,1},{2,14},{6,10},... | collective-permute-start | bytes 393224 | tf_op jit(solution)/shard_map/ppermute | solution.py:17
  23.6 9.4 %expert.2 = (f32[128,2176]{1,0:T(8,128)S(1)}, bf16[128,2176]{1,0:T(8,128)(2,1)S(1)}) custom-call(bf16[256,2048]{1,0:T(8,128)(2,1)S(1)} %slice_dynamic-update-slice_fusion.4.rows_ref, bf16[2,3584,256]{2,1,0:T(8,128)(2,1)S(1)} %get-tuple-element.21.slope_ref, f32[2,256,64]{2,1,0:T(8,128)S(1)} %get-tuple-element.22.down_part_ref, ...), custom_call_target="tpu_custom_call" | custom-call | flops 7516192768 | bytes 29360128 | tf_op jit(solution)/shard_map/expert/pallas_call | solution.py:236
  33.1 1.4 %collective-permute-done.5.block_ref = bf16[32,2048]{1,0:T(8,128)(2,1)S(1)} collective-permute-done((bf16[32,2048]{1,0:T(8,128)(2,1)S(1)}, bf16[32,2048]{1,0:T(8,128)(2,1)S(1)}, u32[]{:S(2)}, u32[]{:S(2)}) %collective-permute-start.5) | collective-permute-done | bytes 131104 | tf_op jit(solution)/shard_map/ppermute | solution.py:17
  34.7 1.9 %collective-permute-done.6.came_ref = bf16[128,2176]{1,0:T(8,128)(2,1)S(1)} collective-permute-done((bf16[128,2176]{1,0:T(8,128)(2,1)S(1)}, bf16[128,2176]{1,0:T(8,128)(2,1)S(1)}, u32[]{:S(2)}, u32[]{:S(2)}) %collective-permute-start.6) | collective-permute-done | bytes 557088 | tf_op jit(solution)/shard_map/ppermute | solution.py:17
  36.9 2.6 %collective-permute-start.7 = (bf16[32,2176]{1,0:T(8,128)(2,1)S(1)}, bf16[32,2176]{1,0:T(8,128)(2,1)S(1)}, u32[]{:S(2)}, u32[]{:S(2)}) collective-permute-start(bf16[32,2176]{1,0:T(8,128)(2,1)S(1)} %get-tuple-element.27.refs_2_), channel_id=1, source_target_pairs={{0,12},{4,8},{8,4},{12,0},{1,13},{5,9},{9,5},{13,1},{2,14},{6,10},... | collective-permute-start | bytes 417800 | tf_op jit(solution)/shard_map/ppermute | solution.py:17
  39.5 1.9 %collective-permute-start.9 = (bf16[32,2176]{1,0:T(8,128)(2,1)S(1)}, bf16[32,2176]{1,0:T(8,128)(2,1)S(1)}, u32[]{:S(2)}, u32[]{:S(2)}) collective-permute-start(bf16[32,2176]{1,0:T(8,128)(2,1)S(1)} %get-tuple-element.29.refs_0_), channel_id=1, source_target_pairs={{0,4},{4,0},{8,12},{12,8},{1,5},{5,1},{9,13},{13,9},{2,6},{6,2},{1... | collective-permute-start | bytes 417800 | tf_op jit(solution)/shard_map/ppermute | solution.py:17
  41.4 9.4 %expert.3 = (f32[128,2176]{1,0:T(8,128)S(1)}, bf16[128,2176]{1,0:T(8,128)(2,1)S(1)}) custom-call(bf16[256,2048]{1,0:T(8,128)(2,1)S(1)} %slice_dynamic-update-slice_fusion.rows_ref, bf16[2,3584,256]{2,1,0:T(8,128)(2,1)S(1)} %get-tuple-element.21.slope_ref, f32[2,256,64]{2,1,0:T(8,128)S(1)} %get-tuple-element.22.down_part_ref, bf16[64,3584]{1,0:T(8,128)(2,1)S(1)} %bitcast.62, ...), custom_call_target="tpu_custom_call" | custom-call | flops 7516192768 | bytes 29360128 | tf_op jit(solution)/shard_map/expert/pallas_call | solution.py:236
  52.1 1.3 %fusion = f32[128,64]{0,1:T(8,128)S(1)} fusion(bf16[1,128,2048]{2,1,0:T(8,128)(2,1)} %param.10, bf16[1,2048,64]{1,2,0:T(8,128)(2,1)S(1)} %copy-done), kind=kOutput, calls=%fused_computation.4 | convolution fusion | flops 33554432 | bytes 819200 | tf_op jit(solution)/shard_map/dot_general | solution.py:366
  53.8 2.7 %collective-permute-start.12 = (bf16[32,2176]{1,0:T(8,128)(2,1)S(1)}, bf16[32,2176]{1,0:T(8,128)(2,1)S(1)}, u32[]{:S(2)}, u32[]{:S(2)}) collective-permute-start(bf16[32,2176]{1,0:T(8,128)(2,1)S(1)} %get-tuple-element.33), channel_id=1, source_target_pairs={{0,12},{4,8},{8,4},{12,0},{1,13},{5,9},{9,5},{13,1},{2,14},{6,10},... | collective-permute-start | bytes 417800 | tf_op jit(solution)/shard_map/ppermute | solution.py:17
  56.8 1.7 %collective-permute-start.15 = (bf16[32,2176]{1,0:T(8,128)(2,1)S(1)}, bf16[32,2176]{1,0:T(8,128)(2,1)S(1)}, u32[]{:S(2)}, u32[]{:S(2)}) collective-permute-start(bf16[32,2176]{1,0:T(8,128)(2,1)S(1)} %get-tuple-element.36), channel_id=1, source_target_pairs={{0,4},{4,0},{8,12},{12,8},{1,5},{5,1},{9,13},{13,9},{2,6},{6,2},{1... | collective-permute-start | bytes 417800 | tf_op jit(solution)/shard_map/ppermute | solution.py:17
  58.5 3.8 %collective-permute-done.12.refs_0_ = bf16[32,2176]{1,0:T(8,128)(2,1)S(1)} collective-permute-done((bf16[32,2176]{1,0:T(8,128)(2,1)S(1)}, bf16[32,2176]{1,0:T(8,128)(2,1)S(1)}, u32[]{:S(2)}, u32[]{:S(2)}) %collective-permute-start.12) | collective-permute-done | bytes 139296 | tf_op jit(solution)/shard_map/ppermute | solution.py:17
  62.3 1.6 %collective-permute-start.13 = (bf16[32,2048]{1,0:T(8,128)(2,1)S(1)}, bf16[32,2048]{1,0:T(8,128)(2,1)S(1)}, u32[]{:S(2)}, u32[]{:S(2)}) collective-permute-start(bf16[32,2048]{1,0:T(8,128)(2,1)S(1)} %held.13), channel_id=1, source_target_pairs={{0,2},{2,0},{1,3},{3,1},{4,6},{6,4},{5,7},{7,5},{8,10},{10,8},{9,1... | collective-permute-start | bytes 393224 | tf_op jit(solution)/shard_map/ppermute | solution.py:298
  64.0 3.8 %collective-permute-done.14.refs_1_ = bf16[32,2176]{1,0:T(8,128)(2,1)S(1)} collective-permute-done((bf16[32,2176]{1,0:T(8,128)(2,1)S(1)}, bf16[32,2176]{1,0:T(8,128)(2,1)S(1)}, u32[]{:S(2)}, u32[]{:S(2)}) %collective-permute-start.14) | collective-permute-done | bytes 139296 | tf_op jit(solution)/shard_map/ppermute | solution.py:17
  68.1 1.6 %collective-permute-start.16 = (bf16[32,2048]{1,0:T(8,128)(2,1)S(1)}, bf16[32,2048]{1,0:T(8,128)(2,1)S(1)}, u32[]{:S(2)}, u32[]{:S(2)}) collective-permute-start(bf16[32,2048]{1,0:T(8,128)(2,1)S(1)} %get-tuple-element.37), channel_id=1, source_target_pairs={{0,2},{2,0},{1,3},{3,1},{4,6},{6,4},{5,7},{7,5},{8,10},{10,8},{9,1... | collective-permute-start | bytes 393224 | tf_op jit(solution)/shard_map/ppermute | solution.py:298
  71.0 1.0 %convolution_bitcast_fusion = f32[4,64,64]{2,1,0:T(8,128)S(1)} fusion(f32[128,64]{0,1:T(8,128)S(1)} %copy.18, f32[128,4]{0,1:T(4,128)S(1)} %convert_bitcast_fusion, f32[1,128,64]{1,2,0:T(8,128)} %param.16), kind=kOutput, calls=%fused_computation | convolution fusion | flops 25198592 | bytes 133120 | tf_op jit(solution)/shard_map/et,ta,tb->eab/dot_general | solution.py:378
  73.4 1.3 %collective-permute-done.18 = bf16[32,2048]{1,0:T(8,128)(2,1)S(1)} collective-permute-done((bf16[32,2048]{1,0:T(8,128)(2,1)S(1)}, bf16[32,2048]{1,0:T(8,128)(2,1)S(1)}, u32[]{:S(2)}, u32[]{:S(2)}) %collective-permute-start.18) | collective-permute-done | bytes 131104 | tf_op jit(solution)/shard_map/ppermute | solution.py:17
  (87 shorter events, 7.8 us)
Async XLA Ops:
  0.6 51.4 %copy-start = (bf16[1,2048,64]{1,2,0:T(8,128)(2,1)S(1)}, bf16[1,2048,64]{1,2,0:T(8,128)(2,1)}, u32[]{:S(2)}) copy-start(bf16[1,2048,64]{1,2,0:T(8,128)(2,1)} %param.17) | copy-start | bytes 786436
  1.6 17.0 %collective-permute-start.1 = (bf16[32,2048]{1,0:T(8,128)(2,1)S(1)}, bf16[32,2048]{1,0:T(8,128)(2,1)S(1)}, u32[]{:S(2)}, u32[]{:S(2)}) collective-permute-start(bf16[32,2048]{1,0:T(8,128)(2,1)S(1)} %get-tuple-element.43.cot_ref), channel_id=1, source_target_pairs={{0,8},{4,12},{8,0},{12,4},{1,9},{5,13},{9,1},{13,5},{2,10},{6,14},... | collective-permute-start | bytes 393224 | tf_op jit(solution)/shard_map/ppermute | solution.py:17
  5.7 12.9 %collective-permute-start.2 = (bf16[32,2048]{1,0:T(8,128)(2,1)S(1)}, bf16[32,2048]{1,0:T(8,128)(2,1)S(1)}, u32[]{:S(2)}, u32[]{:S(2)}) collective-permute-start(bf16[32,2048]{1,0:T(8,128)(2,1)S(1)} %get-tuple-element.43.cot_ref), channel_id=1, source_target_pairs={{0,12},{4,8},{8,4},{12,0},{1,13},{5,9},{9,5},{13,1},{2,14},{6,10},... | collective-permute-start | bytes 393224 | tf_op jit(solution)/shard_map/ppermute | solution.py:17
  8.0 11.9 %collective-permute-start = (bf16[64,2048]{1,0:T(8,128)(2,1)S(1)}, bf16[64,2048]{1,0:T(8,128)(2,1)S(1)}, u32[]{:S(2)}, u32[]{:S(2)}) collective-permute-start(bf16[64,2048]{1,0:T(8,128)(2,1)S(1)} %dynamic-slice_bitcast_fusion), channel_id=1, source_target_pairs={{0,4},{4,0},{8,12},{12,8},{1,5},{5,1},{9,13},{13,9},{2,6},{6,2},{1... | collective-permute-start | bytes 786440 | tf_op jit(solution)/shard_map/ppermute | solution.py:17
  12.2 6.3 %copy-start.5 = (s32[1,1,2]{2,1,0:T(1,128)S(1)}, s32[1,1,2]{2,1,0:T(1,128)}, u32[]{:S(2)}) copy-start(s32[1,1,2]{2,1,0:T(1,128)} %param.11) | copy-start | bytes 28
  12.2 7.9 %copy-start.4 = (bf16[1,128,2048]{2,1,0:T(8,128)(2,1)S(1)}, bf16[1,128,2048]{2,1,0:T(8,128)(2,1)}, u32[]{:S(2)}) copy-start(bf16[1,128,2048]{2,1,0:T(8,128)(2,1)} %param.10) | copy-start | bytes 1572868
  20.0 3.6 %collective-permute-start.3 = (bf16[128,2048]{1,0:T(8,128)(2,1)S(1)}, bf16[128,2048]{1,0:T(8,128)(2,1)S(1)}, u32[]{:S(2)}, u32[]{:S(2)}) collective-permute-start(bf16[128,2048]{1,0:T(8,128)(2,1)S(1)} %pad_maximum_fusion), channel_id=1, source_target_pairs={{0,1},{1,0},{2,3},{3,2},{4,5},{5,4},{6,7},{7,6},{8,9},{9,8},{10,11... | collective-permute-start | bytes 1572872 | tf_op jit(solution)/shard_map/ppermute | solution.py:17
  20.2 12.9 %collective-permute-start.4 = (bf16[32,2048]{1,0:T(8,128)(2,1)S(1)}, bf16[32,2048]{1,0:T(8,128)(2,1)S(1)}, u32[]{:S(2)}, u32[]{:S(2)}) collective-permute-start(bf16[32,2048]{1,0:T(8,128)(2,1)S(1)} %held.7), channel_id=1, source_target_pairs={{0,12},{4,8},{8,4},{12,0},{1,13},{5,9},{9,5},{13,1},{2,14},{6,10},... | collective-permute-start | bytes 393224 | tf_op jit(solution)/shard_map/ppermute | solution.py:17
  23.5 11.0 %collective-permute-start.5 = (bf16[32,2048]{1,0:T(8,128)(2,1)S(1)}, bf16[32,2048]{1,0:T(8,128)(2,1)S(1)}, u32[]{:S(2)}, u32[]{:S(2)}) collective-permute-start(bf16[32,2048]{1,0:T(8,128)(2,1)S(1)} %held.7), channel_id=1, source_target_pairs={{0,8},{4,12},{8,0},{12,4},{1,9},{5,13},{9,1},{13,5},{2,10},{6,14},... | collective-permute-start | bytes 393224 | tf_op jit(solution)/shard_map/ppermute | solution.py:17
  34.6 2.0 %collective-permute-start.6 = (bf16[128,2176]{1,0:T(8,128)(2,1)S(1)}, bf16[128,2176]{1,0:T(8,128)(2,1)S(1)}, u32[]{:S(2)}, u32[]{:S(2)}) collective-permute-start(bf16[128,2176]{1,0:T(8,128)(2,1)S(1)} %held.10), channel_id=1, source_target_pairs={{0,1},{1,0},{2,3},{3,2},{4,5},{5,4},{6,7},{7,6},{8,9},{9,8},{10,11... | collective-permute-start | bytes 1671176 | tf_op jit(solution)/shard_map/ppermute | solution.py:17
  36.7 4.7 %collective-permute-start.10 = (bf16[64,2048]{1,0:T(8,128)(2,1)S(1)}, bf16[64,2048]{1,0:T(8,128)(2,1)S(1)}, u32[]{:S(2)}, u32[]{:S(2)}) collective-permute-start(bf16[64,2048]{1,0:T(8,128)(2,1)S(1)} %held.11), channel_id=1, source_target_pairs={{0,1},{1,0},{2,3},{3,2},{4,5},{5,4},{6,7},{7,6},{8,9},{9,8},{10,11... | collective-permute-start | bytes 786440 | tf_op jit(solution)/shard_map/ppermute | solution.py:17
  36.9 13.9 %collective-permute-start.7 = (bf16[32,2176]{1,0:T(8,128)(2,1)S(1)}, bf16[32,2176]{1,0:T(8,128)(2,1)S(1)}, u32[]{:S(2)}, u32[]{:S(2)}) collective-permute-start(bf16[32,2176]{1,0:T(8,128)(2,1)S(1)} %get-tuple-element.27.refs_2_), channel_id=1, source_target_pairs={{0,12},{4,8},{8,4},{12,0},{1,13},{5,9},{9,5},{13,1},{2,14},{6,10},... | collective-permute-start | bytes 417800 | tf_op jit(solution)/shard_map/ppermute | solution.py:17
  39.5 12.2 %collective-permute-start.8 = (bf16[32,2176]{1,0:T(8,128)(2,1)S(1)}, bf16[32,2176]{1,0:T(8,128)(2,1)S(1)}, u32[]{:S(2)}, u32[]{:S(2)}) collective-permute-start(bf16[32,2176]{1,0:T(8,128)(2,1)S(1)} %get-tuple-element.28.refs_1_), channel_id=1, source_target_pairs={{0,8},{4,12},{8,0},{12,4},{1,9},{5,13},{9,1},{13,5},{2,10},{6,14},... | collective-permute-start | bytes 417800 | tf_op jit(solution)/shard_map/ppermute | solution.py:17
  39.5 12.2 %collective-permute-start.9 = (bf16[32,2176]{1,0:T(8,128)(2,1)S(1)}, bf16[32,2176]{1,0:T(8,128)(2,1)S(1)}, u32[]{:S(2)}, u32[]{:S(2)}) collective-permute-start(bf16[32,2176]{1,0:T(8,128)(2,1)S(1)} %get-tuple-element.29.refs_0_), channel_id=1, source_target_pairs={{0,4},{4,0},{8,12},{12,8},{1,5},{5,1},{9,13},{13,9},{2,6},{6,2},{1... | collective-permute-start | bytes 417800 | tf_op jit(solution)/shard_map/ppermute | solution.py:17
  41.4 10.5 %copy-start.6 = (s32[1,1,4]{2,1,0:T(1,128)S(1)}, s32[1,1,4]{2,1,0:T(1,128)}, u32[]{:S(2)}) copy-start(s32[1,1,4]{2,1,0:T(1,128)} %param.19) | copy-start | bytes 52
  51.7 2.0 %collective-permute-start.11 = (bf16[128,2176]{1,0:T(8,128)(2,1)S(1)}, bf16[128,2176]{1,0:T(8,128)(2,1)S(1)}, u32[]{:S(2)}, u32[]{:S(2)}) collective-permute-start(bf16[128,2176]{1,0:T(8,128)(2,1)S(1)} %held.12), channel_id=1, source_target_pairs={{0,1},{1,0},{2,3},{3,2},{4,5},{5,4},{6,7},{7,6},{8,9},{9,8},{10,11... | collective-permute-start | bytes 1671176 | tf_op jit(solution)/shard_map/ppermute | solution.py:17
  53.8 8.5 %collective-permute-start.12 = (bf16[32,2176]{1,0:T(8,128)(2,1)S(1)}, bf16[32,2176]{1,0:T(8,128)(2,1)S(1)}, u32[]{:S(2)}, u32[]{:S(2)}) collective-permute-start(bf16[32,2176]{1,0:T(8,128)(2,1)S(1)} %get-tuple-element.33), channel_id=1, source_target_pairs={{0,12},{4,8},{8,4},{12,0},{1,13},{5,9},{9,5},{13,1},{2,14},{6,10},... | collective-permute-start | bytes 417800 | tf_op jit(solution)/shard_map/ppermute | solution.py:17
  56.7 11.2 %collective-permute-start.14 = (bf16[32,2176]{1,0:T(8,128)(2,1)S(1)}, bf16[32,2176]{1,0:T(8,128)(2,1)S(1)}, u32[]{:S(2)}, u32[]{:S(2)}) collective-permute-start(bf16[32,2176]{1,0:T(8,128)(2,1)S(1)} %get-tuple-element.35), channel_id=1, source_target_pairs={{0,8},{4,12},{8,0},{12,4},{1,9},{5,13},{9,1},{13,5},{2,10},{6,14},... | collective-permute-start | bytes 417800 | tf_op jit(solution)/shard_map/ppermute | solution.py:17
  56.8 11.1 %collective-permute-start.15 = (bf16[32,2176]{1,0:T(8,128)(2,1)S(1)}, bf16[32,2176]{1,0:T(8,128)(2,1)S(1)}, u32[]{:S(2)}, u32[]{:S(2)}) collective-permute-start(bf16[32,2176]{1,0:T(8,128)(2,1)S(1)} %get-tuple-element.36), channel_id=1, source_target_pairs={{0,4},{4,0},{8,12},{12,8},{1,5},{5,1},{9,13},{13,9},{2,6},{6,2},{1... | collective-permute-start | bytes 417800 | tf_op jit(solution)/shard_map/ppermute | solution.py:17
  62.3 5.6 %collective-permute-start.13 = (bf16[32,2048]{1,0:T(8,128)(2,1)S(1)}, bf16[32,2048]{1,0:T(8,128)(2,1)S(1)}, u32[]{:S(2)}, u32[]{:S(2)}) collective-permute-start(bf16[32,2048]{1,0:T(8,128)(2,1)S(1)} %held.13), channel_id=1, source_target_pairs={{0,2},{2,0},{1,3},{3,1},{4,6},{6,4},{5,7},{7,5},{8,10},{10,8},{9,1... | collective-permute-start | bytes 393224 | tf_op jit(solution)/shard_map/ppermute | solution.py:298
  68.1 5.3 %collective-permute-start.16 = (bf16[32,2048]{1,0:T(8,128)(2,1)S(1)}, bf16[32,2048]{1,0:T(8,128)(2,1)S(1)}, u32[]{:S(2)}, u32[]{:S(2)}) collective-permute-start(bf16[32,2048]{1,0:T(8,128)(2,1)S(1)} %get-tuple-element.37), channel_id=1, source_target_pairs={{0,2},{2,0},{1,3},{3,1},{4,6},{6,4},{5,7},{7,5},{8,10},{10,8},{9,1... | collective-permute-start | bytes 393224 | tf_op jit(solution)/shard_map/ppermute | solution.py:298
  69.6 1.2 %collective-permute-start.19 = (f32[64,128]{1,0:T(8,128)S(1)}, f32[64,128]{1,0:T(8,128)S(1)}, u32[]{:S(2)}, u32[]{:S(2)}) collective-permute-start(f32[64,128]{1,0:T(8,128)S(1)} %constant_dynamic-update-slice_fusion.10), channel_id=1, source_target_pairs={{0,1},{1,0},{2,3},{3,2},{4,5},{5,4},{6,7},{7,6},{8,9},{9,8},{10,11... | collective-permute-start | bytes 98312 | tf_op jit(solution)/shard_map/ppermute | solution.py:17
  69.7 3.7 %collective-permute-start.17 = (bf16[32,2048]{1,0:T(8,128)(2,1)S(1)}, bf16[32,2048]{1,0:T(8,128)(2,1)S(1)}, u32[]{:S(2)}, u32[]{:S(2)}) collective-permute-start(bf16[32,2048]{1,0:T(8,128)(2,1)S(1)} %collective-permute-done.13.refs_3_), channel_id=1, source_target_pairs={{0,1},{1,0},{2,3},{3,2},{4,5},{5,4},{6,7},{7,6},{8,9},{9,8},{10,11... | collective-permute-start | bytes 393224 | tf_op jit(solution)/shard_map/ppermute | solution.py:17
  73.4 1.3 %collective-permute-start.18 = (bf16[32,2048]{1,0:T(8,128)(2,1)S(1)}, bf16[32,2048]{1,0:T(8,128)(2,1)S(1)}, u32[]{:S(2)}, u32[]{:S(2)}) collective-permute-start(bf16[32,2048]{1,0:T(8,128)(2,1)S(1)} %collective-permute-done.16), channel_id=1, source_target_pairs={{0,1},{1,0},{2,3},{3,2},{4,5},{5,4},{6,7},{7,6},{8,9},{9,8},{10,11... | collective-permute-start | bytes 393224 | tf_op jit(solution)/shard_map/ppermute | solution.py:17
  (3 other events, 8.2 us)

commit v8 on v7

--- a/solution.py
+++ b/solution.py
@@ -307,7 +307,7 @@
     weight = jnp.sum(jnp.where(hits, half_gates[:, None, :], 0.0), axis=2)
 
     sketch_t = sketch_local.T
-    cot_mine = lax.dynamic_slice_in_dim(cot, core * half, half, 0)
+    cot_mine = lax.optimization_barrier(lax.dynamic_slice_in_dim(cot, core * half, half, 0))
     cot_theirs = lax.dynamic_slice_in_dim(cot, (1 - core) * half, half, 0)
     order = sorted(range(2, pieces), reverse=True)
     slope, down_part, down_here = slopes(pre_all, sketch_t, down_weight[0, 0], place, core)

time: 76.1 us -> 79.7 us (1.047)
  local copies, waits for them, and re-layouts: 6.31 us -> 10.3 us
  matrix products: 2.64 us -> 0.82 us
  other arithmetic: 2.13 us -> 3.04 us
    unnamed x32 -> x37, local copies, waits for them, and re-layouts: 4.41 us -> 7.6 us
    ppermute x2, waiting for transfers between devices: 0.3 us -> 2.68 us  [below(): lax.ppermute(block, 'section', [(s, (s - 1) % sections) for s in range(se...]
    ppermute x18, waiting for transfers between devices: 15.3 us -> 13.1 us  [xored(): return lax.ppermute(block, axis, [(i, i ^ bits) for i in range(n)])]
    dot_general x1, matrix products: 1.34 us -> 0.3 us  [per_device(): out_vec = jnp.dot(cot, model_sketch[0], preferred_element_type=jnp.float32)]
    concatenate x2, other arithmetic: 0.05 us -> 0.96 us  [per_device(): blocks = jnp.concatenate(blocks, axis=0)]
  transfers between devices with their start and end apart: 20 -> 20, of which waited for: 10 -> 8; matrix products, arithmetic and copies ran while one was open for 8% -> 8% of each run, Pallas kernels for 33% -> 32%
where the time goes in v8:
time: 79.7 us; the launch traced here: 79.3 us
  Pallas kernels  25.8 us (32%)
  starting transfers between devices  22.5 us (28%)
  waiting for transfers between devices  15.8 us (20%)
  local copies, waits for them, and re-layouts  10.3 us (13%)
  other arithmetic  3.04 us (4%)
  between operations  1.04 us (1%)
  matrix products  0.82 us (1%)
    ppermute x18, starting transfers between devices, xored(): return lax.ppermute(block, axis, [(i, i ^ bits) for i in range(n)])  19.4 us
    pallas_call x2, Pallas kernels, expert(): pl.pallas_call(functools.partial(expert_kernel, tile_f, tile_d), grid=(1,...  18.8 us
    ppermute x18, waiting for transfers between devices, xored(): return lax.ppermute(block, axis, [(i, i ^ bits) for i in range(n)])  13.1 us
    unnamed x37, local copies, waits for them, and re-layouts  7.6 us
    pallas_call x1, Pallas kernels, slopes(): pl.pallas_call(functools.partial(slope_kernel, groups), grid_spec=pltpu.P...  6.27 us
    ppermute x2, starting transfers between devices, below(): lax.ppermute(block, 'section', [(s, (s - 1) % sections) for s in range(se...  3.11 us
    ppermute x2, waiting for transfers between devices, below(): lax.ppermute(block, 'section', [(s, (s - 1) % sections) for s in range(se...  2.68 us
    dynamic_slice x1, local copies, waits for them, and re-layouts, per_device(): lax.dynamic_slice_in_dim(cot, core * half, half, 0)  1.71 us
  transfers between devices with their start and end apart: 20, of which 8 were waited for; matrix products, arithmetic and copies ran while one was open for 8% of the time, Pallas kernels for 32%

profile of v8, /device:TPU:0, one launch (start us, length us, event | category | flops | bytes accessed | tf_op | source)
XLA Modules:
  0.0 79.3 jit_solution(3338057373003733653)
XLA Ops:
  0.6 1.7 %dynamic-slice_bitcast_fusion = bf16[64,2048]{1,0:T(8,128)(2,1)} fusion(bf16[1,128,2048]{2,1,0:T(8,128)(2,1)} %param.10, s32[]{:T(128)S(6)} %select_n.45), kind=kLoop, calls=%fused_computation.8 | loop fusion | bytes 524292 | tf_op jit(solution)/shard_map/dynamic_slice | solution.py:310
  2.4 3.0 %collective-permute-start = (bf16[64,2048]{1,0:T(8,128)(2,1)}, bf16[64,2048]{1,0:T(8,128)(2,1)S(1)}, u32[]{:S(2)}, u32[]{:S(2)}) collective-permute-start(bf16[64,2048]{1,0:T(8,128)(2,1)} %dynamic-slice_bitcast_fusion), channel_id=1, source_target_pairs={{0,4},{4,0},{8,12},{12,8},{1,5},{5,1},{9,13},{13,9},{2,6},{6,2},{1... | collective-permute-start | bytes 786440 | tf_op jit(solution)/shard_map/ppermute | solution.py:17
  5.4 1.0 %constant_dynamic-update-slice_fusion.5 = (bf16[256,2048]{1,0:T(8,128)(2,1)S(1)}, bf16[256,2048]{1,0:T(8,128)(2,1)S(1)}, bf16[32,2048]{1,0:T(8,128)(2,1)S(1)}, bf16[32,2048]{1,0:T(8,128)(2,1)S(1)}) fusion(bf16[64,2048]{1,0:T(8,128)(2,1)} %dynamic-slice_bitcast_fusion), kind=kLoop, calls=%fused_computation.41 | loop fusion | bytes 786432
  6.4 2.7 %collective-permute-start.1 = (bf16[32,2048]{1,0:T(8,128)(2,1)S(1)}, bf16[32,2048]{1,0:T(8,128)(2,1)S(1)}, u32[]{:S(2)}, u32[]{:S(2)}) collective-permute-start(bf16[32,2048]{1,0:T(8,128)(2,1)S(1)} %get-tuple-element.47.cot_ref), channel_id=1, source_target_pairs={{0,8},{4,12},{8,0},{12,4},{1,9},{5,13},{9,1},{13,5},{2,10},{6,14},... | collective-permute-start | bytes 393224 | tf_op jit(solution)/shard_map/ppermute | solution.py:17
  9.9 2.0 %copy-done.1 = bf16[1,1,4,128,3584]{4,3,2,1,0:T(8,128)(2,1)S(1)} copy-done((bf16[1,1,4,128,3584]{4,3,2,1,0:T(8,128)(2,1)S(1)}, bf16[1,1,4,128,3584]{4,3,2,1,0:T(8,128)(2,1)}, u32[]{:S(2)}) %copy-start.1) | copy-done | bytes 3670040
  11.9 1.0 %copy-done.2 = bf16[1,1,3584,64]{2,3,1,0:T(8,128)(2,1)S(1)} copy-done((bf16[1,1,3584,64]{2,3,1,0:T(8,128)(2,1)S(1)}, bf16[1,1,3584,64]{2,3,1,0:T(8,128)(2,1)}, u32[]{:S(2)}) %copy-start.2) | copy-done | bytes 458776
  13.0 6.3 %slopes.1 = (bf16[2,3584,256]{2,1,0:T(8,128)(2,1)S(1)}, f32[2,256,64]{2,1,0:T(8,128)S(1)}, bf16[3584,2048]{1,0:T(8,128)(2,1)S(1)}) custom-call(s32[2]{0:T(128)S(1)} %pad_add_fusion.index_ref, bf16[4,2,2,32,3584]{4,3,2,1,0:T(8,128)(2,1)S(1)} %bitcast.46, bf16[4,2,2,32,3584]{4,3,2,1,0:T(8,128)(2,1)S(1)} %bitcast.47, bf16[4,2,2,32,3584]{4,3,2,1,0:T(8,128)(2,1)S(1)} %bitcast.48, ...), custom_call_target="tpu_custom_call" | custom-call | flops 234881024 | bytes 7340032 | tf_op jit(solution)/shard_map/slopes/pallas_call | solution.py:148
  19.4 2.0 %collective-permute-start.5 = (bf16[32,2048]{1,0:T(8,128)(2,1)S(1)}, bf16[32,2048]{1,0:T(8,128)(2,1)S(1)}, u32[]{:S(2)}, u32[]{:S(2)}) collective-permute-start(bf16[32,2048]{1,0:T(8,128)(2,1)S(1)} %held.7), channel_id=1, source_target_pairs={{0,8},{4,12},{8,0},{12,4},{1,9},{5,13},{9,1},{13,5},{2,10},{6,14},... | collective-permute-start | bytes 393224 | tf_op jit(solution)/shard_map/ppermute | solution.py:17
  21.3 2.0 %collective-permute-start.4 = (bf16[32,2048]{1,0:T(8,128)(2,1)S(1)}, bf16[32,2048]{1,0:T(8,128)(2,1)S(1)}, u32[]{:S(2)}, u32[]{:S(2)}) collective-permute-start(bf16[32,2048]{1,0:T(8,128)(2,1)S(1)} %held.7), channel_id=1, source_target_pairs={{0,12},{4,8},{8,4},{12,0},{1,13},{5,9},{9,5},{13,1},{2,14},{6,10},... | collective-permute-start | bytes 393224 | tf_op jit(solution)/shard_map/ppermute | solution.py:17
  26.3 9.4 %expert.2 = (f32[128,2176]{1,0:T(8,128)S(1)}, bf16[128,2176]{1,0:T(8,128)(2,1)S(1)}) custom-call(bf16[256,2048]{1,0:T(8,128)(2,1)S(1)} %slice_dynamic-update-slice_fusion.4.rows_ref, bf16[2,3584,256]{2,1,0:T(8,128)(2,1)S(1)} %get-tuple-element.21.slope_ref, f32[2,256,64]{2,1,0:T(8,128)S(1)} %get-tuple-element.22.down_part_ref, ...), custom_call_target="tpu_custom_call" | custom-call | flops 7516192768 | bytes 29360128 | tf_op jit(solution)/shard_map/expert/pallas_call | solution.py:236
  36.1 1.7 %collective-permute-done.6.came_ref = bf16[128,2176]{1,0:T(8,128)(2,1)S(1)} collective-permute-done((bf16[128,2176]{1,0:T(8,128)(2,1)S(1)}, bf16[128,2176]{1,0:T(8,128)(2,1)S(1)}, u32[]{:S(2)}, u32[]{:S(2)}) %collective-permute-start.6) | collective-permute-done | bytes 557088 | tf_op jit(solution)/shard_map/ppermute | solution.py:17
  38.2 1.9 %collective-permute-start.7 = (bf16[32,2176]{1,0:T(8,128)(2,1)S(1)}, bf16[32,2176]{1,0:T(8,128)(2,1)S(1)}, u32[]{:S(2)}, u32[]{:S(2)}) collective-permute-start(bf16[32,2176]{1,0:T(8,128)(2,1)S(1)} %get-tuple-element.27.refs_2_), channel_id=1, source_target_pairs={{0,12},{4,8},{8,4},{12,0},{1,13},{5,9},{9,5},{13,1},{2,14},{6,10},... | collective-permute-start | bytes 417800 | tf_op jit(solution)/shard_map/ppermute | solution.py:17
  40.3 2.4 %collective-permute-start.9 = (bf16[32,2176]{1,0:T(8,128)(2,1)S(1)}, bf16[32,2176]{1,0:T(8,128)(2,1)S(1)}, u32[]{:S(2)}, u32[]{:S(2)}) collective-permute-start(bf16[32,2176]{1,0:T(8,128)(2,1)S(1)} %get-tuple-element.29.refs_0_), channel_id=1, source_target_pairs={{0,4},{4,0},{8,12},{12,8},{1,5},{5,1},{9,13},{13,9},{2,6},{6,2},{1... | collective-permute-start | bytes 417800 | tf_op jit(solution)/shard_map/ppermute | solution.py:17
  42.7 9.4 %expert.3 = (f32[128,2176]{1,0:T(8,128)S(1)}, bf16[128,2176]{1,0:T(8,128)(2,1)S(1)}) custom-call(bf16[256,2048]{1,0:T(8,128)(2,1)S(1)} %slice_dynamic-update-slice_fusion.rows_ref, bf16[2,3584,256]{2,1,0:T(8,128)(2,1)S(1)} %get-tuple-element.21.slope_ref, f32[2,256,64]{2,1,0:T(8,128)S(1)} %get-tuple-element.22.down_part_ref, bf16[64,3584]{1,0:T(8,128)(2,1)S(1)} %bitcast.56, ...), custom_call_target="tpu_custom_call" | custom-call | flops 7516192768 | bytes 29360128 | tf_op jit(solution)/shard_map/expert/pallas_call | solution.py:236
  54.1 1.4 %collective-permute-done.11.came_ref = bf16[128,2176]{1,0:T(8,128)(2,1)S(1)} collective-permute-done((bf16[128,2176]{1,0:T(8,128)(2,1)S(1)}, bf16[128,2176]{1,0:T(8,128)(2,1)S(1)}, u32[]{:S(2)}, u32[]{:S(2)}) %collective-permute-start.11) | collective-permute-done | bytes 557088 | tf_op jit(solution)/shard_map/ppermute | solution.py:17
  55.5 1.2 %copy-done.5 = f32[128,2176]{1,0:T(8,128)S(1)} copy-done((f32[128,2176]{1,0:T(8,128)S(1)}, f32[128,2176]{1,0:T(8,128)}, u32[]{:S(2)}) %copy-start.5) | copy-done | bytes 1114136
  56.8 2.7 %collective-permute-start.12 = (bf16[32,2176]{1,0:T(8,128)(2,1)S(1)}, bf16[32,2176]{1,0:T(8,128)(2,1)S(1)}, u32[]{:S(2)}, u32[]{:S(2)}) collective-permute-start(bf16[32,2176]{1,0:T(8,128)(2,1)S(1)} %get-tuple-element.33), channel_id=1, source_target_pairs={{0,12},{4,8},{8,4},{12,0},{1,13},{5,9},{9,5},{13,1},{2,14},{6,10},... | collective-permute-start | bytes 417800 | tf_op jit(solution)/shard_map/ppermute | solution.py:17
  59.8 1.7 %collective-permute-start.15 = (bf16[32,2176]{1,0:T(8,128)(2,1)S(1)}, bf16[32,2176]{1,0:T(8,128)(2,1)S(1)}, u32[]{:S(2)}, u32[]{:S(2)}) collective-permute-start(bf16[32,2176]{1,0:T(8,128)(2,1)S(1)} %get-tuple-element.36), channel_id=1, source_target_pairs={{0,4},{4,0},{8,12},{12,8},{1,5},{5,1},{9,13},{13,9},{2,6},{6,2},{1... | collective-permute-start | bytes 417800 | tf_op jit(solution)/shard_map/ppermute | solution.py:17
  61.6 3.8 %collective-permute-done.12.refs_0_ = bf16[32,2176]{1,0:T(8,128)(2,1)S(1)} collective-permute-done((bf16[32,2176]{1,0:T(8,128)(2,1)S(1)}, bf16[32,2176]{1,0:T(8,128)(2,1)S(1)}, u32[]{:S(2)}, u32[]{:S(2)}) %collective-permute-start.12) | collective-permute-done | bytes 139296 | tf_op jit(solution)/shard_map/ppermute | solution.py:17
  65.3 1.6 %collective-permute-start.13 = (bf16[32,2048]{1,0:T(8,128)(2,1)S(1)}, bf16[32,2048]{1,0:T(8,128)(2,1)S(1)}, u32[]{:S(2)}, u32[]{:S(2)}) collective-permute-start(bf16[32,2048]{1,0:T(8,128)(2,1)S(1)} %held.13), channel_id=1, source_target_pairs={{0,2},{2,0},{1,3},{3,1},{4,6},{6,4},{5,7},{7,5},{8,10},{10,8},{9,1... | collective-permute-start | bytes 393224 | tf_op jit(solution)/shard_map/ppermute | solution.py:298
  67.1 3.8 %collective-permute-done.14.refs_1_ = bf16[32,2176]{1,0:T(8,128)(2,1)S(1)} collective-permute-done((bf16[32,2176]{1,0:T(8,128)(2,1)S(1)}, bf16[32,2176]{1,0:T(8,128)(2,1)S(1)}, u32[]{:S(2)}, u32[]{:S(2)}) %collective-permute-start.14) | collective-permute-done | bytes 139296 | tf_op jit(solution)/shard_map/ppermute | solution.py:17
  71.1 1.6 %collective-permute-start.16 = (bf16[32,2048]{1,0:T(8,128)(2,1)S(1)}, bf16[32,2048]{1,0:T(8,128)(2,1)S(1)}, u32[]{:S(2)}, u32[]{:S(2)}) collective-permute-start(bf16[32,2048]{1,0:T(8,128)(2,1)S(1)} %get-tuple-element.37), channel_id=1, source_target_pairs={{0,2},{2,0},{1,3},{3,1},{4,6},{6,4},{5,7},{7,5},{8,10},{10,8},{9,1... | collective-permute-start | bytes 393224 | tf_op jit(solution)/shard_map/ppermute | solution.py:298
  74.4 2.7 %collective-permute-done.16 = bf16[32,2048]{1,0:T(8,128)(2,1)S(1)} collective-permute-done((bf16[32,2048]{1,0:T(8,128)(2,1)S(1)}, bf16[32,2048]{1,0:T(8,128)(2,1)S(1)}, u32[]{:S(2)}, u32[]{:S(2)}) %collective-permute-start.16) | collective-permute-done | bytes 131104 | tf_op jit(solution)/shard_map/ppermute | solution.py:298
  77.1 1.3 %collective-permute-done.18 = bf16[32,2048]{1,0:T(8,128)(2,1)S(1)} collective-permute-done((bf16[32,2048]{1,0:T(8,128)(2,1)S(1)}, bf16[32,2048]{1,0:T(8,128)(2,1)S(1)}, u32[]{:S(2)}, u32[]{:S(2)}) %collective-permute-start.18) | collective-permute-done | bytes 131104 | tf_op jit(solution)/shard_map/ppermute | solution.py:17
  (92 shorter events, 10.0 us)
Async XLA Ops:
  0.6 53.2 %copy-start = (bf16[1,2048,64]{1,2,0:T(8,128)(2,1)S(1)}, bf16[1,2048,64]{1,2,0:T(8,128)(2,1)}, u32[]{:S(2)}) copy-start(bf16[1,2048,64]{1,2,0:T(8,128)(2,1)} %param.17) | copy-start | bytes 786436
  2.4 17.0 %collective-permute-start = (bf16[64,2048]{1,0:T(8,128)(2,1)}, bf16[64,2048]{1,0:T(8,128)(2,1)S(1)}, u32[]{:S(2)}, u32[]{:S(2)}) collective-permute-start(bf16[64,2048]{1,0:T(8,128)(2,1)} %dynamic-slice_bitcast_fusion), channel_id=1, source_target_pairs={{0,4},{4,0},{8,12},{12,8},{1,5},{5,1},{9,13},{13,9},{2,6},{6,2},{1... | collective-permute-start | bytes 786440 | tf_op jit(solution)/shard_map/ppermute | solution.py:17
  6.4 16.9 %collective-permute-start.1 = (bf16[32,2048]{1,0:T(8,128)(2,1)S(1)}, bf16[32,2048]{1,0:T(8,128)(2,1)S(1)}, u32[]{:S(2)}, u32[]{:S(2)}) collective-permute-start(bf16[32,2048]{1,0:T(8,128)(2,1)S(1)} %get-tuple-element.47.cot_ref), channel_id=1, source_target_pairs={{0,8},{4,12},{8,0},{12,4},{1,9},{5,13},{9,1},{13,5},{2,10},{6,14},... | collective-permute-start | bytes 393224 | tf_op jit(solution)/shard_map/ppermute | solution.py:17
  9.1 14.3 %collective-permute-start.2 = (bf16[32,2048]{1,0:T(8,128)(2,1)S(1)}, bf16[32,2048]{1,0:T(8,128)(2,1)}, u32[]{:S(2)}, u32[]{:S(2)}) collective-permute-start(bf16[32,2048]{1,0:T(8,128)(2,1)S(1)} %get-tuple-element.47.cot_ref), channel_id=1, source_target_pairs={{0,12},{4,8},{8,4},{12,0},{1,13},{5,9},{9,5},{13,1},{2,14},{6,10},... | collective-permute-start | bytes 393224 | tf_op jit(solution)/shard_map/ppermute | solution.py:17
  13.0 12.4 %copy-start.6 = (bf16[1,128,2048]{2,1,0:T(8,128)(2,1)S(1)}, bf16[1,128,2048]{2,1,0:T(8,128)(2,1)}, u32[]{:S(2)}) copy-start(bf16[1,128,2048]{2,1,0:T(8,128)(2,1)} %param.10) | copy-start | bytes 1572868
  19.4 16.4 %collective-permute-start.5 = (bf16[32,2048]{1,0:T(8,128)(2,1)S(1)}, bf16[32,2048]{1,0:T(8,128)(2,1)S(1)}, u32[]{:S(2)}, u32[]{:S(2)}) collective-permute-start(bf16[32,2048]{1,0:T(8,128)(2,1)S(1)} %held.7), channel_id=1, source_target_pairs={{0,8},{4,12},{8,0},{12,4},{1,9},{5,13},{9,1},{13,5},{2,10},{6,14},... | collective-permute-start | bytes 393224 | tf_op jit(solution)/shard_map/ppermute | solution.py:17
  21.3 14.4 %collective-permute-start.4 = (bf16[32,2048]{1,0:T(8,128)(2,1)S(1)}, bf16[32,2048]{1,0:T(8,128)(2,1)S(1)}, u32[]{:S(2)}, u32[]{:S(2)}) collective-permute-start(bf16[32,2048]{1,0:T(8,128)(2,1)S(1)} %held.7), channel_id=1, source_target_pairs={{0,12},{4,8},{8,4},{12,0},{1,13},{5,9},{9,5},{13,1},{2,14},{6,10},... | collective-permute-start | bytes 393224 | tf_op jit(solution)/shard_map/ppermute | solution.py:17
  24.3 2.0 %collective-permute-start.3 = (bf16[128,2048]{1,0:T(8,128)(2,1)S(1)}, bf16[128,2048]{1,0:T(8,128)(2,1)S(1)}, u32[]{:S(2)}, u32[]{:S(2)}) collective-permute-start(bf16[128,2048]{1,0:T(8,128)(2,1)S(1)} %pad_maximum_fusion), channel_id=1, source_target_pairs={{0,1},{1,0},{2,3},{3,2},{4,5},{5,4},{6,7},{7,6},{8,9},{9,8},{10,11... | collective-permute-start | bytes 1572872 | tf_op jit(solution)/shard_map/ppermute | solution.py:17
  35.8 2.0 %collective-permute-start.6 = (bf16[128,2176]{1,0:T(8,128)(2,1)S(1)}, bf16[128,2176]{1,0:T(8,128)(2,1)S(1)}, u32[]{:S(2)}, u32[]{:S(2)}) collective-permute-start(bf16[128,2176]{1,0:T(8,128)(2,1)S(1)} %held.10), channel_id=1, source_target_pairs={{0,1},{1,0},{2,3},{3,2},{4,5},{5,4},{6,7},{7,6},{8,9},{9,8},{10,11... | collective-permute-start | bytes 1671176 | tf_op jit(solution)/shard_map/ppermute | solution.py:17
  38.0 4.7 %collective-permute-start.10 = (bf16[64,2048]{1,0:T(8,128)(2,1)S(1)}, bf16[64,2048]{1,0:T(8,128)(2,1)S(1)}, u32[]{:S(2)}, u32[]{:S(2)}) collective-permute-start(bf16[64,2048]{1,0:T(8,128)(2,1)S(1)} %held.11), channel_id=1, source_target_pairs={{0,1},{1,0},{2,3},{3,2},{4,5},{5,4},{6,7},{7,6},{8,9},{9,8},{10,11... | collective-permute-start | bytes 786440 | tf_op jit(solution)/shard_map/ppermute | solution.py:17
  38.2 14.9 %collective-permute-start.7 = (bf16[32,2176]{1,0:T(8,128)(2,1)S(1)}, bf16[32,2176]{1,0:T(8,128)(2,1)S(1)}, u32[]{:S(2)}, u32[]{:S(2)}) collective-permute-start(bf16[32,2176]{1,0:T(8,128)(2,1)S(1)} %get-tuple-element.27.refs_2_), channel_id=1, source_target_pairs={{0,12},{4,8},{8,4},{12,0},{1,13},{5,9},{9,5},{13,1},{2,14},{6,10},... | collective-permute-start | bytes 417800 | tf_op jit(solution)/shard_map/ppermute | solution.py:17
  40.1 13.3 %collective-permute-start.8 = (bf16[32,2176]{1,0:T(8,128)(2,1)S(1)}, bf16[32,2176]{1,0:T(8,128)(2,1)S(1)}, u32[]{:S(2)}, u32[]{:S(2)}) collective-permute-start(bf16[32,2176]{1,0:T(8,128)(2,1)S(1)} %get-tuple-element.28.refs_1_), channel_id=1, source_target_pairs={{0,8},{4,12},{8,0},{12,4},{1,9},{5,13},{9,1},{13,5},{2,10},{6,14},... | collective-permute-start | bytes 417800 | tf_op jit(solution)/shard_map/ppermute | solution.py:17
  40.3 13.1 %collective-permute-start.9 = (bf16[32,2176]{1,0:T(8,128)(2,1)S(1)}, bf16[32,2176]{1,0:T(8,128)(2,1)S(1)}, u32[]{:S(2)}, u32[]{:S(2)}) collective-permute-start(bf16[32,2176]{1,0:T(8,128)(2,1)S(1)} %get-tuple-element.29.refs_0_), channel_id=1, source_target_pairs={{0,4},{4,0},{8,12},{12,8},{1,5},{5,1},{9,13},{13,9},{2,6},{6,2},{1... | collective-permute-start | bytes 417800 | tf_op jit(solution)/shard_map/ppermute | solution.py:17
  42.7 11.0 %copy-start.9 = (s32[1,1,4]{2,1,0:T(1,128)S(1)}, s32[1,1,4]{2,1,0:T(1,128)}, u32[]{:S(2)}) copy-start(s32[1,1,4]{2,1,0:T(1,128)} %param.19) | copy-start | bytes 52
  53.1 19.9 %copy-start.7 = (f32[1,128,64]{1,2,0:T(8,128)S(1)}, f32[1,128,64]{1,2,0:T(8,128)}, u32[]{:S(2)}) copy-start(f32[1,128,64]{1,2,0:T(8,128)} %param.16) | copy-start | bytes 98308
  53.4 2.0 %collective-permute-start.11 = (bf16[128,2176]{1,0:T(8,128)(2,1)S(1)}, bf16[128,2176]{1,0:T(8,128)(2,1)S(1)}, u32[]{:S(2)}, u32[]{:S(2)}) collective-permute-start(bf16[128,2176]{1,0:T(8,128)(2,1)S(1)} %held.12), channel_id=1, source_target_pairs={{0,1},{1,0},{2,3},{3,2},{4,5},{5,4},{6,7},{7,6},{8,9},{9,8},{10,11... | collective-permute-start | bytes 1671176 | tf_op jit(solution)/shard_map/ppermute | solution.py:17
  56.8 8.5 %collective-permute-start.12 = (bf16[32,2176]{1,0:T(8,128)(2,1)S(1)}, bf16[32,2176]{1,0:T(8,128)(2,1)S(1)}, u32[]{:S(2)}, u32[]{:S(2)}) collective-permute-start(bf16[32,2176]{1,0:T(8,128)(2,1)S(1)} %get-tuple-element.33), channel_id=1, source_target_pairs={{0,12},{4,8},{8,4},{12,0},{1,13},{5,9},{9,5},{13,1},{2,14},{6,10},... | collective-permute-start | bytes 417800 | tf_op jit(solution)/shard_map/ppermute | solution.py:17
  59.7 11.1 %collective-permute-start.14 = (bf16[32,2176]{1,0:T(8,128)(2,1)S(1)}, bf16[32,2176]{1,0:T(8,128)(2,1)S(1)}, u32[]{:S(2)}, u32[]{:S(2)}) collective-permute-start(bf16[32,2176]{1,0:T(8,128)(2,1)S(1)} %get-tuple-element.35), channel_id=1, source_target_pairs={{0,8},{4,12},{8,0},{12,4},{1,9},{5,13},{9,1},{13,5},{2,10},{6,14},... | collective-permute-start | bytes 417800 | tf_op jit(solution)/shard_map/ppermute | solution.py:17
  59.8 11.0 %collective-permute-start.15 = (bf16[32,2176]{1,0:T(8,128)(2,1)S(1)}, bf16[32,2176]{1,0:T(8,128)(2,1)S(1)}, u32[]{:S(2)}, u32[]{:S(2)}) collective-permute-start(bf16[32,2176]{1,0:T(8,128)(2,1)S(1)} %get-tuple-element.36), channel_id=1, source_target_pairs={{0,4},{4,0},{8,12},{12,8},{1,5},{5,1},{9,13},{13,9},{2,6},{6,2},{1... | collective-permute-start | bytes 417800 | tf_op jit(solution)/shard_map/ppermute | solution.py:17
  65.3 5.5 %collective-permute-start.13 = (bf16[32,2048]{1,0:T(8,128)(2,1)S(1)}, bf16[32,2048]{1,0:T(8,128)(2,1)S(1)}, u32[]{:S(2)}, u32[]{:S(2)}) collective-permute-start(bf16[32,2048]{1,0:T(8,128)(2,1)S(1)} %held.13), channel_id=1, source_target_pairs={{0,2},{2,0},{1,3},{3,1},{4,6},{6,4},{5,7},{7,5},{8,10},{10,8},{9,1... | collective-permute-start | bytes 393224 | tf_op jit(solution)/shard_map/ppermute | solution.py:298
  71.0 1.8 %collective-permute-start.19 = (f32[64,128]{1,0:T(8,128)S(1)}, f32[64,128]{1,0:T(8,128)S(1)}, u32[]{:S(2)}, u32[]{:S(2)}) collective-permute-start(f32[64,128]{1,0:T(8,128)S(1)} %constant_dynamic-update-slice_fusion.10), channel_id=1, source_target_pairs={{0,1},{1,0},{2,3},{3,2},{4,5},{5,4},{6,7},{7,6},{8,9},{9,8},{10,11... | collective-permute-start | bytes 98312 | tf_op jit(solution)/shard_map/ppermute | solution.py:17
  71.1 5.9 %collective-permute-start.16 = (bf16[32,2048]{1,0:T(8,128)(2,1)S(1)}, bf16[32,2048]{1,0:T(8,128)(2,1)S(1)}, u32[]{:S(2)}, u32[]{:S(2)}) collective-permute-start(bf16[32,2048]{1,0:T(8,128)(2,1)S(1)} %get-tuple-element.37), channel_id=1, source_target_pairs={{0,2},{2,0},{1,3},{3,1},{4,6},{6,4},{5,7},{7,5},{8,10},{10,8},{9,1... | collective-permute-start | bytes 393224 | tf_op jit(solution)/shard_map/ppermute | solution.py:298
  72.7 4.4 %collective-permute-start.17 = (bf16[32,2048]{1,0:T(8,128)(2,1)S(1)}, bf16[32,2048]{1,0:T(8,128)(2,1)S(1)}, u32[]{:S(2)}, u32[]{:S(2)}) collective-permute-start(bf16[32,2048]{1,0:T(8,128)(2,1)S(1)} %collective-permute-done.13.refs_3_), channel_id=1, source_target_pairs={{0,1},{1,0},{2,3},{3,2},{4,5},{5,4},{6,7},{7,6},{8,9},{9,8},{10,11... | collective-permute-start | bytes 393224 | tf_op jit(solution)/shard_map/ppermute | solution.py:17
  77.0 1.3 %collective-permute-start.18 = (bf16[32,2048]{1,0:T(8,128)(2,1)S(1)}, bf16[32,2048]{1,0:T(8,128)(2,1)S(1)}, u32[]{:S(2)}, u32[]{:S(2)}) collective-permute-start(bf16[32,2048]{1,0:T(8,128)(2,1)S(1)} %collective-permute-done.16), channel_id=1, source_target_pairs={{0,1},{1,0},{2,3},{3,2},{4,5},{5,4},{6,7},{7,6},{8,9},{9,8},{10,11... | collective-permute-start | bytes 393224 | tf_op jit(solution)/shard_map/ppermute | solution.py:17
  (6 other events, 18.7 us)

commit v9 on v7

--- a/solution.py
+++ b/solution.py
@@ -36,7 +36,8 @@
     )(block, *events)
 
 
-def merge_kernel(keep_ref, came_ref, own_ref, *sent_refs):
+def merge_kernel(others, keep_ref, came_ref, *refs):
+    own_ref, *sent_refs = refs[-1 - others :]
     rows = own_ref.shape[0]
     own_ref[...] = keep_ref[:rows] + came_ref[:rows].astype(jnp.float32)
     for at, sent_ref in enumerate(sent_refs):
@@ -45,12 +46,12 @@
         sent_ref[...] = total.astype(jnp.bfloat16)
 
 
-def merged(keep, came, rows):
+def merged(keep, came, rows, *events):
     count, wide = keep.shape
     others = count // rows - 1
     return pl.pallas_call(
-        merge_kernel,
-        in_specs=[RESIDENT] * 2,
+        functools.partial(merge_kernel, others),
+        in_specs=[RESIDENT] * 2 + [ANYWHERE] * len(events),
         out_specs=[RESIDENT] * (1 + others),
         out_shape=[jax.ShapeDtypeStruct((rows, wide), jnp.float32)]
         + [jax.ShapeDtypeStruct((rows, wide), jnp.bfloat16)] * others,
@@ -59,7 +60,7 @@
             flops=count * wide, bytes_accessed=8 * count * wide, transcendentals=0
         ),
         name="merge",
-    )(keep, came)
+    )(keep, came, *events)
 
 
 def finish_kernel(slots, own_ref, cot_ref, weight_ref, *refs):
@@ -90,6 +91,36 @@
         ),
         name="finish",
     )(own, cot, weight, *backs, *events)
+
+
+def place_kernel(cuts, index_ref, *refs):
+    out_ref, sems = refs[-2:]
+    half = out_ref.shape[0] // 2
+    rows = half // cuts
+    copies = []
+    for at, block_ref in enumerate(refs[: 2 * cuts]):
+        h, cut = at // cuts, at % cuts
+        start = pl.multiple_of((index_ref[1] ^ h) * half + cut * rows, rows)
+        copies.append(
+            pltpu.make_async_copy(block_ref, out_ref.at[pl.ds(start, rows)], sems.at[at])
+        )
+    for copy in copies:
+        copy.start()
+    for copy in copies:
+        copy.wait()
+
+
+def placed(index, mine, theirs):
+    cuts, (rows, width) = len(mine), mine[0].shape
+    return pl.pallas_call(
+        functools.partial(place_kernel, cuts),
+        in_specs=[pl.BlockSpec(memory_space=pltpu.SMEM)] + [RESIDENT] * (2 * cuts),
+        out_specs=ANYWHERE,
+        out_shape=jax.ShapeDtypeStruct((2 * cuts * rows, width), mine[0].dtype),
+        scratch_shapes=[pltpu.SemaphoreType.DMA((2 * cuts,))],
+        compiler_params=pltpu.CompilerParams(vmem_limit_bytes=1 << 20),
+        name="place",
+    )(index, *mine, *theirs)
 
 
 def tile_of(size, most):
@@ -338,10 +369,10 @@
         if a + 1 < CHUNKS:
             coming = held(cot_mine[(a + 1) * rows : (a + 2) * rows], near_rows)
             fetched = {slot: held(xored(coming, "dp", slot), kept) for slot in order}
-            give = held(give, *fetched.values(), *backs)
+            late = tuple(fetched.values())
         else:
-            give = held(give, *backs)
-        own, *sent = merged(kept, xored(give, "tensor", 1), rows)
+            give, late = held(give, *backs), ()
+        own, *sent = merged(kept, xored(give, "tensor", 1), rows, *late)
         backs = [xored(out, "dp", slot + 1) for slot, out in enumerate(sent)][::-1]
         if grad:
             passed = (below(held(*grad, backs[0])),)
@@ -351,11 +382,8 @@
         vectors.append(vec)
     below_mine.append(below(*grad))
 
-    mine = jnp.concatenate(below_mine, axis=0)
-    theirs = jnp.concatenate([xored(f, "tensor", 1) for f in below_mine], axis=0)
-    handed = jnp.concatenate(
-        [jnp.where(core == 0, mine, theirs), jnp.where(core == 0, theirs, mine)], axis=0
-    )
+    index = jnp.stack([place, core]).astype(jnp.int32)
+    handed = placed(index, below_mine, [xored(block, "tensor", 1) for block in below_mine])
 
     vec_mine = jnp.concatenate(vectors, axis=0)
     vec_theirs = xored(vec_mine, "tensor", 1)

time: 76.1 us -> 75.5 us (level)
  waiting for transfers between devices: 15.6 us -> 17.7 us
  matrix products: 2.64 us -> 0.82 us
  Pallas kernels: 25.8 us -> 27.1 us
  other arithmetic: 2.13 us -> 1.25 us
    ppermute x2, waiting for transfers between devices: 0.3 us -> 3.73 us  [below(): lax.ppermute(block, 'section', [(s, (s - 1) % sections) for s in range(se...]
    pallas_call x2 -> x3, Pallas kernels: 0.19 us -> 1.58 us  [the longest x1 1.36 us: placed(): pl.pallas_call(functools.partial(place_kernel, cuts), in_specs=[pl.BlockS...]
    ppermute x18, waiting for transfers between devices: 15.3 us -> 13.9 us  [xored(): return lax.ppermute(block, axis, [(i, i ^ bits) for i in range(n)])]
    dot_general x1, matrix products: 1.34 us -> 0.3 us  [per_device(): out_vec = jnp.dot(cot, model_sketch[0], preferred_element_type=jnp.float32)]
    broadcast_in_dim x2 -> x1, other arithmetic: 1.6 us -> 0.76 us  [per_device(): return (handed[None], features[None])]
    dot_general x1, matrix products: 1.04 us -> 0.26 us  [per_device(): jnp.einsum('et,ta,tb->eab', member, sketch_sum[:, rank:], input_sketch[0]...]
    unnamed x32 -> x34, local copies, waits for them, and re-layouts: 4.41 us -> 4.38 us
  transfers between devices with their start and end apart: 20 -> 20, of which waited for: 10 -> 8; matrix products, arithmetic and copies ran while one was open for 8% -> 5% of each run, Pallas kernels for 33% -> 34%
where the time goes in v9:
time: 75.5 us; the launch traced here: 75.1 us
  Pallas kernels  27.1 us (36%)
  starting transfers between devices  21.5 us (28%)
  waiting for transfers between devices  17.7 us (23%)
  local copies, waits for them, and re-layouts  5.64 us (7%)
  other arithmetic  1.25 us (2%)
  between operations  1.08 us (1%)
  matrix products  0.82 us (1%)
    pallas_call x2, Pallas kernels, expert(): pl.pallas_call(functools.partial(expert_kernel, tile_f, tile_d), grid=(1,...  18.8 us
    ppermute x18, starting transfers between devices, xored(): return lax.ppermute(block, axis, [(i, i ^ bits) for i in range(n)])  18.5 us
    ppermute x18, waiting for transfers between devices, xored(): return lax.ppermute(block, axis, [(i, i ^ bits) for i in range(n)])  13.9 us
    pallas_call x1, Pallas kernels, slopes(): pl.pallas_call(functools.partial(slope_kernel, groups), grid_spec=pltpu.P...  6.27 us
    unnamed x34, local copies, waits for them, and re-layouts  4.38 us
    ppermute x2, waiting for transfers between devices, below(): lax.ppermute(block, 'section', [(s, (s - 1) % sections) for s in range(se...  3.73 us
    ppermute x2, starting transfers between devices, below(): lax.ppermute(block, 'section', [(s, (s - 1) % sections) for s in range(se...  3.06 us
  transfers between devices with their start and end apart: 20, of which 8 were waited for; matrix products, arithmetic and copies ran while one was open for 5% of the time, Pallas kernels for 34%

profile of v9, /device:TPU:0, one launch (start us, length us, event | category | flops | bytes accessed | tf_op | source)
XLA Modules:
  0.0 75.1 jit_solution(2400403763181157877)
XLA Ops:
  0.7 1.0 %dynamic-slice_bitcast_fusion = bf16[64,2048]{1,0:T(8,128)(2,1)S(1)} fusion(bf16[1,128,2048]{2,1,0:T(8,128)(2,1)} %param.10, s32[]{:T(128)S(6)} %select_n.32), kind=kLoop, calls=%fused_computation.7 | loop fusion | bytes 524292 | tf_op jit(solution)/shard_map/dynamic_slice | solution.py:341
  1.7 3.1 %collective-permute-start = (bf16[64,2048]{1,0:T(8,128)(2,1)S(1)}, bf16[64,2048]{1,0:T(8,128)(2,1)S(1)}, u32[]{:S(2)}, u32[]{:S(2)}) collective-permute-start(bf16[64,2048]{1,0:T(8,128)(2,1)S(1)} %dynamic-slice_bitcast_fusion), channel_id=1, source_target_pairs={{0,4},{4,0},{8,12},{12,8},{1,5},{5,1},{9,13},{13,9},{2,6},{6,2},{1... | collective-permute-start | bytes 786440 | tf_op jit(solution)/shard_map/ppermute | solution.py:17
  4.8 0.9 %constant_dynamic-update-slice_fusion.2 = (bf16[256,2048]{1,0:T(8,128)(2,1)S(1)}, bf16[32,2048]{1,0:T(8,128)(2,1)S(1)}) fusion(bf16[1,128,2048]{2,1,0:T(8,128)(2,1)} %param.10, s32[]{:T(128)S(6)} %select_n.32), kind=kLoop, calls=%fused_computation.37 | loop fusion | bytes 393220
  5.7 2.7 %collective-permute-start.1 = (bf16[32,2048]{1,0:T(8,128)(2,1)S(1)}, bf16[32,2048]{1,0:T(8,128)(2,1)S(1)}, u32[]{:S(2)}, u32[]{:S(2)}) collective-permute-start(bf16[32,2048]{1,0:T(8,128)(2,1)S(1)} %get-tuple-element.43.cot_ref), channel_id=1, source_target_pairs={{0,8},{4,12},{8,0},{12,4},{1,9},{5,13},{9,1},{13,5},{2,10},{6,14},... | collective-permute-start | bytes 393224 | tf_op jit(solution)/shard_map/ppermute | solution.py:17
  8.4 2.0 %copy-done.1 = bf16[1,1,4,128,3584]{4,3,2,1,0:T(8,128)(2,1)S(1)} copy-done((bf16[1,1,4,128,3584]{4,3,2,1,0:T(8,128)(2,1)S(1)}, bf16[1,1,4,128,3584]{4,3,2,1,0:T(8,128)(2,1)}, u32[]{:S(2)}) %copy-start.1) | copy-done | bytes 3670040
  10.5 1.0 %copy-done.2 = bf16[1,1,3584,64]{2,3,1,0:T(8,128)(2,1)S(1)} copy-done((bf16[1,1,3584,64]{2,3,1,0:T(8,128)(2,1)S(1)}, bf16[1,1,3584,64]{2,3,1,0:T(8,128)(2,1)}, u32[]{:S(2)}) %copy-start.2) | copy-done | bytes 458776
  11.5 6.3 %slopes.1 = (bf16[2,3584,256]{2,1,0:T(8,128)(2,1)S(1)}, f32[2,256,64]{2,1,0:T(8,128)S(1)}, bf16[3584,2048]{1,0:T(8,128)(2,1)S(1)}) custom-call(s32[2]{0:T(128)S(1)} %pad_add_fusion.index_ref, bf16[4,2,2,32,3584]{4,3,2,1,0:T(8,128)(2,1)S(1)} %bitcast.51, bf16[4,2,2,32,3584]{4,3,2,1,0:T(8,128)(2,1)S(1)} %bitcast.52, bf16[4,2,2,32,3584]{4,3,2,1,0:T(8,128)(2,1)S(1)} %bitcast.53, ...), custom_call_target="tpu_custom_call" | custom-call | flops 234881024 | bytes 7340032 | tf_op jit(solution)/shard_map/slopes/pallas_call | solution.py:179
  17.8 1.2 %collective-permute-done.2 = bf16[32,2048]{1,0:T(8,128)(2,1)S(1)} collective-permute-done((bf16[32,2048]{1,0:T(8,128)(2,1)S(1)}, bf16[32,2048]{1,0:T(8,128)(2,1)S(1)}, u32[]{:S(2)}, u32[]{:S(2)}) %collective-permute-start.2) | collective-permute-done | bytes 131104 | tf_op jit(solution)/shard_map/ppermute | solution.py:17
  19.2 2.7 %collective-permute-start.5 = (bf16[32,2048]{1,0:T(8,128)(2,1)S(1)}, bf16[32,2048]{1,0:T(8,128)(2,1)S(1)}, u32[]{:S(2)}, u32[]{:S(2)}) collective-permute-start(bf16[32,2048]{1,0:T(8,128)(2,1)S(1)} %held.6), channel_id=1, source_target_pairs={{0,12},{4,8},{8,4},{12,0},{1,13},{5,9},{9,5},{13,1},{2,14},{6,10},... | collective-permute-start | bytes 393224 | tf_op jit(solution)/shard_map/ppermute | solution.py:17
  22.5 9.4 %expert.2 = (f32[128,2176]{1,0:T(8,128)S(1)}, bf16[128,2176]{1,0:T(8,128)(2,1)S(1)}) custom-call(bf16[256,2048]{1,0:T(8,128)(2,1)S(1)} %slice_dynamic-update-slice_fusion.4.rows_ref, bf16[2,3584,256]{2,1,0:T(8,128)(2,1)S(1)} %get-tuple-element.21.slope_ref, f32[2,256,64]{2,1,0:T(8,128)S(1)} %get-tuple-element.22.down_part_ref, ...), custom_call_target="tpu_custom_call" | custom-call | flops 7516192768 | bytes 29360128 | tf_op jit(solution)/shard_map/expert/pallas_call | solution.py:267
  32.0 2.7 %collective-permute-done.6.block_ref = bf16[32,2048]{1,0:T(8,128)(2,1)S(1)} collective-permute-done((bf16[32,2048]{1,0:T(8,128)(2,1)S(1)}, bf16[32,2048]{1,0:T(8,128)(2,1)S(1)}, u32[]{:S(2)}, u32[]{:S(2)}) %collective-permute-start.6) | collective-permute-done | bytes 131104 | tf_op jit(solution)/shard_map/ppermute | solution.py:17
  35.1 2.5 %collective-permute-start.7 = (bf16[32,2176]{1,0:T(8,128)(2,1)S(1)}, bf16[32,2176]{1,0:T(8,128)(2,1)S(1)}, u32[]{:S(2)}, u32[]{:S(2)}) collective-permute-start(bf16[32,2176]{1,0:T(8,128)(2,1)S(1)} %get-tuple-element.27.refs_2_), channel_id=1, source_target_pairs={{0,12},{4,8},{8,4},{12,0},{1,13},{5,9},{9,5},{13,1},{2,14},{6,10},... | collective-permute-start | bytes 417800 | tf_op jit(solution)/shard_map/ppermute | solution.py:17
  37.6 1.9 %collective-permute-start.9 = (bf16[32,2176]{1,0:T(8,128)(2,1)S(1)}, bf16[32,2176]{1,0:T(8,128)(2,1)S(1)}, u32[]{:S(2)}, u32[]{:S(2)}) collective-permute-start(bf16[32,2176]{1,0:T(8,128)(2,1)S(1)} %get-tuple-element.29.refs_0_), channel_id=1, source_target_pairs={{0,4},{4,0},{8,12},{12,8},{1,5},{5,1},{9,13},{13,9},{2,6},{6,2},{1... | collective-permute-start | bytes 417800 | tf_op jit(solution)/shard_map/ppermute | solution.py:17
  39.6 9.4 %expert.3 = (f32[128,2176]{1,0:T(8,128)S(1)}, bf16[128,2176]{1,0:T(8,128)(2,1)S(1)}) custom-call(bf16[256,2048]{1,0:T(8,128)(2,1)S(1)} %slice_dynamic-update-slice_fusion.rows_ref, bf16[2,3584,256]{2,1,0:T(8,128)(2,1)S(1)} %get-tuple-element.21.slope_ref, f32[2,256,64]{2,1,0:T(8,128)S(1)} %get-tuple-element.22.down_part_ref, bf16[64,3584]{1,0:T(8,128)(2,1)S(1)} %bitcast.61, ...), custom_call_target="tpu_custom_call" | custom-call | flops 7516192768 | bytes 29360128 | tf_op jit(solution)/shard_map/expert/pallas_call | solution.py:267
  49.1 0.9 %collective-permute-done.8.refs_1_ = bf16[32,2176]{1,0:T(8,128)(2,1)S(1)} collective-permute-done((bf16[32,2176]{1,0:T(8,128)(2,1)S(1)}, bf16[32,2176]{1,0:T(8,128)(2,1)S(1)}, u32[]{:S(2)}, u32[]{:S(2)}) %collective-permute-start.8) | collective-permute-done | bytes 139296 | tf_op jit(solution)/shard_map/ppermute | solution.py:17
  50.6 1.5 %collective-permute-done.11.came_ref = bf16[128,2176]{1,0:T(8,128)(2,1)S(1)} collective-permute-done((bf16[128,2176]{1,0:T(8,128)(2,1)S(1)}, bf16[128,2176]{1,0:T(8,128)(2,1)S(1)}, u32[]{:S(2)}, u32[]{:S(2)}) %collective-permute-start.11) | collective-permute-done | bytes 557088 | tf_op jit(solution)/shard_map/ppermute | solution.py:17
  52.2 2.7 %collective-permute-start.12 = (bf16[32,2176]{1,0:T(8,128)(2,1)S(1)}, bf16[32,2176]{1,0:T(8,128)(2,1)S(1)}, u32[]{:S(2)}, u32[]{:S(2)}) collective-permute-start(bf16[32,2176]{1,0:T(8,128)(2,1)S(1)} %get-tuple-element.33), channel_id=1, source_target_pairs={{0,12},{4,8},{8,4},{12,0},{1,13},{5,9},{9,5},{13,1},{2,14},{6,10},... | collective-permute-start | bytes 417800 | tf_op jit(solution)/shard_map/ppermute | solution.py:17
  55.4 1.7 %collective-permute-start.15 = (bf16[32,2176]{1,0:T(8,128)(2,1)S(1)}, bf16[32,2176]{1,0:T(8,128)(2,1)S(1)}, u32[]{:S(2)}, u32[]{:S(2)}) collective-permute-start(bf16[32,2176]{1,0:T(8,128)(2,1)S(1)} %get-tuple-element.36), channel_id=1, source_target_pairs={{0,4},{4,0},{8,12},{12,8},{1,5},{5,1},{9,13},{13,9},{2,6},{6,2},{1... | collective-permute-start | bytes 417800 | tf_op jit(solution)/shard_map/ppermute | solution.py:17
  57.2 3.5 %collective-permute-done.12.refs_0_ = bf16[32,2176]{1,0:T(8,128)(2,1)S(1)} collective-permute-done((bf16[32,2176]{1,0:T(8,128)(2,1)S(1)}, bf16[32,2176]{1,0:T(8,128)(2,1)S(1)}, u32[]{:S(2)}, u32[]{:S(2)}) %collective-permute-start.12) | collective-permute-done | bytes 139296 | tf_op jit(solution)/shard_map/ppermute | solution.py:17
  60.7 1.6 %collective-permute-start.13 = (bf16[32,2048]{1,0:T(8,128)(2,1)S(1)}, bf16[32,2048]{1,0:T(8,128)(2,1)S(1)}, u32[]{:S(2)}, u32[]{:S(2)}) collective-permute-start(bf16[32,2048]{1,0:T(8,128)(2,1)S(1)} %held.11), channel_id=1, source_target_pairs={{0,2},{2,0},{1,3},{3,1},{4,6},{6,4},{5,7},{7,5},{8,10},{10,8},{9,1... | collective-permute-start | bytes 393224 | tf_op jit(solution)/shard_map/ppermute | solution.py:329
  62.3 3.8 %collective-permute-done.14.refs_1_ = bf16[32,2176]{1,0:T(8,128)(2,1)S(1)} collective-permute-done((bf16[32,2176]{1,0:T(8,128)(2,1)S(1)}, bf16[32,2176]{1,0:T(8,128)(2,1)S(1)}, u32[]{:S(2)}, u32[]{:S(2)}) %collective-permute-start.14) | collective-permute-done | bytes 139296 | tf_op jit(solution)/shard_map/ppermute | solution.py:17
  66.5 1.5 %collective-permute-start.16 = (bf16[32,2048]{1,0:T(8,128)(2,1)S(1)}, bf16[32,2048]{1,0:T(8,128)(2,1)S(1)}, u32[]{:S(2)}, u32[]{:S(2)}) collective-permute-start(bf16[32,2048]{1,0:T(8,128)(2,1)S(1)} %get-tuple-element.37), channel_id=1, source_target_pairs={{0,2},{2,0},{1,3},{3,1},{4,6},{6,4},{5,7},{7,5},{8,10},{10,8},{9,1... | collective-permute-start | bytes 393224 | tf_op jit(solution)/shard_map/ppermute | solution.py:329
  68.7 3.7 %collective-permute-done.16.refs_1_ = bf16[32,2048]{1,0:T(8,128)(2,1)S(1)} collective-permute-done((bf16[32,2048]{1,0:T(8,128)(2,1)S(1)}, bf16[32,2048]{1,0:T(8,128)(2,1)S(1)}, u32[]{:S(2)}, u32[]{:S(2)}) %collective-permute-start.16) | collective-permute-done | bytes 131104 | tf_op jit(solution)/shard_map/ppermute | solution.py:329
  73.8 1.4 %place.1 = bf16[128,2048]{1,0:T(8,128)(2,1)} custom-call(s32[2]{0:T(128)S(1)} %pad_add_fusion.index_ref, bf16[32,2048]{1,0:T(8,128)(2,1)S(1)} %collective-permute-done.13.refs_3_.refs_0_, bf16[32,2048]{1,0:T(8,128)(2,1)S(1)} %collective-permute-done.16.refs_1_, bf16[32,2048]{1,0:T(8,128)(2,1)S(1)} %collective-permute-done.17.refs_2_, ...), custom_call_target="tpu_custom_call" | custom-call | tf_op jit(solution)/shard_map/place/pallas_call | solution.py:115
  (85 shorter events, 4.9 us)
Async XLA Ops:
  0.6 49.7 %copy-start = (bf16[1,2048,64]{1,2,0:T(8,128)(2,1)S(1)}, bf16[1,2048,64]{1,2,0:T(8,128)(2,1)}, u32[]{:S(2)}) copy-start(bf16[1,2048,64]{1,2,0:T(8,128)(2,1)} %param.17) | copy-start | bytes 786436
  1.7 17.3 %collective-permute-start = (bf16[64,2048]{1,0:T(8,128)(2,1)S(1)}, bf16[64,2048]{1,0:T(8,128)(2,1)S(1)}, u32[]{:S(2)}, u32[]{:S(2)}) collective-permute-start(bf16[64,2048]{1,0:T(8,128)(2,1)S(1)} %dynamic-slice_bitcast_fusion), channel_id=1, source_target_pairs={{0,4},{4,0},{8,12},{12,8},{1,5},{5,1},{9,13},{13,9},{2,6},{6,2},{1... | collective-permute-start | bytes 786440 | tf_op jit(solution)/shard_map/ppermute | solution.py:17
  5.7 12.1 %collective-permute-start.1 = (bf16[32,2048]{1,0:T(8,128)(2,1)S(1)}, bf16[32,2048]{1,0:T(8,128)(2,1)S(1)}, u32[]{:S(2)}, u32[]{:S(2)}) collective-permute-start(bf16[32,2048]{1,0:T(8,128)(2,1)S(1)} %get-tuple-element.43.cot_ref), channel_id=1, source_target_pairs={{0,8},{4,12},{8,0},{12,4},{1,9},{5,13},{9,1},{13,5},{2,10},{6,14},... | collective-permute-start | bytes 393224 | tf_op jit(solution)/shard_map/ppermute | solution.py:17
  8.3 10.6 %collective-permute-start.2 = (bf16[32,2048]{1,0:T(8,128)(2,1)S(1)}, bf16[32,2048]{1,0:T(8,128)(2,1)S(1)}, u32[]{:S(2)}, u32[]{:S(2)}) collective-permute-start(bf16[32,2048]{1,0:T(8,128)(2,1)S(1)} %get-tuple-element.43.cot_ref), channel_id=1, source_target_pairs={{0,12},{4,8},{8,4},{12,0},{1,13},{5,9},{9,5},{13,1},{2,14},{6,10},... | collective-permute-start | bytes 393224 | tf_op jit(solution)/shard_map/ppermute | solution.py:17
  19.0 3.4 %collective-permute-start.3 = (bf16[128,2048]{1,0:T(8,128)(2,1)S(1)}, bf16[128,2048]{1,0:T(8,128)(2,1)S(1)}, u32[]{:S(2)}, u32[]{:S(2)}) collective-permute-start(bf16[128,2048]{1,0:T(8,128)(2,1)S(1)} %pad_maximum_fusion), channel_id=1, source_target_pairs={{0,1},{1,0},{2,3},{3,2},{4,5},{5,4},{6,7},{7,6},{8,9},{9,8},{10,11... | collective-permute-start | bytes 1572872 | tf_op jit(solution)/shard_map/ppermute | solution.py:17
  19.2 15.5 %collective-permute-start.5 = (bf16[32,2048]{1,0:T(8,128)(2,1)S(1)}, bf16[32,2048]{1,0:T(8,128)(2,1)S(1)}, u32[]{:S(2)}, u32[]{:S(2)}) collective-permute-start(bf16[32,2048]{1,0:T(8,128)(2,1)S(1)} %held.6), channel_id=1, source_target_pairs={{0,12},{4,8},{8,4},{12,0},{1,13},{5,9},{9,5},{13,1},{2,14},{6,10},... | collective-permute-start | bytes 393224 | tf_op jit(solution)/shard_map/ppermute | solution.py:17
  21.9 12.8 %collective-permute-start.6 = (bf16[32,2048]{1,0:T(8,128)(2,1)S(1)}, bf16[32,2048]{1,0:T(8,128)(2,1)S(1)}, u32[]{:S(2)}, u32[]{:S(2)}) collective-permute-start(bf16[32,2048]{1,0:T(8,128)(2,1)S(1)} %held.6), channel_id=1, source_target_pairs={{0,8},{4,12},{8,0},{12,4},{1,9},{5,13},{9,1},{13,5},{2,10},{6,14},... | collective-permute-start | bytes 393224 | tf_op jit(solution)/shard_map/ppermute | solution.py:17
  31.9 2.9 %collective-permute-start.4 = (bf16[128,2176]{1,0:T(8,128)(2,1)S(1)}, bf16[128,2176]{1,0:T(8,128)(2,1)S(1)}, u32[]{:S(2)}, u32[]{:S(2)}) collective-permute-start(bf16[128,2176]{1,0:T(8,128)(2,1)S(1)} %get-tuple-element.25), channel_id=1, source_target_pairs={{0,1},{1,0},{2,3},{3,2},{4,5},{5,4},{6,7},{7,6},{8,9},{9,8},{10,11... | collective-permute-start | bytes 1671176 | tf_op jit(solution)/shard_map/ppermute | solution.py:17
  35.0 4.6 %collective-permute-start.10 = (bf16[64,2048]{1,0:T(8,128)(2,1)S(1)}, bf16[64,2048]{1,0:T(8,128)(2,1)S(1)}, u32[]{:S(2)}, u32[]{:S(2)}) collective-permute-start(bf16[64,2048]{1,0:T(8,128)(2,1)S(1)} %held.9), channel_id=1, source_target_pairs={{0,1},{1,0},{2,3},{3,2},{4,5},{5,4},{6,7},{7,6},{8,9},{9,8},{10,11... | collective-permute-start | bytes 786440 | tf_op jit(solution)/shard_map/ppermute | solution.py:17
  35.1 14.0 %collective-permute-start.7 = (bf16[32,2176]{1,0:T(8,128)(2,1)S(1)}, bf16[32,2176]{1,0:T(8,128)(2,1)S(1)}, u32[]{:S(2)}, u32[]{:S(2)}) collective-permute-start(bf16[32,2176]{1,0:T(8,128)(2,1)S(1)} %get-tuple-element.27.refs_2_), channel_id=1, source_target_pairs={{0,12},{4,8},{8,4},{12,0},{1,13},{5,9},{9,5},{13,1},{2,14},{6,10},... | collective-permute-start | bytes 417800 | tf_op jit(solution)/shard_map/ppermute | solution.py:17
  37.6 12.3 %collective-permute-start.8 = (bf16[32,2176]{1,0:T(8,128)(2,1)S(1)}, bf16[32,2176]{1,0:T(8,128)(2,1)S(1)}, u32[]{:S(2)}, u32[]{:S(2)}) collective-permute-start(bf16[32,2176]{1,0:T(8,128)(2,1)S(1)} %get-tuple-element.28.refs_1_), channel_id=1, source_target_pairs={{0,8},{4,12},{8,0},{12,4},{1,9},{5,13},{9,1},{13,5},{2,10},{6,14},... | collective-permute-start | bytes 417800 | tf_op jit(solution)/shard_map/ppermute | solution.py:17
  37.6 12.3 %collective-permute-start.9 = (bf16[32,2176]{1,0:T(8,128)(2,1)S(1)}, bf16[32,2176]{1,0:T(8,128)(2,1)S(1)}, u32[]{:S(2)}, u32[]{:S(2)}) collective-permute-start(bf16[32,2176]{1,0:T(8,128)(2,1)S(1)} %get-tuple-element.29.refs_0_), channel_id=1, source_target_pairs={{0,4},{4,0},{8,12},{12,8},{1,5},{5,1},{9,13},{13,9},{2,6},{6,2},{1... | collective-permute-start | bytes 417800 | tf_op jit(solution)/shard_map/ppermute | solution.py:17
  39.6 10.5 %copy-start.6 = (f32[1,128,2]{1,2,0:T(2,128)S(1)}, f32[1,128,2]{1,2,0:T(2,128)}, u32[]{:S(2)}) copy-start(f32[1,128,2]{1,2,0:T(2,128)} %param.12) | copy-start | bytes 3076
  39.6 10.6 %copy-start.7 = (s32[1,1,2]{2,1,0:T(1,128)S(1)}, s32[1,1,2]{2,1,0:T(1,128)}, u32[]{:S(2)}) copy-start(s32[1,1,2]{2,1,0:T(1,128)} %param.11) | copy-start | bytes 28
  49.0 19.4 %copy-start.5 = (f32[1,128,64]{1,2,0:T(8,128)S(1)}, f32[1,128,64]{1,2,0:T(8,128)}, u32[]{:S(2)}) copy-start(f32[1,128,64]{1,2,0:T(8,128)} %param.16) | copy-start | bytes 98308
  50.0 2.0 %collective-permute-start.11 = (bf16[128,2176]{1,0:T(8,128)(2,1)S(1)}, bf16[128,2176]{1,0:T(8,128)(2,1)S(1)}, u32[]{:S(2)}, u32[]{:S(2)}) collective-permute-start(bf16[128,2176]{1,0:T(8,128)(2,1)S(1)} %held.10), channel_id=1, source_target_pairs={{0,1},{1,0},{2,3},{3,2},{4,5},{5,4},{6,7},{7,6},{8,9},{9,8},{10,11... | collective-permute-start | bytes 1671176 | tf_op jit(solution)/shard_map/ppermute | solution.py:17
  52.2 8.5 %collective-permute-start.12 = (bf16[32,2176]{1,0:T(8,128)(2,1)S(1)}, bf16[32,2176]{1,0:T(8,128)(2,1)S(1)}, u32[]{:S(2)}, u32[]{:S(2)}) collective-permute-start(bf16[32,2176]{1,0:T(8,128)(2,1)S(1)} %get-tuple-element.33), channel_id=1, source_target_pairs={{0,12},{4,8},{8,4},{12,0},{1,13},{5,9},{9,5},{13,1},{2,14},{6,10},... | collective-permute-start | bytes 417800 | tf_op jit(solution)/shard_map/ppermute | solution.py:17
  55.3 10.8 %collective-permute-start.14 = (bf16[32,2176]{1,0:T(8,128)(2,1)S(1)}, bf16[32,2176]{1,0:T(8,128)(2,1)S(1)}, u32[]{:S(2)}, u32[]{:S(2)}) collective-permute-start(bf16[32,2176]{1,0:T(8,128)(2,1)S(1)} %get-tuple-element.35), channel_id=1, source_target_pairs={{0,8},{4,12},{8,0},{12,4},{1,9},{5,13},{9,1},{13,5},{2,10},{6,14},... | collective-permute-start | bytes 417800 | tf_op jit(solution)/shard_map/ppermute | solution.py:17
  55.4 10.7 %collective-permute-start.15 = (bf16[32,2176]{1,0:T(8,128)(2,1)S(1)}, bf16[32,2176]{1,0:T(8,128)(2,1)S(1)}, u32[]{:S(2)}, u32[]{:S(2)}) collective-permute-start(bf16[32,2176]{1,0:T(8,128)(2,1)S(1)} %get-tuple-element.36), channel_id=1, source_target_pairs={{0,4},{4,0},{8,12},{12,8},{1,5},{5,1},{9,13},{13,9},{2,6},{6,2},{1... | collective-permute-start | bytes 417800 | tf_op jit(solution)/shard_map/ppermute | solution.py:17
  60.7 5.5 %collective-permute-start.13 = (bf16[32,2048]{1,0:T(8,128)(2,1)S(1)}, bf16[32,2048]{1,0:T(8,128)(2,1)S(1)}, u32[]{:S(2)}, u32[]{:S(2)}) collective-permute-start(bf16[32,2048]{1,0:T(8,128)(2,1)S(1)} %held.11), channel_id=1, source_target_pairs={{0,2},{2,0},{1,3},{3,1},{4,6},{6,4},{5,7},{7,5},{8,10},{10,8},{9,1... | collective-permute-start | bytes 393224 | tf_op jit(solution)/shard_map/ppermute | solution.py:329
  66.4 1.9 %collective-permute-start.19 = (f32[64,128]{1,0:T(8,128)S(1)}, f32[64,128]{1,0:T(8,128)S(1)}, u32[]{:S(2)}, u32[]{:S(2)}) collective-permute-start(f32[64,128]{1,0:T(8,128)S(1)} %constant_dynamic-update-slice_fusion.6), channel_id=1, source_target_pairs={{0,1},{1,0},{2,3},{3,2},{4,5},{5,4},{6,7},{7,6},{8,9},{9,8},{10,11... | collective-permute-start | bytes 98312 | tf_op jit(solution)/shard_map/ppermute | solution.py:17
  66.5 5.9 %collective-permute-start.16 = (bf16[32,2048]{1,0:T(8,128)(2,1)S(1)}, bf16[32,2048]{1,0:T(8,128)(2,1)S(1)}, u32[]{:S(2)}, u32[]{:S(2)}) collective-permute-start(bf16[32,2048]{1,0:T(8,128)(2,1)S(1)} %get-tuple-element.37), channel_id=1, source_target_pairs={{0,2},{2,0},{1,3},{3,1},{4,6},{6,4},{5,7},{7,5},{8,10},{10,8},{9,1... | collective-permute-start | bytes 393224 | tf_op jit(solution)/shard_map/ppermute | solution.py:329
  68.0 5.4 %collective-permute-start.17 = (bf16[32,2048]{1,0:T(8,128)(2,1)S(1)}, bf16[32,2048]{1,0:T(8,128)(2,1)S(1)}, u32[]{:S(2)}, u32[]{:S(2)}) collective-permute-start(bf16[32,2048]{1,0:T(8,128)(2,1)S(1)} %collective-permute-done.13.refs_3_.refs_0_), channel_id=1, source_target_pairs={{0,1},{1,0},{2,3},{3,2},{4,5},{5,4},{6,7},{7,6},{8,9},{9,8},{10,11... | collective-permute-start | bytes 393224 | tf_op jit(solution)/shard_map/ppermute | solution.py:17
  72.4 1.3 %collective-permute-start.18 = (bf16[32,2048]{1,0:T(8,128)(2,1)S(1)}, bf16[32,2048]{1,0:T(8,128)(2,1)S(1)}, u32[]{:S(2)}, u32[]{:S(2)}) collective-permute-start(bf16[32,2048]{1,0:T(8,128)(2,1)S(1)} %collective-permute-done.16.refs_1_), channel_id=1, source_target_pairs={{0,1},{1,0},{2,3},{3,2},{4,5},{5,4},{6,7},{7,6},{8,9},{9,8},{10,11... | collective-permute-start | bytes 393224 | tf_op jit(solution)/shard_map/ppermute | solution.py:17
  (5 other events, 21.5 us)

commit v10 on v7

--- a/solution.py
+++ b/solution.py
@@ -36,7 +36,8 @@
     )(block, *events)
 
 
-def merge_kernel(keep_ref, came_ref, own_ref, *sent_refs):
+def merge_kernel(others, keep_ref, came_ref, *refs):
+    own_ref, *sent_refs = refs[-1 - others :]
     rows = own_ref.shape[0]
     own_ref[...] = keep_ref[:rows] + came_ref[:rows].astype(jnp.float32)
     for at, sent_ref in enumerate(sent_refs):
@@ -45,12 +46,12 @@
         sent_ref[...] = total.astype(jnp.bfloat16)
 
 
-def merged(keep, came, rows):
+def merged(keep, came, rows, *events):
     count, wide = keep.shape
     others = count // rows - 1
     return pl.pallas_call(
-        merge_kernel,
-        in_specs=[RESIDENT] * 2,
+        functools.partial(merge_kernel, others),
+        in_specs=[RESIDENT] * 2 + [ANYWHERE] * len(events),
         out_specs=[RESIDENT] * (1 + others),
         out_shape=[jax.ShapeDtypeStruct((rows, wide), jnp.float32)]
         + [jax.ShapeDtypeStruct((rows, wide), jnp.bfloat16)] * others,
@@ -59,7 +60,7 @@
             flops=count * wide, bytes_accessed=8 * count * wide, transcendentals=0
         ),
         name="merge",
-    )(keep, came)
+    )(keep, came, *events)
 
 
 def finish_kernel(slots, own_ref, cot_ref, weight_ref, *refs):
@@ -338,10 +339,10 @@
         if a + 1 < CHUNKS:
             coming = held(cot_mine[(a + 1) * rows : (a + 2) * rows], near_rows)
             fetched = {slot: held(xored(coming, "dp", slot), kept) for slot in order}
-            give = held(give, *fetched.values(), *backs)
+            late = tuple(fetched.values())
         else:
-            give = held(give, *backs)
-        own, *sent = merged(kept, xored(give, "tensor", 1), rows)
+            give, late = held(give, *backs), ()
+        own, *sent = merged(kept, xored(give, "tensor", 1), rows, *late)
         backs = [xored(out, "dp", slot + 1) for slot, out in enumerate(sent)][::-1]
         if grad:
             passed = (below(held(*grad, backs[0])),)
@@ -351,11 +352,10 @@
         vectors.append(vec)
     below_mine.append(below(*grad))
 
-    mine = jnp.concatenate(below_mine, axis=0)
-    theirs = jnp.concatenate([xored(f, "tensor", 1) for f in below_mine], axis=0)
-    handed = jnp.concatenate(
-        [jnp.where(core == 0, mine, theirs), jnp.where(core == 0, theirs, mine)], axis=0
-    )
+    theirs = [xored(block, "tensor", 1) for block in below_mine]
+    first = [jnp.where(core == 0, m, t) for m, t in zip(below_mine, theirs)]
+    second = [jnp.where(core == 0, t, m) for m, t in zip(below_mine, theirs)]
+    handed = jnp.concatenate(first + second, axis=0)
 
     vec_mine = jnp.concatenate(vectors, axis=0)
     vec_theirs = xored(vec_mine, "tensor", 1)

time: 76.1 us -> 74.9 us (0.984)
  matrix products: 2.64 us -> 0.82 us
  waiting for transfers between devices: 15.6 us -> 16.6 us
    ppermute x2, waiting for transfers between devices: 0.3 us -> 2.71 us  [below(): lax.ppermute(block, 'section', [(s, (s - 1) % sections) for s in range(se...]
    ppermute x18, waiting for transfers between devices: 15.3 us -> 13.9 us  [xored(): return lax.ppermute(block, axis, [(i, i ^ bits) for i in range(n)])]
    dot_general x1, matrix products: 1.34 us -> 0.3 us  [per_device(): out_vec = jnp.dot(cot, model_sketch[0], preferred_element_type=jnp.float32)]
    dot_general x1, matrix products: 1.04 us -> 0.26 us  [per_device(): jnp.einsum('et,ta,tb->eab', member, sketch_sum[:, rank:], input_sketch[0]...]
    unnamed x32 -> x34, local copies, waits for them, and re-layouts: 4.41 us -> 4.38 us
  transfers between devices with their start and end apart: 20 -> 20, of which waited for: 10 -> 8; matrix products, arithmetic and copies ran while one was open for 8% -> 5% of each run, Pallas kernels for 33% -> 34%
where the time goes in v10:
time: 74.9 us; the launch traced here: 74.6 us
  Pallas kernels  25.8 us (34%)
  starting transfers between devices  22.6 us (30%)
  waiting for transfers between devices  16.6 us (22%)
  local copies, waits for them, and re-layouts  5.63 us (8%)
  other arithmetic  2.14 us (3%)
  between operations  1.07 us (1%)
  matrix products  0.82 us (1%)
    ppermute x18, starting transfers between devices, xored(): return lax.ppermute(block, axis, [(i, i ^ bits) for i in range(n)])  19.5 us
    pallas_call x2, Pallas kernels, expert(): pl.pallas_call(functools.partial(expert_kernel, tile_f, tile_d), grid=(1,...  18.8 us
    ppermute x18, waiting for transfers between devices, xored(): return lax.ppermute(block, axis, [(i, i ^ bits) for i in range(n)])  13.9 us
    pallas_call x1, Pallas kernels, slopes(): pl.pallas_call(functools.partial(slope_kernel, groups), grid_spec=pltpu.P...  6.27 us
    unnamed x34, local copies, waits for them, and re-layouts  4.38 us
    ppermute x2, starting transfers between devices, below(): lax.ppermute(block, 'section', [(s, (s - 1) % sections) for s in range(se...  3.06 us
    ppermute x2, waiting for transfers between devices, below(): lax.ppermute(block, 'section', [(s, (s - 1) % sections) for s in range(se...  2.71 us
    broadcast_in_dim x2, other arithmetic, per_device(): return (handed[None], features[None])  1.6 us
  transfers between devices with their start and end apart: 20, of which 8 were waited for; matrix products, arithmetic and copies ran while one was open for 5% of the time, Pallas kernels for 34%

profile of v10, /device:TPU:0, one launch (start us, length us, event | category | flops | bytes accessed | tf_op | source)
XLA Modules:
  0.0 74.6 jit_solution(16519697999737839569)
XLA Ops:
  0.7 1.0 %dynamic-slice_bitcast_fusion = bf16[64,2048]{1,0:T(8,128)(2,1)S(1)} fusion(bf16[1,128,2048]{2,1,0:T(8,128)(2,1)} %param.10, s32[]{:T(128)S(6)} %select_n.53), kind=kLoop, calls=%fused_computation.8 | loop fusion | bytes 524292 | tf_op jit(solution)/shard_map/dynamic_slice | solution.py:311
  1.7 3.1 %collective-permute-start = (bf16[64,2048]{1,0:T(8,128)(2,1)S(1)}, bf16[64,2048]{1,0:T(8,128)(2,1)S(1)}, u32[]{:S(2)}, u32[]{:S(2)}) collective-permute-start(bf16[64,2048]{1,0:T(8,128)(2,1)S(1)} %dynamic-slice_bitcast_fusion), channel_id=1, source_target_pairs={{0,4},{4,0},{8,12},{12,8},{1,5},{5,1},{9,13},{13,9},{2,6},{6,2},{1... | collective-permute-start | bytes 786440 | tf_op jit(solution)/shard_map/ppermute | solution.py:17
  4.8 0.9 %constant_dynamic-update-slice_fusion.2 = (bf16[256,2048]{1,0:T(8,128)(2,1)S(1)}, bf16[32,2048]{1,0:T(8,128)(2,1)S(1)}) fusion(bf16[1,128,2048]{2,1,0:T(8,128)(2,1)} %param.10, s32[]{:T(128)S(6)} %select_n.53), kind=kLoop, calls=%fused_computation.42 | loop fusion | bytes 393220
  5.7 2.7 %collective-permute-start.1 = (bf16[32,2048]{1,0:T(8,128)(2,1)S(1)}, bf16[32,2048]{1,0:T(8,128)(2,1)S(1)}, u32[]{:S(2)}, u32[]{:S(2)}) collective-permute-start(bf16[32,2048]{1,0:T(8,128)(2,1)S(1)} %get-tuple-element.41.cot_ref), channel_id=1, source_target_pairs={{0,8},{4,12},{8,0},{12,4},{1,9},{5,13},{9,1},{13,5},{2,10},{6,14},... | collective-permute-start | bytes 393224 | tf_op jit(solution)/shard_map/ppermute | solution.py:17
  8.4 2.0 %copy-done.1 = bf16[1,1,4,128,3584]{4,3,2,1,0:T(8,128)(2,1)S(1)} copy-done((bf16[1,1,4,128,3584]{4,3,2,1,0:T(8,128)(2,1)S(1)}, bf16[1,1,4,128,3584]{4,3,2,1,0:T(8,128)(2,1)}, u32[]{:S(2)}) %copy-start.1) | copy-done | bytes 3670040
  10.5 1.0 %copy-done.2 = bf16[1,1,3584,64]{2,3,1,0:T(8,128)(2,1)S(1)} copy-done((bf16[1,1,3584,64]{2,3,1,0:T(8,128)(2,1)S(1)}, bf16[1,1,3584,64]{2,3,1,0:T(8,128)(2,1)}, u32[]{:S(2)}) %copy-start.2) | copy-done | bytes 458776
  11.5 6.3 %slopes.1 = (bf16[2,3584,256]{2,1,0:T(8,128)(2,1)S(1)}, f32[2,256,64]{2,1,0:T(8,128)S(1)}, bf16[3584,2048]{1,0:T(8,128)(2,1)S(1)}) custom-call(s32[2]{0:T(128)S(1)} %pad_add_fusion.index_ref, bf16[4,2,2,32,3584]{4,3,2,1,0:T(8,128)(2,1)S(1)} %bitcast.52, bf16[4,2,2,32,3584]{4,3,2,1,0:T(8,128)(2,1)S(1)} %bitcast.53, bf16[4,2,2,32,3584]{4,3,2,1,0:T(8,128)(2,1)S(1)} %bitcast.54, ...), custom_call_target="tpu_custom_call" | custom-call | flops 234881024 | bytes 7340032 | tf_op jit(solution)/shard_map/slopes/pallas_call | solution.py:149
  17.8 1.2 %collective-permute-done.2 = bf16[32,2048]{1,0:T(8,128)(2,1)S(1)} collective-permute-done((bf16[32,2048]{1,0:T(8,128)(2,1)S(1)}, bf16[32,2048]{1,0:T(8,128)(2,1)S(1)}, u32[]{:S(2)}, u32[]{:S(2)}) %collective-permute-start.2) | collective-permute-done | bytes 131104 | tf_op jit(solution)/shard_map/ppermute | solution.py:17
  19.2 2.7 %collective-permute-start.6 = (bf16[32,2048]{1,0:T(8,128)(2,1)S(1)}, bf16[32,2048]{1,0:T(8,128)(2,1)S(1)}, u32[]{:S(2)}, u32[]{:S(2)}) collective-permute-start(bf16[32,2048]{1,0:T(8,128)(2,1)S(1)} %held.6), channel_id=1, source_target_pairs={{0,8},{4,12},{8,0},{12,4},{1,9},{5,13},{9,1},{13,5},{2,10},{6,14},... | collective-permute-start | bytes 393224 | tf_op jit(solution)/shard_map/ppermute | solution.py:17
  22.0 1.3 %collective-permute-start.5 = (bf16[32,2048]{1,0:T(8,128)(2,1)S(1)}, bf16[32,2048]{1,0:T(8,128)(2,1)S(1)}, u32[]{:S(2)}, u32[]{:S(2)}) collective-permute-start(bf16[32,2048]{1,0:T(8,128)(2,1)S(1)} %held.6), channel_id=1, source_target_pairs={{0,12},{4,8},{8,4},{12,0},{1,13},{5,9},{9,5},{13,1},{2,14},{6,10},... | collective-permute-start | bytes 393224 | tf_op jit(solution)/shard_map/ppermute | solution.py:17
  23.4 9.4 %expert.2 = (f32[128,2176]{1,0:T(8,128)S(1)}, bf16[128,2176]{1,0:T(8,128)(2,1)S(1)}) custom-call(bf16[256,2048]{1,0:T(8,128)(2,1)S(1)} %slice_dynamic-update-slice_fusion.4.rows_ref, bf16[2,3584,256]{2,1,0:T(8,128)(2,1)S(1)} %get-tuple-element.21.slope_ref, f32[2,256,64]{2,1,0:T(8,128)S(1)} %get-tuple-element.22.down_part_ref, ...), custom_call_target="tpu_custom_call" | custom-call | flops 7516192768 | bytes 29360128 | tf_op jit(solution)/shard_map/expert/pallas_call | solution.py:237
  33.1 1.8 %collective-permute-done.4.came_ref = bf16[128,2176]{1,0:T(8,128)(2,1)S(1)} collective-permute-done((bf16[128,2176]{1,0:T(8,128)(2,1)S(1)}, bf16[128,2176]{1,0:T(8,128)(2,1)S(1)}, u32[]{:S(2)}, u32[]{:S(2)}) %collective-permute-start.4) | collective-permute-done | bytes 557088 | tf_op jit(solution)/shard_map/ppermute | solution.py:17
  35.2 2.6 %collective-permute-start.7 = (bf16[32,2176]{1,0:T(8,128)(2,1)S(1)}, bf16[32,2176]{1,0:T(8,128)(2,1)S(1)}, u32[]{:S(2)}, u32[]{:S(2)}) collective-permute-start(bf16[32,2176]{1,0:T(8,128)(2,1)S(1)} %get-tuple-element.27.refs_2_), channel_id=1, source_target_pairs={{0,12},{4,8},{8,4},{12,0},{1,13},{5,9},{9,5},{13,1},{2,14},{6,10},... | collective-permute-start | bytes 417800 | tf_op jit(solution)/shard_map/ppermute | solution.py:17
  37.8 1.9 %collective-permute-start.9 = (bf16[32,2176]{1,0:T(8,128)(2,1)S(1)}, bf16[32,2176]{1,0:T(8,128)(2,1)S(1)}, u32[]{:S(2)}, u32[]{:S(2)}) collective-permute-start(bf16[32,2176]{1,0:T(8,128)(2,1)S(1)} %get-tuple-element.29.refs_0_), channel_id=1, source_target_pairs={{0,4},{4,0},{8,12},{12,8},{1,5},{5,1},{9,13},{13,9},{2,6},{6,2},{1... | collective-permute-start | bytes 417800 | tf_op jit(solution)/shard_map/ppermute | solution.py:17
  39.7 9.4 %expert.3 = (f32[128,2176]{1,0:T(8,128)S(1)}, bf16[128,2176]{1,0:T(8,128)(2,1)S(1)}) custom-call(bf16[256,2048]{1,0:T(8,128)(2,1)S(1)} %slice_dynamic-update-slice_fusion.rows_ref, bf16[2,3584,256]{2,1,0:T(8,128)(2,1)S(1)} %get-tuple-element.21.slope_ref, f32[2,256,64]{2,1,0:T(8,128)S(1)} %get-tuple-element.22.down_part_ref, bf16[64,3584]{1,0:T(8,128)(2,1)S(1)} %bitcast.62, ...), custom_call_target="tpu_custom_call" | custom-call | flops 7516192768 | bytes 29360128 | tf_op jit(solution)/shard_map/expert/pallas_call | solution.py:237
  50.6 1.5 %collective-permute-done.11.came_ref = bf16[128,2176]{1,0:T(8,128)(2,1)S(1)} collective-permute-done((bf16[128,2176]{1,0:T(8,128)(2,1)S(1)}, bf16[128,2176]{1,0:T(8,128)(2,1)S(1)}, u32[]{:S(2)}, u32[]{:S(2)}) %collective-permute-start.11) | collective-permute-done | bytes 557088 | tf_op jit(solution)/shard_map/ppermute | solution.py:17
  52.2 2.7 %collective-permute-start.12 = (bf16[32,2176]{1,0:T(8,128)(2,1)S(1)}, bf16[32,2176]{1,0:T(8,128)(2,1)S(1)}, u32[]{:S(2)}, u32[]{:S(2)}) collective-permute-start(bf16[32,2176]{1,0:T(8,128)(2,1)S(1)} %get-tuple-element.33), channel_id=1, source_target_pairs={{0,12},{4,8},{8,4},{12,0},{1,13},{5,9},{9,5},{13,1},{2,14},{6,10},... | collective-permute-start | bytes 417800 | tf_op jit(solution)/shard_map/ppermute | solution.py:17
  55.4 1.8 %collective-permute-start.16 = (bf16[32,2176]{1,0:T(8,128)(2,1)S(1)}, bf16[32,2176]{1,0:T(8,128)(2,1)S(1)}, u32[]{:S(2)}, u32[]{:S(2)}) collective-permute-start(bf16[32,2176]{1,0:T(8,128)(2,1)S(1)} %get-tuple-element.36), channel_id=1, source_target_pairs={{0,4},{4,0},{8,12},{12,8},{1,5},{5,1},{9,13},{13,9},{2,6},{6,2},{1... | collective-permute-start | bytes 417800 | tf_op jit(solution)/shard_map/ppermute | solution.py:17
  57.2 3.5 %collective-permute-done.12.refs_0_ = bf16[32,2176]{1,0:T(8,128)(2,1)S(1)} collective-permute-done((bf16[32,2176]{1,0:T(8,128)(2,1)S(1)}, bf16[32,2176]{1,0:T(8,128)(2,1)S(1)}, u32[]{:S(2)}, u32[]{:S(2)}) %collective-permute-start.12) | collective-permute-done | bytes 139296 | tf_op jit(solution)/shard_map/ppermute | solution.py:17
  60.7 1.6 %collective-permute-start.13 = (bf16[32,2048]{1,0:T(8,128)(2,1)S(1)}, bf16[32,2048]{1,0:T(8,128)(2,1)S(1)}, u32[]{:S(2)}, u32[]{:S(2)}) collective-permute-start(bf16[32,2048]{1,0:T(8,128)(2,1)S(1)} %held.11), channel_id=1, source_target_pairs={{0,2},{2,0},{1,3},{3,1},{4,6},{6,4},{5,7},{7,5},{8,10},{10,8},{9,1... | collective-permute-start | bytes 393224 | tf_op jit(solution)/shard_map/ppermute | solution.py:299
  62.3 3.8 %collective-permute-done.15.refs_1_ = bf16[32,2176]{1,0:T(8,128)(2,1)S(1)} collective-permute-done((bf16[32,2176]{1,0:T(8,128)(2,1)S(1)}, bf16[32,2176]{1,0:T(8,128)(2,1)S(1)}, u32[]{:S(2)}, u32[]{:S(2)}) %collective-permute-start.15) | collective-permute-done | bytes 139296 | tf_op jit(solution)/shard_map/ppermute | solution.py:17
  66.5 1.5 %collective-permute-start.17 = (bf16[32,2048]{1,0:T(8,128)(2,1)S(1)}, bf16[32,2048]{1,0:T(8,128)(2,1)S(1)}, u32[]{:S(2)}, u32[]{:S(2)}) collective-permute-start(bf16[32,2048]{1,0:T(8,128)(2,1)S(1)} %get-tuple-element.37), channel_id=1, source_target_pairs={{0,2},{2,0},{1,3},{3,1},{4,6},{6,4},{5,7},{7,5},{8,10},{10,8},{9,1... | collective-permute-start | bytes 393224 | tf_op jit(solution)/shard_map/ppermute | solution.py:299
  69.7 2.7 %collective-permute-done.17 = bf16[32,2048]{1,0:T(8,128)(2,1)S(1)} collective-permute-done((bf16[32,2048]{1,0:T(8,128)(2,1)S(1)}, bf16[32,2048]{1,0:T(8,128)(2,1)S(1)}, u32[]{:S(2)}, u32[]{:S(2)}) %collective-permute-start.17) | collective-permute-done | bytes 131104 | tf_op jit(solution)/shard_map/ppermute | solution.py:299
  72.4 1.3 %collective-permute-done.18 = bf16[32,2048]{1,0:T(8,128)(2,1)S(1)} collective-permute-done((bf16[32,2048]{1,0:T(8,128)(2,1)S(1)}, bf16[32,2048]{1,0:T(8,128)(2,1)S(1)}, u32[]{:S(2)}, u32[]{:S(2)}) %collective-permute-start.18) | collective-permute-done | bytes 131104 | tf_op jit(solution)/shard_map/ppermute | solution.py:17
  (87 shorter events, 5.9 us)
Async XLA Ops:
  0.6 49.7 %copy-start = (bf16[1,2048,64]{1,2,0:T(8,128)(2,1)S(1)}, bf16[1,2048,64]{1,2,0:T(8,128)(2,1)}, u32[]{:S(2)}) copy-start(bf16[1,2048,64]{1,2,0:T(8,128)(2,1)} %param.17) | copy-start | bytes 786436
  1.7 17.3 %collective-permute-start = (bf16[64,2048]{1,0:T(8,128)(2,1)S(1)}, bf16[64,2048]{1,0:T(8,128)(2,1)S(1)}, u32[]{:S(2)}, u32[]{:S(2)}) collective-permute-start(bf16[64,2048]{1,0:T(8,128)(2,1)S(1)} %dynamic-slice_bitcast_fusion), channel_id=1, source_target_pairs={{0,4},{4,0},{8,12},{12,8},{1,5},{5,1},{9,13},{13,9},{2,6},{6,2},{1... | collective-permute-start | bytes 786440 | tf_op jit(solution)/shard_map/ppermute | solution.py:17
  5.7 12.1 %collective-permute-start.1 = (bf16[32,2048]{1,0:T(8,128)(2,1)S(1)}, bf16[32,2048]{1,0:T(8,128)(2,1)S(1)}, u32[]{:S(2)}, u32[]{:S(2)}) collective-permute-start(bf16[32,2048]{1,0:T(8,128)(2,1)S(1)} %get-tuple-element.41.cot_ref), channel_id=1, source_target_pairs={{0,8},{4,12},{8,0},{12,4},{1,9},{5,13},{9,1},{13,5},{2,10},{6,14},... | collective-permute-start | bytes 393224 | tf_op jit(solution)/shard_map/ppermute | solution.py:17
  8.3 10.6 %collective-permute-start.2 = (bf16[32,2048]{1,0:T(8,128)(2,1)S(1)}, bf16[32,2048]{1,0:T(8,128)(2,1)S(1)}, u32[]{:S(2)}, u32[]{:S(2)}) collective-permute-start(bf16[32,2048]{1,0:T(8,128)(2,1)S(1)} %get-tuple-element.41.cot_ref), channel_id=1, source_target_pairs={{0,12},{4,8},{8,4},{12,0},{1,13},{5,9},{9,5},{13,1},{2,14},{6,10},... | collective-permute-start | bytes 393224 | tf_op jit(solution)/shard_map/ppermute | solution.py:17
  19.0 4.3 %collective-permute-start.3 = (bf16[128,2048]{1,0:T(8,128)(2,1)S(1)}, bf16[128,2048]{1,0:T(8,128)(2,1)S(1)}, u32[]{:S(2)}, u32[]{:S(2)}) collective-permute-start(bf16[128,2048]{1,0:T(8,128)(2,1)S(1)} %pad_maximum_fusion), channel_id=1, source_target_pairs={{0,1},{1,0},{2,3},{3,2},{4,5},{5,4},{6,7},{7,6},{8,9},{9,8},{10,11... | collective-permute-start | bytes 1572872 | tf_op jit(solution)/shard_map/ppermute | solution.py:17
  19.2 13.7 %collective-permute-start.6 = (bf16[32,2048]{1,0:T(8,128)(2,1)S(1)}, bf16[32,2048]{1,0:T(8,128)(2,1)S(1)}, u32[]{:S(2)}, u32[]{:S(2)}) collective-permute-start(bf16[32,2048]{1,0:T(8,128)(2,1)S(1)} %held.6), channel_id=1, source_target_pairs={{0,8},{4,12},{8,0},{12,4},{1,9},{5,13},{9,1},{13,5},{2,10},{6,14},... | collective-permute-start | bytes 393224 | tf_op jit(solution)/shard_map/ppermute | solution.py:17
  22.0 11.0 %collective-permute-start.5 = (bf16[32,2048]{1,0:T(8,128)(2,1)S(1)}, bf16[32,2048]{1,0:T(8,128)(2,1)S(1)}, u32[]{:S(2)}, u32[]{:S(2)}) collective-permute-start(bf16[32,2048]{1,0:T(8,128)(2,1)S(1)} %held.6), channel_id=1, source_target_pairs={{0,12},{4,8},{8,4},{12,0},{1,13},{5,9},{9,5},{13,1},{2,14},{6,10},... | collective-permute-start | bytes 393224 | tf_op jit(solution)/shard_map/ppermute | solution.py:17
  32.8 2.0 %collective-permute-start.4 = (bf16[128,2176]{1,0:T(8,128)(2,1)S(1)}, bf16[128,2176]{1,0:T(8,128)(2,1)S(1)}, u32[]{:S(2)}, u32[]{:S(2)}) collective-permute-start(bf16[128,2176]{1,0:T(8,128)(2,1)S(1)} %get-tuple-element.25), channel_id=1, source_target_pairs={{0,1},{1,0},{2,3},{3,2},{4,5},{5,4},{6,7},{7,6},{8,9},{9,8},{10,11... | collective-permute-start | bytes 1671176 | tf_op jit(solution)/shard_map/ppermute | solution.py:17
  35.0 4.7 %collective-permute-start.10 = (bf16[64,2048]{1,0:T(8,128)(2,1)S(1)}, bf16[64,2048]{1,0:T(8,128)(2,1)S(1)}, u32[]{:S(2)}, u32[]{:S(2)}) collective-permute-start(bf16[64,2048]{1,0:T(8,128)(2,1)S(1)} %held.9), channel_id=1, source_target_pairs={{0,1},{1,0},{2,3},{3,2},{4,5},{5,4},{6,7},{7,6},{8,9},{9,8},{10,11... | collective-permute-start | bytes 786440 | tf_op jit(solution)/shard_map/ppermute | solution.py:17
  35.2 14.0 %collective-permute-start.7 = (bf16[32,2176]{1,0:T(8,128)(2,1)S(1)}, bf16[32,2176]{1,0:T(8,128)(2,1)S(1)}, u32[]{:S(2)}, u32[]{:S(2)}) collective-permute-start(bf16[32,2176]{1,0:T(8,128)(2,1)S(1)} %get-tuple-element.27.refs_2_), channel_id=1, source_target_pairs={{0,12},{4,8},{8,4},{12,0},{1,13},{5,9},{9,5},{13,1},{2,14},{6,10},... | collective-permute-start | bytes 417800 | tf_op jit(solution)/shard_map/ppermute | solution.py:17
  37.8 12.2 %collective-permute-start.8 = (bf16[32,2176]{1,0:T(8,128)(2,1)S(1)}, bf16[32,2176]{1,0:T(8,128)(2,1)S(1)}, u32[]{:S(2)}, u32[]{:S(2)}) collective-permute-start(bf16[32,2176]{1,0:T(8,128)(2,1)S(1)} %get-tuple-element.28.refs_1_), channel_id=1, source_target_pairs={{0,8},{4,12},{8,0},{12,4},{1,9},{5,13},{9,1},{13,5},{2,10},{6,14},... | collective-permute-start | bytes 417800 | tf_op jit(solution)/shard_map/ppermute | solution.py:17
  37.8 12.2 %collective-permute-start.9 = (bf16[32,2176]{1,0:T(8,128)(2,1)S(1)}, bf16[32,2176]{1,0:T(8,128)(2,1)S(1)}, u32[]{:S(2)}, u32[]{:S(2)}) collective-permute-start(bf16[32,2176]{1,0:T(8,128)(2,1)S(1)} %get-tuple-element.29.refs_0_), channel_id=1, source_target_pairs={{0,4},{4,0},{8,12},{12,8},{1,5},{5,1},{9,13},{13,9},{2,6},{6,2},{1... | collective-permute-start | bytes 417800 | tf_op jit(solution)/shard_map/ppermute | solution.py:17
  39.7 10.4 %copy-start.6 = (f32[1,128,2]{1,2,0:T(2,128)S(1)}, f32[1,128,2]{1,2,0:T(2,128)}, u32[]{:S(2)}) copy-start(f32[1,128,2]{1,2,0:T(2,128)} %param.12) | copy-start | bytes 3076
  39.7 10.5 %copy-start.7 = (s32[1,1,2]{2,1,0:T(1,128)S(1)}, s32[1,1,2]{2,1,0:T(1,128)}, u32[]{:S(2)}) copy-start(s32[1,1,2]{2,1,0:T(1,128)} %param.11) | copy-start | bytes 28
  49.2 19.2 %copy-start.5 = (f32[1,128,64]{1,2,0:T(8,128)S(1)}, f32[1,128,64]{1,2,0:T(8,128)}, u32[]{:S(2)}) copy-start(f32[1,128,64]{1,2,0:T(8,128)} %param.16) | copy-start | bytes 98308
  50.0 2.0 %collective-permute-start.11 = (bf16[128,2176]{1,0:T(8,128)(2,1)S(1)}, bf16[128,2176]{1,0:T(8,128)(2,1)S(1)}, u32[]{:S(2)}, u32[]{:S(2)}) collective-permute-start(bf16[128,2176]{1,0:T(8,128)(2,1)S(1)} %held.10), channel_id=1, source_target_pairs={{0,1},{1,0},{2,3},{3,2},{4,5},{5,4},{6,7},{7,6},{8,9},{9,8},{10,11... | collective-permute-start | bytes 1671176 | tf_op jit(solution)/shard_map/ppermute | solution.py:17
  52.2 8.5 %collective-permute-start.12 = (bf16[32,2176]{1,0:T(8,128)(2,1)S(1)}, bf16[32,2176]{1,0:T(8,128)(2,1)S(1)}, u32[]{:S(2)}, u32[]{:S(2)}) collective-permute-start(bf16[32,2176]{1,0:T(8,128)(2,1)S(1)} %get-tuple-element.33), channel_id=1, source_target_pairs={{0,12},{4,8},{8,4},{12,0},{1,13},{5,9},{9,5},{13,1},{2,14},{6,10},... | collective-permute-start | bytes 417800 | tf_op jit(solution)/shard_map/ppermute | solution.py:17
  55.3 10.8 %collective-permute-start.15 = (bf16[32,2176]{1,0:T(8,128)(2,1)S(1)}, bf16[32,2176]{1,0:T(8,128)(2,1)S(1)}, u32[]{:S(2)}, u32[]{:S(2)}) collective-permute-start(bf16[32,2176]{1,0:T(8,128)(2,1)S(1)} %get-tuple-element.35), channel_id=1, source_target_pairs={{0,8},{4,12},{8,0},{12,4},{1,9},{5,13},{9,1},{13,5},{2,10},{6,14},... | collective-permute-start | bytes 417800 | tf_op jit(solution)/shard_map/ppermute | solution.py:17
  55.4 10.7 %collective-permute-start.16 = (bf16[32,2176]{1,0:T(8,128)(2,1)S(1)}, bf16[32,2176]{1,0:T(8,128)(2,1)S(1)}, u32[]{:S(2)}, u32[]{:S(2)}) collective-permute-start(bf16[32,2176]{1,0:T(8,128)(2,1)S(1)} %get-tuple-element.36), channel_id=1, source_target_pairs={{0,4},{4,0},{8,12},{12,8},{1,5},{5,1},{9,13},{13,9},{2,6},{6,2},{1... | collective-permute-start | bytes 417800 | tf_op jit(solution)/shard_map/ppermute | solution.py:17
  60.7 5.5 %collective-permute-start.13 = (bf16[32,2048]{1,0:T(8,128)(2,1)S(1)}, bf16[32,2048]{1,0:T(8,128)(2,1)S(1)}, u32[]{:S(2)}, u32[]{:S(2)}) collective-permute-start(bf16[32,2048]{1,0:T(8,128)(2,1)S(1)} %held.11), channel_id=1, source_target_pairs={{0,2},{2,0},{1,3},{3,1},{4,6},{6,4},{5,7},{7,5},{8,10},{10,8},{9,1... | collective-permute-start | bytes 393224 | tf_op jit(solution)/shard_map/ppermute | solution.py:299
  66.3 1.9 %collective-permute-start.19 = (f32[64,128]{1,0:T(8,128)S(1)}, f32[64,128]{1,0:T(8,128)S(1)}, u32[]{:S(2)}, u32[]{:S(2)}) collective-permute-start(f32[64,128]{1,0:T(8,128)S(1)} %constant_dynamic-update-slice_fusion.6), channel_id=1, source_target_pairs={{0,1},{1,0},{2,3},{3,2},{4,5},{5,4},{6,7},{7,6},{8,9},{9,8},{10,11... | collective-permute-start | bytes 98312 | tf_op jit(solution)/shard_map/ppermute | solution.py:17
  66.5 5.9 %collective-permute-start.17 = (bf16[32,2048]{1,0:T(8,128)(2,1)S(1)}, bf16[32,2048]{1,0:T(8,128)(2,1)S(1)}, u32[]{:S(2)}, u32[]{:S(2)}) collective-permute-start(bf16[32,2048]{1,0:T(8,128)(2,1)S(1)} %get-tuple-element.37), channel_id=1, source_target_pairs={{0,2},{2,0},{1,3},{3,1},{4,6},{6,4},{5,7},{7,5},{8,10},{10,8},{9,1... | collective-permute-start | bytes 393224 | tf_op jit(solution)/shard_map/ppermute | solution.py:299
  68.0 4.4 %collective-permute-start.14 = (bf16[32,2048]{1,0:T(8,128)(2,1)S(1)}, bf16[32,2048]{1,0:T(8,128)(2,1)S(1)}, u32[]{:S(2)}, u32[]{:S(2)}) collective-permute-start(bf16[32,2048]{1,0:T(8,128)(2,1)S(1)} %collective-permute-done.13.refs_3_), channel_id=1, source_target_pairs={{0,1},{1,0},{2,3},{3,2},{4,5},{5,4},{6,7},{7,6},{8,9},{9,8},{10,11... | collective-permute-start | bytes 393224 | tf_op jit(solution)/shard_map/ppermute | solution.py:17
  72.4 1.3 %collective-permute-start.18 = (bf16[32,2048]{1,0:T(8,128)(2,1)S(1)}, bf16[32,2048]{1,0:T(8,128)(2,1)S(1)}, u32[]{:S(2)}, u32[]{:S(2)}) collective-permute-start(bf16[32,2048]{1,0:T(8,128)(2,1)S(1)} %collective-permute-done.17), channel_id=1, source_target_pairs={{0,1},{1,0},{2,3},{3,2},{4,5},{5,4},{6,7},{7,6},{8,9},{9,8},{10,11... | collective-permute-start | bytes 393224 | tf_op jit(solution)/shard_map/ppermute | solution.py:17
  (5 other events, 22.3 us)

commit v11 on v10

--- a/solution.py
+++ b/solution.py
@@ -9,6 +9,8 @@
 
 EXPERTS = 4
 CHUNKS = 2
+LANES = 128
+PARTS = 3
 NT = (((1,), (1,)), ((), ()))
 
 
@@ -63,23 +65,110 @@
     )(keep, came, *events)
 
 
-def finish_kernel(slots, own_ref, cot_ref, weight_ref, *refs):
+def label_kernel(rows_ref, weight_ref, *refs):
+    out_ref = refs[-1]
+    rows, width = rows_ref.shape
+    column = lax.broadcasted_iota(jnp.int32, (rows, LANES), 1)
+    table = jnp.zeros((rows, LANES), jnp.float32)
+    for slot in range(weight_ref.shape[1]):
+        rest = weight_ref[:, slot : slot + 1]
+        for j in range(PARTS):
+            rounded = rest.astype(jnp.bfloat16).astype(jnp.float32)
+            table = jnp.where(column == PARTS * slot + j, rounded, table)
+            rest -= rounded
+    out_ref[:, :width] = rows_ref[...]
+    out_ref[:, width:] = table.astype(jnp.bfloat16)
+
+
+def labelled(rows, weight, *events):
+    count, width = rows.shape
+    return pl.pallas_call(
+        label_kernel,
+        in_specs=[RESIDENT] * 2 + [ANYWHERE] * len(events),
+        out_specs=RESIDENT,
+        out_shape=jax.ShapeDtypeStruct((count, width + LANES), rows.dtype),
+        compiler_params=pltpu.CompilerParams(vmem_limit_bytes=2 << 20),
+        name="label",
+    )(rows, weight, *events)
+
+
+def sort_kernel(slots, keep_ref, came_ref, *refs):
+    labels = refs[: slots - 2]
+    own_ref, near_ref, odd_ref, *even_refs = refs[slots - 2 :]
+    rows = own_ref.shape[0]
+    first = labels[0].shape[1] - LANES
+
+    def total(slot):
+        part = slice(slot * rows, (slot + 1) * rows)
+        return keep_ref[part] + came_ref[part].astype(jnp.float32)
+
+    def weighted(slot):
+        table = labels[slot - 2][:, first:].astype(jnp.float32)
+        owner = lax.broadcasted_iota(jnp.int32, table.shape, 1) // PARTS
+        weight = jnp.sum(jnp.where(owner == slot, table, 0.0), axis=1, keepdims=True)
+        return weight * total(slot)
+
+    own_ref[...] = total(0)
+    near_ref[...] = total(1).astype(jnp.bfloat16)
+    for at, even_ref in enumerate(even_refs):
+        even_ref[...] = weighted(2 * at + 2)
+        odd_ref[at * rows : (at + 1) * rows] = weighted(2 * at + 3).astype(jnp.bfloat16)
+
+
+def sorted_sums(keep, came, labels):
+    wide, slots = keep.shape[1], len(labels) + 2
+    rows, pairs = keep.shape[0] // slots, len(labels) // 2
+    own, *evens = [jax.ShapeDtypeStruct((rows, wide), jnp.float32)] * (1 + pairs)
+    near = jax.ShapeDtypeStruct((rows, wide), jnp.bfloat16)
+    odd = jax.ShapeDtypeStruct((pairs * rows, wide), jnp.bfloat16)
+    return pl.pallas_call(
+        functools.partial(sort_kernel, slots),
+        in_specs=[RESIDENT] * (2 + len(labels)),
+        out_specs=[RESIDENT] * (3 + pairs),
+        out_shape=[own, near, odd, *evens],
+        compiler_params=pltpu.CompilerParams(vmem_limit_bytes=4 << 20),
+        name="sort",
+    )(keep, came, *labels)
+
+
+def join_kernel(pairs, came_ref, *refs):
+    rows = refs[0].shape[0]
+    for at in range(pairs):
+        total = refs[at][...] + came_ref[at * rows : (at + 1) * rows].astype(jnp.float32)
+        refs[pairs + at][...] = total.astype(jnp.bfloat16)
+
+
+def joined(came, evens):
+    pairs = len(evens)
+    return pl.pallas_call(
+        functools.partial(join_kernel, pairs),
+        in_specs=[RESIDENT] * (1 + pairs),
+        out_specs=[RESIDENT] * pairs,
+        out_shape=[jax.ShapeDtypeStruct(evens[0].shape, jnp.bfloat16)] * pairs,
+        compiler_params=pltpu.CompilerParams(vmem_limit_bytes=4 << 20),
+        name="join",
+    )(came, *evens)
+
+
+def finish_kernel(slots, plain, own_ref, cot_ref, weight_ref, *refs):
     grad_ref, vec_ref = refs[-2:]
     width = grad_ref.shape[1]
     total = weight_ref[:, :1] * own_ref[...]
     for slot in range(1, slots):
-        back = refs[slots - 1 - slot][...].astype(jnp.float32)
+        back = refs[plain + slots - 1 - slot][...].astype(jnp.float32)
         total += weight_ref[:, slot : slot + 1] * back
+    for back_ref in refs[:plain]:
+        total += back_ref[...].astype(jnp.float32)
     grad_ref[...] = (cot_ref[...].astype(jnp.float32) + total[:, :width]).astype(jnp.bfloat16)
     vec_ref[...] = total[:, width:]
 
 
-def finished(own, cot, weight, backs, *events):
+def finished(own, cot, weight, backs, plain, *events):
     rows, wide = own.shape
     width = cot.shape[1]
     return pl.pallas_call(
-        functools.partial(finish_kernel, 1 + len(backs)),
-        in_specs=[RESIDENT] * (3 + len(backs)) + [ANYWHERE] * len(events),
+        functools.partial(finish_kernel, 1 + len(backs), len(plain)),
+        in_specs=[RESIDENT] * (3 + len(backs) + len(plain)) + [ANYWHERE] * len(events),
         out_specs=[RESIDENT] * 2,
         out_shape=[
             jax.ShapeDtypeStruct((rows, width), jnp.bfloat16),
@@ -90,7 +179,7 @@
             flops=8 * rows * wide, bytes_accessed=12 * rows * wide, transcendentals=0
         ),
         name="finish",
-    )(own, cot, weight, *backs, *events)
+    )(own, cot, weight, *plain, *backs, *events)
 
 
 def tile_of(size, most):
@@ -318,12 +407,13 @@
     below_mine, vectors = [], []
     for a in range(CHUNKS):
         part = slice(a * rows, (a + 1) * rows)
-        blocks = [fetched[slot] for slot in order] + [near_rows] * (a == 0)
+        rows_of = {slot: block[:, :width] for slot, block in fetched.items()}
+        blocks = [rows_of[slot] for slot in order] + [near_rows] * (a == 0)
         blocks = jnp.concatenate(blocks, axis=0)
         if a > 0:
             blocks = held(blocks, own)
         traded = xored(blocks, "tensor", 1)
-        mine = dict(fetched)
+        mine = dict(rows_of)
         theirs = {slot: traded[at * rows : (at + 1) * rows] for at, slot in enumerate(order)}
         if a == 0:
             near_theirs = traded[len(order) * rows :]
@@ -337,17 +427,24 @@
             a, rows_in, slope, down_part, sketch_t, down_here, up_weight[0, 0], *sent
         )
         if a + 1 < CHUNKS:
-            coming = held(cot_mine[(a + 1) * rows : (a + 2) * rows], near_rows)
+            part_next = slice((a + 1) * rows, (a + 2) * rows)
+            coming = labelled(cot_mine[part_next], weight[part_next], near_rows)
             fetched = {slot: held(xored(coming, "dp", slot), kept) for slot in order}
             late = tuple(fetched.values())
         else:
             give, late = held(give, *backs), ()
-        own, *sent = merged(kept, xored(give, "tensor", 1), rows, *late)
-        backs = [xored(out, "dp", slot + 1) for slot, out in enumerate(sent)][::-1]
-        if grad:
-            passed = (below(held(*grad, backs[0])),)
-            below_mine.append(*passed)
-        new, vec = finished(own, cot_mine[part], weight[part], backs, *passed)
+        came = xored(give, "tensor", 1)
+        if a == 0:
+            own, *sent = merged(kept, came, rows, *late)
+            backs = [xored(out, "dp", slot + 1) for slot, out in enumerate(sent)][::-1]
+            new, vec = finished(own, cot_mine[part], weight[part], backs, [])
+        else:
+            own, near, odd, *evens = sorted_sums(kept, came, [fetched[k] for k in order[::-1]])
+            sums = joined(xored(odd, "dp", 1), evens)
+            plain = [xored(block, "dp", 2 * at + 2) for at, block in enumerate(sums)]
+            near = xored(held(near, sums[0]), "dp", 1)
+            below_mine.append(below(held(*grad, sums[0])))
+            new, vec = finished(own, cot_mine[part], weight[part], [near], plain, *below_mine)
         grad = (new,)
         vectors.append(vec)
     below_mine.append(below(*grad))

time: 74.9 us -> 79.8 us (1.065)
  waiting for transfers between devices: 16.6 us -> 22.1 us
  starting transfers between devices: 22.6 us -> 20.4 us
    ppermute x18, waiting for transfers between devices: 13.9 us -> 17.2 us  [xored(): return lax.ppermute(block, axis, [(i, i ^ bits) for i in range(n)])]
    ppermute x2, waiting for transfers between devices: 2.71 us -> 4.97 us  [below(): lax.ppermute(block, 'section', [(s, (s - 1) % sections) for s in range(se...]
    ppermute x18, starting transfers between devices: 19.5 us -> 18.3 us  [xored(): return lax.ppermute(block, axis, [(i, i ^ bits) for i in range(n)])]
    ppermute x2, starting transfers between devices: 3.06 us -> 2.09 us  [below(): lax.ppermute(block, 'section', [(s, (s - 1) % sections) for s in range(se...]
    unnamed x34 -> x28, local copies, waits for them, and re-layouts: 4.38 us -> 4.4 us
  transfers between devices with their start and end apart: 20 -> 20, of which waited for: 8 -> 11; matrix products, arithmetic and copies ran while one was open for 5% -> 6% of each run, Pallas kernels for 34% -> 32%
where the time goes in v11:
time: 79.8 us; the launch traced here: 79.5 us
  Pallas kernels  25.9 us (32%)
  waiting for transfers between devices  22.1 us (28%)
  starting transfers between devices  20.4 us (26%)
  local copies, waits for them, and re-layouts  6.32 us (8%)
  other arithmetic  2.8 us (4%)
  between operations  1.04 us (1%)
  matrix products  0.82 us (1%)
    pallas_call x2, Pallas kernels, expert(): pl.pallas_call(functools.partial(expert_kernel, tile_f, tile_d), grid=(1,...  18.8 us
    ppermute x18, starting transfers between devices, xored(): return lax.ppermute(block, axis, [(i, i ^ bits) for i in range(n)])  18.3 us
    ppermute x18, waiting for transfers between devices, xored(): return lax.ppermute(block, axis, [(i, i ^ bits) for i in range(n)])  17.2 us
    pallas_call x1, Pallas kernels, slopes(): pl.pallas_call(functools.partial(slope_kernel, groups), grid_spec=pltpu.P...  6.27 us
    ppermute x2, waiting for transfers between devices, below(): lax.ppermute(block, 'section', [(s, (s - 1) % sections) for s in range(se...  4.97 us
    unnamed x28, local copies, waits for them, and re-layouts  4.4 us
    ppermute x2, starting transfers between devices, below(): lax.ppermute(block, 'section', [(s, (s - 1) % sections) for s in range(se...  2.09 us
    broadcast_in_dim x2, other arithmetic, per_device(): return (handed[None], features[None])  1.6 us
  transfers between devices with their start and end apart: 20, of which 11 were waited for; matrix products, arithmetic and copies ran while one was open for 6% of the time, Pallas kernels for 32%

profile of v11, /device:TPU:0, one launch (start us, length us, event | category | flops | bytes accessed | tf_op | source)
XLA Modules:
  0.0 79.5 jit_solution(2868682734015113788)
XLA Ops:
  0.7 1.0 %constant_dynamic-update-slice_fusion.2 = (bf16[256,2048]{1,0:T(8,128)(2,1)S(1)}, bf16[32,2048]{1,0:T(8,128)(2,1)S(1)}) fusion(bf16[1,128,2048]{2,1,0:T(8,128)(2,1)} %param.10, s32[]{:T(128)S(6)} %select_n.53), kind=kLoop, calls=%fused_computation.42 | loop fusion | bytes 393220
  1.6 4.1 %collective-permute-start.1 = (bf16[32,2048]{1,0:T(8,128)(2,1)S(1)}, bf16[32,2048]{1,0:T(8,128)(2,1)S(1)}, u32[]{:S(2)}, u32[]{:S(2)}) collective-permute-start(bf16[32,2048]{1,0:T(8,128)(2,1)S(1)} %get-tuple-element.41.cot_ref), channel_id=1, source_target_pairs={{0,8},{4,12},{8,0},{12,4},{1,9},{5,13},{9,1},{13,5},{2,10},{6,14},... | collective-permute-start | bytes 393224 | tf_op jit(solution)/shard_map/ppermute | solution.py:19
  5.7 1.3 %collective-permute-start.2 = (bf16[32,2048]{1,0:T(8,128)(2,1)S(1)}, bf16[32,2048]{1,0:T(8,128)(2,1)S(1)}, u32[]{:S(2)}, u32[]{:S(2)}) collective-permute-start(bf16[32,2048]{1,0:T(8,128)(2,1)S(1)} %get-tuple-element.41.cot_ref), channel_id=1, source_target_pairs={{0,12},{4,8},{8,4},{12,0},{1,13},{5,9},{9,5},{13,1},{2,14},{6,10},... | collective-permute-start | bytes 393224 | tf_op jit(solution)/shard_map/ppermute | solution.py:19
  7.1 1.0 %dynamic-slice_bitcast_fusion = bf16[64,2048]{1,0:T(8,128)(2,1)S(1)} fusion(bf16[1,128,2048]{2,1,0:T(8,128)(2,1)} %param.10, s32[]{:T(128)S(6)} %select_n.53), kind=kLoop, calls=%fused_computation.8 | loop fusion | bytes 524292 | tf_op jit(solution)/shard_map/dynamic_slice | solution.py:400
  10.1 2.0 %copy-done.1 = bf16[1,1,4,128,3584]{4,3,2,1,0:T(8,128)(2,1)S(1)} copy-done((bf16[1,1,4,128,3584]{4,3,2,1,0:T(8,128)(2,1)S(1)}, bf16[1,1,4,128,3584]{4,3,2,1,0:T(8,128)(2,1)}, u32[]{:S(2)}) %copy-start.1) | copy-done | bytes 3670040
  12.1 1.0 %copy-done.2 = bf16[1,1,3584,64]{2,3,1,0:T(8,128)(2,1)S(1)} copy-done((bf16[1,1,3584,64]{2,3,1,0:T(8,128)(2,1)S(1)}, bf16[1,1,3584,64]{2,3,1,0:T(8,128)(2,1)}, u32[]{:S(2)}) %copy-start.2) | copy-done | bytes 458776
  13.1 6.3 %slopes.1 = (bf16[2,3584,256]{2,1,0:T(8,128)(2,1)S(1)}, f32[2,256,64]{2,1,0:T(8,128)S(1)}, bf16[3584,2048]{1,0:T(8,128)(2,1)S(1)}) custom-call(s32[2]{0:T(128)S(1)} %pad_add_fusion.index_ref, bf16[4,2,2,32,3584]{4,3,2,1,0:T(8,128)(2,1)S(1)} %bitcast.52, bf16[4,2,2,32,3584]{4,3,2,1,0:T(8,128)(2,1)S(1)} %bitcast.53, bf16[4,2,2,32,3584]{4,3,2,1,0:T(8,128)(2,1)S(1)} %bitcast.54, ...), custom_call_target="tpu_custom_call" | custom-call | flops 234881024 | bytes 7340032 | tf_op jit(solution)/shard_map/slopes/pallas_call | solution.py:238
  20.3 2.4 %collective-permute-start.6 = (bf16[32,2176]{1,0:T(8,128)(2,1)S(1)}, bf16[32,2176]{1,0:T(8,128)(2,1)S(1)}, u32[]{:S(2)}, u32[]{:S(2)}) collective-permute-start(bf16[32,2176]{1,0:T(8,128)(2,1)S(1)} %label.1), channel_id=1, source_target_pairs={{0,8},{4,12},{8,0},{12,4},{1,9},{5,13},{9,1},{13,5},{2,10},{6,14},... | collective-permute-start | bytes 417800 | tf_op jit(solution)/shard_map/ppermute | solution.py:19
  22.7 1.3 %collective-permute-start.5 = (bf16[32,2176]{1,0:T(8,128)(2,1)S(1)}, bf16[32,2176]{1,0:T(8,128)(2,1)S(1)}, u32[]{:S(2)}, u32[]{:S(2)}) collective-permute-start(bf16[32,2176]{1,0:T(8,128)(2,1)S(1)} %label.1), channel_id=1, source_target_pairs={{0,12},{4,8},{8,4},{12,0},{1,13},{5,9},{9,5},{13,1},{2,14},{6,10},... | collective-permute-start | bytes 417800 | tf_op jit(solution)/shard_map/ppermute | solution.py:19
  24.1 9.4 %expert.2 = (f32[128,2176]{1,0:T(8,128)S(1)}, bf16[128,2176]{1,0:T(8,128)(2,1)S(1)}) custom-call(bf16[256,2048]{1,0:T(8,128)(2,1)S(1)} %slice_dynamic-update-slice_fusion.4.rows_ref, bf16[2,3584,256]{2,1,0:T(8,128)(2,1)S(1)} %get-tuple-element.21.slope_ref, f32[2,256,64]{2,1,0:T(8,128)S(1)} %get-tuple-element.22.down_part_ref, ...), custom_call_target="tpu_custom_call" | custom-call | flops 7516192768 | bytes 29360128 | tf_op jit(solution)/shard_map/expert/pallas_call | solution.py:326
  33.8 1.7 %collective-permute-done.4.came_ref = bf16[128,2176]{1,0:T(8,128)(2,1)S(1)} collective-permute-done((bf16[128,2176]{1,0:T(8,128)(2,1)S(1)}, bf16[128,2176]{1,0:T(8,128)(2,1)S(1)}, u32[]{:S(2)}, u32[]{:S(2)}) %collective-permute-start.4) | collective-permute-done | bytes 557088 | tf_op jit(solution)/shard_map/ppermute | solution.py:19
  35.9 2.6 %collective-permute-start.7 = (bf16[32,2176]{1,0:T(8,128)(2,1)S(1)}, bf16[32,2176]{1,0:T(8,128)(2,1)S(1)}, u32[]{:S(2)}, u32[]{:S(2)}) collective-permute-start(bf16[32,2176]{1,0:T(8,128)(2,1)S(1)} %get-tuple-element.27.refs_2_), channel_id=1, source_target_pairs={{0,12},{4,8},{8,4},{12,0},{1,13},{5,9},{9,5},{13,1},{2,14},{6,10},... | collective-permute-start | bytes 417800 | tf_op jit(solution)/shard_map/ppermute | solution.py:19
  39.1 1.2 %collective-permute-start.9 = (bf16[32,2176]{1,0:T(8,128)(2,1)S(1)}, bf16[32,2176]{1,0:T(8,128)(2,1)S(1)}, u32[]{:S(2)}, u32[]{:S(2)}) collective-permute-start(bf16[32,2176]{1,0:T(8,128)(2,1)S(1)} %get-tuple-element.29.refs_0_), channel_id=1, source_target_pairs={{0,4},{4,0},{8,12},{12,8},{1,5},{5,1},{9,13},{13,9},{2,6},{6,2},{1... | collective-permute-start | bytes 417800 | tf_op jit(solution)/shard_map/ppermute | solution.py:19
  40.4 9.4 %expert.3 = (f32[128,2176]{1,0:T(8,128)S(1)}, bf16[128,2176]{1,0:T(8,128)(2,1)S(1)}) custom-call(bf16[256,2048]{1,0:T(8,128)(2,1)S(1)} %slice_dynamic-update-slice_fusion.rows_ref, bf16[2,3584,256]{2,1,0:T(8,128)(2,1)S(1)} %get-tuple-element.21.slope_ref, f32[2,256,64]{2,1,0:T(8,128)S(1)} %get-tuple-element.22.down_part_ref, bf16[64,3584]{1,0:T(8,128)(2,1)S(1)} %bitcast.62, ...), custom_call_target="tpu_custom_call" | custom-call | flops 7516192768 | bytes 29360128 | tf_op jit(solution)/shard_map/expert/pallas_call | solution.py:326
  49.8 2.4 %collective-permute-done.8.refs_1_ = bf16[32,2176]{1,0:T(8,128)(2,1)S(1)} collective-permute-done((bf16[32,2176]{1,0:T(8,128)(2,1)S(1)}, bf16[32,2176]{1,0:T(8,128)(2,1)S(1)}, u32[]{:S(2)}, u32[]{:S(2)}) %collective-permute-start.8) | collective-permute-done | bytes 139296 | tf_op jit(solution)/shard_map/ppermute | solution.py:19
  52.4 1.9 %collective-permute-done.11.came_ref = bf16[128,2176]{1,0:T(8,128)(2,1)S(1)} collective-permute-done((bf16[128,2176]{1,0:T(8,128)(2,1)S(1)}, bf16[128,2176]{1,0:T(8,128)(2,1)S(1)}, u32[]{:S(2)}, u32[]{:S(2)}) %collective-permute-start.11) | collective-permute-done | bytes 557088 | tf_op jit(solution)/shard_map/ppermute | solution.py:19
  55.3 5.0 %collective-permute-done.12.came_ref = bf16[32,2176]{1,0:T(8,128)(2,1)S(1)} collective-permute-done((bf16[32,2176]{1,0:T(8,128)(2,1)S(1)}, bf16[32,2176]{1,0:T(8,128)(2,1)S(1)}, u32[]{:S(2)}, u32[]{:S(2)}) %collective-permute-start.12) | collective-permute-done | bytes 139296 | tf_op jit(solution)/shard_map/ppermute | solution.py:19
  60.3 1.5 %collective-permute-start.15 = (bf16[32,2176]{1,0:T(8,128)(2,1)S(1)}, bf16[32,2176]{1,0:T(8,128)(2,1)S(1)}, u32[]{:S(2)}, u32[]{:S(2)}) collective-permute-start(bf16[32,2176]{1,0:T(8,128)(2,1)S(1)} %join.1.refs_0_), channel_id=1, source_target_pairs={{0,8},{4,12},{8,0},{12,4},{1,9},{5,13},{9,1},{13,5},{2,10},{6,14},... | collective-permute-start | bytes 417800 | tf_op jit(solution)/shard_map/ppermute | solution.py:19
  61.9 1.6 %collective-permute-start.13 = (bf16[32,2048]{1,0:T(8,128)(2,1)S(1)}, bf16[32,2048]{1,0:T(8,128)(2,1)S(1)}, u32[]{:S(2)}, u32[]{:S(2)}) collective-permute-start(bf16[32,2048]{1,0:T(8,128)(2,1)S(1)} %held.10), channel_id=1, source_target_pairs={{0,2},{2,0},{1,3},{3,1},{4,6},{6,4},{5,7},{7,5},{8,10},{10,8},{9,1... | collective-permute-start | bytes 393224 | tf_op jit(solution)/shard_map/ppermute | solution.py:388
  63.5 1.8 %collective-permute-start.16 = (bf16[32,2176]{1,0:T(8,128)(2,1)S(1)}, bf16[32,2176]{1,0:T(8,128)(2,1)S(1)}, u32[]{:S(2)}, u32[]{:S(2)}) collective-permute-start(bf16[32,2176]{1,0:T(8,128)(2,1)S(1)} %held.11), channel_id=1, source_target_pairs={{0,4},{4,0},{8,12},{12,8},{1,5},{5,1},{9,13},{13,9},{2,6},{6,2},{1... | collective-permute-start | bytes 417800 | tf_op jit(solution)/shard_map/ppermute | solution.py:19
  65.3 1.7 %collective-permute-done.13.refs_2_ = bf16[32,2048]{1,0:T(8,128)(2,1)S(1)} collective-permute-done((bf16[32,2048]{1,0:T(8,128)(2,1)S(1)}, bf16[32,2048]{1,0:T(8,128)(2,1)S(1)}, u32[]{:S(2)}, u32[]{:S(2)}) %collective-permute-start.13) | collective-permute-done | bytes 131104 | tf_op jit(solution)/shard_map/ppermute | solution.py:388
  66.9 4.1 %collective-permute-done.16.refs_1_ = bf16[32,2176]{1,0:T(8,128)(2,1)S(1)} collective-permute-done((bf16[32,2176]{1,0:T(8,128)(2,1)S(1)}, bf16[32,2176]{1,0:T(8,128)(2,1)S(1)}, u32[]{:S(2)}, u32[]{:S(2)}) %collective-permute-start.16) | collective-permute-done | bytes 139296 | tf_op jit(solution)/shard_map/ppermute | solution.py:19
  73.9 3.3 %collective-permute-done.17 = bf16[32,2048]{1,0:T(8,128)(2,1)S(1)} collective-permute-done((bf16[32,2048]{1,0:T(8,128)(2,1)S(1)}, bf16[32,2048]{1,0:T(8,128)(2,1)S(1)}, u32[]{:S(2)}, u32[]{:S(2)}) %collective-permute-start.17) | collective-permute-done | bytes 131104 | tf_op jit(solution)/shard_map/ppermute | solution.py:388
  77.3 1.3 %collective-permute-done.18 = bf16[32,2048]{1,0:T(8,128)(2,1)S(1)} collective-permute-done((bf16[32,2048]{1,0:T(8,128)(2,1)S(1)}, bf16[32,2048]{1,0:T(8,128)(2,1)S(1)}, u32[]{:S(2)}, u32[]{:S(2)}) %collective-permute-start.18) | collective-permute-done | bytes 131104 | tf_op jit(solution)/shard_map/ppermute | solution.py:19
  (85 shorter events, 9.0 us)
Async XLA Ops:
  0.6 54.0 %copy-start = (bf16[1,2048,64]{1,2,0:T(8,128)(2,1)S(1)}, bf16[1,2048,64]{1,2,0:T(8,128)(2,1)}, u32[]{:S(2)}) copy-start(bf16[1,2048,64]{1,2,0:T(8,128)(2,1)} %param.17) | copy-start | bytes 786436
  1.6 17.8 %collective-permute-start.1 = (bf16[32,2048]{1,0:T(8,128)(2,1)S(1)}, bf16[32,2048]{1,0:T(8,128)(2,1)S(1)}, u32[]{:S(2)}, u32[]{:S(2)}) collective-permute-start(bf16[32,2048]{1,0:T(8,128)(2,1)S(1)} %get-tuple-element.41.cot_ref), channel_id=1, source_target_pairs={{0,8},{4,12},{8,0},{12,4},{1,9},{5,13},{9,1},{13,5},{2,10},{6,14},... | collective-permute-start | bytes 393224 | tf_op jit(solution)/shard_map/ppermute | solution.py:19
  5.7 13.7 %collective-permute-start.2 = (bf16[32,2048]{1,0:T(8,128)(2,1)S(1)}, bf16[32,2048]{1,0:T(8,128)(2,1)S(1)}, u32[]{:S(2)}, u32[]{:S(2)}) collective-permute-start(bf16[32,2048]{1,0:T(8,128)(2,1)S(1)} %get-tuple-element.41.cot_ref), channel_id=1, source_target_pairs={{0,12},{4,8},{8,4},{12,0},{1,13},{5,9},{9,5},{13,1},{2,14},{6,10},... | collective-permute-start | bytes 393224 | tf_op jit(solution)/shard_map/ppermute | solution.py:19
  8.0 11.9 %collective-permute-start = (bf16[64,2048]{1,0:T(8,128)(2,1)S(1)}, bf16[64,2048]{1,0:T(8,128)(2,1)S(1)}, u32[]{:S(2)}, u32[]{:S(2)}) collective-permute-start(bf16[64,2048]{1,0:T(8,128)(2,1)S(1)} %dynamic-slice_bitcast_fusion), channel_id=1, source_target_pairs={{0,4},{4,0},{8,12},{12,8},{1,5},{5,1},{9,13},{13,9},{2,6},{6,2},{1... | collective-permute-start | bytes 786440 | tf_op jit(solution)/shard_map/ppermute | solution.py:19
  13.1 7.0 %copy-start.4 = (bf16[1,128,2048]{2,1,0:T(8,128)(2,1)S(1)}, bf16[1,128,2048]{2,1,0:T(8,128)(2,1)}, u32[]{:S(2)}) copy-start(bf16[1,128,2048]{2,1,0:T(8,128)(2,1)} %param.10) | copy-start | bytes 1572868
  20.0 4.0 %collective-permute-start.3 = (bf16[128,2048]{1,0:T(8,128)(2,1)S(1)}, bf16[128,2048]{1,0:T(8,128)(2,1)S(1)}, u32[]{:S(2)}, u32[]{:S(2)}) collective-permute-start(bf16[128,2048]{1,0:T(8,128)(2,1)S(1)} %pad_maximum_fusion), channel_id=1, source_target_pairs={{0,1},{1,0},{2,3},{3,2},{4,5},{5,4},{6,7},{7,6},{8,9},{9,8},{10,11... | collective-permute-start | bytes 1572872 | tf_op jit(solution)/shard_map/ppermute | solution.py:19
  20.3 13.4 %collective-permute-start.6 = (bf16[32,2176]{1,0:T(8,128)(2,1)S(1)}, bf16[32,2176]{1,0:T(8,128)(2,1)S(1)}, u32[]{:S(2)}, u32[]{:S(2)}) collective-permute-start(bf16[32,2176]{1,0:T(8,128)(2,1)S(1)} %label.1), channel_id=1, source_target_pairs={{0,8},{4,12},{8,0},{12,4},{1,9},{5,13},{9,1},{13,5},{2,10},{6,14},... | collective-permute-start | bytes 417800 | tf_op jit(solution)/shard_map/ppermute | solution.py:19
  22.7 11.1 %collective-permute-start.5 = (bf16[32,2176]{1,0:T(8,128)(2,1)S(1)}, bf16[32,2176]{1,0:T(8,128)(2,1)S(1)}, u32[]{:S(2)}, u32[]{:S(2)}) collective-permute-start(bf16[32,2176]{1,0:T(8,128)(2,1)S(1)} %label.1), channel_id=1, source_target_pairs={{0,12},{4,8},{8,4},{12,0},{1,13},{5,9},{9,5},{13,1},{2,14},{6,10},... | collective-permute-start | bytes 417800 | tf_op jit(solution)/shard_map/ppermute | solution.py:19
  33.5 2.0 %collective-permute-start.4 = (bf16[128,2176]{1,0:T(8,128)(2,1)S(1)}, bf16[128,2176]{1,0:T(8,128)(2,1)S(1)}, u32[]{:S(2)}, u32[]{:S(2)}) collective-permute-start(bf16[128,2176]{1,0:T(8,128)(2,1)S(1)} %get-tuple-element.25), channel_id=1, source_target_pairs={{0,1},{1,0},{2,3},{3,2},{4,5},{5,4},{6,7},{7,6},{8,9},{9,8},{10,11... | collective-permute-start | bytes 1671176 | tf_op jit(solution)/shard_map/ppermute | solution.py:19
  35.7 4.7 %collective-permute-start.10 = (bf16[64,2048]{1,0:T(8,128)(2,1)S(1)}, bf16[64,2048]{1,0:T(8,128)(2,1)S(1)}, u32[]{:S(2)}, u32[]{:S(2)}) collective-permute-start(bf16[64,2048]{1,0:T(8,128)(2,1)S(1)} %held.8), channel_id=1, source_target_pairs={{0,1},{1,0},{2,3},{3,2},{4,5},{5,4},{6,7},{7,6},{8,9},{9,8},{10,11... | collective-permute-start | bytes 786440 | tf_op jit(solution)/shard_map/ppermute | solution.py:19
  35.9 13.9 %collective-permute-start.7 = (bf16[32,2176]{1,0:T(8,128)(2,1)S(1)}, bf16[32,2176]{1,0:T(8,128)(2,1)S(1)}, u32[]{:S(2)}, u32[]{:S(2)}) collective-permute-start(bf16[32,2176]{1,0:T(8,128)(2,1)S(1)} %get-tuple-element.27.refs_2_), channel_id=1, source_target_pairs={{0,12},{4,8},{8,4},{12,0},{1,13},{5,9},{9,5},{13,1},{2,14},{6,10},... | collective-permute-start | bytes 417800 | tf_op jit(solution)/shard_map/ppermute | solution.py:19
  38.5 13.8 %collective-permute-start.8 = (bf16[32,2176]{1,0:T(8,128)(2,1)S(1)}, bf16[32,2176]{1,0:T(8,128)(2,1)S(1)}, u32[]{:S(2)}, u32[]{:S(2)}) collective-permute-start(bf16[32,2176]{1,0:T(8,128)(2,1)S(1)} %get-tuple-element.28.refs_1_), channel_id=1, source_target_pairs={{0,8},{4,12},{8,0},{12,4},{1,9},{5,13},{9,1},{13,5},{2,10},{6,14},... | collective-permute-start | bytes 417800 | tf_op jit(solution)/shard_map/ppermute | solution.py:19
  39.1 13.2 %collective-permute-start.9 = (bf16[32,2176]{1,0:T(8,128)(2,1)S(1)}, bf16[32,2176]{1,0:T(8,128)(2,1)S(1)}, u32[]{:S(2)}, u32[]{:S(2)}) collective-permute-start(bf16[32,2176]{1,0:T(8,128)(2,1)S(1)} %get-tuple-element.29.refs_0_), channel_id=1, source_target_pairs={{0,4},{4,0},{8,12},{12,8},{1,5},{5,1},{9,13},{13,9},{2,6},{6,2},{1... | collective-permute-start | bytes 417800 | tf_op jit(solution)/shard_map/ppermute | solution.py:19
  49.8 5.2 %copy-start.6 = (s32[1,1,4]{2,1,0:T(1,128)S(1)}, s32[1,1,4]{2,1,0:T(1,128)}, u32[]{:S(2)}) copy-start(s32[1,1,4]{2,1,0:T(1,128)} %param.19) | copy-start | bytes 52
  52.3 20.3 %copy-start.5 = (f32[1,128,64]{1,2,0:T(8,128)S(1)}, f32[1,128,64]{1,2,0:T(8,128)}, u32[]{:S(2)}) copy-start(f32[1,128,64]{1,2,0:T(8,128)} %param.16) | copy-start | bytes 98308
  52.3 2.0 %collective-permute-start.11 = (bf16[128,2176]{1,0:T(8,128)(2,1)S(1)}, bf16[128,2176]{1,0:T(8,128)(2,1)S(1)}, u32[]{:S(2)}, u32[]{:S(2)}) collective-permute-start(bf16[128,2176]{1,0:T(8,128)(2,1)S(1)} %held.9), channel_id=1, source_target_pairs={{0,1},{1,0},{2,3},{3,2},{4,5},{5,4},{6,7},{7,6},{8,9},{9,8},{10,11... | collective-permute-start | bytes 1671176 | tf_op jit(solution)/shard_map/ppermute | solution.py:19
  54.5 5.8 %collective-permute-start.12 = (bf16[32,2176]{1,0:T(8,128)(2,1)S(1)}, bf16[32,2176]{1,0:T(8,128)(2,1)S(1)}, u32[]{:S(2)}, u32[]{:S(2)}) collective-permute-start(bf16[32,2176]{1,0:T(8,128)(2,1)S(1)} %get-tuple-element.33), channel_id=1, source_target_pairs={{0,4},{4,0},{8,12},{12,8},{1,5},{5,1},{9,13},{13,9},{2,6},{6,2},{1... | collective-permute-start | bytes 417800 | tf_op jit(solution)/shard_map/ppermute | solution.py:19
  60.3 10.7 %collective-permute-start.15 = (bf16[32,2176]{1,0:T(8,128)(2,1)S(1)}, bf16[32,2176]{1,0:T(8,128)(2,1)S(1)}, u32[]{:S(2)}, u32[]{:S(2)}) collective-permute-start(bf16[32,2176]{1,0:T(8,128)(2,1)S(1)} %join.1.refs_0_), channel_id=1, source_target_pairs={{0,8},{4,12},{8,0},{12,4},{1,9},{5,13},{9,1},{13,5},{2,10},{6,14},... | collective-permute-start | bytes 417800 | tf_op jit(solution)/shard_map/ppermute | solution.py:19
  61.9 5.0 %collective-permute-start.13 = (bf16[32,2048]{1,0:T(8,128)(2,1)S(1)}, bf16[32,2048]{1,0:T(8,128)(2,1)S(1)}, u32[]{:S(2)}, u32[]{:S(2)}) collective-permute-start(bf16[32,2048]{1,0:T(8,128)(2,1)S(1)} %held.10), channel_id=1, source_target_pairs={{0,2},{2,0},{1,3},{3,1},{4,6},{6,4},{5,7},{7,5},{8,10},{10,8},{9,1... | collective-permute-start | bytes 393224 | tf_op jit(solution)/shard_map/ppermute | solution.py:388
  63.5 7.6 %collective-permute-start.16 = (bf16[32,2176]{1,0:T(8,128)(2,1)S(1)}, bf16[32,2176]{1,0:T(8,128)(2,1)S(1)}, u32[]{:S(2)}, u32[]{:S(2)}) collective-permute-start(bf16[32,2176]{1,0:T(8,128)(2,1)S(1)} %held.11), channel_id=1, source_target_pairs={{0,4},{4,0},{8,12},{12,8},{1,5},{5,1},{9,13},{13,9},{2,6},{6,2},{1... | collective-permute-start | bytes 417800 | tf_op jit(solution)/shard_map/ppermute | solution.py:19
  71.2 1.3 %collective-permute-start.19 = (f32[64,128]{1,0:T(8,128)S(1)}, f32[64,128]{1,0:T(8,128)S(1)}, u32[]{:S(2)}, u32[]{:S(2)}) collective-permute-start(f32[64,128]{1,0:T(8,128)S(1)} %constant_dynamic-update-slice_fusion.6), channel_id=1, source_target_pairs={{0,1},{1,0},{2,3},{3,2},{4,5},{5,4},{6,7},{7,6},{8,9},{9,8},{10,11... | collective-permute-start | bytes 98312 | tf_op jit(solution)/shard_map/ppermute | solution.py:19
  71.3 5.9 %collective-permute-start.14 = (bf16[32,2048]{1,0:T(8,128)(2,1)S(1)}, bf16[32,2048]{1,0:T(8,128)(2,1)S(1)}, u32[]{:S(2)}, u32[]{:S(2)}) collective-permute-start(bf16[32,2048]{1,0:T(8,128)(2,1)S(1)} %collective-permute-done.13.refs_2_), channel_id=1, source_target_pairs={{0,1},{1,0},{2,3},{3,2},{4,5},{5,4},{6,7},{7,6},{8,9},{9,8},{10,11... | collective-permute-start | bytes 393224 | tf_op jit(solution)/shard_map/ppermute | solution.py:19
  71.8 5.4 %collective-permute-start.17 = (bf16[32,2048]{1,0:T(8,128)(2,1)S(1)}, bf16[32,2048]{1,0:T(8,128)(2,1)S(1)}, u32[]{:S(2)}, u32[]{:S(2)}) collective-permute-start(bf16[32,2048]{1,0:T(8,128)(2,1)S(1)} %get-tuple-element.37), channel_id=1, source_target_pairs={{0,2},{2,0},{1,3},{3,1},{4,6},{6,4},{5,7},{7,5},{8,10},{10,8},{9,1... | collective-permute-start | bytes 393224 | tf_op jit(solution)/shard_map/ppermute | solution.py:388
  77.3 1.3 %collective-permute-start.18 = (bf16[32,2048]{1,0:T(8,128)(2,1)S(1)}, bf16[32,2048]{1,0:T(8,128)(2,1)S(1)}, u32[]{:S(2)}, u32[]{:S(2)}) collective-permute-start(bf16[32,2048]{1,0:T(8,128)(2,1)S(1)} %collective-permute-done.17), channel_id=1, source_target_pairs={{0,1},{1,0},{2,3},{3,2},{4,5},{5,4},{6,7},{7,6},{8,9},{9,8},{10,11... | collective-permute-start | bytes 393224 | tf_op jit(solution)/shard_map/ppermute | solution.py:19
  (3 other events, 7.8 us)

commit v12 on v10

--- a/solution.py
+++ b/solution.py
@@ -177,7 +177,7 @@
 
 
 def expert_kernel(
-    tile_f, tile_d, rows_ref, slope_ref, down_part_ref, sketch_ref, down_ref, up_hbm, *refs
+    chunk, tile_f, tile_d, rows_ref, slope_ref, down_part_ref, sketch_ref, down_ref, up_hbm, *refs
 ):
     keep_ref, give_ref, rows_buf, grad_buf, up_buf, up_sem = refs[-6:]
     hidden_cols, width = down_ref.shape
@@ -205,14 +205,14 @@
         grad_hidden = jnp.dot(
             down_ref[part, :], rows_buf[...], preferred_element_type=jnp.float32
         )
-        slope = slope_ref[0, part, :].astype(jnp.float32)
+        slope = slope_ref[chunk, part, :].astype(jnp.float32)
         grad_buf[part, :] = (grad_hidden * slope).astype(jnp.bfloat16)
         return carry
 
     lax.fori_loop(0, steps_f, first, 0)
 
     up_part = jnp.dot(sketch_ref[...], grad_buf[...], preferred_element_type=jnp.float32).T
-    vectors = jnp.concatenate([down_part_ref[0], up_part], axis=1)
+    vectors = jnp.concatenate([down_part_ref[chunk], up_part], axis=1)
     keep_ref[:, width:] = vectors[:half]
     give_ref[:, width:] = vectors[half:].astype(jnp.bfloat16)
 
@@ -235,14 +235,8 @@
     tile_f, tile_d = tile_of(hidden_cols, 1792), tile_of(width, 1024)
     up_local = pltpu.with_memory_space_constraint(up_local, pltpu.HBM)
     return pl.pallas_call(
-        functools.partial(expert_kernel, tile_f, tile_d),
-        grid=(1,),
-        in_specs=[
-            RESIDENT,
-            pl.BlockSpec((1, hidden_cols, count), lambda i: (chunk, 0, 0)),
-            pl.BlockSpec((1, count, rank), lambda i: (chunk, 0, 0)),
-        ]
-        + [RESIDENT] * 2
+        functools.partial(expert_kernel, chunk, tile_f, tile_d),
+        in_specs=[RESIDENT] * 5
         + [pl.BlockSpec(memory_space=pltpu.HBM)]
         + [ANYWHERE] * len(events),
         out_specs=[RESIDENT] * 2,

time: 74.9 us -> 74.9 us (level)
  no operation moved by 1% of the time
where the time goes in v12:
time: 74.9 us; the launch traced here: 74.6 us
  Pallas kernels  25.8 us (34%)
  starting transfers between devices  22.6 us (30%)
  waiting for transfers between devices  16.6 us (22%)
  local copies, waits for them, and re-layouts  5.63 us (8%)
  other arithmetic  2.14 us (3%)
  between operations  1.07 us (1%)
  matrix products  0.82 us (1%)
    ppermute x18, starting transfers between devices, xored(): return lax.ppermute(block, axis, [(i, i ^ bits) for i in range(n)])  19.5 us
    pallas_call x2, Pallas kernels, expert(): pl.pallas_call(functools.partial(expert_kernel, chunk, tile_f, tile_d), i...  18.8 us
    ppermute x18, waiting for transfers between devices, xored(): return lax.ppermute(block, axis, [(i, i ^ bits) for i in range(n)])  13.9 us
    pallas_call x1, Pallas kernels, slopes(): pl.pallas_call(functools.partial(slope_kernel, groups), grid_spec=pltpu.P...  6.27 us
    unnamed x34, local copies, waits for them, and re-layouts  4.38 us
    ppermute x2, starting transfers between devices, below(): lax.ppermute(block, 'section', [(s, (s - 1) % sections) for s in range(se...  3.06 us
    ppermute x2, waiting for transfers between devices, below(): lax.ppermute(block, 'section', [(s, (s - 1) % sections) for s in range(se...  2.71 us
    broadcast_in_dim x2, other arithmetic, per_device(): return (handed[None], features[None])  1.6 us
  transfers between devices with their start and end apart: 20, of which 8 were waited for; matrix products, arithmetic and copies ran while one was open for 5% of the time, Pallas kernels for 34%

profile of v12, /device:TPU:0, one launch (start us, length us, event | category | flops | bytes accessed | tf_op | source)
XLA Modules:
  0.0 74.6 jit_solution(16519697999737839569)
XLA Ops:
  0.7 1.0 %dynamic-slice_bitcast_fusion = bf16[64,2048]{1,0:T(8,128)(2,1)S(1)} fusion(bf16[1,128,2048]{2,1,0:T(8,128)(2,1)} %param.10, s32[]{:T(128)S(6)} %select_n.53), kind=kLoop, calls=%fused_computation.8 | loop fusion | bytes 524292 | tf_op jit(solution)/shard_map/dynamic_slice | solution.py:305
  1.7 3.1 %collective-permute-start = (bf16[64,2048]{1,0:T(8,128)(2,1)S(1)}, bf16[64,2048]{1,0:T(8,128)(2,1)S(1)}, u32[]{:S(2)}, u32[]{:S(2)}) collective-permute-start(bf16[64,2048]{1,0:T(8,128)(2,1)S(1)} %dynamic-slice_bitcast_fusion), channel_id=1, source_target_pairs={{0,4},{4,0},{8,12},{12,8},{1,5},{5,1},{9,13},{13,9},{2,6},{6,2},{1... | collective-permute-start | bytes 786440 | tf_op jit(solution)/shard_map/ppermute | solution.py:17
  4.8 0.9 %constant_dynamic-update-slice_fusion.2 = (bf16[256,2048]{1,0:T(8,128)(2,1)S(1)}, bf16[32,2048]{1,0:T(8,128)(2,1)S(1)}) fusion(bf16[1,128,2048]{2,1,0:T(8,128)(2,1)} %param.10, s32[]{:T(128)S(6)} %select_n.53), kind=kLoop, calls=%fused_computation.42 | loop fusion | bytes 393220
  5.7 2.7 %collective-permute-start.1 = (bf16[32,2048]{1,0:T(8,128)(2,1)S(1)}, bf16[32,2048]{1,0:T(8,128)(2,1)S(1)}, u32[]{:S(2)}, u32[]{:S(2)}) collective-permute-start(bf16[32,2048]{1,0:T(8,128)(2,1)S(1)} %get-tuple-element.41.cot_ref), channel_id=1, source_target_pairs={{0,8},{4,12},{8,0},{12,4},{1,9},{5,13},{9,1},{13,5},{2,10},{6,14},... | collective-permute-start | bytes 393224 | tf_op jit(solution)/shard_map/ppermute | solution.py:17
  8.4 2.0 %copy-done.1 = bf16[1,1,4,128,3584]{4,3,2,1,0:T(8,128)(2,1)S(1)} copy-done((bf16[1,1,4,128,3584]{4,3,2,1,0:T(8,128)(2,1)S(1)}, bf16[1,1,4,128,3584]{4,3,2,1,0:T(8,128)(2,1)}, u32[]{:S(2)}) %copy-start.1) | copy-done | bytes 3670040
  10.5 1.0 %copy-done.2 = bf16[1,1,3584,64]{2,3,1,0:T(8,128)(2,1)S(1)} copy-done((bf16[1,1,3584,64]{2,3,1,0:T(8,128)(2,1)S(1)}, bf16[1,1,3584,64]{2,3,1,0:T(8,128)(2,1)}, u32[]{:S(2)}) %copy-start.2) | copy-done | bytes 458776
  11.5 6.3 %slopes.1 = (bf16[2,3584,256]{2,1,0:T(8,128)(2,1)S(1)}, f32[2,256,64]{2,1,0:T(8,128)S(1)}, bf16[3584,2048]{1,0:T(8,128)(2,1)S(1)}) custom-call(s32[2]{0:T(128)S(1)} %pad_add_fusion.index_ref, bf16[4,2,2,32,3584]{4,3,2,1,0:T(8,128)(2,1)S(1)} %bitcast.52, bf16[4,2,2,32,3584]{4,3,2,1,0:T(8,128)(2,1)S(1)} %bitcast.53, bf16[4,2,2,32,3584]{4,3,2,1,0:T(8,128)(2,1)S(1)} %bitcast.54, ...), custom_call_target="tpu_custom_call" | custom-call | flops 234881024 | bytes 7340032 | tf_op jit(solution)/shard_map/slopes/pallas_call | solution.py:149
  17.8 1.2 %collective-permute-done.2 = bf16[32,2048]{1,0:T(8,128)(2,1)S(1)} collective-permute-done((bf16[32,2048]{1,0:T(8,128)(2,1)S(1)}, bf16[32,2048]{1,0:T(8,128)(2,1)S(1)}, u32[]{:S(2)}, u32[]{:S(2)}) %collective-permute-start.2) | collective-permute-done | bytes 131104 | tf_op jit(solution)/shard_map/ppermute | solution.py:17
  19.2 2.7 %collective-permute-start.6 = (bf16[32,2048]{1,0:T(8,128)(2,1)S(1)}, bf16[32,2048]{1,0:T(8,128)(2,1)S(1)}, u32[]{:S(2)}, u32[]{:S(2)}) collective-permute-start(bf16[32,2048]{1,0:T(8,128)(2,1)S(1)} %held.6), channel_id=1, source_target_pairs={{0,8},{4,12},{8,0},{12,4},{1,9},{5,13},{9,1},{13,5},{2,10},{6,14},... | collective-permute-start | bytes 393224 | tf_op jit(solution)/shard_map/ppermute | solution.py:17
  22.0 1.3 %collective-permute-start.5 = (bf16[32,2048]{1,0:T(8,128)(2,1)S(1)}, bf16[32,2048]{1,0:T(8,128)(2,1)S(1)}, u32[]{:S(2)}, u32[]{:S(2)}) collective-permute-start(bf16[32,2048]{1,0:T(8,128)(2,1)S(1)} %held.6), channel_id=1, source_target_pairs={{0,12},{4,8},{8,4},{12,0},{1,13},{5,9},{9,5},{13,1},{2,14},{6,10},... | collective-permute-start | bytes 393224 | tf_op jit(solution)/shard_map/ppermute | solution.py:17
  23.4 9.4 %expert.2 = (f32[128,2176]{1,0:T(8,128)S(1)}, bf16[128,2176]{1,0:T(8,128)(2,1)S(1)}) custom-call(bf16[256,2048]{1,0:T(8,128)(2,1)S(1)} %slice_dynamic-update-slice_fusion.4.rows_ref, bf16[2,3584,256]{2,1,0:T(8,128)(2,1)S(1)} %get-tuple-element.21.slope_ref, f32[2,256,64]{2,1,0:T(8,128)S(1)} %get-tuple-element.22.down_part_ref, ...), custom_call_target="tpu_custom_call" | custom-call | flops 7516192768 | bytes 29360128 | tf_op jit(solution)/shard_map/expert/pallas_call | solution.py:237
  33.1 1.8 %collective-permute-done.4.came_ref = bf16[128,2176]{1,0:T(8,128)(2,1)S(1)} collective-permute-done((bf16[128,2176]{1,0:T(8,128)(2,1)S(1)}, bf16[128,2176]{1,0:T(8,128)(2,1)S(1)}, u32[]{:S(2)}, u32[]{:S(2)}) %collective-permute-start.4) | collective-permute-done | bytes 557088 | tf_op jit(solution)/shard_map/ppermute | solution.py:17
  35.2 2.6 %collective-permute-start.7 = (bf16[32,2176]{1,0:T(8,128)(2,1)S(1)}, bf16[32,2176]{1,0:T(8,128)(2,1)S(1)}, u32[]{:S(2)}, u32[]{:S(2)}) collective-permute-start(bf16[32,2176]{1,0:T(8,128)(2,1)S(1)} %get-tuple-element.27.refs_2_), channel_id=1, source_target_pairs={{0,12},{4,8},{8,4},{12,0},{1,13},{5,9},{9,5},{13,1},{2,14},{6,10},... | collective-permute-start | bytes 417800 | tf_op jit(solution)/shard_map/ppermute | solution.py:17
  37.8 1.9 %collective-permute-start.9 = (bf16[32,2176]{1,0:T(8,128)(2,1)S(1)}, bf16[32,2176]{1,0:T(8,128)(2,1)S(1)}, u32[]{:S(2)}, u32[]{:S(2)}) collective-permute-start(bf16[32,2176]{1,0:T(8,128)(2,1)S(1)} %get-tuple-element.29.refs_0_), channel_id=1, source_target_pairs={{0,4},{4,0},{8,12},{12,8},{1,5},{5,1},{9,13},{13,9},{2,6},{6,2},{1... | collective-permute-start | bytes 417800 | tf_op jit(solution)/shard_map/ppermute | solution.py:17
  39.7 9.4 %expert.3 = (f32[128,2176]{1,0:T(8,128)S(1)}, bf16[128,2176]{1,0:T(8,128)(2,1)S(1)}) custom-call(bf16[256,2048]{1,0:T(8,128)(2,1)S(1)} %slice_dynamic-update-slice_fusion.rows_ref, bf16[2,3584,256]{2,1,0:T(8,128)(2,1)S(1)} %get-tuple-element.21.slope_ref, f32[2,256,64]{2,1,0:T(8,128)S(1)} %get-tuple-element.22.down_part_ref, bf16[64,3584]{1,0:T(8,128)(2,1)S(1)} %bitcast.62, ...), custom_call_target="tpu_custom_call" | custom-call | flops 7516192768 | bytes 29360128 | tf_op jit(solution)/shard_map/expert/pallas_call | solution.py:237
  50.6 1.5 %collective-permute-done.11.came_ref = bf16[128,2176]{1,0:T(8,128)(2,1)S(1)} collective-permute-done((bf16[128,2176]{1,0:T(8,128)(2,1)S(1)}, bf16[128,2176]{1,0:T(8,128)(2,1)S(1)}, u32[]{:S(2)}, u32[]{:S(2)}) %collective-permute-start.11) | collective-permute-done | bytes 557088 | tf_op jit(solution)/shard_map/ppermute | solution.py:17
  52.2 2.7 %collective-permute-start.12 = (bf16[32,2176]{1,0:T(8,128)(2,1)S(1)}, bf16[32,2176]{1,0:T(8,128)(2,1)S(1)}, u32[]{:S(2)}, u32[]{:S(2)}) collective-permute-start(bf16[32,2176]{1,0:T(8,128)(2,1)S(1)} %get-tuple-element.33), channel_id=1, source_target_pairs={{0,12},{4,8},{8,4},{12,0},{1,13},{5,9},{9,5},{13,1},{2,14},{6,10},... | collective-permute-start | bytes 417800 | tf_op jit(solution)/shard_map/ppermute | solution.py:17
  55.4 1.8 %collective-permute-start.16 = (bf16[32,2176]{1,0:T(8,128)(2,1)S(1)}, bf16[32,2176]{1,0:T(8,128)(2,1)S(1)}, u32[]{:S(2)}, u32[]{:S(2)}) collective-permute-start(bf16[32,2176]{1,0:T(8,128)(2,1)S(1)} %get-tuple-element.36), channel_id=1, source_target_pairs={{0,4},{4,0},{8,12},{12,8},{1,5},{5,1},{9,13},{13,9},{2,6},{6,2},{1... | collective-permute-start | bytes 417800 | tf_op jit(solution)/shard_map/ppermute | solution.py:17
  57.2 3.5 %collective-permute-done.12.refs_0_ = bf16[32,2176]{1,0:T(8,128)(2,1)S(1)} collective-permute-done((bf16[32,2176]{1,0:T(8,128)(2,1)S(1)}, bf16[32,2176]{1,0:T(8,128)(2,1)S(1)}, u32[]{:S(2)}, u32[]{:S(2)}) %collective-permute-start.12) | collective-permute-done | bytes 139296 | tf_op jit(solution)/shard_map/ppermute | solution.py:17
  60.7 1.6 %collective-permute-start.13 = (bf16[32,2048]{1,0:T(8,128)(2,1)S(1)}, bf16[32,2048]{1,0:T(8,128)(2,1)S(1)}, u32[]{:S(2)}, u32[]{:S(2)}) collective-permute-start(bf16[32,2048]{1,0:T(8,128)(2,1)S(1)} %held.11), channel_id=1, source_target_pairs={{0,2},{2,0},{1,3},{3,1},{4,6},{6,4},{5,7},{7,5},{8,10},{10,8},{9,1... | collective-permute-start | bytes 393224 | tf_op jit(solution)/shard_map/ppermute | solution.py:293
  62.3 3.8 %collective-permute-done.15.refs_1_ = bf16[32,2176]{1,0:T(8,128)(2,1)S(1)} collective-permute-done((bf16[32,2176]{1,0:T(8,128)(2,1)S(1)}, bf16[32,2176]{1,0:T(8,128)(2,1)S(1)}, u32[]{:S(2)}, u32[]{:S(2)}) %collective-permute-start.15) | collective-permute-done | bytes 139296 | tf_op jit(solution)/shard_map/ppermute | solution.py:17
  66.5 1.5 %collective-permute-start.17 = (bf16[32,2048]{1,0:T(8,128)(2,1)S(1)}, bf16[32,2048]{1,0:T(8,128)(2,1)S(1)}, u32[]{:S(2)}, u32[]{:S(2)}) collective-permute-start(bf16[32,2048]{1,0:T(8,128)(2,1)S(1)} %get-tuple-element.37), channel_id=1, source_target_pairs={{0,2},{2,0},{1,3},{3,1},{4,6},{6,4},{5,7},{7,5},{8,10},{10,8},{9,1... | collective-permute-start | bytes 393224 | tf_op jit(solution)/shard_map/ppermute | solution.py:293
  69.7 2.7 %collective-permute-done.17 = bf16[32,2048]{1,0:T(8,128)(2,1)S(1)} collective-permute-done((bf16[32,2048]{1,0:T(8,128)(2,1)S(1)}, bf16[32,2048]{1,0:T(8,128)(2,1)S(1)}, u32[]{:S(2)}, u32[]{:S(2)}) %collective-permute-start.17) | collective-permute-done | bytes 131104 | tf_op jit(solution)/shard_map/ppermute | solution.py:293
  72.4 1.3 %collective-permute-done.18 = bf16[32,2048]{1,0:T(8,128)(2,1)S(1)} collective-permute-done((bf16[32,2048]{1,0:T(8,128)(2,1)S(1)}, bf16[32,2048]{1,0:T(8,128)(2,1)S(1)}, u32[]{:S(2)}, u32[]{:S(2)}) %collective-permute-start.18) | collective-permute-done | bytes 131104 | tf_op jit(solution)/shard_map/ppermute | solution.py:17
  (87 shorter events, 5.9 us)
Async XLA Ops:
  0.6 49.7 %copy-start = (bf16[1,2048,64]{1,2,0:T(8,128)(2,1)S(1)}, bf16[1,2048,64]{1,2,0:T(8,128)(2,1)}, u32[]{:S(2)}) copy-start(bf16[1,2048,64]{1,2,0:T(8,128)(2,1)} %param.17) | copy-start | bytes 786436
  1.7 17.3 %collective-permute-start = (bf16[64,2048]{1,0:T(8,128)(2,1)S(1)}, bf16[64,2048]{1,0:T(8,128)(2,1)S(1)}, u32[]{:S(2)}, u32[]{:S(2)}) collective-permute-start(bf16[64,2048]{1,0:T(8,128)(2,1)S(1)} %dynamic-slice_bitcast_fusion), channel_id=1, source_target_pairs={{0,4},{4,0},{8,12},{12,8},{1,5},{5,1},{9,13},{13,9},{2,6},{6,2},{1... | collective-permute-start | bytes 786440 | tf_op jit(solution)/shard_map/ppermute | solution.py:17
  5.7 12.1 %collective-permute-start.1 = (bf16[32,2048]{1,0:T(8,128)(2,1)S(1)}, bf16[32,2048]{1,0:T(8,128)(2,1)S(1)}, u32[]{:S(2)}, u32[]{:S(2)}) collective-permute-start(bf16[32,2048]{1,0:T(8,128)(2,1)S(1)} %get-tuple-element.41.cot_ref), channel_id=1, source_target_pairs={{0,8},{4,12},{8,0},{12,4},{1,9},{5,13},{9,1},{13,5},{2,10},{6,14},... | collective-permute-start | bytes 393224 | tf_op jit(solution)/shard_map/ppermute | solution.py:17
  8.3 10.6 %collective-permute-start.2 = (bf16[32,2048]{1,0:T(8,128)(2,1)S(1)}, bf16[32,2048]{1,0:T(8,128)(2,1)S(1)}, u32[]{:S(2)}, u32[]{:S(2)}) collective-permute-start(bf16[32,2048]{1,0:T(8,128)(2,1)S(1)} %get-tuple-element.41.cot_ref), channel_id=1, source_target_pairs={{0,12},{4,8},{8,4},{12,0},{1,13},{5,9},{9,5},{13,1},{2,14},{6,10},... | collective-permute-start | bytes 393224 | tf_op jit(solution)/shard_map/ppermute | solution.py:17
  19.0 4.3 %collective-permute-start.3 = (bf16[128,2048]{1,0:T(8,128)(2,1)S(1)}, bf16[128,2048]{1,0:T(8,128)(2,1)S(1)}, u32[]{:S(2)}, u32[]{:S(2)}) collective-permute-start(bf16[128,2048]{1,0:T(8,128)(2,1)S(1)} %pad_maximum_fusion), channel_id=1, source_target_pairs={{0,1},{1,0},{2,3},{3,2},{4,5},{5,4},{6,7},{7,6},{8,9},{9,8},{10,11... | collective-permute-start | bytes 1572872 | tf_op jit(solution)/shard_map/ppermute | solution.py:17
  19.2 13.7 %collective-permute-start.6 = (bf16[32,2048]{1,0:T(8,128)(2,1)S(1)}, bf16[32,2048]{1,0:T(8,128)(2,1)S(1)}, u32[]{:S(2)}, u32[]{:S(2)}) collective-permute-start(bf16[32,2048]{1,0:T(8,128)(2,1)S(1)} %held.6), channel_id=1, source_target_pairs={{0,8},{4,12},{8,0},{12,4},{1,9},{5,13},{9,1},{13,5},{2,10},{6,14},... | collective-permute-start | bytes 393224 | tf_op jit(solution)/shard_map/ppermute | solution.py:17
  22.0 11.0 %collective-permute-start.5 = (bf16[32,2048]{1,0:T(8,128)(2,1)S(1)}, bf16[32,2048]{1,0:T(8,128)(2,1)S(1)}, u32[]{:S(2)}, u32[]{:S(2)}) collective-permute-start(bf16[32,2048]{1,0:T(8,128)(2,1)S(1)} %held.6), channel_id=1, source_target_pairs={{0,12},{4,8},{8,4},{12,0},{1,13},{5,9},{9,5},{13,1},{2,14},{6,10},... | collective-permute-start | bytes 393224 | tf_op jit(solution)/shard_map/ppermute | solution.py:17
  32.8 2.0 %collective-permute-start.4 = (bf16[128,2176]{1,0:T(8,128)(2,1)S(1)}, bf16[128,2176]{1,0:T(8,128)(2,1)S(1)}, u32[]{:S(2)}, u32[]{:S(2)}) collective-permute-start(bf16[128,2176]{1,0:T(8,128)(2,1)S(1)} %get-tuple-element.25), channel_id=1, source_target_pairs={{0,1},{1,0},{2,3},{3,2},{4,5},{5,4},{6,7},{7,6},{8,9},{9,8},{10,11... | collective-permute-start | bytes 1671176 | tf_op jit(solution)/shard_map/ppermute | solution.py:17
  35.0 4.7 %collective-permute-start.10 = (bf16[64,2048]{1,0:T(8,128)(2,1)S(1)}, bf16[64,2048]{1,0:T(8,128)(2,1)S(1)}, u32[]{:S(2)}, u32[]{:S(2)}) collective-permute-start(bf16[64,2048]{1,0:T(8,128)(2,1)S(1)} %held.9), channel_id=1, source_target_pairs={{0,1},{1,0},{2,3},{3,2},{4,5},{5,4},{6,7},{7,6},{8,9},{9,8},{10,11... | collective-permute-start | bytes 786440 | tf_op jit(solution)/shard_map/ppermute | solution.py:17
  35.2 14.0 %collective-permute-start.7 = (bf16[32,2176]{1,0:T(8,128)(2,1)S(1)}, bf16[32,2176]{1,0:T(8,128)(2,1)S(1)}, u32[]{:S(2)}, u32[]{:S(2)}) collective-permute-start(bf16[32,2176]{1,0:T(8,128)(2,1)S(1)} %get-tuple-element.27.refs_2_), channel_id=1, source_target_pairs={{0,12},{4,8},{8,4},{12,0},{1,13},{5,9},{9,5},{13,1},{2,14},{6,10},... | collective-permute-start | bytes 417800 | tf_op jit(solution)/shard_map/ppermute | solution.py:17
  37.8 12.2 %collective-permute-start.8 = (bf16[32,2176]{1,0:T(8,128)(2,1)S(1)}, bf16[32,2176]{1,0:T(8,128)(2,1)S(1)}, u32[]{:S(2)}, u32[]{:S(2)}) collective-permute-start(bf16[32,2176]{1,0:T(8,128)(2,1)S(1)} %get-tuple-element.28.refs_1_), channel_id=1, source_target_pairs={{0,8},{4,12},{8,0},{12,4},{1,9},{5,13},{9,1},{13,5},{2,10},{6,14},... | collective-permute-start | bytes 417800 | tf_op jit(solution)/shard_map/ppermute | solution.py:17
  37.8 12.2 %collective-permute-start.9 = (bf16[32,2176]{1,0:T(8,128)(2,1)S(1)}, bf16[32,2176]{1,0:T(8,128)(2,1)S(1)}, u32[]{:S(2)}, u32[]{:S(2)}) collective-permute-start(bf16[32,2176]{1,0:T(8,128)(2,1)S(1)} %get-tuple-element.29.refs_0_), channel_id=1, source_target_pairs={{0,4},{4,0},{8,12},{12,8},{1,5},{5,1},{9,13},{13,9},{2,6},{6,2},{1... | collective-permute-start | bytes 417800 | tf_op jit(solution)/shard_map/ppermute | solution.py:17
  39.7 10.4 %copy-start.6 = (f32[1,128,2]{1,2,0:T(2,128)S(1)}, f32[1,128,2]{1,2,0:T(2,128)}, u32[]{:S(2)}) copy-start(f32[1,128,2]{1,2,0:T(2,128)} %param.12) | copy-start | bytes 3076
  39.7 10.5 %copy-start.7 = (s32[1,1,2]{2,1,0:T(1,128)S(1)}, s32[1,1,2]{2,1,0:T(1,128)}, u32[]{:S(2)}) copy-start(s32[1,1,2]{2,1,0:T(1,128)} %param.11) | copy-start | bytes 28
  49.2 19.2 %copy-start.5 = (f32[1,128,64]{1,2,0:T(8,128)S(1)}, f32[1,128,64]{1,2,0:T(8,128)}, u32[]{:S(2)}) copy-start(f32[1,128,64]{1,2,0:T(8,128)} %param.16) | copy-start | bytes 98308
  50.0 2.0 %collective-permute-start.11 = (bf16[128,2176]{1,0:T(8,128)(2,1)S(1)}, bf16[128,2176]{1,0:T(8,128)(2,1)S(1)}, u32[]{:S(2)}, u32[]{:S(2)}) collective-permute-start(bf16[128,2176]{1,0:T(8,128)(2,1)S(1)} %held.10), channel_id=1, source_target_pairs={{0,1},{1,0},{2,3},{3,2},{4,5},{5,4},{6,7},{7,6},{8,9},{9,8},{10,11... | collective-permute-start | bytes 1671176 | tf_op jit(solution)/shard_map/ppermute | solution.py:17
  52.2 8.5 %collective-permute-start.12 = (bf16[32,2176]{1,0:T(8,128)(2,1)S(1)}, bf16[32,2176]{1,0:T(8,128)(2,1)S(1)}, u32[]{:S(2)}, u32[]{:S(2)}) collective-permute-start(bf16[32,2176]{1,0:T(8,128)(2,1)S(1)} %get-tuple-element.33), channel_id=1, source_target_pairs={{0,12},{4,8},{8,4},{12,0},{1,13},{5,9},{9,5},{13,1},{2,14},{6,10},... | collective-permute-start | bytes 417800 | tf_op jit(solution)/shard_map/ppermute | solution.py:17
  55.3 10.8 %collective-permute-start.15 = (bf16[32,2176]{1,0:T(8,128)(2,1)S(1)}, bf16[32,2176]{1,0:T(8,128)(2,1)S(1)}, u32[]{:S(2)}, u32[]{:S(2)}) collective-permute-start(bf16[32,2176]{1,0:T(8,128)(2,1)S(1)} %get-tuple-element.35), channel_id=1, source_target_pairs={{0,8},{4,12},{8,0},{12,4},{1,9},{5,13},{9,1},{13,5},{2,10},{6,14},... | collective-permute-start | bytes 417800 | tf_op jit(solution)/shard_map/ppermute | solution.py:17
  55.4 10.7 %collective-permute-start.16 = (bf16[32,2176]{1,0:T(8,128)(2,1)S(1)}, bf16[32,2176]{1,0:T(8,128)(2,1)S(1)}, u32[]{:S(2)}, u32[]{:S(2)}) collective-permute-start(bf16[32,2176]{1,0:T(8,128)(2,1)S(1)} %get-tuple-element.36), channel_id=1, source_target_pairs={{0,4},{4,0},{8,12},{12,8},{1,5},{5,1},{9,13},{13,9},{2,6},{6,2},{1... | collective-permute-start | bytes 417800 | tf_op jit(solution)/shard_map/ppermute | solution.py:17
  60.7 5.5 %collective-permute-start.13 = (bf16[32,2048]{1,0:T(8,128)(2,1)S(1)}, bf16[32,2048]{1,0:T(8,128)(2,1)S(1)}, u32[]{:S(2)}, u32[]{:S(2)}) collective-permute-start(bf16[32,2048]{1,0:T(8,128)(2,1)S(1)} %held.11), channel_id=1, source_target_pairs={{0,2},{2,0},{1,3},{3,1},{4,6},{6,4},{5,7},{7,5},{8,10},{10,8},{9,1... | collective-permute-start | bytes 393224 | tf_op jit(solution)/shard_map/ppermute | solution.py:293
  66.3 1.9 %collective-permute-start.19 = (f32[64,128]{1,0:T(8,128)S(1)}, f32[64,128]{1,0:T(8,128)S(1)}, u32[]{:S(2)}, u32[]{:S(2)}) collective-permute-start(f32[64,128]{1,0:T(8,128)S(1)} %constant_dynamic-update-slice_fusion.6), channel_id=1, source_target_pairs={{0,1},{1,0},{2,3},{3,2},{4,5},{5,4},{6,7},{7,6},{8,9},{9,8},{10,11... | collective-permute-start | bytes 98312 | tf_op jit(solution)/shard_map/ppermute | solution.py:17
  66.5 5.9 %collective-permute-start.17 = (bf16[32,2048]{1,0:T(8,128)(2,1)S(1)}, bf16[32,2048]{1,0:T(8,128)(2,1)S(1)}, u32[]{:S(2)}, u32[]{:S(2)}) collective-permute-start(bf16[32,2048]{1,0:T(8,128)(2,1)S(1)} %get-tuple-element.37), channel_id=1, source_target_pairs={{0,2},{2,0},{1,3},{3,1},{4,6},{6,4},{5,7},{7,5},{8,10},{10,8},{9,1... | collective-permute-start | bytes 393224 | tf_op jit(solution)/shard_map/ppermute | solution.py:293
  68.0 4.4 %collective-permute-start.14 = (bf16[32,2048]{1,0:T(8,128)(2,1)S(1)}, bf16[32,2048]{1,0:T(8,128)(2,1)S(1)}, u32[]{:S(2)}, u32[]{:S(2)}) collective-permute-start(bf16[32,2048]{1,0:T(8,128)(2,1)S(1)} %collective-permute-done.13.refs_3_), channel_id=1, source_target_pairs={{0,1},{1,0},{2,3},{3,2},{4,5},{5,4},{6,7},{7,6},{8,9},{9,8},{10,11... | collective-permute-start | bytes 393224 | tf_op jit(solution)/shard_map/ppermute | solution.py:17
  72.4 1.3 %collective-permute-start.18 = (bf16[32,2048]{1,0:T(8,128)(2,1)S(1)}, bf16[32,2048]{1,0:T(8,128)(2,1)S(1)}, u32[]{:S(2)}, u32[]{:S(2)}) collective-permute-start(bf16[32,2048]{1,0:T(8,128)(2,1)S(1)} %collective-permute-done.17), channel_id=1, source_target_pairs={{0,1},{1,0},{2,3},{3,2},{4,5},{5,4},{6,7},{7,6},{8,9},{9,8},{10,11... | collective-permute-start | bytes 393224 | tf_op jit(solution)/shard_map/ppermute | solution.py:17
  (5 other events, 22.3 us)

commit v13 on v12

--- a/solution.py
+++ b/solution.py
@@ -335,7 +335,7 @@
             fetched = {slot: held(xored(coming, "dp", slot), kept) for slot in order}
             late = tuple(fetched.values())
         else:
-            give, late = held(give, *backs), ()
+            give, late = held(give, *backs), grad
         own, *sent = merged(kept, xored(give, "tensor", 1), rows, *late)
         backs = [xored(out, "dp", slot + 1) for slot, out in enumerate(sent)][::-1]
         if grad:

time: 74.9 us -> 74.9 us (level)
  matrix products: 0.82 us -> 1.86 us
  waiting for transfers between devices: 16.6 us -> 15.7 us
    dot_general x1, matrix products: 0.3 us -> 1.34 us  [per_device(): out_vec = jnp.dot(cot, model_sketch[0], preferred_element_type=jnp.float32)]
    ppermute x18, waiting for transfers between devices: 13.9 us -> 13 us  [xored(): return lax.ppermute(block, axis, [(i, i ^ bits) for i in range(n)])]
  transfers between devices with their start and end apart: 20 -> 20, of which waited for: 8 -> 8; matrix products, arithmetic and copies ran while one was open for 5% -> 6% of each run, Pallas kernels for 34% -> 34%
where the time goes in v13:
time: 74.9 us; the launch traced here: 74.6 us
  Pallas kernels  25.7 us (34%)
  starting transfers between devices  22.6 us (30%)
  waiting for transfers between devices  15.7 us (21%)
  local copies, waits for them, and re-layouts  5.64 us (8%)
  other arithmetic  2.14 us (3%)
  matrix products  1.86 us (2%)
  between operations  1.08 us (1%)
    ppermute x18, starting transfers between devices, xored(): return lax.ppermute(block, axis, [(i, i ^ bits) for i in range(n)])  19.5 us
    pallas_call x2, Pallas kernels, expert(): pl.pallas_call(functools.partial(expert_kernel, chunk, tile_f, tile_d), i...  18.7 us
    ppermute x18, waiting for transfers between devices, xored(): return lax.ppermute(block, axis, [(i, i ^ bits) for i in range(n)])  13 us
    pallas_call x1, Pallas kernels, slopes(): pl.pallas_call(functools.partial(slope_kernel, groups), grid_spec=pltpu.P...  6.27 us
    unnamed x34, local copies, waits for them, and re-layouts  4.38 us
    ppermute x2, starting transfers between devices, below(): lax.ppermute(block, 'section', [(s, (s - 1) % sections) for s in range(se...  3.06 us
    ppermute x2, waiting for transfers between devices, below(): lax.ppermute(block, 'section', [(s, (s - 1) % sections) for s in range(se...  2.71 us
    broadcast_in_dim x2, other arithmetic, per_device(): return (handed[None], features[None])  1.6 us
  transfers between devices with their start and end apart: 20, of which 8 were waited for; matrix products, arithmetic and copies ran while one was open for 6% of the time, Pallas kernels for 34%

profile of v13, /device:TPU:0, one launch (start us, length us, event | category | flops | bytes accessed | tf_op | source)
XLA Modules:
  0.0 74.6 jit_solution(12889228503874842109)
XLA Ops:
  0.7 1.0 %dynamic-slice_bitcast_fusion = bf16[64,2048]{1,0:T(8,128)(2,1)S(1)} fusion(bf16[1,128,2048]{2,1,0:T(8,128)(2,1)} %param.10, s32[]{:T(128)S(6)} %select_n.53), kind=kLoop, calls=%fused_computation.8 | loop fusion | bytes 524292 | tf_op jit(solution)/shard_map/dynamic_slice | solution.py:305
  1.7 3.1 %collective-permute-start = (bf16[64,2048]{1,0:T(8,128)(2,1)S(1)}, bf16[64,2048]{1,0:T(8,128)(2,1)S(1)}, u32[]{:S(2)}, u32[]{:S(2)}) collective-permute-start(bf16[64,2048]{1,0:T(8,128)(2,1)S(1)} %dynamic-slice_bitcast_fusion), channel_id=1, source_target_pairs={{0,4},{4,0},{8,12},{12,8},{1,5},{5,1},{9,13},{13,9},{2,6},{6,2},{1... | collective-permute-start | bytes 786440 | tf_op jit(solution)/shard_map/ppermute | solution.py:17
  5.7 2.7 %collective-permute-start.1 = (bf16[32,2048]{1,0:T(8,128)(2,1)S(1)}, bf16[32,2048]{1,0:T(8,128)(2,1)S(1)}, u32[]{:S(2)}, u32[]{:S(2)}) collective-permute-start(bf16[32,2048]{1,0:T(8,128)(2,1)S(1)} %get-tuple-element.41.cot_ref), channel_id=1, source_target_pairs={{0,8},{4,12},{8,0},{12,4},{1,9},{5,13},{9,1},{13,5},{2,10},{6,14},... | collective-permute-start | bytes 393224 | tf_op jit(solution)/shard_map/ppermute | solution.py:17
  8.4 2.0 %copy-done.1 = bf16[1,1,4,128,3584]{4,3,2,1,0:T(8,128)(2,1)S(1)} copy-done((bf16[1,1,4,128,3584]{4,3,2,1,0:T(8,128)(2,1)S(1)}, bf16[1,1,4,128,3584]{4,3,2,1,0:T(8,128)(2,1)}, u32[]{:S(2)}) %copy-start.1) | copy-done | bytes 3670040
  10.5 1.0 %copy-done.2 = bf16[1,1,3584,64]{2,3,1,0:T(8,128)(2,1)S(1)} copy-done((bf16[1,1,3584,64]{2,3,1,0:T(8,128)(2,1)S(1)}, bf16[1,1,3584,64]{2,3,1,0:T(8,128)(2,1)}, u32[]{:S(2)}) %copy-start.2) | copy-done | bytes 458776
  11.5 6.3 %slopes.1 = (bf16[2,3584,256]{2,1,0:T(8,128)(2,1)S(1)}, f32[2,256,64]{2,1,0:T(8,128)S(1)}, bf16[3584,2048]{1,0:T(8,128)(2,1)S(1)}) custom-call(s32[2]{0:T(128)S(1)} %pad_add_fusion.index_ref, bf16[4,2,2,32,3584]{4,3,2,1,0:T(8,128)(2,1)S(1)} %bitcast.52, bf16[4,2,2,32,3584]{4,3,2,1,0:T(8,128)(2,1)S(1)} %bitcast.53, bf16[4,2,2,32,3584]{4,3,2,1,0:T(8,128)(2,1)S(1)} %bitcast.54, ...), custom_call_target="tpu_custom_call" | custom-call | flops 234881024 | bytes 7340032 | tf_op jit(solution)/shard_map/slopes/pallas_call | solution.py:149
  17.8 1.2 %collective-permute-done.2 = bf16[32,2048]{1,0:T(8,128)(2,1)S(1)} collective-permute-done((bf16[32,2048]{1,0:T(8,128)(2,1)S(1)}, bf16[32,2048]{1,0:T(8,128)(2,1)S(1)}, u32[]{:S(2)}, u32[]{:S(2)}) %collective-permute-start.2) | collective-permute-done | bytes 131104 | tf_op jit(solution)/shard_map/ppermute | solution.py:17
  19.2 2.7 %collective-permute-start.6 = (bf16[32,2048]{1,0:T(8,128)(2,1)S(1)}, bf16[32,2048]{1,0:T(8,128)(2,1)S(1)}, u32[]{:S(2)}, u32[]{:S(2)}) collective-permute-start(bf16[32,2048]{1,0:T(8,128)(2,1)S(1)} %held.6), channel_id=1, source_target_pairs={{0,8},{4,12},{8,0},{12,4},{1,9},{5,13},{9,1},{13,5},{2,10},{6,14},... | collective-permute-start | bytes 393224 | tf_op jit(solution)/shard_map/ppermute | solution.py:17
  22.0 1.3 %collective-permute-start.5 = (bf16[32,2048]{1,0:T(8,128)(2,1)S(1)}, bf16[32,2048]{1,0:T(8,128)(2,1)S(1)}, u32[]{:S(2)}, u32[]{:S(2)}) collective-permute-start(bf16[32,2048]{1,0:T(8,128)(2,1)S(1)} %held.6), channel_id=1, source_target_pairs={{0,12},{4,8},{8,4},{12,0},{1,13},{5,9},{9,5},{13,1},{2,14},{6,10},... | collective-permute-start | bytes 393224 | tf_op jit(solution)/shard_map/ppermute | solution.py:17
  23.4 9.4 %expert.2 = (f32[128,2176]{1,0:T(8,128)S(1)}, bf16[128,2176]{1,0:T(8,128)(2,1)S(1)}) custom-call(bf16[256,2048]{1,0:T(8,128)(2,1)S(1)} %slice_dynamic-update-slice_fusion.4.rows_ref, bf16[2,3584,256]{2,1,0:T(8,128)(2,1)S(1)} %get-tuple-element.21.slope_ref, f32[2,256,64]{2,1,0:T(8,128)S(1)} %get-tuple-element.22.down_part_ref, ...), custom_call_target="tpu_custom_call" | custom-call | flops 7516192768 | bytes 29360128 | tf_op jit(solution)/shard_map/expert/pallas_call | solution.py:237
  33.0 1.8 %collective-permute-done.4.came_ref = bf16[128,2176]{1,0:T(8,128)(2,1)S(1)} collective-permute-done((bf16[128,2176]{1,0:T(8,128)(2,1)S(1)}, bf16[128,2176]{1,0:T(8,128)(2,1)S(1)}, u32[]{:S(2)}, u32[]{:S(2)}) %collective-permute-start.4) | collective-permute-done | bytes 557088 | tf_op jit(solution)/shard_map/ppermute | solution.py:17
  35.1 2.6 %collective-permute-start.7 = (bf16[32,2176]{1,0:T(8,128)(2,1)S(1)}, bf16[32,2176]{1,0:T(8,128)(2,1)S(1)}, u32[]{:S(2)}, u32[]{:S(2)}) collective-permute-start(bf16[32,2176]{1,0:T(8,128)(2,1)S(1)} %get-tuple-element.27.refs_2_), channel_id=1, source_target_pairs={{0,12},{4,8},{8,4},{12,0},{1,13},{5,9},{9,5},{13,1},{2,14},{6,10},... | collective-permute-start | bytes 417800 | tf_op jit(solution)/shard_map/ppermute | solution.py:17
  37.7 1.9 %collective-permute-start.9 = (bf16[32,2176]{1,0:T(8,128)(2,1)S(1)}, bf16[32,2176]{1,0:T(8,128)(2,1)S(1)}, u32[]{:S(2)}, u32[]{:S(2)}) collective-permute-start(bf16[32,2176]{1,0:T(8,128)(2,1)S(1)} %get-tuple-element.29.refs_0_), channel_id=1, source_target_pairs={{0,4},{4,0},{8,12},{12,8},{1,5},{5,1},{9,13},{13,9},{2,6},{6,2},{1... | collective-permute-start | bytes 417800 | tf_op jit(solution)/shard_map/ppermute | solution.py:17
  39.7 9.4 %expert.3 = (f32[128,2176]{1,0:T(8,128)S(1)}, bf16[128,2176]{1,0:T(8,128)(2,1)S(1)}) custom-call(bf16[256,2048]{1,0:T(8,128)(2,1)S(1)} %slice_dynamic-update-slice_fusion.rows_ref, bf16[2,3584,256]{2,1,0:T(8,128)(2,1)S(1)} %get-tuple-element.21.slope_ref, f32[2,256,64]{2,1,0:T(8,128)S(1)} %get-tuple-element.22.down_part_ref, bf16[64,3584]{1,0:T(8,128)(2,1)S(1)} %bitcast.62, ...), custom_call_target="tpu_custom_call" | custom-call | flops 7516192768 | bytes 29360128 | tf_op jit(solution)/shard_map/expert/pallas_call | solution.py:237
  50.6 1.4 %collective-permute-done.11.came_ref = bf16[128,2176]{1,0:T(8,128)(2,1)S(1)} collective-permute-done((bf16[128,2176]{1,0:T(8,128)(2,1)S(1)}, bf16[128,2176]{1,0:T(8,128)(2,1)S(1)}, u32[]{:S(2)}, u32[]{:S(2)}) %collective-permute-start.11) | collective-permute-done | bytes 557088 | tf_op jit(solution)/shard_map/ppermute | solution.py:17
  52.2 2.7 %collective-permute-start.12 = (bf16[32,2176]{1,0:T(8,128)(2,1)S(1)}, bf16[32,2176]{1,0:T(8,128)(2,1)S(1)}, u32[]{:S(2)}, u32[]{:S(2)}) collective-permute-start(bf16[32,2176]{1,0:T(8,128)(2,1)S(1)} %get-tuple-element.33), channel_id=1, source_target_pairs={{0,12},{4,8},{8,4},{12,0},{1,13},{5,9},{9,5},{13,1},{2,14},{6,10},... | collective-permute-start | bytes 417800 | tf_op jit(solution)/shard_map/ppermute | solution.py:17
  54.8 1.3 %fusion = f32[128,64]{0,1:T(8,128)S(1)} fusion(bf16[1,128,2048]{2,1,0:T(8,128)(2,1)} %param.10, bf16[1,2048,64]{1,2,0:T(8,128)(2,1)S(1)} %copy-done), kind=kOutput, calls=%fused_computation.4 | convolution fusion | flops 33554432 | bytes 819200 | tf_op jit(solution)/shard_map/dot_general | solution.py:360
  56.4 1.8 %collective-permute-start.16 = (bf16[32,2176]{1,0:T(8,128)(2,1)S(1)}, bf16[32,2176]{1,0:T(8,128)(2,1)S(1)}, u32[]{:S(2)}, u32[]{:S(2)}) collective-permute-start(bf16[32,2176]{1,0:T(8,128)(2,1)S(1)} %get-tuple-element.36), channel_id=1, source_target_pairs={{0,4},{4,0},{8,12},{12,8},{1,5},{5,1},{9,13},{13,9},{2,6},{6,2},{1... | collective-permute-start | bytes 417800 | tf_op jit(solution)/shard_map/ppermute | solution.py:17
  58.2 2.5 %collective-permute-done.12.refs_0_ = bf16[32,2176]{1,0:T(8,128)(2,1)S(1)} collective-permute-done((bf16[32,2176]{1,0:T(8,128)(2,1)S(1)}, bf16[32,2176]{1,0:T(8,128)(2,1)S(1)}, u32[]{:S(2)}, u32[]{:S(2)}) %collective-permute-start.12) | collective-permute-done | bytes 139296 | tf_op jit(solution)/shard_map/ppermute | solution.py:17
  60.7 1.6 %collective-permute-start.13 = (bf16[32,2048]{1,0:T(8,128)(2,1)S(1)}, bf16[32,2048]{1,0:T(8,128)(2,1)S(1)}, u32[]{:S(2)}, u32[]{:S(2)}) collective-permute-start(bf16[32,2048]{1,0:T(8,128)(2,1)S(1)} %held.11), channel_id=1, source_target_pairs={{0,2},{2,0},{1,3},{3,1},{4,6},{6,4},{5,7},{7,5},{8,10},{10,8},{9,1... | collective-permute-start | bytes 393224 | tf_op jit(solution)/shard_map/ppermute | solution.py:293
  62.3 3.8 %collective-permute-done.15.refs_1_ = bf16[32,2176]{1,0:T(8,128)(2,1)S(1)} collective-permute-done((bf16[32,2176]{1,0:T(8,128)(2,1)S(1)}, bf16[32,2176]{1,0:T(8,128)(2,1)S(1)}, u32[]{:S(2)}, u32[]{:S(2)}) %collective-permute-start.15) | collective-permute-done | bytes 139296 | tf_op jit(solution)/shard_map/ppermute | solution.py:17
  66.5 1.5 %collective-permute-start.17 = (bf16[32,2048]{1,0:T(8,128)(2,1)S(1)}, bf16[32,2048]{1,0:T(8,128)(2,1)S(1)}, u32[]{:S(2)}, u32[]{:S(2)}) collective-permute-start(bf16[32,2048]{1,0:T(8,128)(2,1)S(1)} %get-tuple-element.37), channel_id=1, source_target_pairs={{0,2},{2,0},{1,3},{3,1},{4,6},{6,4},{5,7},{7,5},{8,10},{10,8},{9,1... | collective-permute-start | bytes 393224 | tf_op jit(solution)/shard_map/ppermute | solution.py:293
  69.7 2.7 %collective-permute-done.17 = bf16[32,2048]{1,0:T(8,128)(2,1)S(1)} collective-permute-done((bf16[32,2048]{1,0:T(8,128)(2,1)S(1)}, bf16[32,2048]{1,0:T(8,128)(2,1)S(1)}, u32[]{:S(2)}, u32[]{:S(2)}) %collective-permute-start.17) | collective-permute-done | bytes 131104 | tf_op jit(solution)/shard_map/ppermute | solution.py:293
  72.4 1.3 %collective-permute-done.18 = bf16[32,2048]{1,0:T(8,128)(2,1)S(1)} collective-permute-done((bf16[32,2048]{1,0:T(8,128)(2,1)S(1)}, bf16[32,2048]{1,0:T(8,128)(2,1)S(1)}, u32[]{:S(2)}, u32[]{:S(2)}) %collective-permute-start.18) | collective-permute-done | bytes 131104 | tf_op jit(solution)/shard_map/ppermute | solution.py:17
  (87 shorter events, 6.6 us)
Async XLA Ops:
  0.6 54.2 %copy-start = (bf16[1,2048,64]{1,2,0:T(8,128)(2,1)S(1)}, bf16[1,2048,64]{1,2,0:T(8,128)(2,1)}, u32[]{:S(2)}) copy-start(bf16[1,2048,64]{1,2,0:T(8,128)(2,1)} %param.17) | copy-start | bytes 786436
  1.7 17.3 %collective-permute-start = (bf16[64,2048]{1,0:T(8,128)(2,1)S(1)}, bf16[64,2048]{1,0:T(8,128)(2,1)S(1)}, u32[]{:S(2)}, u32[]{:S(2)}) collective-permute-start(bf16[64,2048]{1,0:T(8,128)(2,1)S(1)} %dynamic-slice_bitcast_fusion), channel_id=1, source_target_pairs={{0,4},{4,0},{8,12},{12,8},{1,5},{5,1},{9,13},{13,9},{2,6},{6,2},{1... | collective-permute-start | bytes 786440 | tf_op jit(solution)/shard_map/ppermute | solution.py:17
  5.7 12.1 %collective-permute-start.1 = (bf16[32,2048]{1,0:T(8,128)(2,1)S(1)}, bf16[32,2048]{1,0:T(8,128)(2,1)S(1)}, u32[]{:S(2)}, u32[]{:S(2)}) collective-permute-start(bf16[32,2048]{1,0:T(8,128)(2,1)S(1)} %get-tuple-element.41.cot_ref), channel_id=1, source_target_pairs={{0,8},{4,12},{8,0},{12,4},{1,9},{5,13},{9,1},{13,5},{2,10},{6,14},... | collective-permute-start | bytes 393224 | tf_op jit(solution)/shard_map/ppermute | solution.py:17
  8.3 10.6 %collective-permute-start.2 = (bf16[32,2048]{1,0:T(8,128)(2,1)S(1)}, bf16[32,2048]{1,0:T(8,128)(2,1)S(1)}, u32[]{:S(2)}, u32[]{:S(2)}) collective-permute-start(bf16[32,2048]{1,0:T(8,128)(2,1)S(1)} %get-tuple-element.41.cot_ref), channel_id=1, source_target_pairs={{0,12},{4,8},{8,4},{12,0},{1,13},{5,9},{9,5},{13,1},{2,14},{6,10},... | collective-permute-start | bytes 393224 | tf_op jit(solution)/shard_map/ppermute | solution.py:17
  19.0 4.3 %collective-permute-start.3 = (bf16[128,2048]{1,0:T(8,128)(2,1)S(1)}, bf16[128,2048]{1,0:T(8,128)(2,1)S(1)}, u32[]{:S(2)}, u32[]{:S(2)}) collective-permute-start(bf16[128,2048]{1,0:T(8,128)(2,1)S(1)} %pad_maximum_fusion), channel_id=1, source_target_pairs={{0,1},{1,0},{2,3},{3,2},{4,5},{5,4},{6,7},{7,6},{8,9},{9,8},{10,11... | collective-permute-start | bytes 1572872 | tf_op jit(solution)/shard_map/ppermute | solution.py:17
  19.2 13.6 %collective-permute-start.6 = (bf16[32,2048]{1,0:T(8,128)(2,1)S(1)}, bf16[32,2048]{1,0:T(8,128)(2,1)S(1)}, u32[]{:S(2)}, u32[]{:S(2)}) collective-permute-start(bf16[32,2048]{1,0:T(8,128)(2,1)S(1)} %held.6), channel_id=1, source_target_pairs={{0,8},{4,12},{8,0},{12,4},{1,9},{5,13},{9,1},{13,5},{2,10},{6,14},... | collective-permute-start | bytes 393224 | tf_op jit(solution)/shard_map/ppermute | solution.py:17
  22.0 10.9 %collective-permute-start.5 = (bf16[32,2048]{1,0:T(8,128)(2,1)S(1)}, bf16[32,2048]{1,0:T(8,128)(2,1)S(1)}, u32[]{:S(2)}, u32[]{:S(2)}) collective-permute-start(bf16[32,2048]{1,0:T(8,128)(2,1)S(1)} %held.6), channel_id=1, source_target_pairs={{0,12},{4,8},{8,4},{12,0},{1,13},{5,9},{9,5},{13,1},{2,14},{6,10},... | collective-permute-start | bytes 393224 | tf_op jit(solution)/shard_map/ppermute | solution.py:17
  32.8 2.0 %collective-permute-start.4 = (bf16[128,2176]{1,0:T(8,128)(2,1)S(1)}, bf16[128,2176]{1,0:T(8,128)(2,1)S(1)}, u32[]{:S(2)}, u32[]{:S(2)}) collective-permute-start(bf16[128,2176]{1,0:T(8,128)(2,1)S(1)} %get-tuple-element.25), channel_id=1, source_target_pairs={{0,1},{1,0},{2,3},{3,2},{4,5},{5,4},{6,7},{7,6},{8,9},{9,8},{10,11... | collective-permute-start | bytes 1671176 | tf_op jit(solution)/shard_map/ppermute | solution.py:17
  34.9 4.7 %collective-permute-start.10 = (bf16[64,2048]{1,0:T(8,128)(2,1)S(1)}, bf16[64,2048]{1,0:T(8,128)(2,1)S(1)}, u32[]{:S(2)}, u32[]{:S(2)}) collective-permute-start(bf16[64,2048]{1,0:T(8,128)(2,1)S(1)} %held.9), channel_id=1, source_target_pairs={{0,1},{1,0},{2,3},{3,2},{4,5},{5,4},{6,7},{7,6},{8,9},{9,8},{10,11... | collective-permute-start | bytes 786440 | tf_op jit(solution)/shard_map/ppermute | solution.py:17
  35.1 13.9 %collective-permute-start.7 = (bf16[32,2176]{1,0:T(8,128)(2,1)S(1)}, bf16[32,2176]{1,0:T(8,128)(2,1)S(1)}, u32[]{:S(2)}, u32[]{:S(2)}) collective-permute-start(bf16[32,2176]{1,0:T(8,128)(2,1)S(1)} %get-tuple-element.27.refs_2_), channel_id=1, source_target_pairs={{0,12},{4,8},{8,4},{12,0},{1,13},{5,9},{9,5},{13,1},{2,14},{6,10},... | collective-permute-start | bytes 417800 | tf_op jit(solution)/shard_map/ppermute | solution.py:17
  37.7 12.3 %collective-permute-start.8 = (bf16[32,2176]{1,0:T(8,128)(2,1)S(1)}, bf16[32,2176]{1,0:T(8,128)(2,1)S(1)}, u32[]{:S(2)}, u32[]{:S(2)}) collective-permute-start(bf16[32,2176]{1,0:T(8,128)(2,1)S(1)} %get-tuple-element.28.refs_1_), channel_id=1, source_target_pairs={{0,8},{4,12},{8,0},{12,4},{1,9},{5,13},{9,1},{13,5},{2,10},{6,14},... | collective-permute-start | bytes 417800 | tf_op jit(solution)/shard_map/ppermute | solution.py:17
  37.7 12.3 %collective-permute-start.9 = (bf16[32,2176]{1,0:T(8,128)(2,1)S(1)}, bf16[32,2176]{1,0:T(8,128)(2,1)S(1)}, u32[]{:S(2)}, u32[]{:S(2)}) collective-permute-start(bf16[32,2176]{1,0:T(8,128)(2,1)S(1)} %get-tuple-element.29.refs_0_), channel_id=1, source_target_pairs={{0,4},{4,0},{8,12},{12,8},{1,5},{5,1},{9,13},{13,9},{2,6},{6,2},{1... | collective-permute-start | bytes 417800 | tf_op jit(solution)/shard_map/ppermute | solution.py:17
  39.6 10.5 %copy-start.6 = (f32[1,128,2]{1,2,0:T(2,128)S(1)}, f32[1,128,2]{1,2,0:T(2,128)}, u32[]{:S(2)}) copy-start(f32[1,128,2]{1,2,0:T(2,128)} %param.12) | copy-start | bytes 3076
  39.6 10.5 %copy-start.7 = (s32[1,1,2]{2,1,0:T(1,128)S(1)}, s32[1,1,2]{2,1,0:T(1,128)}, u32[]{:S(2)}) copy-start(s32[1,1,2]{2,1,0:T(1,128)} %param.11) | copy-start | bytes 28
  49.0 19.3 %copy-start.5 = (f32[1,128,64]{1,2,0:T(8,128)S(1)}, f32[1,128,64]{1,2,0:T(8,128)}, u32[]{:S(2)}) copy-start(f32[1,128,64]{1,2,0:T(8,128)} %param.16) | copy-start | bytes 98308
  50.0 2.0 %collective-permute-start.11 = (bf16[128,2176]{1,0:T(8,128)(2,1)S(1)}, bf16[128,2176]{1,0:T(8,128)(2,1)S(1)}, u32[]{:S(2)}, u32[]{:S(2)}) collective-permute-start(bf16[128,2176]{1,0:T(8,128)(2,1)S(1)} %held.10), channel_id=1, source_target_pairs={{0,1},{1,0},{2,3},{3,2},{4,5},{5,4},{6,7},{7,6},{8,9},{9,8},{10,11... | collective-permute-start | bytes 1671176 | tf_op jit(solution)/shard_map/ppermute | solution.py:17
  52.2 8.5 %collective-permute-start.12 = (bf16[32,2176]{1,0:T(8,128)(2,1)S(1)}, bf16[32,2176]{1,0:T(8,128)(2,1)S(1)}, u32[]{:S(2)}, u32[]{:S(2)}) collective-permute-start(bf16[32,2176]{1,0:T(8,128)(2,1)S(1)} %get-tuple-element.33), channel_id=1, source_target_pairs={{0,12},{4,8},{8,4},{12,0},{1,13},{5,9},{9,5},{13,1},{2,14},{6,10},... | collective-permute-start | bytes 417800 | tf_op jit(solution)/shard_map/ppermute | solution.py:17
  56.3 9.8 %collective-permute-start.15 = (bf16[32,2176]{1,0:T(8,128)(2,1)S(1)}, bf16[32,2176]{1,0:T(8,128)(2,1)S(1)}, u32[]{:S(2)}, u32[]{:S(2)}) collective-permute-start(bf16[32,2176]{1,0:T(8,128)(2,1)S(1)} %get-tuple-element.35), channel_id=1, source_target_pairs={{0,8},{4,12},{8,0},{12,4},{1,9},{5,13},{9,1},{13,5},{2,10},{6,14},... | collective-permute-start | bytes 417800 | tf_op jit(solution)/shard_map/ppermute | solution.py:17
  56.4 9.7 %collective-permute-start.16 = (bf16[32,2176]{1,0:T(8,128)(2,1)S(1)}, bf16[32,2176]{1,0:T(8,128)(2,1)S(1)}, u32[]{:S(2)}, u32[]{:S(2)}) collective-permute-start(bf16[32,2176]{1,0:T(8,128)(2,1)S(1)} %get-tuple-element.36), channel_id=1, source_target_pairs={{0,4},{4,0},{8,12},{12,8},{1,5},{5,1},{9,13},{13,9},{2,6},{6,2},{1... | collective-permute-start | bytes 417800 | tf_op jit(solution)/shard_map/ppermute | solution.py:17
  60.7 5.5 %collective-permute-start.13 = (bf16[32,2048]{1,0:T(8,128)(2,1)S(1)}, bf16[32,2048]{1,0:T(8,128)(2,1)S(1)}, u32[]{:S(2)}, u32[]{:S(2)}) collective-permute-start(bf16[32,2048]{1,0:T(8,128)(2,1)S(1)} %held.11), channel_id=1, source_target_pairs={{0,2},{2,0},{1,3},{3,1},{4,6},{6,4},{5,7},{7,5},{8,10},{10,8},{9,1... | collective-permute-start | bytes 393224 | tf_op jit(solution)/shard_map/ppermute | solution.py:293
  66.3 1.9 %collective-permute-start.19 = (f32[64,128]{1,0:T(8,128)S(1)}, f32[64,128]{1,0:T(8,128)S(1)}, u32[]{:S(2)}, u32[]{:S(2)}) collective-permute-start(f32[64,128]{1,0:T(8,128)S(1)} %constant_dynamic-update-slice_fusion.6), channel_id=1, source_target_pairs={{0,1},{1,0},{2,3},{3,2},{4,5},{5,4},{6,7},{7,6},{8,9},{9,8},{10,11... | collective-permute-start | bytes 98312 | tf_op jit(solution)/shard_map/ppermute | solution.py:17
  66.5 5.9 %collective-permute-start.17 = (bf16[32,2048]{1,0:T(8,128)(2,1)S(1)}, bf16[32,2048]{1,0:T(8,128)(2,1)S(1)}, u32[]{:S(2)}, u32[]{:S(2)}) collective-permute-start(bf16[32,2048]{1,0:T(8,128)(2,1)S(1)} %get-tuple-element.37), channel_id=1, source_target_pairs={{0,2},{2,0},{1,3},{3,1},{4,6},{6,4},{5,7},{7,5},{8,10},{10,8},{9,1... | collective-permute-start | bytes 393224 | tf_op jit(solution)/shard_map/ppermute | solution.py:293
  68.0 4.4 %collective-permute-start.14 = (bf16[32,2048]{1,0:T(8,128)(2,1)S(1)}, bf16[32,2048]{1,0:T(8,128)(2,1)S(1)}, u32[]{:S(2)}, u32[]{:S(2)}) collective-permute-start(bf16[32,2048]{1,0:T(8,128)(2,1)S(1)} %collective-permute-done.13.refs_3_), channel_id=1, source_target_pairs={{0,1},{1,0},{2,3},{3,2},{4,5},{5,4},{6,7},{7,6},{8,9},{9,8},{10,11... | collective-permute-start | bytes 393224 | tf_op jit(solution)/shard_map/ppermute | solution.py:17
  72.4 1.3 %collective-permute-start.18 = (bf16[32,2048]{1,0:T(8,128)(2,1)S(1)}, bf16[32,2048]{1,0:T(8,128)(2,1)S(1)}, u32[]{:S(2)}, u32[]{:S(2)}) collective-permute-start(bf16[32,2048]{1,0:T(8,128)(2,1)S(1)} %collective-permute-done.17), channel_id=1, source_target_pairs={{0,1},{1,0},{2,3},{3,2},{4,5},{5,4},{6,7},{7,6},{8,9},{9,8},{10,11... | collective-permute-start | bytes 393224 | tf_op jit(solution)/shard_map/ppermute | solution.py:17
  (5 other events, 23.6 us)

commit v14 on v13

--- a/solution.py
+++ b/solution.py
@@ -308,7 +308,8 @@
     slope, down_part, down_here = slopes(pre_all, sketch_t, down_weight[0, 0], place, core)
     near_rows = xored(cot_mine, "dp", 1)
     fetched = {slot: xored(cot_mine[:rows], "dp", slot) for slot in order}
-    own, sent, grad, passed, backs = (), (), (), (), ()
+    out_vec = jnp.dot(cot, model_sketch[0], preferred_element_type=jnp.float32)
+    own, sent, grad, passed, backs = (), (out_vec,), (), (), ()
     below_mine, vectors = [], []
     for a in range(CHUNKS):
         part = slice(a * rows, (a + 1) * rows)
@@ -357,7 +358,6 @@
         [jnp.where(core == 0, vec_mine, vec_theirs), jnp.where(core == 0, vec_theirs, vec_mine)],
         axis=0,
     )
-    out_vec = jnp.dot(cot, model_sketch[0], preferred_element_type=jnp.float32)
     counts = lengths[0, 0]
     upto = jnp.arange(counts.shape[0])
     ends = jnp.sum(jnp.where(upto[None, :] <= upto[:, None], counts[None, :], 0), axis=1)

time: 74.9 us -> 77.3 us (1.032)
  waiting for transfers between devices: 15.7 us -> 17.3 us
  Pallas kernels: 25.7 us -> 26.8 us
    ppermute x18, waiting for transfers between devices: 13 us -> 14.6 us  [xored(): return lax.ppermute(block, axis, [(i, i ^ bits) for i in range(n)])]
    pallas_call x6, Pallas kernels: 0.1 us -> 0.9 us  [held(): pl.pallas_call(held_kernel, in_specs=[RESIDENT] + [ANYWHERE] * len(events...]
    unnamed x34 -> x36, local copies, waits for them, and re-layouts: 4.38 us -> 4.43 us
  transfers between devices with their start and end apart: 20 -> 20, of which waited for: 8 -> 8; matrix products, arithmetic and copies ran while one was open for 6% -> 6% of each run, Pallas kernels for 34% -> 33%
where the time goes in v14:
time: 77.3 us; the launch traced here: 76.9 us
  Pallas kernels  26.8 us (35%)
  starting transfers between devices  22 us (28%)
  waiting for transfers between devices  17.3 us (22%)
  local copies, waits for them, and re-layouts  5.74 us (7%)
  other arithmetic  2.14 us (3%)
  matrix products  1.86 us (2%)
  between operations  1.04 us (1%)
    pallas_call x2, Pallas kernels, expert(): pl.pallas_call(functools.partial(expert_kernel, chunk, tile_f, tile_d), i...  19 us
    ppermute x18, starting transfers between devices, xored(): return lax.ppermute(block, axis, [(i, i ^ bits) for i in range(n)])  19 us
    ppermute x18, waiting for transfers between devices, xored(): return lax.ppermute(block, axis, [(i, i ^ bits) for i in range(n)])  14.6 us
    pallas_call x1, Pallas kernels, slopes(): pl.pallas_call(functools.partial(slope_kernel, groups), grid_spec=pltpu.P...  6.27 us
    unnamed x36, local copies, waits for them, and re-layouts  4.43 us
    ppermute x2, starting transfers between devices, below(): lax.ppermute(block, 'section', [(s, (s - 1) % sections) for s in range(se...  3.06 us
    ppermute x2, waiting for transfers between devices, below(): lax.ppermute(block, 'section', [(s, (s - 1) % sections) for s in range(se...  2.71 us
    broadcast_in_dim x2, other arithmetic, per_device(): return (handed[None], features[None])  1.6 us
  transfers between devices with their start and end apart: 20, of which 8 were waited for; matrix products, arithmetic and copies ran while one was open for 6% of the time, Pallas kernels for 33%

profile of v14, /device:TPU:0, one launch (start us, length us, event | category | flops | bytes accessed | tf_op | source)
XLA Modules:
  0.0 76.9 jit_solution(1091623320379847060)
XLA Ops:
  0.7 1.0 %constant_dynamic-update-slice_fusion.2 = (bf16[256,2048]{1,0:T(8,128)(2,1)S(1)}, bf16[32,2048]{1,0:T(8,128)(2,1)S(1)}) fusion(bf16[1,128,2048]{2,1,0:T(8,128)(2,1)} %param.10, s32[]{:T(128)S(6)} %select_n.53), kind=kLoop, calls=%fused_computation.42 | loop fusion | bytes 393220
  1.6 4.1 %collective-permute-start.1 = (bf16[32,2048]{1,0:T(8,128)(2,1)S(1)}, bf16[32,2048]{1,0:T(8,128)(2,1)S(1)}, u32[]{:S(2)}, u32[]{:S(2)}) collective-permute-start(bf16[32,2048]{1,0:T(8,128)(2,1)S(1)} %get-tuple-element.41.cot_ref), channel_id=1, source_target_pairs={{0,8},{4,12},{8,0},{12,4},{1,9},{5,13},{9,1},{13,5},{2,10},{6,14},... | collective-permute-start | bytes 393224 | tf_op jit(solution)/shard_map/ppermute | solution.py:17
  5.7 1.3 %collective-permute-start.2 = (bf16[32,2048]{1,0:T(8,128)(2,1)S(1)}, bf16[32,2048]{1,0:T(8,128)(2,1)S(1)}, u32[]{:S(2)}, u32[]{:S(2)}) collective-permute-start(bf16[32,2048]{1,0:T(8,128)(2,1)S(1)} %get-tuple-element.41.cot_ref), channel_id=1, source_target_pairs={{0,12},{4,8},{8,4},{12,0},{1,13},{5,9},{9,5},{13,1},{2,14},{6,10},... | collective-permute-start | bytes 393224 | tf_op jit(solution)/shard_map/ppermute | solution.py:17
  8.3 1.3 %fusion = f32[128,64]{0,1:T(8,128)S(1)} fusion(bf16[1,128,2048]{2,1,0:T(8,128)(2,1)} %param.10, bf16[1,2048,64]{1,2,0:T(8,128)(2,1)S(1)} %copy-done), kind=kOutput, calls=%fused_computation.4 | convolution fusion | flops 33554432 | bytes 819200 | tf_op jit(solution)/shard_map/dot_general | solution.py:311
  9.9 2.0 %copy-done.2 = bf16[1,1,4,128,3584]{4,3,2,1,0:T(8,128)(2,1)S(1)} copy-done((bf16[1,1,4,128,3584]{4,3,2,1,0:T(8,128)(2,1)S(1)}, bf16[1,1,4,128,3584]{4,3,2,1,0:T(8,128)(2,1)}, u32[]{:S(2)}) %copy-start.2) | copy-done | bytes 3670040
  11.9 1.0 %copy-done.3 = bf16[1,1,3584,64]{2,3,1,0:T(8,128)(2,1)S(1)} copy-done((bf16[1,1,3584,64]{2,3,1,0:T(8,128)(2,1)S(1)}, bf16[1,1,3584,64]{2,3,1,0:T(8,128)(2,1)}, u32[]{:S(2)}) %copy-start.3) | copy-done | bytes 458776
  12.9 6.3 %slopes.1 = (bf16[2,3584,256]{2,1,0:T(8,128)(2,1)S(1)}, f32[2,256,64]{2,1,0:T(8,128)S(1)}, bf16[3584,2048]{1,0:T(8,128)(2,1)S(1)}) custom-call(s32[2]{0:T(128)S(1)} %pad_add_fusion.index_ref, bf16[4,2,2,32,3584]{4,3,2,1,0:T(8,128)(2,1)S(1)} %bitcast.52, bf16[4,2,2,32,3584]{4,3,2,1,0:T(8,128)(2,1)S(1)} %bitcast.53, bf16[4,2,2,32,3584]{4,3,2,1,0:T(8,128)(2,1)S(1)} %bitcast.54, ...), custom_call_target="tpu_custom_call" | custom-call | flops 234881024 | bytes 7340032 | tf_op jit(solution)/shard_map/slopes/pallas_call | solution.py:149
  20.2 2.2 %collective-permute-start.6 = (bf16[32,2048]{1,0:T(8,128)(2,1)S(1)}, bf16[32,2048]{1,0:T(8,128)(2,1)S(1)}, u32[]{:S(2)}, u32[]{:S(2)}) collective-permute-start(bf16[32,2048]{1,0:T(8,128)(2,1)S(1)} %held.6), channel_id=1, source_target_pairs={{0,8},{4,12},{8,0},{12,4},{1,9},{5,13},{9,1},{13,5},{2,10},{6,14},... | collective-permute-start | bytes 393224 | tf_op jit(solution)/shard_map/ppermute | solution.py:17
  22.4 1.4 %collective-permute-start.5 = (bf16[32,2048]{1,0:T(8,128)(2,1)S(1)}, bf16[32,2048]{1,0:T(8,128)(2,1)S(1)}, u32[]{:S(2)}, u32[]{:S(2)}) collective-permute-start(bf16[32,2048]{1,0:T(8,128)(2,1)S(1)} %held.6), channel_id=1, source_target_pairs={{0,12},{4,8},{8,4},{12,0},{1,13},{5,9},{9,5},{13,1},{2,14},{6,10},... | collective-permute-start | bytes 393224 | tf_op jit(solution)/shard_map/ppermute | solution.py:17
  23.8 9.5 %expert.2 = (f32[128,2176]{1,0:T(8,128)S(1)}, bf16[128,2176]{1,0:T(8,128)(2,1)S(1)}) custom-call(bf16[256,2048]{1,0:T(8,128)(2,1)S(1)} %slice_dynamic-update-slice_fusion.4.rows_ref, bf16[2,3584,256]{2,1,0:T(8,128)(2,1)S(1)} %get-tuple-element.21.slope_ref, f32[2,256,64]{2,1,0:T(8,128)S(1)} %get-tuple-element.22.down_part_ref, ...), custom_call_target="tpu_custom_call" | custom-call | flops 7516192768 | bytes 29360128 | tf_op jit(solution)/shard_map/expert/pallas_call | solution.py:237
  33.6 1.7 %collective-permute-done.4.came_ref = bf16[128,2176]{1,0:T(8,128)(2,1)S(1)} collective-permute-done((bf16[128,2176]{1,0:T(8,128)(2,1)S(1)}, bf16[128,2176]{1,0:T(8,128)(2,1)S(1)}, u32[]{:S(2)}, u32[]{:S(2)}) %collective-permute-start.4) | collective-permute-done | bytes 557088 | tf_op jit(solution)/shard_map/ppermute | solution.py:17
  35.8 2.5 %collective-permute-start.7 = (bf16[32,2176]{1,0:T(8,128)(2,1)S(1)}, bf16[32,2176]{1,0:T(8,128)(2,1)S(1)}, u32[]{:S(2)}, u32[]{:S(2)}) collective-permute-start(bf16[32,2176]{1,0:T(8,128)(2,1)S(1)} %get-tuple-element.27.refs_2_), channel_id=1, source_target_pairs={{0,12},{4,8},{8,4},{12,0},{1,13},{5,9},{9,5},{13,1},{2,14},{6,10},... | collective-permute-start | bytes 417800 | tf_op jit(solution)/shard_map/ppermute | solution.py:17
  38.3 1.9 %collective-permute-start.9 = (bf16[32,2176]{1,0:T(8,128)(2,1)S(1)}, bf16[32,2176]{1,0:T(8,128)(2,1)S(1)}, u32[]{:S(2)}, u32[]{:S(2)}) collective-permute-start(bf16[32,2176]{1,0:T(8,128)(2,1)S(1)} %get-tuple-element.29.refs_0_), channel_id=1, source_target_pairs={{0,4},{4,0},{8,12},{12,8},{1,5},{5,1},{9,13},{13,9},{2,6},{6,2},{1... | collective-permute-start | bytes 417800 | tf_op jit(solution)/shard_map/ppermute | solution.py:17
  40.3 9.5 %expert.3 = (f32[128,2176]{1,0:T(8,128)S(1)}, bf16[128,2176]{1,0:T(8,128)(2,1)S(1)}) custom-call(bf16[256,2048]{1,0:T(8,128)(2,1)S(1)} %slice_dynamic-update-slice_fusion.rows_ref, bf16[2,3584,256]{2,1,0:T(8,128)(2,1)S(1)} %get-tuple-element.21.slope_ref, f32[2,256,64]{2,1,0:T(8,128)S(1)} %get-tuple-element.22.down_part_ref, bf16[64,3584]{1,0:T(8,128)(2,1)S(1)} %bitcast.62, ...), custom_call_target="tpu_custom_call" | custom-call | flops 7516192768 | bytes 29360128 | tf_op jit(solution)/shard_map/expert/pallas_call | solution.py:237
  49.8 1.5 %collective-permute-done.8.refs_1_ = bf16[32,2176]{1,0:T(8,128)(2,1)S(1)} collective-permute-done((bf16[32,2176]{1,0:T(8,128)(2,1)S(1)}, bf16[32,2176]{1,0:T(8,128)(2,1)S(1)}, u32[]{:S(2)}, u32[]{:S(2)}) %collective-permute-start.8) | collective-permute-done | bytes 139296 | tf_op jit(solution)/shard_map/ppermute | solution.py:17
  52.7 1.6 %collective-permute-done.11.came_ref = bf16[128,2176]{1,0:T(8,128)(2,1)S(1)} collective-permute-done((bf16[128,2176]{1,0:T(8,128)(2,1)}, bf16[128,2176]{1,0:T(8,128)(2,1)S(1)}, u32[]{:S(2)}, u32[]{:S(2)}) %collective-permute-start.11) | collective-permute-done | bytes 557088 | tf_op jit(solution)/shard_map/ppermute | solution.py:17
  54.4 2.7 %collective-permute-start.12 = (bf16[32,2176]{1,0:T(8,128)(2,1)S(1)}, bf16[32,2176]{1,0:T(8,128)(2,1)S(1)}, u32[]{:S(2)}, u32[]{:S(2)}) collective-permute-start(bf16[32,2176]{1,0:T(8,128)(2,1)S(1)} %get-tuple-element.33), channel_id=1, source_target_pairs={{0,12},{4,8},{8,4},{12,0},{1,13},{5,9},{9,5},{13,1},{2,14},{6,10},... | collective-permute-start | bytes 417800 | tf_op jit(solution)/shard_map/ppermute | solution.py:17
  57.3 1.7 %collective-permute-start.16 = (bf16[32,2176]{1,0:T(8,128)(2,1)S(1)}, bf16[32,2176]{1,0:T(8,128)(2,1)S(1)}, u32[]{:S(2)}, u32[]{:S(2)}) collective-permute-start(bf16[32,2176]{1,0:T(8,128)(2,1)S(1)} %get-tuple-element.36), channel_id=1, source_target_pairs={{0,4},{4,0},{8,12},{12,8},{1,5},{5,1},{9,13},{13,9},{2,6},{6,2},{1... | collective-permute-start | bytes 417800 | tf_op jit(solution)/shard_map/ppermute | solution.py:17
  59.0 3.8 %collective-permute-done.12.refs_0_ = bf16[32,2176]{1,0:T(8,128)(2,1)S(1)} collective-permute-done((bf16[32,2176]{1,0:T(8,128)(2,1)S(1)}, bf16[32,2176]{1,0:T(8,128)(2,1)S(1)}, u32[]{:S(2)}, u32[]{:S(2)}) %collective-permute-start.12) | collective-permute-done | bytes 139296 | tf_op jit(solution)/shard_map/ppermute | solution.py:17
  62.9 1.6 %collective-permute-start.13 = (bf16[32,2048]{1,0:T(8,128)(2,1)S(1)}, bf16[32,2048]{1,0:T(8,128)(2,1)S(1)}, u32[]{:S(2)}, u32[]{:S(2)}) collective-permute-start(bf16[32,2048]{1,0:T(8,128)(2,1)S(1)} %held.11), channel_id=1, source_target_pairs={{0,2},{2,0},{1,3},{3,1},{4,6},{6,4},{5,7},{7,5},{8,10},{10,8},{9,1... | collective-permute-start | bytes 393224 | tf_op jit(solution)/shard_map/ppermute | solution.py:293
  64.6 3.9 %collective-permute-done.15.refs_1_ = bf16[32,2176]{1,0:T(8,128)(2,1)S(1)} collective-permute-done((bf16[32,2176]{1,0:T(8,128)(2,1)S(1)}, bf16[32,2176]{1,0:T(8,128)(2,1)S(1)}, u32[]{:S(2)}, u32[]{:S(2)}) %collective-permute-start.15) | collective-permute-done | bytes 139296 | tf_op jit(solution)/shard_map/ppermute | solution.py:17
  68.8 1.5 %collective-permute-start.17 = (bf16[32,2048]{1,0:T(8,128)(2,1)S(1)}, bf16[32,2048]{1,0:T(8,128)(2,1)S(1)}, u32[]{:S(2)}, u32[]{:S(2)}) collective-permute-start(bf16[32,2048]{1,0:T(8,128)(2,1)S(1)} %get-tuple-element.37), channel_id=1, source_target_pairs={{0,2},{2,0},{1,3},{3,1},{4,6},{6,4},{5,7},{7,5},{8,10},{10,8},{9,1... | collective-permute-start | bytes 393224 | tf_op jit(solution)/shard_map/ppermute | solution.py:293
  72.0 2.7 %collective-permute-done.17 = bf16[32,2048]{1,0:T(8,128)(2,1)S(1)} collective-permute-done((bf16[32,2048]{1,0:T(8,128)(2,1)S(1)}, bf16[32,2048]{1,0:T(8,128)(2,1)S(1)}, u32[]{:S(2)}, u32[]{:S(2)}) %collective-permute-start.17) | collective-permute-done | bytes 131104 | tf_op jit(solution)/shard_map/ppermute | solution.py:293
  74.7 1.3 %collective-permute-done.18 = bf16[32,2048]{1,0:T(8,128)(2,1)S(1)} collective-permute-done((bf16[32,2048]{1,0:T(8,128)(2,1)S(1)}, bf16[32,2048]{1,0:T(8,128)(2,1)S(1)}, u32[]{:S(2)}, u32[]{:S(2)}) %collective-permute-start.18) | collective-permute-done | bytes 131104 | tf_op jit(solution)/shard_map/ppermute | solution.py:17
  (90 shorter events, 7.7 us)
Async XLA Ops:
  1.6 17.6 %collective-permute-start.1 = (bf16[32,2048]{1,0:T(8,128)(2,1)S(1)}, bf16[32,2048]{1,0:T(8,128)(2,1)S(1)}, u32[]{:S(2)}, u32[]{:S(2)}) collective-permute-start(bf16[32,2048]{1,0:T(8,128)(2,1)S(1)} %get-tuple-element.41.cot_ref), channel_id=1, source_target_pairs={{0,8},{4,12},{8,0},{12,4},{1,9},{5,13},{9,1},{13,5},{2,10},{6,14},... | collective-permute-start | bytes 393224 | tf_op jit(solution)/shard_map/ppermute | solution.py:17
  5.7 13.5 %collective-permute-start.2 = (bf16[32,2048]{1,0:T(8,128)(2,1)S(1)}, bf16[32,2048]{1,0:T(8,128)(2,1)S(1)}, u32[]{:S(2)}, u32[]{:S(2)}) collective-permute-start(bf16[32,2048]{1,0:T(8,128)(2,1)S(1)} %get-tuple-element.41.cot_ref), channel_id=1, source_target_pairs={{0,12},{4,8},{8,4},{12,0},{1,13},{5,9},{9,5},{13,1},{2,14},{6,10},... | collective-permute-start | bytes 393224 | tf_op jit(solution)/shard_map/ppermute | solution.py:17
  8.0 11.9 %collective-permute-start = (bf16[64,2048]{1,0:T(8,128)(2,1)S(1)}, bf16[64,2048]{1,0:T(8,128)(2,1)S(1)}, u32[]{:S(2)}, u32[]{:S(2)}) collective-permute-start(bf16[64,2048]{1,0:T(8,128)(2,1)S(1)} %dynamic-slice_bitcast_fusion), channel_id=1, source_target_pairs={{0,4},{4,0},{8,12},{12,8},{1,5},{5,1},{9,13},{13,9},{2,6},{6,2},{1... | collective-permute-start | bytes 786440 | tf_op jit(solution)/shard_map/ppermute | solution.py:17
  20.0 3.8 %collective-permute-start.3 = (bf16[128,2048]{1,0:T(8,128)(2,1)S(1)}, bf16[128,2048]{1,0:T(8,128)(2,1)S(1)}, u32[]{:S(2)}, u32[]{:S(2)}) collective-permute-start(bf16[128,2048]{1,0:T(8,128)(2,1)S(1)} %pad_maximum_fusion), channel_id=1, source_target_pairs={{0,1},{1,0},{2,3},{3,2},{4,5},{5,4},{6,7},{7,6},{8,9},{9,8},{10,11... | collective-permute-start | bytes 1572872 | tf_op jit(solution)/shard_map/ppermute | solution.py:17
  20.2 13.3 %collective-permute-start.6 = (bf16[32,2048]{1,0:T(8,128)(2,1)S(1)}, bf16[32,2048]{1,0:T(8,128)(2,1)S(1)}, u32[]{:S(2)}, u32[]{:S(2)}) collective-permute-start(bf16[32,2048]{1,0:T(8,128)(2,1)S(1)} %held.6), channel_id=1, source_target_pairs={{0,8},{4,12},{8,0},{12,4},{1,9},{5,13},{9,1},{13,5},{2,10},{6,14},... | collective-permute-start | bytes 393224 | tf_op jit(solution)/shard_map/ppermute | solution.py:17
  22.4 11.2 %collective-permute-start.5 = (bf16[32,2048]{1,0:T(8,128)(2,1)S(1)}, bf16[32,2048]{1,0:T(8,128)(2,1)S(1)}, u32[]{:S(2)}, u32[]{:S(2)}) collective-permute-start(bf16[32,2048]{1,0:T(8,128)(2,1)S(1)} %held.6), channel_id=1, source_target_pairs={{0,12},{4,8},{8,4},{12,0},{1,13},{5,9},{9,5},{13,1},{2,14},{6,10},... | collective-permute-start | bytes 393224 | tf_op jit(solution)/shard_map/ppermute | solution.py:17
  33.3 2.0 %collective-permute-start.4 = (bf16[128,2176]{1,0:T(8,128)(2,1)S(1)}, bf16[128,2176]{1,0:T(8,128)(2,1)S(1)}, u32[]{:S(2)}, u32[]{:S(2)}) collective-permute-start(bf16[128,2176]{1,0:T(8,128)(2,1)S(1)} %get-tuple-element.25), channel_id=1, source_target_pairs={{0,1},{1,0},{2,3},{3,2},{4,5},{5,4},{6,7},{7,6},{8,9},{9,8},{10,11... | collective-permute-start | bytes 1671176 | tf_op jit(solution)/shard_map/ppermute | solution.py:17
  35.5 4.7 %collective-permute-start.10 = (bf16[64,2048]{1,0:T(8,128)(2,1)S(1)}, bf16[64,2048]{1,0:T(8,128)(2,1)S(1)}, u32[]{:S(2)}, u32[]{:S(2)}) collective-permute-start(bf16[64,2048]{1,0:T(8,128)(2,1)S(1)} %held.9), channel_id=1, source_target_pairs={{0,1},{1,0},{2,3},{3,2},{4,5},{5,4},{6,7},{7,6},{8,9},{9,8},{10,11... | collective-permute-start | bytes 786440 | tf_op jit(solution)/shard_map/ppermute | solution.py:17
  35.8 14.1 %collective-permute-start.7 = (bf16[32,2176]{1,0:T(8,128)(2,1)S(1)}, bf16[32,2176]{1,0:T(8,128)(2,1)S(1)}, u32[]{:S(2)}, u32[]{:S(2)}) collective-permute-start(bf16[32,2176]{1,0:T(8,128)(2,1)S(1)} %get-tuple-element.27.refs_2_), channel_id=1, source_target_pairs={{0,12},{4,8},{8,4},{12,0},{1,13},{5,9},{9,5},{13,1},{2,14},{6,10},... | collective-permute-start | bytes 417800 | tf_op jit(solution)/shard_map/ppermute | solution.py:17
  38.3 13.0 %collective-permute-start.8 = (bf16[32,2176]{1,0:T(8,128)(2,1)S(1)}, bf16[32,2176]{1,0:T(8,128)(2,1)S(1)}, u32[]{:S(2)}, u32[]{:S(2)}) collective-permute-start(bf16[32,2176]{1,0:T(8,128)(2,1)S(1)} %get-tuple-element.28.refs_1_), channel_id=1, source_target_pairs={{0,8},{4,12},{8,0},{12,4},{1,9},{5,13},{9,1},{13,5},{2,10},{6,14},... | collective-permute-start | bytes 417800 | tf_op jit(solution)/shard_map/ppermute | solution.py:17
  38.3 13.0 %collective-permute-start.9 = (bf16[32,2176]{1,0:T(8,128)(2,1)S(1)}, bf16[32,2176]{1,0:T(8,128)(2,1)S(1)}, u32[]{:S(2)}, u32[]{:S(2)}) collective-permute-start(bf16[32,2176]{1,0:T(8,128)(2,1)S(1)} %get-tuple-element.29.refs_0_), channel_id=1, source_target_pairs={{0,4},{4,0},{8,12},{12,8},{1,5},{5,1},{9,13},{13,9},{2,6},{6,2},{1... | collective-permute-start | bytes 417800 | tf_op jit(solution)/shard_map/ppermute | solution.py:17
  40.3 11.9 %copy-start.7 = (f32[1,128,2]{1,2,0:T(2,128)S(1)}, f32[1,128,2]{1,2,0:T(2,128)}, u32[]{:S(2)}) copy-start(f32[1,128,2]{1,2,0:T(2,128)} %param.12) | copy-start | bytes 3076
  40.3 12.0 %copy-start.8 = (s32[1,1,2]{2,1,0:T(1,128)S(1)}, s32[1,1,2]{2,1,0:T(1,128)}, u32[]{:S(2)}) copy-start(s32[1,1,2]{2,1,0:T(1,128)} %param.11) | copy-start | bytes 28
  49.8 20.9 %copy-start.6 = (f32[1,128,64]{1,2,0:T(8,128)S(1)}, f32[1,128,64]{1,2,0:T(8,128)}, u32[]{:S(2)}) copy-start(f32[1,128,64]{1,2,0:T(8,128)} %param.16) | copy-start | bytes 98308
  52.2 2.2 %collective-permute-start.11 = (bf16[128,2176]{1,0:T(8,128)(2,1)}, bf16[128,2176]{1,0:T(8,128)(2,1)S(1)}, u32[]{:S(2)}, u32[]{:S(2)}) collective-permute-start(bf16[128,2176]{1,0:T(8,128)(2,1)} %held.10), channel_id=1, source_target_pairs={{0,1},{1,0},{2,3},{3,2},{4,5},{5,4},{6,7},{7,6},{8,9},{9,8},{10,11... | collective-permute-start | bytes 1671176 | tf_op jit(solution)/shard_map/ppermute | solution.py:17
  52.4 24.5 %copy-start.1 = (bf16[1,2048,64]{1,2,0:T(8,128)(2,1)S(1)}, bf16[1,2048,64]{1,2,0:T(8,128)(2,1)}, u32[]{:S(2)}) copy-start(bf16[1,2048,64]{1,2,0:T(8,128)(2,1)} %param.17) | copy-start | bytes 786436
  54.4 8.5 %collective-permute-start.12 = (bf16[32,2176]{1,0:T(8,128)(2,1)S(1)}, bf16[32,2176]{1,0:T(8,128)(2,1)S(1)}, u32[]{:S(2)}, u32[]{:S(2)}) collective-permute-start(bf16[32,2176]{1,0:T(8,128)(2,1)S(1)} %get-tuple-element.33), channel_id=1, source_target_pairs={{0,12},{4,8},{8,4},{12,0},{1,13},{5,9},{9,5},{13,1},{2,14},{6,10},... | collective-permute-start | bytes 417800 | tf_op jit(solution)/shard_map/ppermute | solution.py:17
  57.2 11.2 %collective-permute-start.15 = (bf16[32,2176]{1,0:T(8,128)(2,1)S(1)}, bf16[32,2176]{1,0:T(8,128)(2,1)S(1)}, u32[]{:S(2)}, u32[]{:S(2)}) collective-permute-start(bf16[32,2176]{1,0:T(8,128)(2,1)S(1)} %get-tuple-element.35), channel_id=1, source_target_pairs={{0,8},{4,12},{8,0},{12,4},{1,9},{5,13},{9,1},{13,5},{2,10},{6,14},... | collective-permute-start | bytes 417800 | tf_op jit(solution)/shard_map/ppermute | solution.py:17
  57.3 11.1 %collective-permute-start.16 = (bf16[32,2176]{1,0:T(8,128)(2,1)S(1)}, bf16[32,2176]{1,0:T(8,128)(2,1)S(1)}, u32[]{:S(2)}, u32[]{:S(2)}) collective-permute-start(bf16[32,2176]{1,0:T(8,128)(2,1)S(1)} %get-tuple-element.36), channel_id=1, source_target_pairs={{0,4},{4,0},{8,12},{12,8},{1,5},{5,1},{9,13},{13,9},{2,6},{6,2},{1... | collective-permute-start | bytes 417800 | tf_op jit(solution)/shard_map/ppermute | solution.py:17
  62.9 5.5 %collective-permute-start.13 = (bf16[32,2048]{1,0:T(8,128)(2,1)S(1)}, bf16[32,2048]{1,0:T(8,128)(2,1)S(1)}, u32[]{:S(2)}, u32[]{:S(2)}) collective-permute-start(bf16[32,2048]{1,0:T(8,128)(2,1)S(1)} %held.11), channel_id=1, source_target_pairs={{0,2},{2,0},{1,3},{3,1},{4,6},{6,4},{5,7},{7,5},{8,10},{10,8},{9,1... | collective-permute-start | bytes 393224 | tf_op jit(solution)/shard_map/ppermute | solution.py:293
  68.6 1.9 %collective-permute-start.19 = (f32[64,128]{1,0:T(8,128)S(1)}, f32[64,128]{1,0:T(8,128)S(1)}, u32[]{:S(2)}, u32[]{:S(2)}) collective-permute-start(f32[64,128]{1,0:T(8,128)S(1)} %constant_dynamic-update-slice_fusion.6), channel_id=1, source_target_pairs={{0,1},{1,0},{2,3},{3,2},{4,5},{5,4},{6,7},{7,6},{8,9},{9,8},{10,11... | collective-permute-start | bytes 98312 | tf_op jit(solution)/shard_map/ppermute | solution.py:17
  68.8 5.9 %collective-permute-start.17 = (bf16[32,2048]{1,0:T(8,128)(2,1)S(1)}, bf16[32,2048]{1,0:T(8,128)(2,1)S(1)}, u32[]{:S(2)}, u32[]{:S(2)}) collective-permute-start(bf16[32,2048]{1,0:T(8,128)(2,1)S(1)} %get-tuple-element.37), channel_id=1, source_target_pairs={{0,2},{2,0},{1,3},{3,1},{4,6},{6,4},{5,7},{7,5},{8,10},{10,8},{9,1... | collective-permute-start | bytes 393224 | tf_op jit(solution)/shard_map/ppermute | solution.py:293
  70.3 4.4 %collective-permute-start.14 = (bf16[32,2048]{1,0:T(8,128)(2,1)S(1)}, bf16[32,2048]{1,0:T(8,128)(2,1)S(1)}, u32[]{:S(2)}, u32[]{:S(2)}) collective-permute-start(bf16[32,2048]{1,0:T(8,128)(2,1)S(1)} %collective-permute-done.13.refs_3_), channel_id=1, source_target_pairs={{0,1},{1,0},{2,3},{3,2},{4,5},{5,4},{6,7},{7,6},{8,9},{9,8},{10,11... | collective-permute-start | bytes 393224 | tf_op jit(solution)/shard_map/ppermute | solution.py:17
  74.7 1.3 %collective-permute-start.18 = (bf16[32,2048]{1,0:T(8,128)(2,1)S(1)}, bf16[32,2048]{1,0:T(8,128)(2,1)S(1)}, u32[]{:S(2)}, u32[]{:S(2)}) collective-permute-start(bf16[32,2048]{1,0:T(8,128)(2,1)S(1)} %collective-permute-done.17), channel_id=1, source_target_pairs={{0,1},{1,0},{2,3},{3,2},{4,5},{5,4},{6,7},{7,6},{8,9},{9,8},{10,11... | collective-permute-start | bytes 393224 | tf_op jit(solution)/shard_map/ppermute | solution.py:17
  (6 other events, 29.9 us)

commit v15 on v14

--- a/solution.py
+++ b/solution.py
@@ -309,7 +309,7 @@
     near_rows = xored(cot_mine, "dp", 1)
     fetched = {slot: xored(cot_mine[:rows], "dp", slot) for slot in order}
     out_vec = jnp.dot(cot, model_sketch[0], preferred_element_type=jnp.float32)
-    own, sent, grad, passed, backs = (), (out_vec,), (), (), ()
+    own, sent, grad, passed, backs = (), (), (), (), ()
     below_mine, vectors = [], []
     for a in range(CHUNKS):
         part = slice(a * rows, (a + 1) * rows)
@@ -336,7 +336,7 @@
             fetched = {slot: held(xored(coming, "dp", slot), kept) for slot in order}
             late = tuple(fetched.values())
         else:
-            give, late = held(give, *backs), grad
+            give, late = held(give, *backs), (*grad, out_vec)
         own, *sent = merged(kept, xored(give, "tensor", 1), rows, *late)
         backs = [xored(out, "dp", slot + 1) for slot, out in enumerate(sent)][::-1]
         if grad:

time: 77.3 us -> 77.4 us (level)
  local copies, waits for them, and re-layouts: 5.74 us -> 7.2 us
  Pallas kernels: 26.8 us -> 25.7 us
    unnamed x36, local copies, waits for them, and re-layouts: 4.43 us -> 5.26 us
    pallas_call x6, Pallas kernels: 0.9 us -> 0.1 us  [held(): pl.pallas_call(held_kernel, in_specs=[RESIDENT] + [ANYWHERE] * len(events...]
  transfers between devices with their start and end apart: 20 -> 20, of which waited for: 8 -> 7; matrix products, arithmetic and copies ran while one was open for 6% -> 7% of each run, Pallas kernels for 33% -> 33%
where the time goes in v15:
time: 77.4 us; the launch traced here: 77.1 us
  Pallas kernels  25.7 us (33%)
  starting transfers between devices  22.3 us (29%)
  waiting for transfers between devices  16.9 us (22%)
  local copies, waits for them, and re-layouts  7.2 us (9%)
  other arithmetic  2.14 us (3%)
  matrix products  1.87 us (2%)
  between operations  1.04 us (1%)
    ppermute x18, starting transfers between devices, xored(): return lax.ppermute(block, axis, [(i, i ^ bits) for i in range(n)])  19.1 us
    pallas_call x2, Pallas kernels, expert(): pl.pallas_call(functools.partial(expert_kernel, chunk, tile_f, tile_d), i...  18.7 us
    ppermute x18, waiting for transfers between devices, xored(): return lax.ppermute(block, axis, [(i, i ^ bits) for i in range(n)])  14.2 us
    pallas_call x1, Pallas kernels, slopes(): pl.pallas_call(functools.partial(slope_kernel, groups), grid_spec=pltpu.P...  6.27 us
    unnamed x36, local copies, waits for them, and re-layouts  5.26 us
    ppermute x2, starting transfers between devices, below(): lax.ppermute(block, 'section', [(s, (s - 1) % sections) for s in range(se...  3.13 us
    ppermute x2, waiting for transfers between devices, below(): lax.ppermute(block, 'section', [(s, (s - 1) % sections) for s in range(se...  2.63 us
    broadcast_in_dim x2, other arithmetic, per_device(): return (handed[None], features[None])  1.6 us
  transfers between devices with their start and end apart: 20, of which 7 were waited for; matrix products, arithmetic and copies ran while one was open for 7% of the time, Pallas kernels for 33%

profile of v15, /device:TPU:0, one launch (start us, length us, event | category | flops | bytes accessed | tf_op | source)
XLA Modules:
  0.0 77.1 jit_solution(5477546579963078951)
XLA Ops:
  0.7 1.0 %constant_dynamic-update-slice_fusion.2 = (bf16[256,2048]{1,0:T(8,128)(2,1)S(1)}, bf16[32,2048]{1,0:T(8,128)(2,1)S(1)}) fusion(bf16[1,128,2048]{2,1,0:T(8,128)(2,1)} %param.10, s32[]{:T(128)S(6)} %select_n.53), kind=kLoop, calls=%fused_computation.42 | loop fusion | bytes 393220
  1.6 4.1 %collective-permute-start.1 = (bf16[32,2048]{1,0:T(8,128)(2,1)S(1)}, bf16[32,2048]{1,0:T(8,128)(2,1)S(1)}, u32[]{:S(2)}, u32[]{:S(2)}) collective-permute-start(bf16[32,2048]{1,0:T(8,128)(2,1)S(1)} %get-tuple-element.41.cot_ref), channel_id=1, source_target_pairs={{0,8},{4,12},{8,0},{12,4},{1,9},{5,13},{9,1},{13,5},{2,10},{6,14},... | collective-permute-start | bytes 393224 | tf_op jit(solution)/shard_map/ppermute | solution.py:17
  5.7 1.3 %collective-permute-start.2 = (bf16[32,2048]{1,0:T(8,128)(2,1)S(1)}, bf16[32,2048]{1,0:T(8,128)(2,1)S(1)}, u32[]{:S(2)}, u32[]{:S(2)}) collective-permute-start(bf16[32,2048]{1,0:T(8,128)(2,1)S(1)} %get-tuple-element.41.cot_ref), channel_id=1, source_target_pairs={{0,12},{4,8},{8,4},{12,0},{1,13},{5,9},{9,5},{13,1},{2,14},{6,10},... | collective-permute-start | bytes 393224 | tf_op jit(solution)/shard_map/ppermute | solution.py:17
  8.4 2.0 %copy-done.1 = bf16[1,1,4,128,3584]{4,3,2,1,0:T(8,128)(2,1)S(1)} copy-done((bf16[1,1,4,128,3584]{4,3,2,1,0:T(8,128)(2,1)S(1)}, bf16[1,1,4,128,3584]{4,3,2,1,0:T(8,128)(2,1)}, u32[]{:S(2)}) %copy-start.1) | copy-done | bytes 3670040
  10.5 1.0 %copy-done.2 = bf16[1,1,3584,64]{2,3,1,0:T(8,128)(2,1)S(1)} copy-done((bf16[1,1,3584,64]{2,3,1,0:T(8,128)(2,1)S(1)}, bf16[1,1,3584,64]{2,3,1,0:T(8,128)(2,1)}, u32[]{:S(2)}) %copy-start.2) | copy-done | bytes 458776
  11.5 6.3 %slopes.1 = (bf16[2,3584,256]{2,1,0:T(8,128)(2,1)S(1)}, f32[2,256,64]{2,1,0:T(8,128)S(1)}, bf16[3584,2048]{1,0:T(8,128)(2,1)S(1)}) custom-call(s32[2]{0:T(128)S(1)} %pad_add_fusion.index_ref, bf16[4,2,2,32,3584]{4,3,2,1,0:T(8,128)(2,1)S(1)} %bitcast.52, bf16[4,2,2,32,3584]{4,3,2,1,0:T(8,128)(2,1)S(1)} %bitcast.53, bf16[4,2,2,32,3584]{4,3,2,1,0:T(8,128)(2,1)S(1)} %bitcast.54, ...), custom_call_target="tpu_custom_call" | custom-call | flops 234881024 | bytes 7340032 | tf_op jit(solution)/shard_map/slopes/pallas_call | solution.py:149
  17.9 2.1 %collective-permute-done.refs_0_ = bf16[64,2048]{1,0:T(8,128)(2,1)S(1)} collective-permute-done((bf16[64,2048]{1,0:T(8,128)(2,1)S(1)}, bf16[64,2048]{1,0:T(8,128)(2,1)S(1)}, u32[]{:S(2)}, u32[]{:S(2)}) %collective-permute-start) | collective-permute-done | bytes 262176 | tf_op jit(solution)/shard_map/ppermute | solution.py:17
  20.2 1.4 %collective-permute-start.6 = (bf16[32,2048]{1,0:T(8,128)(2,1)S(1)}, bf16[32,2048]{1,0:T(8,128)(2,1)S(1)}, u32[]{:S(2)}, u32[]{:S(2)}) collective-permute-start(bf16[32,2048]{1,0:T(8,128)(2,1)S(1)} %held.6), channel_id=1, source_target_pairs={{0,8},{4,12},{8,0},{12,4},{1,9},{5,13},{9,1},{13,5},{2,10},{6,14},... | collective-permute-start | bytes 393224 | tf_op jit(solution)/shard_map/ppermute | solution.py:17
  21.6 2.0 %collective-permute-start.5 = (bf16[32,2048]{1,0:T(8,128)(2,1)S(1)}, bf16[32,2048]{1,0:T(8,128)(2,1)S(1)}, u32[]{:S(2)}, u32[]{:S(2)}) collective-permute-start(bf16[32,2048]{1,0:T(8,128)(2,1)S(1)} %held.6), channel_id=1, source_target_pairs={{0,12},{4,8},{8,4},{12,0},{1,13},{5,9},{9,5},{13,1},{2,14},{6,10},... | collective-permute-start | bytes 393224 | tf_op jit(solution)/shard_map/ppermute | solution.py:17
  23.7 9.4 %expert.2 = (f32[128,2176]{1,0:T(8,128)S(1)}, bf16[128,2176]{1,0:T(8,128)(2,1)S(1)}) custom-call(bf16[256,2048]{1,0:T(8,128)(2,1)S(1)} %slice_dynamic-update-slice_fusion.4.rows_ref, bf16[2,3584,256]{2,1,0:T(8,128)(2,1)S(1)} %get-tuple-element.21.slope_ref, f32[2,256,64]{2,1,0:T(8,128)S(1)} %get-tuple-element.22.down_part_ref, ...), custom_call_target="tpu_custom_call" | custom-call | flops 7516192768 | bytes 29360128 | tf_op jit(solution)/shard_map/expert/pallas_call | solution.py:237
  33.5 1.6 %collective-permute-done.4.came_ref = bf16[128,2176]{1,0:T(8,128)(2,1)S(1)} collective-permute-done((bf16[128,2176]{1,0:T(8,128)(2,1)S(1)}, bf16[128,2176]{1,0:T(8,128)(2,1)S(1)}, u32[]{:S(2)}, u32[]{:S(2)}) %collective-permute-start.4) | collective-permute-done | bytes 557088 | tf_op jit(solution)/shard_map/ppermute | solution.py:17
  35.5 1.8 %collective-permute-start.7 = (bf16[32,2176]{1,0:T(8,128)(2,1)S(1)}, bf16[32,2176]{1,0:T(8,128)(2,1)S(1)}, u32[]{:S(2)}, u32[]{:S(2)}) collective-permute-start(bf16[32,2176]{1,0:T(8,128)(2,1)S(1)} %get-tuple-element.27.refs_2_), channel_id=1, source_target_pairs={{0,12},{4,8},{8,4},{12,0},{1,13},{5,9},{9,5},{13,1},{2,14},{6,10},... | collective-permute-start | bytes 417800 | tf_op jit(solution)/shard_map/ppermute | solution.py:17
  37.9 2.1 %collective-permute-start.9 = (bf16[32,2176]{1,0:T(8,128)(2,1)S(1)}, bf16[32,2176]{1,0:T(8,128)(2,1)S(1)}, u32[]{:S(2)}, u32[]{:S(2)}) collective-permute-start(bf16[32,2176]{1,0:T(8,128)(2,1)S(1)} %get-tuple-element.29.refs_0_), channel_id=1, source_target_pairs={{0,4},{4,0},{8,12},{12,8},{1,5},{5,1},{9,13},{13,9},{2,6},{6,2},{1... | collective-permute-start | bytes 417800 | tf_op jit(solution)/shard_map/ppermute | solution.py:17
  40.0 9.4 %expert.3 = (f32[128,2176]{1,0:T(8,128)S(1)}, bf16[128,2176]{1,0:T(8,128)(2,1)S(1)}) custom-call(bf16[256,2048]{1,0:T(8,128)(2,1)S(1)} %slice_dynamic-update-slice_fusion.rows_ref, bf16[2,3584,256]{2,1,0:T(8,128)(2,1)S(1)} %get-tuple-element.21.slope_ref, f32[2,256,64]{2,1,0:T(8,128)S(1)} %get-tuple-element.22.down_part_ref, bf16[64,3584]{1,0:T(8,128)(2,1)S(1)} %bitcast.62, ...), custom_call_target="tpu_custom_call" | custom-call | flops 7516192768 | bytes 29360128 | tf_op jit(solution)/shard_map/expert/pallas_call | solution.py:237
  49.4 1.5 %collective-permute-done.8.refs_1_ = bf16[32,2176]{1,0:T(8,128)(2,1)S(1)} collective-permute-done((bf16[32,2176]{1,0:T(8,128)(2,1)S(1)}, bf16[32,2176]{1,0:T(8,128)(2,1)S(1)}, u32[]{:S(2)}, u32[]{:S(2)}) %collective-permute-start.8) | collective-permute-done | bytes 139296 | tf_op jit(solution)/shard_map/ppermute | solution.py:17
  51.3 1.3 %fusion = f32[128,64]{0,1:T(8,128)S(1)} fusion(bf16[1,128,2048]{2,1,0:T(8,128)(2,1)} %param.10, bf16[1,2048,64]{1,2,0:T(8,128)(2,1)S(1)} %copy-done), kind=kOutput, calls=%fused_computation.4 | convolution fusion | flops 33554432 | bytes 819200 | tf_op jit(solution)/shard_map/dot_general | solution.py:311
  54.5 2.4 %collective-permute-start.12 = (bf16[32,2176]{1,0:T(8,128)(2,1)S(1)}, bf16[32,2176]{1,0:T(8,128)(2,1)S(1)}, u32[]{:S(2)}, u32[]{:S(2)}) collective-permute-start(bf16[32,2176]{1,0:T(8,128)(2,1)S(1)} %get-tuple-element.33), channel_id=1, source_target_pairs={{0,12},{4,8},{8,4},{12,0},{1,13},{5,9},{9,5},{13,1},{2,14},{6,10},... | collective-permute-start | bytes 417800 | tf_op jit(solution)/shard_map/ppermute | solution.py:17
  57.1 2.0 %collective-permute-start.16 = (bf16[32,2176]{1,0:T(8,128)(2,1)S(1)}, bf16[32,2176]{1,0:T(8,128)(2,1)S(1)}, u32[]{:S(2)}, u32[]{:S(2)}) collective-permute-start(bf16[32,2176]{1,0:T(8,128)(2,1)S(1)} %get-tuple-element.36), channel_id=1, source_target_pairs={{0,4},{4,0},{8,12},{12,8},{1,5},{5,1},{9,13},{13,9},{2,6},{6,2},{1... | collective-permute-start | bytes 417800 | tf_op jit(solution)/shard_map/ppermute | solution.py:17
  59.2 3.8 %collective-permute-done.12.refs_0_ = bf16[32,2176]{1,0:T(8,128)(2,1)S(1)} collective-permute-done((bf16[32,2176]{1,0:T(8,128)(2,1)S(1)}, bf16[32,2176]{1,0:T(8,128)(2,1)S(1)}, u32[]{:S(2)}, u32[]{:S(2)}) %collective-permute-start.12) | collective-permute-done | bytes 139296 | tf_op jit(solution)/shard_map/ppermute | solution.py:17
  63.0 1.6 %collective-permute-start.13 = (bf16[32,2048]{1,0:T(8,128)(2,1)S(1)}, bf16[32,2048]{1,0:T(8,128)(2,1)S(1)}, u32[]{:S(2)}, u32[]{:S(2)}) collective-permute-start(bf16[32,2048]{1,0:T(8,128)(2,1)S(1)} %held.11), channel_id=1, source_target_pairs={{0,2},{2,0},{1,3},{3,1},{4,6},{6,4},{5,7},{7,5},{8,10},{10,8},{9,1... | collective-permute-start | bytes 393224 | tf_op jit(solution)/shard_map/ppermute | solution.py:293
  64.7 3.9 %collective-permute-done.15.refs_1_ = bf16[32,2176]{1,0:T(8,128)(2,1)S(1)} collective-permute-done((bf16[32,2176]{1,0:T(8,128)(2,1)S(1)}, bf16[32,2176]{1,0:T(8,128)(2,1)S(1)}, u32[]{:S(2)}, u32[]{:S(2)}) %collective-permute-start.15) | collective-permute-done | bytes 139296 | tf_op jit(solution)/shard_map/ppermute | solution.py:17
  69.0 1.5 %collective-permute-start.17 = (bf16[32,2048]{1,0:T(8,128)(2,1)S(1)}, bf16[32,2048]{1,0:T(8,128)(2,1)S(1)}, u32[]{:S(2)}, u32[]{:S(2)}) collective-permute-start(bf16[32,2048]{1,0:T(8,128)(2,1)S(1)} %get-tuple-element.37), channel_id=1, source_target_pairs={{0,2},{2,0},{1,3},{3,1},{4,6},{6,4},{5,7},{7,5},{8,10},{10,8},{9,1... | collective-permute-start | bytes 393224 | tf_op jit(solution)/shard_map/ppermute | solution.py:293
  72.2 2.6 %collective-permute-done.17 = bf16[32,2048]{1,0:T(8,128)(2,1)S(1)} collective-permute-done((bf16[32,2048]{1,0:T(8,128)(2,1)S(1)}, bf16[32,2048]{1,0:T(8,128)(2,1)S(1)}, u32[]{:S(2)}, u32[]{:S(2)}) %collective-permute-start.17) | collective-permute-done | bytes 131104 | tf_op jit(solution)/shard_map/ppermute | solution.py:293
  74.9 1.3 %collective-permute-done.18 = bf16[32,2048]{1,0:T(8,128)(2,1)S(1)} collective-permute-done((bf16[32,2048]{1,0:T(8,128)(2,1)S(1)}, bf16[32,2048]{1,0:T(8,128)(2,1)S(1)}, u32[]{:S(2)}, u32[]{:S(2)}) %collective-permute-start.18) | collective-permute-done | bytes 131104 | tf_op jit(solution)/shard_map/ppermute | solution.py:17
  (90 shorter events, 8.5 us)
Async XLA Ops:
  0.6 50.6 %copy-start = (bf16[1,2048,64]{1,2,0:T(8,128)(2,1)S(1)}, bf16[1,2048,64]{1,2,0:T(8,128)(2,1)}, u32[]{:S(2)}) copy-start(bf16[1,2048,64]{1,2,0:T(8,128)(2,1)} %param.17) | copy-start | bytes 786436
  1.6 16.2 %collective-permute-start.1 = (bf16[32,2048]{1,0:T(8,128)(2,1)S(1)}, bf16[32,2048]{1,0:T(8,128)(2,1)S(1)}, u32[]{:S(2)}, u32[]{:S(2)}) collective-permute-start(bf16[32,2048]{1,0:T(8,128)(2,1)S(1)} %get-tuple-element.41.cot_ref), channel_id=1, source_target_pairs={{0,8},{4,12},{8,0},{12,4},{1,9},{5,13},{9,1},{13,5},{2,10},{6,14},... | collective-permute-start | bytes 393224 | tf_op jit(solution)/shard_map/ppermute | solution.py:17
  5.7 12.1 %collective-permute-start.2 = (bf16[32,2048]{1,0:T(8,128)(2,1)S(1)}, bf16[32,2048]{1,0:T(8,128)(2,1)S(1)}, u32[]{:S(2)}, u32[]{:S(2)}) collective-permute-start(bf16[32,2048]{1,0:T(8,128)(2,1)S(1)} %get-tuple-element.41.cot_ref), channel_id=1, source_target_pairs={{0,12},{4,8},{8,4},{12,0},{1,13},{5,9},{9,5},{13,1},{2,14},{6,10},... | collective-permute-start | bytes 393224 | tf_op jit(solution)/shard_map/ppermute | solution.py:17
  8.0 11.9 %collective-permute-start = (bf16[64,2048]{1,0:T(8,128)(2,1)S(1)}, bf16[64,2048]{1,0:T(8,128)(2,1)S(1)}, u32[]{:S(2)}, u32[]{:S(2)}) collective-permute-start(bf16[64,2048]{1,0:T(8,128)(2,1)S(1)} %dynamic-slice_bitcast_fusion), channel_id=1, source_target_pairs={{0,4},{4,0},{8,12},{12,8},{1,5},{5,1},{9,13},{13,9},{2,6},{6,2},{1... | collective-permute-start | bytes 786440 | tf_op jit(solution)/shard_map/ppermute | solution.py:17
  11.5 8.6 %copy-start.5 = (bf16[1,128,2048]{2,1,0:T(8,128)(2,1)S(1)}, bf16[1,128,2048]{2,1,0:T(8,128)(2,1)}, u32[]{:S(2)}) copy-start(bf16[1,128,2048]{2,1,0:T(8,128)(2,1)} %param.10) | copy-start | bytes 1572868
  20.0 3.6 %collective-permute-start.3 = (bf16[128,2048]{1,0:T(8,128)(2,1)S(1)}, bf16[128,2048]{1,0:T(8,128)(2,1)S(1)}, u32[]{:S(2)}, u32[]{:S(2)}) collective-permute-start(bf16[128,2048]{1,0:T(8,128)(2,1)S(1)} %pad_maximum_fusion), channel_id=1, source_target_pairs={{0,1},{1,0},{2,3},{3,2},{4,5},{5,4},{6,7},{7,6},{8,9},{9,8},{10,11... | collective-permute-start | bytes 1572872 | tf_op jit(solution)/shard_map/ppermute | solution.py:17
  20.2 13.1 %collective-permute-start.6 = (bf16[32,2048]{1,0:T(8,128)(2,1)S(1)}, bf16[32,2048]{1,0:T(8,128)(2,1)S(1)}, u32[]{:S(2)}, u32[]{:S(2)}) collective-permute-start(bf16[32,2048]{1,0:T(8,128)(2,1)S(1)} %held.6), channel_id=1, source_target_pairs={{0,8},{4,12},{8,0},{12,4},{1,9},{5,13},{9,1},{13,5},{2,10},{6,14},... | collective-permute-start | bytes 393224 | tf_op jit(solution)/shard_map/ppermute | solution.py:17
  21.6 11.8 %collective-permute-start.5 = (bf16[32,2048]{1,0:T(8,128)(2,1)S(1)}, bf16[32,2048]{1,0:T(8,128)(2,1)S(1)}, u32[]{:S(2)}, u32[]{:S(2)}) collective-permute-start(bf16[32,2048]{1,0:T(8,128)(2,1)S(1)} %held.6), channel_id=1, source_target_pairs={{0,12},{4,8},{8,4},{12,0},{1,13},{5,9},{9,5},{13,1},{2,14},{6,10},... | collective-permute-start | bytes 393224 | tf_op jit(solution)/shard_map/ppermute | solution.py:17
  33.1 2.0 %collective-permute-start.4 = (bf16[128,2176]{1,0:T(8,128)(2,1)S(1)}, bf16[128,2176]{1,0:T(8,128)(2,1)S(1)}, u32[]{:S(2)}, u32[]{:S(2)}) collective-permute-start(bf16[128,2176]{1,0:T(8,128)(2,1)S(1)} %get-tuple-element.25), channel_id=1, source_target_pairs={{0,1},{1,0},{2,3},{3,2},{4,5},{5,4},{6,7},{7,6},{8,9},{9,8},{10,11... | collective-permute-start | bytes 1671176 | tf_op jit(solution)/shard_map/ppermute | solution.py:17
  35.2 4.7 %collective-permute-start.10 = (bf16[64,2048]{1,0:T(8,128)(2,1)S(1)}, bf16[64,2048]{1,0:T(8,128)(2,1)S(1)}, u32[]{:S(2)}, u32[]{:S(2)}) collective-permute-start(bf16[64,2048]{1,0:T(8,128)(2,1)S(1)} %held.9), channel_id=1, source_target_pairs={{0,1},{1,0},{2,3},{3,2},{4,5},{5,4},{6,7},{7,6},{8,9},{9,8},{10,11... | collective-permute-start | bytes 786440 | tf_op jit(solution)/shard_map/ppermute | solution.py:17
  35.5 13.9 %collective-permute-start.7 = (bf16[32,2176]{1,0:T(8,128)(2,1)S(1)}, bf16[32,2176]{1,0:T(8,128)(2,1)S(1)}, u32[]{:S(2)}, u32[]{:S(2)}) collective-permute-start(bf16[32,2176]{1,0:T(8,128)(2,1)S(1)} %get-tuple-element.27.refs_2_), channel_id=1, source_target_pairs={{0,12},{4,8},{8,4},{12,0},{1,13},{5,9},{9,5},{13,1},{2,14},{6,10},... | collective-permute-start | bytes 417800 | tf_op jit(solution)/shard_map/ppermute | solution.py:17
  37.3 13.6 %collective-permute-start.8 = (bf16[32,2176]{1,0:T(8,128)(2,1)S(1)}, bf16[32,2176]{1,0:T(8,128)(2,1)S(1)}, u32[]{:S(2)}, u32[]{:S(2)}) collective-permute-start(bf16[32,2176]{1,0:T(8,128)(2,1)S(1)} %get-tuple-element.28.refs_1_), channel_id=1, source_target_pairs={{0,8},{4,12},{8,0},{12,4},{1,9},{5,13},{9,1},{13,5},{2,10},{6,14},... | collective-permute-start | bytes 417800 | tf_op jit(solution)/shard_map/ppermute | solution.py:17
  37.9 13.0 %collective-permute-start.9 = (bf16[32,2176]{1,0:T(8,128)(2,1)S(1)}, bf16[32,2176]{1,0:T(8,128)(2,1)S(1)}, u32[]{:S(2)}, u32[]{:S(2)}) collective-permute-start(bf16[32,2176]{1,0:T(8,128)(2,1)S(1)} %get-tuple-element.29.refs_0_), channel_id=1, source_target_pairs={{0,4},{4,0},{8,12},{12,8},{1,5},{5,1},{9,13},{13,9},{2,6},{6,2},{1... | collective-permute-start | bytes 417800 | tf_op jit(solution)/shard_map/ppermute | solution.py:17
  40.0 11.0 %copy-start.8 = (s32[1,1,2]{2,1,0:T(1,128)S(1)}, s32[1,1,2]{2,1,0:T(1,128)}, u32[]{:S(2)}) copy-start(s32[1,1,2]{2,1,0:T(1,128)} %param.11) | copy-start | bytes 28
  49.4 21.5 %copy-start.6 = (f32[1,128,64]{1,2,0:T(8,128)S(1)}, f32[1,128,64]{1,2,0:T(8,128)}, u32[]{:S(2)}) copy-start(f32[1,128,64]{1,2,0:T(8,128)} %param.16) | copy-start | bytes 98308
  50.9 2.6 %collective-permute-start.11 = (bf16[128,2176]{1,0:T(8,128)(2,1)S(1)}, bf16[128,2176]{1,0:T(8,128)(2,1)S(1)}, u32[]{:S(2)}, u32[]{:S(2)}) collective-permute-start(bf16[128,2176]{1,0:T(8,128)(2,1)S(1)} %held.10), channel_id=1, source_target_pairs={{0,1},{1,0},{2,3},{3,2},{4,5},{5,4},{6,7},{7,6},{8,9},{9,8},{10,11... | collective-permute-start | bytes 1671176 | tf_op jit(solution)/shard_map/ppermute | solution.py:17
  54.5 8.5 %collective-permute-start.12 = (bf16[32,2176]{1,0:T(8,128)(2,1)S(1)}, bf16[32,2176]{1,0:T(8,128)(2,1)S(1)}, u32[]{:S(2)}, u32[]{:S(2)}) collective-permute-start(bf16[32,2176]{1,0:T(8,128)(2,1)S(1)} %get-tuple-element.33), channel_id=1, source_target_pairs={{0,12},{4,8},{8,4},{12,0},{1,13},{5,9},{9,5},{13,1},{2,14},{6,10},... | collective-permute-start | bytes 417800 | tf_op jit(solution)/shard_map/ppermute | solution.py:17
  57.1 11.5 %collective-permute-start.15 = (bf16[32,2176]{1,0:T(8,128)(2,1)S(1)}, bf16[32,2176]{1,0:T(8,128)(2,1)S(1)}, u32[]{:S(2)}, u32[]{:S(2)}) collective-permute-start(bf16[32,2176]{1,0:T(8,128)(2,1)S(1)} %get-tuple-element.35), channel_id=1, source_target_pairs={{0,8},{4,12},{8,0},{12,4},{1,9},{5,13},{9,1},{13,5},{2,10},{6,14},... | collective-permute-start | bytes 417800 | tf_op jit(solution)/shard_map/ppermute | solution.py:17
  57.1 11.4 %collective-permute-start.16 = (bf16[32,2176]{1,0:T(8,128)(2,1)S(1)}, bf16[32,2176]{1,0:T(8,128)(2,1)S(1)}, u32[]{:S(2)}, u32[]{:S(2)}) collective-permute-start(bf16[32,2176]{1,0:T(8,128)(2,1)S(1)} %get-tuple-element.36), channel_id=1, source_target_pairs={{0,4},{4,0},{8,12},{12,8},{1,5},{5,1},{9,13},{13,9},{2,6},{6,2},{1... | collective-permute-start | bytes 417800 | tf_op jit(solution)/shard_map/ppermute | solution.py:17
  63.0 5.6 %collective-permute-start.13 = (bf16[32,2048]{1,0:T(8,128)(2,1)S(1)}, bf16[32,2048]{1,0:T(8,128)(2,1)S(1)}, u32[]{:S(2)}, u32[]{:S(2)}) collective-permute-start(bf16[32,2048]{1,0:T(8,128)(2,1)S(1)} %held.11), channel_id=1, source_target_pairs={{0,2},{2,0},{1,3},{3,1},{4,6},{6,4},{5,7},{7,5},{8,10},{10,8},{9,1... | collective-permute-start | bytes 393224 | tf_op jit(solution)/shard_map/ppermute | solution.py:293
  68.8 1.9 %collective-permute-start.19 = (f32[64,128]{1,0:T(8,128)S(1)}, f32[64,128]{1,0:T(8,128)S(1)}, u32[]{:S(2)}, u32[]{:S(2)}) collective-permute-start(f32[64,128]{1,0:T(8,128)S(1)} %constant_dynamic-update-slice_fusion.6), channel_id=1, source_target_pairs={{0,1},{1,0},{2,3},{3,2},{4,5},{5,4},{6,7},{7,6},{8,9},{9,8},{10,11... | collective-permute-start | bytes 98312 | tf_op jit(solution)/shard_map/ppermute | solution.py:17
  69.0 5.8 %collective-permute-start.17 = (bf16[32,2048]{1,0:T(8,128)(2,1)S(1)}, bf16[32,2048]{1,0:T(8,128)(2,1)S(1)}, u32[]{:S(2)}, u32[]{:S(2)}) collective-permute-start(bf16[32,2048]{1,0:T(8,128)(2,1)S(1)} %get-tuple-element.37), channel_id=1, source_target_pairs={{0,2},{2,0},{1,3},{3,1},{4,6},{6,4},{5,7},{7,5},{8,10},{10,8},{9,1... | collective-permute-start | bytes 393224 | tf_op jit(solution)/shard_map/ppermute | solution.py:293
  70.6 4.3 %collective-permute-start.14 = (bf16[32,2048]{1,0:T(8,128)(2,1)S(1)}, bf16[32,2048]{1,0:T(8,128)(2,1)S(1)}, u32[]{:S(2)}, u32[]{:S(2)}) collective-permute-start(bf16[32,2048]{1,0:T(8,128)(2,1)S(1)} %collective-permute-done.13.refs_3_), channel_id=1, source_target_pairs={{0,1},{1,0},{2,3},{3,2},{4,5},{5,4},{6,7},{7,6},{8,9},{9,8},{10,11... | collective-permute-start | bytes 393224 | tf_op jit(solution)/shard_map/ppermute | solution.py:17
  74.8 1.3 %collective-permute-start.18 = (bf16[32,2048]{1,0:T(8,128)(2,1)S(1)}, bf16[32,2048]{1,0:T(8,128)(2,1)S(1)}, u32[]{:S(2)}, u32[]{:S(2)}) collective-permute-start(bf16[32,2048]{1,0:T(8,128)(2,1)S(1)} %collective-permute-done.17), channel_id=1, source_target_pairs={{0,1},{1,0},{2,3},{3,2},{4,5},{5,4},{6,7},{7,6},{8,9},{9,8},{10,11... | collective-permute-start | bytes 393224 | tf_op jit(solution)/shard_map/ppermute | solution.py:17
  (6 other events, 23.7 us)
